TPU v7x, 256 devices: a whole 4x4x8 slice. The times are simulated.
256 devices in a mesh: sta: 16 (over z, y_lo), seg: 16 (over y_hi, x, core).
Axes of the slice: x: 4, y: 4 (y_hi: 2, y_lo: 2; y = y_hi * 2 + y_lo), z: 8, core: 2. Of those that a mesh axis runs over, the one named last changes fastest.
Arguments:
- spectra: bfloat16 [2, 32, 512, 4096], P(None, 'seg', None, 'sta'), may hold values from -6 to 6
- bin_index: int32 [512], replicated, may hold values from 0 to 4096
Outputs:
- correlation: float32 [2, 4096, 4096], P(None, ('sta', 'seg'))
All inputs are finite; a program needn't handle non-finite values.
Results may differ from a plain program's by a relative error of at most 0.012.
Values may be sent and summed in bfloat16 or wider, within the bound.
No kernel may reach another device: no remote copies, remote signals or barrier semaphores. Data moves between devices by JAX's collectives and lax.ppermute only.
A program may use at most 64 MiB of HBM per device.

v0:
```python
import math

import jax
import jax.numpy as jnp
from jax import lax
from jax.sharding import Mesh
from jax.sharding import PartitionSpec as P

NFFT = 8192
LAGS = 2
LAG_STEP = 37
HALF = 64
STA = ("sta_0", "sta_1")
STA_SEG = ("sta_0", "sta_1", "seg")


def gather_axes(x, axes, dim):
    if not axes:
        return x
    nearer = lax.all_gather(x, axes[-1], axis=dim, tiled=True)
    return gather_axes(nearer, axes[:-1], dim)


def whiten(spectra):
    values = spectra.astype(jnp.float32)
    energy = values[0] * values[0] + values[1] * values[1]
    freq_bins = values.shape[2]
    bin_pos = jnp.arange(freq_bins, dtype=jnp.int32)
    window = (jnp.abs(bin_pos[:, None] - bin_pos[None, :]) <= HALF).astype(jnp.float32)
    bin_count = jnp.sum(window, axis=1)
    smoothed = (
        jnp.einsum("gf,sfc->sgc", window, energy, precision=lax.Precision.HIGHEST)
        / bin_count[None, :, None]
    )
    return (values / jnp.sqrt(smoothed + 1e-06)[None]).astype(jnp.bfloat16)


def phases(bin_index):
    lag_samples = (jnp.arange(LAGS, dtype=jnp.int32) + 1) * LAG_STEP
    phase_turn = lag_samples[:, None] * bin_index[None, :] % NFFT
    phase_angle = 2.0 * math.pi / NFFT * phase_turn.astype(jnp.float32)
    return (jnp.cos(phase_angle), jnp.sin(phase_angle))


def rotate(whitened, cosine, sine_part):
    real_part = whitened[0].astype(jnp.float32)[None]
    imag_part = whitened[1].astype(jnp.float32)[None]
    cos_part = cosine[:, None, :, None]
    sin_part = sine_part[:, None, :, None]
    rot_real = real_part * cos_part - imag_part * sin_part
    rot_imag = real_part * sin_part + imag_part * cos_part
    stacked = jnp.stack([rot_real, rot_imag], axis=1).astype(jnp.bfloat16)
    return stacked.reshape(cosine.shape[0], -1, whitened.shape[3])


def pair_block(rotated, columns, norm_scale):
    product = jnp.einsum("mki,kj->mij", rotated, columns, preferred_element_type=jnp.float32)
    return (product * norm_scale).astype(jnp.bfloat16)


def body(spectra, bin_index):
    whitened = whiten(spectra)
    cosine, sine_part = phases(bin_index)
    seg_local = whitened.shape[1]
    freq_bins = whitened.shape[2]
    norm_scale = 1.0 / math.sqrt(seg_local * lax.axis_size("seg") * freq_bins)
    rotated = rotate(whitened, cosine, sine_part)
    shard_cols = gather_axes(whitened, STA, 3)
    columns = shard_cols.reshape(-1, shard_cols.shape[3])
    product = pair_block(rotated, columns, norm_scale)
    return lax.psum_scatter(product, "seg", scatter_dimension=1, tiled=True).astype(jnp.float32)


def solution(mesh):
    torus = Mesh(mesh.devices.reshape(8, 2, mesh.shape["seg"]), ("sta_0", "sta_1", "seg"))
    placed = (P(None, "seg", None, STA), P())
    return jax.shard_map(
        body, mesh=torus, in_specs=placed, out_specs=P(None, STA_SEG, None), check_vma=False
    )
```

profile of v0, /device:TPU:1, one launch (start us, length us, event | category | flops | bytes accessed | tf_op | source)
XLA Modules:
  0.0 338.2 jit_solution(11787432547748694073)
XLA Ops:
  6.5 0.0 all-gather.3.cloned.1.call-start
  6.5 0.2 convert_reduce_fusion
  6.7 1.4 convert_element_type.30
  8.1 2.0 fusion.10
  10.2 0.0 copy-start.1
  10.2 0.3 copy.4
  10.5 0.9 copy-done.1
  11.4 1.3 divide_convert_fusion
  12.7 0.0 copy-start
  12.7 0.0 all-gather.3.cloned.1.call-update
  12.7 0.0 all-gather.5.cloned.1.call-start
  12.8 42.1 %all-gather.3.cloned.1.call-done = bf16[2,2,512,512]{3,2,1,0:T(8,128)(2,1)} async-done(((bf16[2,2,512,256]{3,2,1,0:T(8,128)(2,1)}), bf16[2,2,512,512]{3,2,1,0:T(8,128)(2,1)}) %all-gather.3.cloned.1.call-update) | async-done | bytes 2097168 | tf_op jit(solution)/shard_map/all_gather | solution.py:20
  54.9 0.0 all-gather.5.cloned.1.call-update
  54.9 0.0 reduce-scatter.2.cloned.1.call-start
  54.9 0.0 copy-done
  54.9 0.2 fusion.16
  55.1 0.0 copy-start.2
  55.1 0.3 copy.5
  55.5 0.3 copy.6
  55.8 0.0 copy-done.2
  55.8 0.2 fusion.22
  56.0 1.6 subtract_convert_fusion
  57.6 172.8 %all-gather.5.cloned.1.call-done = bf16[2,2,512,4096]{3,2,1,0:T(8,128)(2,1)} async-done(((bf16[2,2,512,512]{3,2,1,0:T(8,128)(2,1)}), bf16[2,2,512,4096]{3,2,1,0:T(8,128)(2,1)}) %all-gather.5.cloned.1.call-update) | async-done | bytes 16777232 | tf_op jit(solution)/shard_map/all_gather | solution.py:20
  230.4 14.0 %fusion.2 = bf16[2,256,4096]{2,1,0:T(8,128)(2,1)} fusion(bf16[2,2,512,4096]{3,2,1,0:T(8,128)(2,1)} %all-gather.5.cloned.1.call-done, bf16[2,1,2,512,256]{3,4,2,1,0:T(8,128)(2,1)} %get-tuple-element.6, bf16[2,1,2,512,256]{3,4,2,1,0:T(8,128)(2,1)S(1)} %get-tuple-element.5), kind=kOutput, calls=%fused_computation.3 | convolution fusion | flops 8595177472 | bytes 23068672 | tf_op jit(solution)/shard_map/mki,kj->mij/dot_general | solution.py:57
  244.4 0.0 reduce-scatter.2.cloned.1.call-update
  244.4 85.4 %reduce-scatter.2.cloned.1.call-done = bf16[2,16,4096]{2,1,0:T(8,128)(2,1)} async-done(((bf16[2,256,4096]{2,1,0:T(8,128)(2,1)}), bf16[2,16,4096]{2,1,0:T(8,128)(2,1)}) %reduce-scatter.2.cloned.1.call-update) | async-done | bytes 262160 | tf_op jit(solution)/shard_map/reduce_scatter | solution.py:71
  329.9 1.8 convert_element_type.35
  (1 shorter events, 0.0 us)
Async XLA Ops:
  6.5 48.3 %all-gather.3.cloned.1.call-start = ((), (), s32[]{:S(2)}) async-start(), calls=%async_computation.1 | async-start | bytes 3145728 | tf_op jit(solution)/shard_map/all_gather | solution.py:20
  10.2 1.2 copy-start.1
  12.7 42.2 %copy-start = (bf16[2,2,512,256]{3,2,1,0:T(8,128)(2,1)S(1)}, bf16[2,2,512,256]{3,2,1,0:T(8,128)(2,1)}, u32[]{:S(2)}) copy-start(bf16[2,2,512,256]{3,2,1,0:T(8,128)(2,1)} %divide_convert_fusion) | copy-start | bytes 3145732
  12.7 217.7 %all-gather.5.cloned.1.call-start = ((), (), s32[]{:S(2)}) async-start(), calls=%async_computation.2 | async-start | bytes 18874368 | tf_op jit(solution)/shard_map/all_gather | solution.py:20
  54.9 275.0 %reduce-scatter.2.cloned.1.call-start = ((), (), s32[]{:S(2)}) async-start(), calls=%async_computation.3 | async-start | bytes 4456448 | tf_op jit(solution)/shard_map/reduce_scatter | solution.py:71
  55.1 0.7 copy-start.2
Sparse Core Ops, SparseCore 0:
  12.8 41.9 all-gather.2
  56.6 173.7 all-gather.4
  244.6 85.2 reduce-scatter.1
where the time goes:
time: 339 us; the launch traced here: 338 us
  waiting for transfers between devices  300 us (88%)
  matrix products  16 us (5%)
  between operations  13.2 us (4%)
  other arithmetic  6.58 us (2%)
    all_gather x2, waiting for transfers between devices, gather_axes(): nearer = lax.all_gather(x, axes[-1], axis=dim, tiled=True)  215 us
    reduce_scatter x1, waiting for transfers between devices, body(): lax.psum_scatter(product, 'seg', scatter_dimension=1, tiled=True)  85.4 us
    dot_general x1, matrix products, pair_block(): jnp.einsum('mki,kj->mij', rotated, columns, preferred_element_type=jnp.fl...  14 us
  transfers between devices with their start and end apart: 3, of which 3 were waited for; matrix products, arithmetic and copies ran while one was open for 1% of the time, Pallas kernels for 0%

commit v1 on v0

v1 whole, which is shorter than its diff:
```python
import math

import jax
import jax.numpy as jnp
import numpy as np
from jax import lax
from jax.experimental import pallas as pl
from jax.experimental.pallas import tpu as pltpu
from jax.sharding import Mesh
from jax.sharding import PartitionSpec as P

NFFT = 8192
LAGS = 2
LAG_STEP = 37
HALF = 64
BINS = 512
BLOCK = 256
DEPTH = 2048
AXES = ("z", "ylo", "yhi", "x", "c")
SIZES = (8, 2, 2, 4, 2)
F32 = jnp.float32
BF16 = jnp.bfloat16
MIB = 1 << 20


def dot_nt(a, b):
    return lax.dot_general(a, b, (((1,), (1,)), ((), ())), preferred_element_type=F32)


def params(mib, **kw):
    return pltpu.CompilerParams(vmem_limit_bytes=mib * MIB, **kw)


def cost(flops, bytes_accessed):
    return pl.CostEstimate(flops=flops, bytes_accessed=bytes_accessed, transcendentals=0)


def move(x, step):
    pairs = []
    for i, at in enumerate(np.ndindex(*SIZES)):
        to = tuple(int(v) % s for v, s in zip(step(*at), SIZES))
        pairs.append((i, int(np.ravel_multi_index(to, SIZES))))
    return lax.ppermute(x, AXES, pairs)


def sign(c):
    return 1 - 2 * c


def whiten_kernel(x_ref, o_ref):
    row = lax.broadcasted_iota(jnp.int32, (BINS, BINS), 0)
    col = lax.broadcasted_iota(jnp.int32, (BINS, BINS), 1)
    window = (jnp.abs(row - col) <= HALF).astype(F32).astype(BF16)
    pos = lax.broadcasted_iota(jnp.int32, (1, BINS), 1)
    count = jnp.minimum(pos + HALF, BINS - 1) - jnp.maximum(pos - HALF, 0) + 1
    inverse = 1.0 / count.astype(F32)
    for s in range(2):
        re = x_ref[0, s].astype(F32).T
        im = x_ref[1, s].astype(F32).T
        energy = re * re + im * im
        high = energy.astype(BF16)
        low = (energy - high.astype(F32)).astype(BF16)
        total = jnp.dot(high, window, preferred_element_type=F32)
        total += jnp.dot(low, window, preferred_element_type=F32)
        scale = lax.rsqrt(total * inverse + 1e-06)
        o_ref[:, s * BINS : (s + 1) * BINS] = (re * scale).astype(BF16)
        o_ref[:, (2 + s) * BINS : (3 + s) * BINS] = (im * scale).astype(BF16)


def whiten(spectra, half):
    return pl.pallas_call(
        whiten_kernel,
        grid=(1,),
        in_specs=[pl.BlockSpec((2, 2, BINS, 128), lambda i: (0, 0, 0, half))],
        out_specs=pl.BlockSpec((128, DEPTH), lambda i: (0, 0)),
        out_shape=jax.ShapeDtypeStruct((128, DEPTH), BF16),
        compiler_params=params(16),
        cost_estimate=cost(2 * 4 * 128 * 512 * 512, MIB),
        name="whiten",
    )(spectra)


def phases(bin_index):
    lag_samples = (jnp.arange(LAGS, dtype=jnp.int32) + 1) * LAG_STEP
    phase_turn = lag_samples[:, None] * bin_index[None, :] % NFFT
    phase_angle = 2.0 * math.pi / NFFT * phase_turn.astype(F32)
    cosine, sine = jnp.cos(phase_angle), jnp.sin(phase_angle)
    return jnp.concatenate([cosine, cosine], 1), jnp.concatenate([sine, sine], 1)


def rotate_kernel(a_ref, b_ref, cos_ref, sin_ref, plus_ref, minus_ref):
    half = DEPTH // 2
    for n, ref in enumerate((a_ref, b_ref)):

        @pl.loop(0, 8)
        def _(i):
            at = pl.ds(pl.multiple_of(i * 16, 16), 16)
            to = pl.ds(pl.multiple_of(n * 128 + i * 16, 16), 16)
            re = ref[at, :half].astype(F32)
            im = ref[at, half:].astype(F32)
            for m in range(LAGS):
                cosine, sine = cos_ref[m : m + 1, :], sin_ref[m : m + 1, :]
                rc, rs, ic, is_ = re * cosine, re * sine, im * cosine, im * sine
                plus_ref[m, to, :half] = (rc - is_).astype(BF16)
                plus_ref[m, to, half:] = (rs + ic).astype(BF16)
                minus_ref[m, to, :half] = (rc + is_).astype(BF16)
                minus_ref[m, to, half:] = (ic - rs).astype(BF16)


def rotations(chunks, cosine, sine):
    shape = jax.ShapeDtypeStruct((LAGS, BLOCK, DEPTH), BF16)
    return pl.pallas_call(
        rotate_kernel,
        out_shape=(shape, shape),
        compiler_params=params(16),
        cost_estimate=cost(2 * 8 * 256 * 2048, 6 * MIB),
        name="rotate",
    )(*chunks, cosine, sine)


def store_product(acc_ref, m, first, value, scale):
    n = value.shape[1]
    for h in range(2):
        for x in range(4):
            at = h * 128 + x * 32
            acc_ref[m, h, x, :, first : first + n] = (value[at : at + 32] * scale).astype(BF16)


def products(xi, parts, chunks, wide, scale, name):
    count = len(chunks)

    def kernel(xi_ref, *refs):
        ins, outs, acc_ref = refs[:count], refs[count : count + 4], refs[count + 4]
        for m in range(LAGS):
            for first, value in parts(m, ins):
                store_product(acc_ref, m, first, value, scale)
        for s in range(4):
            to = lax.rem(xi_ref[0] + s, 4)
            for m in range(LAGS):
                for h in range(2):
                    outs[s][h, m] = acc_ref[m, h, to]

    shape = jax.ShapeDtypeStruct((2, LAGS, 32, wide), BF16)
    whole = pl.BlockSpec(memory_space=pltpu.VMEM)
    return pl.pallas_call(
        kernel,
        in_specs=[pl.BlockSpec(memory_space=pltpu.SMEM)] + [whole] * count,
        out_specs=[whole] * 4,
        out_shape=(shape,) * 4,
        scratch_shapes=[pltpu.VMEM((LAGS, 2, 4, 32, wide), BF16)],
        compiler_params=params(28),
        cost_estimate=cost(2 * 2 * 256 * wide * DEPTH, 8 * MIB),
        name=name,
    )(xi, *chunks)


def both(a_ref, b_ref):
    return jnp.concatenate([a_ref[...], b_ref[...]], 0)


def sum_x(yi, groups):
    widths = [g[0].shape[3] for g in groups]
    total = sum(widths)
    flat = [a for g in groups for a in g]

    def kernel(yi_ref, *refs):
        keep_ref, send_ref = refs[-2:]
        mine, other = yi_ref[0], 1 - yi_ref[0]
        first = 0
        for k, n in enumerate(widths):
            four = refs[4 * k : 4 * k + 4]
            for m in range(LAGS):
                for r in range(0, 32, 16):
                    at = pl.ds(r, 16)
                    val = [f[mine, m, at, :].astype(F32) for f in four]
                    keep_ref[m, at, first : first + n] = (val[0] + val[1]) + (val[2] + val[3])
                    val = [f[other, m, at, :].astype(F32) for f in four]
                    send_ref[m, at, first : first + n] = ((val[0] + val[1]) + (val[2] + val[3])).astype(BF16)
            first += n

    whole = pl.BlockSpec(memory_space=pltpu.VMEM)
    return pl.pallas_call(
        kernel,
        in_specs=[pl.BlockSpec(memory_space=pltpu.SMEM)] + [whole] * len(flat),
        out_specs=[whole] * 2,
        out_shape=(jax.ShapeDtypeStruct((LAGS, 32, total), F32), jax.ShapeDtypeStruct((LAGS, 32, total), BF16)),
        compiler_params=params(16),
        cost_estimate=cost(1000, 2 * MIB),
        name="sum_x",
    )(yi, *flat)


def sum_y(ci, keep, recv, outputs):
    def kernel(ci_ref, keep_ref, recv_ref, *outs):
        for which in ("same", "other"):
            core = ci_ref[0] if which == "same" else 1 - ci_ref[0]
            at = pl.ds(pl.multiple_of(core * 16, 16), 16)
            for m in range(LAGS):
                for out, (pieces, kind) in zip(outs, outputs):
                    if kind != which:
                        continue
                    to = 0
                    for first, n in pieces:
                        cols = slice(first, first + n)
                        value = keep_ref[m, at, cols] + recv_ref[m, at, cols].astype(F32)
                        out[m, :, to : to + n] = value.astype(BF16)
                        to += n

    shapes = [jax.ShapeDtypeStruct((LAGS, 16, sum(n for _, n in p)), BF16) for p, _ in outputs]
    whole = pl.BlockSpec(memory_space=pltpu.VMEM)
    return pl.pallas_call(
        kernel,
        in_specs=[pl.BlockSpec(memory_space=pltpu.SMEM), whole, whole],
        out_specs=[whole] * len(shapes),
        out_shape=tuple(shapes),
        compiler_params=params(16),
        cost_estimate=cost(1000, MIB),
        name="sum_y",
    )(ci, keep, recv)


def finish(place, same, other):
    arrays = [a for a, _ in same] + [a for a, _ in other]
    lists = [(b, 0) for _, b in same] + [(b, 1) for _, b in other]

    def kernel(place_ref, *refs):
        out = refs[-1]
        z, y, c = place_ref[0], place_ref[1], place_ref[2]
        for ref, (blocks, kind) in zip(refs[:-1], lists):
            way = 1 - 2 * c if kind == 0 else 2 * c - 1
            for n, (dist, dy) in enumerate(blocks):
                zz = lax.rem(z - way * dist + 16, 8)
                yy = y if dy == 0 else 1 - y
                cols = pl.ds(pl.multiple_of((zz * 2 + yy) * BLOCK, BLOCK), BLOCK)
                for m in range(LAGS):
                    value = ref[m, :, n * BLOCK : (n + 1) * BLOCK].astype(F32)
                    if kind == 0:
                        out[m, :, cols] = value
                    else:
                        out[m, :, cols] += value

    whole = pl.BlockSpec(memory_space=pltpu.VMEM)
    return pl.pallas_call(
        kernel,
        in_specs=[pl.BlockSpec(memory_space=pltpu.SMEM)] + [whole] * len(arrays),
        out_specs=whole,
        out_shape=jax.ShapeDtypeStruct((LAGS, 16, 4096), F32),
        compiler_params=params(16),
        cost_estimate=cost(1000, MIB),
        name="finish",
    )(place, *arrays)


def chain_step(z, ylo, yhi, x, c):
    return z + sign(c), ylo, yhi, x, c


def y_step(z, ylo, yhi, x, c):
    return z, 1 - ylo, yhi, x, c


def y_cross(z, ylo, yhi, x, c):
    return z, 1 - ylo, yhi, x, 1 - c


def yhi_step(z, ylo, yhi, x, c):
    return z, ylo, 1 - yhi, x, c


def core_step(z, ylo, yhi, x, c):
    return z, ylo, yhi, x, 1 - c


def x_step(s):
    return lambda z, ylo, yhi, x, c: (z, ylo, yhi, x + s, c)


def back(d):
    return lambda z, ylo, yhi, x, c: (z - sign(c) * d, ylo, yhi, x, c)


def back_cross(d):
    return lambda z, ylo, yhi, x, c: (z - sign(c) * d, ylo, yhi, x, 1 - c)


def reduce_x(slots):
    return [slots[0]] + [move(slots[s], x_step(s)) for s in (1, 3, 2)]


def batch(yi, ci, groups, classes):
    keep, send = sum_x(yi, groups)
    recv = move(send, yhi_step)
    own, wy, ret = [], [], []
    first = 0
    for g, (n_own, n_wy, d) in zip(groups, classes):
        own.append((first, n_own))
        if n_wy:
            wy.append((first + n_own, n_wy))
        if d:
            ret.append((d, first + n_own + n_wy))
        first += g[0].shape[3]
    outputs = [(own, "same"), (own, "other"), (wy, "same"), (wy, "other")]
    for d, at in ret:
        outputs += [([(at, 2 * BLOCK)], "same"), ([(at, 2 * BLOCK)], "other")]
    got = sum_y(ci, keep, recv, outputs)
    same = [got[0], move(got[2], y_step)]
    other = [move(got[1], core_step), move(got[3], y_cross)]
    for k, (d, _) in enumerate(ret):
        same.append(move(got[4 + 2 * k], back(d)))
        other.append(move(got[5 + 2 * k], back_cross(d)))
    return same, other


def body(spectra, bin_index):
    scale = 1.0 / math.sqrt(32 * BINS)
    z, y = lax.axis_index("z"), lax.axis_index("ylo")
    yi, xi, ci = (lax.axis_index(a).astype(jnp.int32).reshape(1) for a in ("yhi", "x", "c"))
    place = jnp.stack([z, y, lax.axis_index("c")]).astype(jnp.int32)

    own = [whiten(spectra, 0), whiten(spectra, 1)]
    block = own
    arrived = []
    for _ in range(4):
        block = [move(b, chain_step) for b in block]
        arrived.append(block)
    near = [move(b, y_step) for b in own]

    cosine, sine = phases(bin_index)
    own_plus, own_minus = rotations(own, cosine, sine)
    near_plus, near_minus = rotations(near, cosine, sine)

    def all_pairs(m, ins, at=0):
        b = both(ins[at], ins[at + 1])
        op, om, np_, nm = ins[-4:]
        yield 0, dot_nt(op[m], b)
        yield BLOCK, dot_nt(np_[m], b)
        yield 2 * BLOCK, dot_nt(b, om[m])
        yield 3 * BLOCK, dot_nt(b, nm[m])

    def first_pairs(m, ins):
        op, om, np_, nm = ins[-4:]
        b = both(ins[0], ins[1])
        yield 0, dot_nt(op[m], both(ins[2], ins[3]))
        yield BLOCK, dot_nt(op[m], both(ins[4], ins[5]))
        yield 2 * BLOCK, dot_nt(op[m], b)
        yield 3 * BLOCK, dot_nt(np_[m], b)
        yield 4 * BLOCK, dot_nt(b, om[m])
        yield 5 * BLOCK, dot_nt(b, nm[m])

    def last_pairs(m, ins):
        b = both(ins[0], ins[1])
        yield 0, dot_nt(ins[2][m], b)
        yield BLOCK, dot_nt(ins[3][m], b)

    rotated = [own_plus, own_minus, near_plus, near_minus]
    g1 = reduce_x(products(xi, first_pairs, arrived[0] + own + near + rotated, 6 * BLOCK, scale, "pairs_0_1"))
    g2 = reduce_x(products(xi, all_pairs, arrived[1] + rotated, 4 * BLOCK, scale, "pairs_2"))
    g3 = reduce_x(products(xi, all_pairs, arrived[2] + rotated, 4 * BLOCK, scale, "pairs_3"))
    g4 = reduce_x(products(xi, last_pairs, arrived[3] + [own_plus, near_plus], 2 * BLOCK, scale, "pairs_4"))

    same1, other1 = batch(yi, ci, [g1, g2], [(3 * BLOCK, BLOCK, 1), (BLOCK, BLOCK, 2)])
    same2, other2 = batch(yi, ci, [g3, g4], [(BLOCK, BLOCK, 3), (BLOCK, BLOCK, 0)])
    blocks1 = [[(0, 0), (0, 1), (1, 0), (2, 0)], [(1, 1), (2, 1)], [(-1, 0), (-1, 1)], [(-2, 0), (-2, 1)]]
    blocks2 = [[(3, 0), (4, 0)], [(3, 1), (4, 1)], [(-3, 0), (-3, 1)]]
    ids = blocks1 + blocks2
    return finish(place, list(zip(same1 + same2, ids)), list(zip(other1 + other2, ids)))


def solution(mesh):
    torus = Mesh(mesh.devices.reshape(SIZES), AXES)
    placed = (P(None, ("yhi", "x", "c"), None, ("z", "ylo")), P())
    return jax.shard_map(
        body, mesh=torus, in_specs=placed, out_specs=P(None, AXES, None), check_vma=False
    )
```

time: 339 us -> 141 us (0.42)
  waiting for transfers between devices: 300 us -> 43.5 us
  starting transfers between devices: 0.08 us -> 58 us
  Pallas kernels: 0 us -> 25.4 us
  matrix products: 16 us -> 0 us
  between operations: 13.2 us -> 0.26 us
  local copies, waits for them, and re-layouts: 1.88 us -> 12.9 us
  other arithmetic: 6.58 us -> 0.24 us
    all_gather x2 -> x0, waiting for transfers between devices: 215 us -> none  [gather_axes(): nearer = lax.all_gather(x, axes[-1], axis=dim, tiled=True)]
    reduce_scatter x1 -> x0, waiting for transfers between devices: 85.4 us -> none  [body(): lax.psum_scatter(product, 'seg', scatter_dimension=1, tiled=True)]
    ppermute x0 -> x36, starting transfers between devices: none -> 58 us  [move(): return lax.ppermute(x, AXES, pairs)]
    ppermute x0 -> x36, waiting for transfers between devices: none -> 43.5 us  [move(): return lax.ppermute(x, AXES, pairs)]
    pallas_call x0 -> x13, Pallas kernels: none -> 25.4 us  [the longest x4 16.2 us: products(): pl.pallas_call(kernel, in_specs=[pl.BlockSpec(memory_space=pltpu.SMEM)] +...]
    dot_general x2 -> x0, matrix products: 16 us -> none  [the longest x1 14 us: pair_block(): jnp.einsum('mki,kj->mij', rotated, columns, preferred_element_type=jnp.fl...]
    unnamed x6 -> x48, local copies, waits for them, and re-layouts: 0.89 us -> 12.9 us
    convert_element_type x3 -> x0, other arithmetic: 4.47 us -> none  [the longest x1 1.78 us: body(): lax.psum_scatter(product, 'seg', scatter_dimension=1, tiled=True)]
  transfers between devices with their start and end apart: 3 -> 36, of which waited for: 3 -> 17; matrix products, arithmetic and copies ran while one was open for 1% -> 0% of each run, Pallas kernels for 0% -> 17%
where the time goes in v1:
time: 141 us; the launch traced here: 140 us
  starting transfers between devices  58 us (41%)
  waiting for transfers between devices  43.5 us (31%)
  Pallas kernels  25.4 us (18%)
  local copies, waits for them, and re-layouts  12.9 us (9%)
    ppermute x36, starting transfers between devices, move(): return lax.ppermute(x, AXES, pairs)  58 us
    ppermute x36, waiting for transfers between devices, move(): return lax.ppermute(x, AXES, pairs)  43.5 us
    pallas_call x4, Pallas kernels, products(): pl.pallas_call(kernel, in_specs=[pl.BlockSpec(memory_space=pltpu.SMEM)] +...  16.2 us
    unnamed x48, local copies, waits for them, and re-layouts  12.9 us
    pallas_call x2, Pallas kernels, rotations(): pl.pallas_call(rotate_kernel, out_shape=(shape, shape), compiler_params=p...  3.15 us
  transfers between devices with their start and end apart: 36, of which 17 were waited for; matrix products, arithmetic and copies ran while one was open for 0% of the time, Pallas kernels for 17%

profile of v1, /device:TPU:1, one launch (start us, length us, event | category | flops | bytes accessed | tf_op | source)
XLA Modules:
  0.0 140.3 jit_solution(12965310792071225990)
XLA Ops:
  0.0 1.2 copy-done.2
  1.8 6.5 %collective-permute-start = (bf16[128,2048]{1,0:T(8,128)(2,1)S(1)}, bf16[128,2048]{1,0:T(8,128)(2,1)S(1)}, u32[]{:S(2)}, u32[]{:S(2)}) collective-permute-start(bf16[128,2048]{1,0:T(8,128)(2,1)S(1)} %whiten.2.a_ref.refs_2_), channel_id=1, source_target_pairs={{0,32},{1,225},{2,34},{3,227},{4,36},{5,229},{6,38},{7,231},{8,40}... | collective-permute-start | bytes 1572872 | tf_op jit(solution)/shard_map/ppermute | solution.py:43
  9.7 4.7 %collective-permute-done.refs_0_ = bf16[128,2048]{1,0:T(8,128)(2,1)S(1)} collective-permute-done((bf16[128,2048]{1,0:T(8,128)(2,1)S(1)}, bf16[128,2048]{1,0:T(8,128)(2,1)S(1)}, u32[]{:S(2)}, u32[]{:S(2)}) %collective-permute-start) | collective-permute-done | bytes 524320 | tf_op jit(solution)/shard_map/ppermute | solution.py:43
  14.4 3.1 %collective-permute-start.7 = (bf16[128,2048]{1,0:T(8,128)(2,1)S(1)}, bf16[128,2048]{1,0:T(8,128)(2,1)}, u32[]{:S(2)}, u32[]{:S(2)}) collective-permute-start(bf16[128,2048]{1,0:T(8,128)(2,1)S(1)} %collective-permute-done.refs_0_), channel_id=1, source_target_pairs={{0,32},{1,225},{2,34},{3,227},{4,36},{5,229},{6,38},{7,231},{8,40}... | collective-permute-start | bytes 1572872 | tf_op jit(solution)/shard_map/ppermute | solution.py:43
  18.4 1.7 %collective-permute-done.1.refs_1_ = bf16[128,2048]{1,0:T(8,128)(2,1)S(1)} collective-permute-done((bf16[128,2048]{1,0:T(8,128)(2,1)S(1)}, bf16[128,2048]{1,0:T(8,128)(2,1)S(1)}, u32[]{:S(2)}, u32[]{:S(2)}) %collective-permute-start.1) | collective-permute-done | bytes 524320 | tf_op jit(solution)/shard_map/ppermute | solution.py:43
  20.1 3.1 %collective-permute-start.8 = (bf16[128,2048]{1,0:T(8,128)(2,1)S(1)}, bf16[128,2048]{1,0:T(8,128)(2,1)}, u32[]{:S(2)}, u32[]{:S(2)}) collective-permute-start(bf16[128,2048]{1,0:T(8,128)(2,1)S(1)} %collective-permute-done.1.refs_1_), channel_id=1, source_target_pairs={{0,32},{1,225},{2,34},{3,227},{4,36},{5,229},{6,38},{7,231},{8,40}... | collective-permute-start | bytes 1572872 | tf_op jit(solution)/shard_map/ppermute | solution.py:43
  24.0 1.3 collective-permute-start.2
  25.7 3.2 %collective-permute-start.16 = (bf16[128,2048]{1,0:T(8,128)(2,1)}, bf16[128,2048]{1,0:T(8,128)(2,1)}, u32[]{:S(2)}, u32[]{:S(2)}) collective-permute-start(bf16[128,2048]{1,0:T(8,128)(2,1)} %collective-permute-done.7.refs_0_), channel_id=1, source_target_pairs={{0,32},{1,225},{2,34},{3,227},{4,36},{5,229},{6,38},{7,231},{8,40}... | collective-permute-start | bytes 1572872 | tf_op jit(solution)/shard_map/ppermute | solution.py:43
  28.9 2.4 %collective-permute-done.8.refs_1_ = bf16[128,2048]{1,0:T(8,128)(2,1)} collective-permute-done((bf16[128,2048]{1,0:T(8,128)(2,1)S(1)}, bf16[128,2048]{1,0:T(8,128)(2,1)}, u32[]{:S(2)}, u32[]{:S(2)}) %collective-permute-start.8) | collective-permute-done | bytes 524320 | tf_op jit(solution)/shard_map/ppermute | solution.py:43
  31.3 3.2 %collective-permute-start.17 = (bf16[128,2048]{1,0:T(8,128)(2,1)}, bf16[128,2048]{1,0:T(8,128)(2,1)}, u32[]{:S(2)}, u32[]{:S(2)}) collective-permute-start(bf16[128,2048]{1,0:T(8,128)(2,1)} %collective-permute-done.8.refs_1_), channel_id=1, source_target_pairs={{0,32},{1,225},{2,34},{3,227},{4,36},{5,229},{6,38},{7,231},{8,40}... | collective-permute-start | bytes 1572872 | tf_op jit(solution)/shard_map/ppermute | solution.py:43
  34.6 1.0 rotate.2
  35.5 2.4 %collective-permute-done.2.a_ref.refs_4_ = bf16[128,2048]{1,0:T(8,128)(2,1)} collective-permute-done((bf16[128,2048]{1,0:T(8,128)(2,1)S(1)}, bf16[128,2048]{1,0:T(8,128)(2,1)}, u32[]{:S(2)}, u32[]{:S(2)}) %collective-permute-start.2) | collective-permute-done | bytes 524320 | tf_op jit(solution)/shard_map/ppermute | solution.py:43
  38.0 10.3 %collective-permute-done.3.b_ref.refs_5_ = bf16[128,2048]{1,0:T(8,128)(2,1)} collective-permute-done((bf16[128,2048]{1,0:T(8,128)(2,1)S(1)}, bf16[128,2048]{1,0:T(8,128)(2,1)}, u32[]{:S(2)}, u32[]{:S(2)}) %collective-permute-start.3) | collective-permute-done | bytes 524320 | tf_op jit(solution)/shard_map/ppermute | solution.py:43
  48.3 2.2 %rotate.3 = (bf16[2,256,2048]{2,1,0:T(8,128)(2,1)S(1)}, bf16[2,256,2048]{2,1,0:T(8,128)(2,1)S(1)}) custom-call(bf16[128,2048]{1,0:T(8,128)(2,1)} %collective-permute-done.2.a_ref.refs_4_, bf16[128,2048]{1,0:T(8,128)(2,1)} %collective-permute-done.3.b_ref.refs_5_, f32[2,1024]{1,0:T(2,128)S(1)} %get-tuple-element.83.cos_ref, ...), custom_call_target="tpu_custom_call" | custom-call | flops 8388608 | bytes 6291456 | tf_op jit(solution)/shard_map/rotate/pallas_call | solution.py:112
  50.5 5.6 %pairs_0_1.1 = (bf16[2,2,32,1536]{3,2,1,0:T(8,128)(2,1)S(1)}, bf16[2,2,32,1536]{3,2,1,0:T(8,128)(2,1)S(1)}, bf16[2,2,32,1536]{3,2,1,0:T(8,128)(2,1)S(1)}, bf16[2,2,32,1536]{3,2,1,0:T(8,128)(2,1)S(1)}) custom-call(s32[1]{0:T(128)} %bitcast.4.xi_ref, bf16[128,2048]{1,0:T(8,128)(2,1)S(1)} %copy-done.20, bf16[128,2048]{1,0:T(8,128)(2,1)S(1)} %copy-done.22, ...), custom_call_target="tpu_custom_call" | custom-call | flops 3221225472 | bytes 8388608 | tf_op jit(solution)/shard_map/pairs_0_1/pallas_call | solution.py:145
  56.1 1.3 collective-permute-start.4
  57.5 1.5 %collective-permute-start.5 = (bf16[2,2,32,1536]{3,2,1,0:T(8,128)(2,1)S(1)}, bf16[2,2,32,1536]{3,2,1,0:T(8,128)(2,1)S(1)}, u32[]{:S(2)}, u32[]{:S(2)}) collective-permute-start(bf16[2,2,32,1536]{3,2,1,0:T(8,128)(2,1)S(1)} %get-tuple-element.49), channel_id=1, source_target_pairs={{0,6},{1,7},{2,0},{3,1},{4,2},{5,3},{6,4},{7,5},{8,14},{9,15},{10,... | collective-permute-start | bytes 1179656 | tf_op jit(solution)/shard_map/ppermute | solution.py:43
  58.9 1.5 %collective-permute-start.6 = (bf16[2,2,32,1536]{3,2,1,0:T(8,128)(2,1)S(1)}, bf16[2,2,32,1536]{3,2,1,0:T(8,128)(2,1)S(1)}, u32[]{:S(2)}, u32[]{:S(2)}) collective-permute-start(bf16[2,2,32,1536]{3,2,1,0:T(8,128)(2,1)S(1)} %get-tuple-element.50), channel_id=1, source_target_pairs={{0,4},{1,5},{2,6},{3,7},{4,0},{5,1},{6,2},{7,3},{8,12},{9,13},{10,... | collective-permute-start | bytes 1179656 | tf_op jit(solution)/shard_map/ppermute | solution.py:43
  60.5 3.7 %pairs_2.1 = (bf16[2,2,32,1024]{3,2,1,0:T(8,128)(2,1)S(1)}, bf16[2,2,32,1024]{3,2,1,0:T(8,128)(2,1)S(1)}, bf16[2,2,32,1024]{3,2,1,0:T(8,128)(2,1)S(1)}, bf16[2,2,32,1024]{3,2,1,0:T(8,128)(2,1)S(1)}) custom-call(s32[1]{0:T(128)} %bitcast.4.xi_ref, bf16[128,2048]{1,0:T(8,128)(2,1)} %collective-permute-done.7.refs_0_, ...), custom_call_target="tpu_custom_call" | custom-call | flops 2147483648 | bytes 8388608 | tf_op jit(solution)/shard_map/pairs_2/pallas_call | solution.py:145
  64.2 3.9 %collective-permute-done.4.refs_1_ = bf16[2,2,32,1536]{3,2,1,0:T(8,128)(2,1)S(1)} collective-permute-done((bf16[2,2,32,1536]{3,2,1,0:T(8,128)(2,1)S(1)}, bf16[2,2,32,1536]{3,2,1,0:T(8,128)(2,1)S(1)}, u32[]{:S(2)}, u32[]{:S(2)}) %collective-permute-start.4) | collective-permute-done | bytes 393248 | tf_op jit(solution)/shard_map/ppermute | solution.py:43
  68.2 2.7 %collective-permute-start.10 = (bf16[2,2,32,1024]{3,2,1,0:T(8,128)(2,1)S(1)}, bf16[2,2,32,1024]{3,2,1,0:T(8,128)(2,1)S(1)}, u32[]{:S(2)}, u32[]{:S(2)}) collective-permute-start(bf16[2,2,32,1024]{3,2,1,0:T(8,128)(2,1)S(1)} %get-tuple-element.53), channel_id=1, source_target_pairs={{0,6},{1,7},{2,0},{3,1},{4,2},{5,3},{6,4},{7,5},{8,14},{9,15},{10,... | collective-permute-start | bytes 786440 | tf_op jit(solution)/shard_map/ppermute | solution.py:43
  70.8 6.8 %collective-permute-done.6.refs_3_ = bf16[2,2,32,1536]{3,2,1,0:T(8,128)(2,1)S(1)} collective-permute-done((bf16[2,2,32,1536]{3,2,1,0:T(8,128)(2,1)S(1)}, bf16[2,2,32,1536]{3,2,1,0:T(8,128)(2,1)S(1)}, u32[]{:S(2)}, u32[]{:S(2)}) %collective-permute-start.6) | collective-permute-done | bytes 393248 | tf_op jit(solution)/shard_map/ppermute | solution.py:43
  78.2 4.6 %pairs_3.1 = (bf16[2,2,32,1024]{3,2,1,0:T(8,128)(2,1)S(1)}, bf16[2,2,32,1024]{3,2,1,0:T(8,128)(2,1)}, bf16[2,2,32,1024]{3,2,1,0:T(8,128)(2,1)}, bf16[2,2,32,1024]{3,2,1,0:T(8,128)(2,1)}) custom-call(s32[1]{0:T(128)} %bitcast.4.xi_ref, bf16[128,2048]{1,0:T(8,128)(2,1)} %collective-permute-done.16.refs_0_, bf16[128,2048]{1,0:T(8,128)(2,1)} %collective-permute-done.17.refs_1_, ...), custom_call_target="tpu_custom_call" | custom-call | flops 2147483648 | bytes 8388608 | tf_op jit(solution)/shard_map/pairs_3/pallas_call | solution.py:145
  82.8 1.0 collective-permute-done.9.refs_5_
  85.3 2.6 %collective-permute-start.19 = (bf16[2,2,32,1024]{3,2,1,0:T(8,128)(2,1)}, bf16[2,2,32,1024]{3,2,1,0:T(8,128)(2,1)}, u32[]{:S(2)}, u32[]{:S(2)}) collective-permute-start(bf16[2,2,32,1024]{3,2,1,0:T(8,128)(2,1)} %get-tuple-element.63), channel_id=1, source_target_pairs={{0,6},{1,7},{2,0},{3,1},{4,2},{5,3},{6,4},{7,5},{8,14},{9,15},{10,... | collective-permute-start | bytes 786440 | tf_op jit(solution)/shard_map/ppermute | solution.py:43
  88.9 1.2 collective-permute-start.20
  90.0 1.1 copy-done.4
  91.2 1.0 copy-done.6
  92.2 1.0 copy-done.8
  93.2 1.0 copy-done.10
  98.0 1.0 sum_x.2
  99.0 2.9 %collective-permute-start.12 = (bf16[2,32,2560]{2,1,0:T(8,128)(2,1)}, bf16[2,32,2560]{2,1,0:T(8,128)(2,1)}, u32[]{:S(2)}, u32[]{:S(2)}) collective-permute-start(bf16[2,32,2560]{2,1,0:T(8,128)(2,1)} %get-tuple-element.56), channel_id=1, source_target_pairs={{0,8},{1,9},{2,10},{3,11},{4,12},{5,13},{6,14},{7,15},{8,0},{9,1},... | collective-permute-start | bytes 983048 | tf_op jit(solution)/shard_map/ppermute | solution.py:43
  101.9 2.4 %pairs_4.1 = (bf16[2,2,32,512]{3,2,1,0:T(8,128)(2,1)S(1)}, bf16[2,2,32,512]{3,2,1,0:T(8,128)(2,1)S(1)}, bf16[2,2,32,512]{3,2,1,0:T(8,128)(2,1)S(1)}, bf16[2,2,32,512]{3,2,1,0:T(8,128)(2,1)S(1)}) custom-call(s32[1]{0:T(128)} %bitcast.4.xi_ref, bf16[128,2048]{1,0:T(8,128)(2,1)S(1)} %collective-permute-done.21.refs_0_, ...), custom_call_target="tpu_custom_call" | custom-call | flops 1073741824 | bytes 8388608 | tf_op jit(solution)/shard_map/pairs_4/pallas_call | solution.py:145
  104.6 2.7 %collective-permute-start.24 = (bf16[2,2,32,512]{3,2,1,0:T(8,128)(2,1)S(1)}, bf16[2,2,32,512]{3,2,1,0:T(8,128)(2,1)S(1)}, u32[]{:S(2)}, u32[]{:S(2)}) collective-permute-start(bf16[2,2,32,512]{3,2,1,0:T(8,128)(2,1)S(1)} %get-tuple-element.67), channel_id=1, source_target_pairs={{0,6},{1,7},{2,0},{3,1},{4,2},{5,3},{6,4},{7,5},{8,14},{9,15},{10,... | collective-permute-start | bytes 393224 | tf_op jit(solution)/shard_map/ppermute | solution.py:43
  107.8 2.2 %collective-permute-done.23.refs_5_ = bf16[2,2,32,512]{3,2,1,0:T(8,128)(2,1)S(1)} collective-permute-done((bf16[2,2,32,512]{3,2,1,0:T(8,128)(2,1)S(1)}, bf16[2,2,32,512]{3,2,1,0:T(8,128)(2,1)S(1)}, u32[]{:S(2)}, u32[]{:S(2)}) %collective-permute-start.23) | collective-permute-done | bytes 131104 | tf_op jit(solution)/shard_map/ppermute | solution.py:43
  110.5 2.0 %collective-permute-done.25.refs_7_ = bf16[2,2,32,512]{3,2,1,0:T(8,128)(2,1)S(1)} collective-permute-done((bf16[2,2,32,512]{3,2,1,0:T(8,128)(2,1)S(1)}, bf16[2,2,32,512]{3,2,1,0:T(8,128)(2,1)S(1)}, u32[]{:S(2)}, u32[]{:S(2)}) %collective-permute-start.25) | collective-permute-done | bytes 131104 | tf_op jit(solution)/shard_map/ppermute | solution.py:43
  112.6 1.3 sum_x.3
  114.0 1.0 sum_y.2
  115.0 1.8 %collective-permute-start.13 = (bf16[2,16,512]{2,1,0:T(8,128)(2,1)S(1)}, bf16[2,16,512]{2,1,0:T(8,128)(2,1)S(1)}, u32[]{:S(2)}, u32[]{:S(2)}) collective-permute-start(bf16[2,16,512]{2,1,0:T(8,128)(2,1)S(1)} %get-tuple-element.58), channel_id=1, source_target_pairs={{0,16},{1,17},{2,18},{3,19},{4,20},{5,21},{6,22},{7,23},{8,24},{9,... | collective-permute-start | bytes 98312 | tf_op jit(solution)/shard_map/ppermute | solution.py:43
  116.8 6.2 %collective-permute-start.29 = (bf16[2,16,1024]{2,1,0:T(8,128)(2,1)S(1)}, bf16[2,16,1024]{2,1,0:T(8,128)(2,1)S(1)}, u32[]{:S(2)}, u32[]{:S(2)}) collective-permute-start(bf16[2,16,1024]{2,1,0:T(8,128)(2,1)S(1)} %get-tuple-element.74), channel_id=1, source_target_pairs={{0,1},{1,0},{2,3},{3,2},{4,5},{5,4},{6,7},{7,6},{8,9},{9,8},{10,11... | collective-permute-start | bytes 196616 | tf_op jit(solution)/shard_map/ppermute | solution.py:43
  123.0 3.5 %collective-permute-start.30 = (bf16[2,16,512]{2,1,0:T(8,128)(2,1)S(1)}, bf16[2,16,512]{2,1,0:T(8,128)(2,1)S(1)}, u32[]{:S(2)}, u32[]{:S(2)}) collective-permute-start(bf16[2,16,512]{2,1,0:T(8,128)(2,1)S(1)} %get-tuple-element.75), channel_id=1, source_target_pairs={{0,17},{1,16},{2,19},{3,18},{4,21},{5,20},{6,23},{7,22},{8,25},{9,... | collective-permute-start | bytes 98312 | tf_op jit(solution)/shard_map/ppermute | solution.py:43
  126.7 1.2 collective-permute-done.15.refs_3_
  128.1 1.4 %collective-permute-start.28 = (bf16[2,16,512]{2,1,0:T(8,128)(2,1)S(1)}, bf16[2,16,512]{2,1,0:T(8,128)(2,1)S(1)}, u32[]{:S(2)}, u32[]{:S(2)}) collective-permute-start(bf16[2,16,512]{2,1,0:T(8,128)(2,1)S(1)} %get-tuple-element.73), channel_id=1, source_target_pairs={{0,160},{1,97},{2,162},{3,99},{4,164},{5,101},{6,166},{7,103},{8,1... | collective-permute-start | bytes 98312 | tf_op jit(solution)/shard_map/ppermute | solution.py:43
  129.8 2.2 %collective-permute-start.33 = (bf16[2,16,512]{2,1,0:T(8,128)(2,1)S(1)}, bf16[2,16,512]{2,1,0:T(8,128)(2,1)S(1)}, u32[]{:S(2)}, u32[]{:S(2)}) collective-permute-start(bf16[2,16,512]{2,1,0:T(8,128)(2,1)S(1)} %get-tuple-element.78), channel_id=1, source_target_pairs={{0,1},{1,0},{2,3},{3,2},{4,5},{5,4},{6,7},{7,6},{8,9},{9,8},{10,11... | collective-permute-start | bytes 98312 | tf_op jit(solution)/shard_map/ppermute | solution.py:43
  132.0 1.3 collective-permute-start.34
  133.4 1.8 %collective-permute-start.35 = (bf16[2,16,512]{2,1,0:T(8,128)(2,1)S(1)}, bf16[2,16,512]{2,1,0:T(8,128)(2,1)S(1)}, u32[]{:S(2)}, u32[]{:S(2)}) collective-permute-start(bf16[2,16,512]{2,1,0:T(8,128)(2,1)S(1)} %get-tuple-element.80), channel_id=1, source_target_pairs={{0,161},{1,96},{2,163},{3,98},{4,165},{5,100},{6,167},{7,102},{8,1... | collective-permute-start | bytes 98312 | tf_op jit(solution)/shard_map/ppermute | solution.py:43
  135.7 3.1 %collective-permute-done.35.refs_13_ = bf16[2,16,512]{2,1,0:T(8,128)(2,1)S(1)} collective-permute-done((bf16[2,16,512]{2,1,0:T(8,128)(2,1)S(1)}, bf16[2,16,512]{2,1,0:T(8,128)(2,1)S(1)}, u32[]{:S(2)}, u32[]{:S(2)}) %collective-permute-start.35) | collective-permute-done | bytes 32800 | tf_op jit(solution)/shard_map/ppermute | solution.py:43
  138.8 1.5 %finish.1 = f32[2,16,4096]{2,1,0:T(8,128)} custom-call(s32[3]{0:T(128)S(1)} %pad_add_fusion.place_ref, bf16[2,16,1024]{2,1,0:T(8,128)(2,1)S(1)} %get-tuple-element.57.refs_0_, bf16[2,16,512]{2,1,0:T(8,128)(2,1)S(1)} %collective-permute-done.13.refs_1_, bf16[2,16,512]{2,1,0:T(8,128)(2,1)S(1)} %collective-permute-done.14.refs_2_, ...), custom_call_target="tpu_custom_call" | custom-call | flops 1000 | bytes 1048576 | tf_op jit(solution)/shard_map/finish/pallas_call | solution.py:243
  (89 shorter events, 13.8 us)
Async XLA Ops:
  0.0 1.2 copy-start.2
  1.2 24.2 %copy-start.23 = (s32[512]{0:T(512)S(1)}, s32[512]{0:T(512)}, u32[]{:S(2)}) copy-start(s32[512]{0:T(512)} %param.3) | copy-start | bytes 6148
  1.8 12.6 %collective-permute-start = (bf16[128,2048]{1,0:T(8,128)(2,1)S(1)}, bf16[128,2048]{1,0:T(8,128)(2,1)S(1)}, u32[]{:S(2)}, u32[]{:S(2)}) collective-permute-start(bf16[128,2048]{1,0:T(8,128)(2,1)S(1)} %whiten.2.a_ref.refs_2_), channel_id=1, source_target_pairs={{0,32},{1,225},{2,34},{3,227},{4,36},{5,229},{6,38},{7,231},{8,40}... | collective-permute-start | bytes 1572872 | tf_op jit(solution)/shard_map/ppermute | solution.py:43
  8.9 11.1 %collective-permute-start.1 = (bf16[128,2048]{1,0:T(8,128)(2,1)S(1)}, bf16[128,2048]{1,0:T(8,128)(2,1)S(1)}, u32[]{:S(2)}, u32[]{:S(2)}) collective-permute-start(bf16[128,2048]{1,0:T(8,128)(2,1)S(1)} %whiten.3.b_ref.refs_3_), channel_id=1, source_target_pairs={{0,32},{1,225},{2,34},{3,227},{4,36},{5,229},{6,38},{7,231},{8,40}... | collective-permute-start | bytes 1572872 | tf_op jit(solution)/shard_map/ppermute | solution.py:43
  14.4 11.2 %collective-permute-start.7 = (bf16[128,2048]{1,0:T(8,128)(2,1)S(1)}, bf16[128,2048]{1,0:T(8,128)(2,1)}, u32[]{:S(2)}, u32[]{:S(2)}) collective-permute-start(bf16[128,2048]{1,0:T(8,128)(2,1)S(1)} %collective-permute-done.refs_0_), channel_id=1, source_target_pairs={{0,32},{1,225},{2,34},{3,227},{4,36},{5,229},{6,38},{7,231},{8,40}... | collective-permute-start | bytes 1572872 | tf_op jit(solution)/shard_map/ppermute | solution.py:43
  20.1 11.2 %collective-permute-start.8 = (bf16[128,2048]{1,0:T(8,128)(2,1)S(1)}, bf16[128,2048]{1,0:T(8,128)(2,1)}, u32[]{:S(2)}, u32[]{:S(2)}) collective-permute-start(bf16[128,2048]{1,0:T(8,128)(2,1)S(1)} %collective-permute-done.1.refs_1_), channel_id=1, source_target_pairs={{0,32},{1,225},{2,34},{3,227},{4,36},{5,229},{6,38},{7,231},{8,40}... | collective-permute-start | bytes 1572872 | tf_op jit(solution)/shard_map/ppermute | solution.py:43
  24.0 14.0 %collective-permute-start.2 = (bf16[128,2048]{1,0:T(8,128)(2,1)S(1)}, bf16[128,2048]{1,0:T(8,128)(2,1)}, u32[]{:S(2)}, u32[]{:S(2)}) collective-permute-start(bf16[128,2048]{1,0:T(8,128)(2,1)S(1)} %whiten.2.a_ref.refs_2_), channel_id=1, source_target_pairs={{0,16},{1,17},{2,18},{3,19},{4,20},{5,21},{6,22},{7,23},{8,24},{9,... | collective-permute-start | bytes 1572872 | tf_op jit(solution)/shard_map/ppermute | solution.py:43
  25.3 23.0 %collective-permute-start.3 = (bf16[128,2048]{1,0:T(8,128)(2,1)S(1)}, bf16[128,2048]{1,0:T(8,128)(2,1)}, u32[]{:S(2)}, u32[]{:S(2)}) collective-permute-start(bf16[128,2048]{1,0:T(8,128)(2,1)S(1)} %whiten.3.b_ref.refs_3_), channel_id=1, source_target_pairs={{0,16},{1,17},{2,18},{3,19},{4,20},{5,21},{6,22},{7,23},{8,24},{9,... | collective-permute-start | bytes 1572872 | tf_op jit(solution)/shard_map/ppermute | solution.py:43
  25.7 34.8 %collective-permute-start.16 = (bf16[128,2048]{1,0:T(8,128)(2,1)}, bf16[128,2048]{1,0:T(8,128)(2,1)}, u32[]{:S(2)}, u32[]{:S(2)}) collective-permute-start(bf16[128,2048]{1,0:T(8,128)(2,1)} %collective-permute-done.7.refs_0_), channel_id=1, source_target_pairs={{0,32},{1,225},{2,34},{3,227},{4,36},{5,229},{6,38},{7,231},{8,40}... | collective-permute-start | bytes 1572872 | tf_op jit(solution)/shard_map/ppermute | solution.py:43
  31.3 29.2 %collective-permute-start.17 = (bf16[128,2048]{1,0:T(8,128)(2,1)}, bf16[128,2048]{1,0:T(8,128)(2,1)}, u32[]{:S(2)}, u32[]{:S(2)}) collective-permute-start(bf16[128,2048]{1,0:T(8,128)(2,1)} %collective-permute-done.8.refs_1_), channel_id=1, source_target_pairs={{0,32},{1,225},{2,34},{3,227},{4,36},{5,229},{6,38},{7,231},{8,40}... | collective-permute-start | bytes 1572872 | tf_op jit(solution)/shard_map/ppermute | solution.py:43
  34.5 16.0 %copy-start.20 = (bf16[128,2048]{1,0:T(8,128)(2,1)S(1)}, bf16[128,2048]{1,0:T(8,128)(2,1)}, u32[]{:S(2)}) copy-start(bf16[128,2048]{1,0:T(8,128)(2,1)} %copy-done.19) | copy-start | bytes 1572868
  34.6 16.0 %copy-start.22 = (bf16[128,2048]{1,0:T(8,128)(2,1)S(1)}, bf16[128,2048]{1,0:T(8,128)(2,1)}, u32[]{:S(2)}) copy-start(bf16[128,2048]{1,0:T(8,128)(2,1)} %copy-done.21) | copy-start | bytes 1572868
  50.5 27.7 %copy-start = (bf16[2,256,2048]{2,1,0:T(8,128)(2,1)}, bf16[2,256,2048]{2,1,0:T(8,128)(2,1)S(1)}, u32[]{:S(2)}) copy-start(bf16[2,256,2048]{2,1,0:T(8,128)(2,1)S(1)} %get-tuple-element.45.refs_8_.refs_4_.refs_3_) | copy-start | bytes 6291460
  56.1 8.1 %copy-start.3 = (bf16[2,2,32,1536]{3,2,1,0:T(8,128)(2,1)}, bf16[2,2,32,1536]{3,2,1,0:T(8,128)(2,1)S(1)}, u32[]{:S(2)}) copy-start(bf16[2,2,32,1536]{3,2,1,0:T(8,128)(2,1)S(1)} %get-tuple-element.47.refs_0_) | copy-start | bytes 1179652
  56.1 12.0 %collective-permute-start.4 = (bf16[2,2,32,1536]{3,2,1,0:T(8,128)(2,1)S(1)}, bf16[2,2,32,1536]{3,2,1,0:T(8,128)(2,1)S(1)}, u32[]{:S(2)}, u32[]{:S(2)}) collective-permute-start(bf16[2,2,32,1536]{3,2,1,0:T(8,128)(2,1)S(1)} %get-tuple-element.48), channel_id=1, source_target_pairs={{0,2},{1,3},{2,4},{3,5},{4,6},{5,7},{6,0},{7,1},{8,10},{9,11},{10,... | collective-permute-start | bytes 1179656 | tf_op jit(solution)/shard_map/ppermute | solution.py:43
  57.5 10.7 %collective-permute-start.5 = (bf16[2,2,32,1536]{3,2,1,0:T(8,128)(2,1)S(1)}, bf16[2,2,32,1536]{3,2,1,0:T(8,128)(2,1)S(1)}, u32[]{:S(2)}, u32[]{:S(2)}) collective-permute-start(bf16[2,2,32,1536]{3,2,1,0:T(8,128)(2,1)S(1)} %get-tuple-element.49), channel_id=1, source_target_pairs={{0,6},{1,7},{2,0},{3,1},{4,2},{5,3},{6,4},{7,5},{8,14},{9,15},{10,... | collective-permute-start | bytes 1179656 | tf_op jit(solution)/shard_map/ppermute | solution.py:43
  58.9 18.7 %collective-permute-start.6 = (bf16[2,2,32,1536]{3,2,1,0:T(8,128)(2,1)S(1)}, bf16[2,2,32,1536]{3,2,1,0:T(8,128)(2,1)S(1)}, u32[]{:S(2)}, u32[]{:S(2)}) collective-permute-start(bf16[2,2,32,1536]{3,2,1,0:T(8,128)(2,1)S(1)} %get-tuple-element.50), channel_id=1, source_target_pairs={{0,4},{1,5},{2,6},{3,7},{4,0},{5,1},{6,2},{7,3},{8,12},{9,13},{10,... | collective-permute-start | bytes 1179656 | tf_op jit(solution)/shard_map/ppermute | solution.py:43
  60.4 38.5 %collective-permute-start.21 = (bf16[128,2048]{1,0:T(8,128)(2,1)}, bf16[128,2048]{1,0:T(8,128)(2,1)S(1)}, u32[]{:S(2)}, u32[]{:S(2)}) collective-permute-start(bf16[128,2048]{1,0:T(8,128)(2,1)} %collective-permute-done.16.refs_0_), channel_id=1, source_target_pairs={{0,32},{1,225},{2,34},{3,227},{4,36},{5,229},{6,38},{7,231},{8,40}... | collective-permute-start | bytes 1572872 | tf_op jit(solution)/shard_map/ppermute | solution.py:43
  60.5 41.4 %collective-permute-start.22 = (bf16[128,2048]{1,0:T(8,128)(2,1)}, bf16[128,2048]{1,0:T(8,128)(2,1)}, u32[]{:S(2)}, u32[]{:S(2)}) collective-permute-start(bf16[128,2048]{1,0:T(8,128)(2,1)} %collective-permute-done.17.refs_1_), channel_id=1, source_target_pairs={{0,32},{1,225},{2,34},{3,227},{4,36},{5,229},{6,38},{7,231},{8,40}... | collective-permute-start | bytes 1572872 | tf_op jit(solution)/shard_map/ppermute | solution.py:43
  64.2 18.6 %copy-start.11 = (bf16[2,2,32,1024]{3,2,1,0:T(8,128)(2,1)}, bf16[2,2,32,1024]{3,2,1,0:T(8,128)(2,1)S(1)}, u32[]{:S(2)}) copy-start(bf16[2,2,32,1024]{3,2,1,0:T(8,128)(2,1)S(1)} %get-tuple-element.51.refs_4_) | copy-start | bytes 786436
  68.1 14.7 %copy-start.5 = (bf16[2,2,32,1536]{3,2,1,0:T(8,128)(2,1)}, bf16[2,2,32,1536]{3,2,1,0:T(8,128)(2,1)S(1)}, u32[]{:S(2)}) copy-start(bf16[2,2,32,1536]{3,2,1,0:T(8,128)(2,1)S(1)} %collective-permute-done.4.refs_1_) | copy-start | bytes 1179652
  68.1 15.7 %collective-permute-start.9 = (bf16[2,2,32,1024]{3,2,1,0:T(8,128)(2,1)S(1)}, bf16[2,2,32,1024]{3,2,1,0:T(8,128)(2,1)S(1)}, u32[]{:S(2)}, u32[]{:S(2)}) collective-permute-start(bf16[2,2,32,1024]{3,2,1,0:T(8,128)(2,1)S(1)} %get-tuple-element.52), channel_id=1, source_target_pairs={{0,2},{1,3},{2,4},{3,5},{4,6},{5,7},{6,0},{7,1},{8,10},{9,11},{10,... | collective-permute-start | bytes 786440 | tf_op jit(solution)/shard_map/ppermute | solution.py:43
  68.1 14.6 %copy-start.7 = (bf16[2,2,32,1536]{3,2,1,0:T(8,128)(2,1)}, bf16[2,2,32,1536]{3,2,1,0:T(8,128)(2,1)S(1)}, u32[]{:S(2)}) copy-start(bf16[2,2,32,1536]{3,2,1,0:T(8,128)(2,1)S(1)} %collective-permute-done.5.refs_2_) | copy-start | bytes 1179652
  68.2 16.4 %collective-permute-start.10 = (bf16[2,2,32,1024]{3,2,1,0:T(8,128)(2,1)S(1)}, bf16[2,2,32,1024]{3,2,1,0:T(8,128)(2,1)S(1)}, u32[]{:S(2)}, u32[]{:S(2)}) collective-permute-start(bf16[2,2,32,1024]{3,2,1,0:T(8,128)(2,1)S(1)} %get-tuple-element.53), channel_id=1, source_target_pairs={{0,6},{1,7},{2,0},{3,1},{4,2},{5,3},{6,4},{7,5},{8,14},{9,15},{10,... | collective-permute-start | bytes 786440 | tf_op jit(solution)/shard_map/ppermute | solution.py:43
  77.6 5.2 %copy-start.9 = (bf16[2,2,32,1536]{3,2,1,0:T(8,128)(2,1)}, bf16[2,2,32,1536]{3,2,1,0:T(8,128)(2,1)S(1)}, u32[]{:S(2)}) copy-start(bf16[2,2,32,1536]{3,2,1,0:T(8,128)(2,1)S(1)} %collective-permute-done.6.refs_3_) | copy-start | bytes 1179652
  77.6 10.6 %collective-permute-start.11 = (bf16[2,2,32,1024]{3,2,1,0:T(8,128)(2,1)S(1)}, bf16[2,2,32,1024]{3,2,1,0:T(8,128)(2,1)S(1)}, u32[]{:S(2)}, u32[]{:S(2)}) collective-permute-start(bf16[2,2,32,1024]{3,2,1,0:T(8,128)(2,1)S(1)} %get-tuple-element.54), channel_id=1, source_target_pairs={{0,4},{1,5},{2,6},{3,7},{4,0},{5,1},{6,2},{7,3},{8,12},{9,13},{10,... | collective-permute-start | bytes 786440 | tf_op jit(solution)/shard_map/ppermute | solution.py:43
  84.5 20.0 %collective-permute-start.18 = (bf16[2,2,32,1024]{3,2,1,0:T(8,128)(2,1)}, bf16[2,2,32,1024]{3,2,1,0:T(8,128)(2,1)}, u32[]{:S(2)}, u32[]{:S(2)}) collective-permute-start(bf16[2,2,32,1024]{3,2,1,0:T(8,128)(2,1)} %get-tuple-element.62), channel_id=1, source_target_pairs={{0,2},{1,3},{2,4},{3,5},{4,6},{5,7},{6,0},{7,1},{8,10},{9,11},{10,... | collective-permute-start | bytes 786440 | tf_op jit(solution)/shard_map/ppermute | solution.py:43
  85.3 22.0 %collective-permute-start.19 = (bf16[2,2,32,1024]{3,2,1,0:T(8,128)(2,1)}, bf16[2,2,32,1024]{3,2,1,0:T(8,128)(2,1)}, u32[]{:S(2)}, u32[]{:S(2)}) collective-permute-start(bf16[2,2,32,1024]{3,2,1,0:T(8,128)(2,1)} %get-tuple-element.63), channel_id=1, source_target_pairs={{0,6},{1,7},{2,0},{3,1},{4,2},{5,3},{6,4},{7,5},{8,14},{9,15},{10,... | collective-permute-start | bytes 786440 | tf_op jit(solution)/shard_map/ppermute | solution.py:43
  88.9 18.9 %collective-permute-start.20 = (bf16[2,2,32,1024]{3,2,1,0:T(8,128)(2,1)}, bf16[2,2,32,1024]{3,2,1,0:T(8,128)(2,1)}, u32[]{:S(2)}, u32[]{:S(2)}) collective-permute-start(bf16[2,2,32,1024]{3,2,1,0:T(8,128)(2,1)} %get-tuple-element.64), channel_id=1, source_target_pairs={{0,4},{1,5},{2,6},{3,7},{4,0},{5,1},{6,2},{7,3},{8,12},{9,13},{10,... | collective-permute-start | bytes 786440 | tf_op jit(solution)/shard_map/ppermute | solution.py:43
  90.0 11.8 %copy-start.1 = (bf16[2,256,2048]{2,1,0:T(8,128)(2,1)S(1)}, bf16[2,256,2048]{2,1,0:T(8,128)(2,1)}, u32[]{:S(2)}) copy-start(bf16[2,256,2048]{2,1,0:T(8,128)(2,1)} %copy-done) | copy-start | bytes 6291460
  90.0 1.1 copy-start.4
  99.0 15.0 %collective-permute-start.12 = (bf16[2,32,2560]{2,1,0:T(8,128)(2,1)}, bf16[2,32,2560]{2,1,0:T(8,128)(2,1)}, u32[]{:S(2)}, u32[]{:S(2)}) collective-permute-start(bf16[2,32,2560]{2,1,0:T(8,128)(2,1)} %get-tuple-element.56), channel_id=1, source_target_pairs={{0,8},{1,9},{2,10},{3,11},{4,12},{5,13},{6,14},{7,15},{8,0},{9,1},... | collective-permute-start | bytes 983048 | tf_op jit(solution)/shard_map/ppermute | solution.py:43
  104.3 5.7 %collective-permute-start.23 = (bf16[2,2,32,512]{3,2,1,0:T(8,128)(2,1)S(1)}, bf16[2,2,32,512]{3,2,1,0:T(8,128)(2,1)S(1)}, u32[]{:S(2)}, u32[]{:S(2)}) collective-permute-start(bf16[2,2,32,512]{3,2,1,0:T(8,128)(2,1)S(1)} %get-tuple-element.66), channel_id=1, source_target_pairs={{0,2},{1,3},{2,4},{3,5},{4,6},{5,7},{6,0},{7,1},{8,10},{9,11},{10,... | collective-permute-start | bytes 393224 | tf_op jit(solution)/shard_map/ppermute | solution.py:43
  104.6 6.0 %collective-permute-start.24 = (bf16[2,2,32,512]{3,2,1,0:T(8,128)(2,1)S(1)}, bf16[2,2,32,512]{3,2,1,0:T(8,128)(2,1)S(1)}, u32[]{:S(2)}, u32[]{:S(2)}) collective-permute-start(bf16[2,2,32,512]{3,2,1,0:T(8,128)(2,1)S(1)} %get-tuple-element.67), channel_id=1, source_target_pairs={{0,6},{1,7},{2,0},{3,1},{4,2},{5,3},{6,4},{7,5},{8,14},{9,15},{10,... | collective-permute-start | bytes 393224 | tf_op jit(solution)/shard_map/ppermute | solution.py:43
  107.2 5.3 %collective-permute-start.25 = (bf16[2,2,32,512]{3,2,1,0:T(8,128)(2,1)S(1)}, bf16[2,2,32,512]{3,2,1,0:T(8,128)(2,1)S(1)}, u32[]{:S(2)}, u32[]{:S(2)}) collective-permute-start(bf16[2,2,32,512]{3,2,1,0:T(8,128)(2,1)S(1)} %get-tuple-element.68), channel_id=1, source_target_pairs={{0,4},{1,5},{2,6},{3,7},{4,0},{5,1},{6,2},{7,3},{8,12},{9,13},{10,... | collective-permute-start | bytes 393224 | tf_op jit(solution)/shard_map/ppermute | solution.py:43
  113.9 12.7 %collective-permute-start.26 = (bf16[2,32,1536]{2,1,0:T(8,128)(2,1)S(1)}, bf16[2,32,1536]{2,1,0:T(8,128)(2,1)S(1)}, u32[]{:S(2)}, u32[]{:S(2)}) collective-permute-start(bf16[2,32,1536]{2,1,0:T(8,128)(2,1)S(1)} %get-tuple-element.70), channel_id=1, source_target_pairs={{0,8},{1,9},{2,10},{3,11},{4,12},{5,13},{6,14},{7,15},{8,0},{9,1},... | collective-permute-start | bytes 589832 | tf_op jit(solution)/shard_map/ppermute | solution.py:43
  115.0 8.0 %collective-permute-start.13 = (bf16[2,16,512]{2,1,0:T(8,128)(2,1)S(1)}, bf16[2,16,512]{2,1,0:T(8,128)(2,1)S(1)}, u32[]{:S(2)}, u32[]{:S(2)}) collective-permute-start(bf16[2,16,512]{2,1,0:T(8,128)(2,1)S(1)} %get-tuple-element.58), channel_id=1, source_target_pairs={{0,16},{1,17},{2,18},{3,19},{4,20},{5,21},{6,22},{7,23},{8,24},{9,... | collective-permute-start | bytes 98312 | tf_op jit(solution)/shard_map/ppermute | solution.py:43
  116.8 9.7 %collective-permute-start.14 = (bf16[2,16,512]{2,1,0:T(8,128)(2,1)S(1)}, bf16[2,16,512]{2,1,0:T(8,128)(2,1)S(1)}, u32[]{:S(2)}, u32[]{:S(2)}) collective-permute-start(bf16[2,16,512]{2,1,0:T(8,128)(2,1)S(1)} %get-tuple-element.59), channel_id=1, source_target_pairs={{0,224},{1,33},{2,226},{3,35},{4,228},{5,37},{6,230},{7,39},{8,232... | collective-permute-start | bytes 98312 | tf_op jit(solution)/shard_map/ppermute | solution.py:43
  116.8 16.6 %collective-permute-start.29 = (bf16[2,16,1024]{2,1,0:T(8,128)(2,1)S(1)}, bf16[2,16,1024]{2,1,0:T(8,128)(2,1)S(1)}, u32[]{:S(2)}, u32[]{:S(2)}) collective-permute-start(bf16[2,16,1024]{2,1,0:T(8,128)(2,1)S(1)} %get-tuple-element.74), channel_id=1, source_target_pairs={{0,1},{1,0},{2,3},{3,2},{4,5},{5,4},{6,7},{7,6},{8,9},{9,8},{10,11... | collective-permute-start | bytes 196616 | tf_op jit(solution)/shard_map/ppermute | solution.py:43
  123.0 4.9 %collective-permute-start.15 = (bf16[2,16,512]{2,1,0:T(8,128)(2,1)S(1)}, bf16[2,16,512]{2,1,0:T(8,128)(2,1)S(1)}, u32[]{:S(2)}, u32[]{:S(2)}) collective-permute-start(bf16[2,16,512]{2,1,0:T(8,128)(2,1)S(1)} %get-tuple-element.60), channel_id=1, source_target_pairs={{0,192},{1,65},{2,194},{3,67},{4,196},{5,69},{6,198},{7,71},{8,200... | collective-permute-start | bytes 98312 | tf_op jit(solution)/shard_map/ppermute | solution.py:43
  123.0 5.1 %collective-permute-start.30 = (bf16[2,16,512]{2,1,0:T(8,128)(2,1)S(1)}, bf16[2,16,512]{2,1,0:T(8,128)(2,1)S(1)}, u32[]{:S(2)}, u32[]{:S(2)}) collective-permute-start(bf16[2,16,512]{2,1,0:T(8,128)(2,1)S(1)} %get-tuple-element.75), channel_id=1, source_target_pairs={{0,17},{1,16},{2,19},{3,18},{4,21},{5,20},{6,23},{7,22},{8,25},{9,... | collective-permute-start | bytes 98312 | tf_op jit(solution)/shard_map/ppermute | solution.py:43
  126.5 3.3 %collective-permute-start.31 = (bf16[2,16,512]{2,1,0:T(8,128)(2,1)S(1)}, bf16[2,16,512]{2,1,0:T(8,128)(2,1)S(1)}, u32[]{:S(2)}, u32[]{:S(2)}) collective-permute-start(bf16[2,16,512]{2,1,0:T(8,128)(2,1)S(1)} %get-tuple-element.76), channel_id=1, source_target_pairs={{0,225},{1,32},{2,227},{3,34},{4,229},{5,36},{6,231},{7,38},{8,233... | collective-permute-start | bytes 98312 | tf_op jit(solution)/shard_map/ppermute | solution.py:43
  126.5 5.5 %collective-permute-start.32 = (bf16[2,16,512]{2,1,0:T(8,128)(2,1)S(1)}, bf16[2,16,512]{2,1,0:T(8,128)(2,1)S(1)}, u32[]{:S(2)}, u32[]{:S(2)}) collective-permute-start(bf16[2,16,512]{2,1,0:T(8,128)(2,1)S(1)} %get-tuple-element.77), channel_id=1, source_target_pairs={{0,193},{1,64},{2,195},{3,66},{4,197},{5,68},{6,199},{7,70},{8,201... | collective-permute-start | bytes 98312 | tf_op jit(solution)/shard_map/ppermute | solution.py:43
  127.9 7.4 %collective-permute-start.27 = (bf16[2,16,512]{2,1,0:T(8,128)(2,1)S(1)}, bf16[2,16,512]{2,1,0:T(8,128)(2,1)S(1)}, u32[]{:S(2)}, u32[]{:S(2)}) collective-permute-start(bf16[2,16,512]{2,1,0:T(8,128)(2,1)S(1)} %get-tuple-element.72), channel_id=1, source_target_pairs={{0,16},{1,17},{2,18},{3,19},{4,20},{5,21},{6,22},{7,23},{8,24},{9,... | collective-permute-start | bytes 98312 | tf_op jit(solution)/shard_map/ppermute | solution.py:43
  128.1 7.1 %collective-permute-start.28 = (bf16[2,16,512]{2,1,0:T(8,128)(2,1)S(1)}, bf16[2,16,512]{2,1,0:T(8,128)(2,1)S(1)}, u32[]{:S(2)}, u32[]{:S(2)}) collective-permute-start(bf16[2,16,512]{2,1,0:T(8,128)(2,1)S(1)} %get-tuple-element.73), channel_id=1, source_target_pairs={{0,160},{1,97},{2,162},{3,99},{4,164},{5,101},{6,166},{7,103},{8,1... | collective-permute-start | bytes 98312 | tf_op jit(solution)/shard_map/ppermute | solution.py:43
  129.8 5.4 %collective-permute-start.33 = (bf16[2,16,512]{2,1,0:T(8,128)(2,1)S(1)}, bf16[2,16,512]{2,1,0:T(8,128)(2,1)S(1)}, u32[]{:S(2)}, u32[]{:S(2)}) collective-permute-start(bf16[2,16,512]{2,1,0:T(8,128)(2,1)S(1)} %get-tuple-element.78), channel_id=1, source_target_pairs={{0,1},{1,0},{2,3},{3,2},{4,5},{5,4},{6,7},{7,6},{8,9},{9,8},{10,11... | collective-permute-start | bytes 98312 | tf_op jit(solution)/shard_map/ppermute | solution.py:43
  132.0 3.6 %collective-permute-start.34 = (bf16[2,16,512]{2,1,0:T(8,128)(2,1)S(1)}, bf16[2,16,512]{2,1,0:T(8,128)(2,1)S(1)}, u32[]{:S(2)}, u32[]{:S(2)}) collective-permute-start(bf16[2,16,512]{2,1,0:T(8,128)(2,1)S(1)} %get-tuple-element.79), channel_id=1, source_target_pairs={{0,17},{1,16},{2,19},{3,18},{4,21},{5,20},{6,23},{7,22},{8,25},{9,... | collective-permute-start | bytes 98312 | tf_op jit(solution)/shard_map/ppermute | solution.py:43
  133.4 5.4 %collective-permute-start.35 = (bf16[2,16,512]{2,1,0:T(8,128)(2,1)S(1)}, bf16[2,16,512]{2,1,0:T(8,128)(2,1)S(1)}, u32[]{:S(2)}, u32[]{:S(2)}) collective-permute-start(bf16[2,16,512]{2,1,0:T(8,128)(2,1)S(1)} %get-tuple-element.80), channel_id=1, source_target_pairs={{0,161},{1,96},{2,163},{3,98},{4,165},{5,100},{6,167},{7,102},{8,1... | collective-permute-start | bytes 98312 | tf_op jit(solution)/shard_map/ppermute | solution.py:43
  (12 other events, 10.5 us)

commit v2 on v1

--- a/solution.py
+++ b/solution.py
@@ -126,39 +126,62 @@
             acc_ref[m, h, x, :, first : first + n] = (value[at : at + 32] * scale).astype(BF16)
 
 
-def products(xi, parts, chunks, wide, scale, name):
+def products(at, parts, chunks, wide, scale, name):
     count = len(chunks)
 
-    def kernel(xi_ref, *refs):
-        ins, outs, acc_ref = refs[:count], refs[count : count + 4], refs[count + 4]
+    def kernel(at_ref, *refs):
+        ins, (keep_ref, send_ref), acc_ref = refs[:count], refs[count : count + 2], refs[count + 2]
+        x, c = at_ref[0], at_ref[1]
+        near, far = 1 + 2 * c, 3 - 2 * c
         for m in range(LAGS):
             for first, value in parts(m, ins):
                 store_product(acc_ref, m, first, value, scale)
-        for s in range(4):
-            to = lax.rem(xi_ref[0] + s, 4)
+        slices = ((keep_ref, 0, x), (keep_ref, 1, x ^ far), (send_ref, 0, x ^ near), (send_ref, 1, x ^ 2))
+        for out, k, which in slices:
             for m in range(LAGS):
                 for h in range(2):
-                    outs[s][h, m] = acc_ref[m, h, to]
-
-    shape = jax.ShapeDtypeStruct((2, LAGS, 32, wide), BF16)
+                    out[k, h, m] = acc_ref[m, h, which]
+
+    shape = jax.ShapeDtypeStruct((2, 2, LAGS, 32, wide), BF16)
     whole = pl.BlockSpec(memory_space=pltpu.VMEM)
     return pl.pallas_call(
         kernel,
         in_specs=[pl.BlockSpec(memory_space=pltpu.SMEM)] + [whole] * count,
-        out_specs=[whole] * 4,
-        out_shape=(shape,) * 4,
+        out_specs=[whole] * 2,
+        out_shape=(shape,) * 2,
         scratch_shapes=[pltpu.VMEM((LAGS, 2, 4, 32, wide), BF16)],
-        compiler_params=params(28),
+        compiler_params=params(24),
         cost_estimate=cost(2 * 2 * 256 * wide * DEPTH, 8 * MIB),
         name=name,
-    )(xi, *chunks)
+    )(at, *chunks)
 
 
 def both(a_ref, b_ref):
     return jnp.concatenate([a_ref[...], b_ref[...]], 0)
 
 
-def sum_x(yi, groups):
+def sum_1(keep, recv):
+    n = keep.shape[4]
+
+    def kernel(keep_ref, recv_ref, kept_ref, send_ref):
+        for h in range(2):
+            for m in range(LAGS):
+                kept_ref[h, m] = keep_ref[0, h, m].astype(F32) + recv_ref[0, h, m].astype(F32)
+                send_ref[h, m] = (keep_ref[1, h, m].astype(F32) + recv_ref[1, h, m].astype(F32)).astype(BF16)
+
+    whole = pl.BlockSpec(memory_space=pltpu.VMEM)
+    return pl.pallas_call(
+        kernel,
+        in_specs=[whole] * 2,
+        out_specs=[whole] * 2,
+        out_shape=tuple(jax.ShapeDtypeStruct((2, LAGS, 32, n), t) for t in (F32, BF16)),
+        compiler_params=params(16),
+        cost_estimate=cost(1000, MIB),
+        name="sum_1",
+    )(keep, recv)
+
+
+def sum_2(yi, groups):
     widths = [g[0].shape[3] for g in groups]
     total = sum(widths)
     flat = [a for g in groups for a in g]
@@ -168,14 +191,10 @@
         mine, other = yi_ref[0], 1 - yi_ref[0]
         first = 0
         for k, n in enumerate(widths):
-            four = refs[4 * k : 4 * k + 4]
+            kept, recv = refs[2 * k], refs[2 * k + 1]
             for m in range(LAGS):
-                for r in range(0, 32, 16):
-                    at = pl.ds(r, 16)
-                    val = [f[mine, m, at, :].astype(F32) for f in four]
-                    keep_ref[m, at, first : first + n] = (val[0] + val[1]) + (val[2] + val[3])
-                    val = [f[other, m, at, :].astype(F32) for f in four]
-                    send_ref[m, at, first : first + n] = ((val[0] + val[1]) + (val[2] + val[3])).astype(BF16)
+                keep_ref[m, :, first : first + n] = kept[mine, m] + recv[mine, m].astype(F32)
+                send_ref[m, :, first : first + n] = (kept[other, m] + recv[other, m].astype(F32)).astype(BF16)
             first += n
 
     whole = pl.BlockSpec(memory_space=pltpu.VMEM)
@@ -185,8 +204,8 @@
         out_specs=[whole] * 2,
         out_shape=(jax.ShapeDtypeStruct((LAGS, 32, total), F32), jax.ShapeDtypeStruct((LAGS, 32, total), BF16)),
         compiler_params=params(16),
-        cost_estimate=cost(1000, 2 * MIB),
-        name="sum_x",
+        cost_estimate=cost(1000, MIB),
+        name="sum_2",
     )(yi, *flat)
 
 
@@ -271,8 +290,12 @@
     return z, ylo, yhi, x, 1 - c
 
 
-def x_step(s):
-    return lambda z, ylo, yhi, x, c: (z, ylo, yhi, x + s, c)
+def x_near(z, ylo, yhi, x, c):
+    return z, ylo, yhi, x ^ (1 + 2 * c), c
+
+
+def x_far(z, ylo, yhi, x, c):
+    return z, ylo, yhi, x ^ (3 - 2 * c), c
 
 
 def back(d):
@@ -283,12 +306,12 @@
     return lambda z, ylo, yhi, x, c: (z - sign(c) * d, ylo, yhi, x, 1 - c)
 
 
-def reduce_x(slots):
-    return [slots[0]] + [move(slots[s], x_step(s)) for s in (1, 3, 2)]
+def after(value, *others):
+    return lax.optimization_barrier((value,) + others)[0]
 
 
 def batch(yi, ci, groups, classes):
-    keep, send = sum_x(yi, groups)
+    keep, send = sum_2(yi, groups)
     recv = move(send, yhi_step)
     own, wy, ret = [], [], []
     first = 0
@@ -314,7 +337,8 @@
 def body(spectra, bin_index):
     scale = 1.0 / math.sqrt(32 * BINS)
     z, y = lax.axis_index("z"), lax.axis_index("ylo")
-    yi, xi, ci = (lax.axis_index(a).astype(jnp.int32).reshape(1) for a in ("yhi", "x", "c"))
+    yi, ci = (lax.axis_index(a).astype(jnp.int32).reshape(1) for a in ("yhi", "c"))
+    at = jnp.stack([lax.axis_index("x"), lax.axis_index("c")]).astype(jnp.int32)
     place = jnp.stack([z, y, lax.axis_index("c")]).astype(jnp.int32)
 
     own = [whiten(spectra, 0), whiten(spectra, 1)]
@@ -353,13 +377,28 @@
         yield BLOCK, dot_nt(ins[3][m], b)
 
     rotated = [own_plus, own_minus, near_plus, near_minus]
-    g1 = reduce_x(products(xi, first_pairs, arrived[0] + own + near + rotated, 6 * BLOCK, scale, "pairs_0_1"))
-    g2 = reduce_x(products(xi, all_pairs, arrived[1] + rotated, 4 * BLOCK, scale, "pairs_2"))
-    g3 = reduce_x(products(xi, all_pairs, arrived[2] + rotated, 4 * BLOCK, scale, "pairs_3"))
-    g4 = reduce_x(products(xi, last_pairs, arrived[3] + [own_plus, near_plus], 2 * BLOCK, scale, "pairs_4"))
-
-    same1, other1 = batch(yi, ci, [g1, g2], [(3 * BLOCK, BLOCK, 1), (BLOCK, BLOCK, 2)])
-    same2, other2 = batch(yi, ci, [g3, g4], [(BLOCK, BLOCK, 3), (BLOCK, BLOCK, 0)])
+    at_a = after(at, arrived[1][0])
+    keep_a, send_a = products(at_a, first_pairs, arrived[0] + own + near + rotated, 6 * BLOCK, scale, "pairs_0_1")
+    recv_a = move(send_a, x_near)
+    keep_b, send_b = products(after(at, keep_a), all_pairs, arrived[1] + rotated, 4 * BLOCK, scale, "pairs_2")
+    recv_b = move(send_b, x_near)
+    kept_a, send_a = sum_1(after(keep_a, arrived[2][1]), recv_a)
+    recv_a = move(send_a, x_far)
+    at_c = after(at, kept_a)
+    keep_c, send_c = products(at_c, all_pairs, arrived[2] + rotated, 4 * BLOCK, scale, "pairs_3")
+    recv_c = move(send_c, x_near)
+    kept_b, send_b = sum_1(after(keep_b, keep_c), recv_b)
+    recv_b = move(send_b, x_far)
+    at_d = after(at, kept_b)
+    keep_d, send_d = products(at_d, last_pairs, arrived[3] + [own_plus, near_plus], 2 * BLOCK, scale, "pairs_4")
+    recv_d = move(send_d, x_near)
+    kept_c, send_c = sum_1(after(keep_c, keep_d), recv_c)
+    recv_c = move(send_c, x_far)
+    kept_a = after(kept_a, kept_c)
+    same1, other1 = batch(yi, ci, [(kept_a, recv_a), (kept_b, recv_b)], [(3 * BLOCK, BLOCK, 1), (BLOCK, BLOCK, 2)])
+    kept_d, send_d = sum_1(keep_d, recv_d)
+    recv_d = move(send_d, x_far)
+    same2, other2 = batch(yi, ci, [(kept_c, recv_c), (kept_d, recv_d)], [(BLOCK, BLOCK, 3), (BLOCK, BLOCK, 0)])
     blocks1 = [[(0, 0), (0, 1), (1, 0), (2, 0)], [(1, 1), (2, 1)], [(-1, 0), (-1, 1)], [(-2, 0), (-2, 1)]]
     blocks2 = [[(3, 0), (4, 0)], [(3, 1), (4, 1)], [(-3, 0), (-3, 1)]]
     ids = blocks1 + blocks2

time: 141 us -> 110 us (0.78)
  local copies, waits for them, and re-layouts: 12.9 us -> 1.23 us
  starting transfers between devices: 58 us -> 48.3 us
  Pallas kernels: 25.4 us -> 19.3 us
  waiting for transfers between devices: 43.5 us -> 40.5 us
    unnamed x48 -> x4, local copies, waits for them, and re-layouts: 12.9 us -> 1.23 us
    ppermute x36 -> x32, starting transfers between devices: 58 us -> 48.3 us  [move(): return lax.ppermute(x, AXES, pairs)]
    pallas_call x4, Pallas kernels: 16.2 us -> 12 us  [products(): pl.pallas_call(kernel, in_specs=[pl.BlockSpec(memory_space=pltpu.SMEM)] +...]
    ppermute x36 -> x32, waiting for transfers between devices: 43.5 us -> 40.5 us  [move(): return lax.ppermute(x, AXES, pairs)]
  transfers between devices with their start and end apart: 36 -> 32, of which waited for: 17 -> 15; matrix products, arithmetic and copies ran while one was open for 0% -> 0% of each run, Pallas kernels for 17% -> 16%
where the time goes in v2:
time: 110 us
  starting transfers between devices  48.3 us (44%)
  waiting for transfers between devices  40.5 us (37%)
  Pallas kernels  19.3 us (18%)
  local copies, waits for them, and re-layouts  1.23 us (1%)
    ppermute x32, starting transfers between devices, move(): return lax.ppermute(x, AXES, pairs)  48.3 us
    ppermute x32, waiting for transfers between devices, move(): return lax.ppermute(x, AXES, pairs)  40.5 us
    pallas_call x4, Pallas kernels, products(): pl.pallas_call(kernel, in_specs=[pl.BlockSpec(memory_space=pltpu.SMEM)] +...  12 us
    pallas_call x4, Pallas kernels, sum_1(): pl.pallas_call(kernel, in_specs=[whole] * 2, out_specs=[whole] * 2, out_s...  2.46 us
  transfers between devices with their start and end apart: 32, of which 15 were waited for; matrix products, arithmetic and copies ran while one was open for 0% of the time, Pallas kernels for 16%

profile of v2, /device:TPU:1, one launch (start us, length us, event | category | flops | bytes accessed | tf_op | source)
XLA Modules:
  0.0 109.8 jit_solution(11614305107086967053)
XLA Ops:
  0.0 1.2 %copy-done = bf16[2,2,512,256]{3,2,1,0:T(8,128)(2,1)S(1)} copy-done((bf16[2,2,512,256]{3,2,1,0:T(8,128)(2,1)S(1)}, bf16[2,2,512,256]{3,2,1,0:T(8,128)(2,1)}, u32[]{:S(2)}) %copy-start) | copy-done | bytes 1048600
  1.2 0.6 whiten.2.a_ref.refs_2_
  1.8 6.5 %collective-permute-start = (bf16[128,2048]{1,0:T(8,128)(2,1)S(1)}, bf16[128,2048]{1,0:T(8,128)(2,1)S(1)}, u32[]{:S(2)}, u32[]{:S(2)}) collective-permute-start(bf16[128,2048]{1,0:T(8,128)(2,1)S(1)} %whiten.2.a_ref.refs_2_), channel_id=1, source_target_pairs={{0,32},{1,225},{2,34},{3,227},{4,36},{5,229},{6,38},{7,231},{8,40}... | collective-permute-start | bytes 1572872 | tf_op jit(solution)/shard_map/ppermute | solution.py:43
  8.3 1.3 %collective-permute-start.3 = (bf16[128,2048]{1,0:T(8,128)(2,1)S(1)}, bf16[128,2048]{1,0:T(8,128)(2,1)S(1)}, u32[]{:S(2)}, u32[]{:S(2)}) collective-permute-start(bf16[128,2048]{1,0:T(8,128)(2,1)S(1)} %whiten.2.a_ref.refs_2_), channel_id=1, source_target_pairs={{0,16},{1,17},{2,18},{3,19},{4,20},{5,21},{6,22},{7,23},{8,24},{9,... | collective-permute-start | bytes 1572872 | tf_op jit(solution)/shard_map/ppermute | solution.py:43
  9.6 0.6 whiten.3.b_ref.refs_3_
  10.5 0.7 collective-permute-start.2
  11.2 3.2 %collective-permute-done.refs_0_ = bf16[128,2048]{1,0:T(8,128)(2,1)S(1)} collective-permute-done((bf16[128,2048]{1,0:T(8,128)(2,1)S(1)}, bf16[128,2048]{1,0:T(8,128)(2,1)S(1)}, u32[]{:S(2)}, u32[]{:S(2)}) %collective-permute-start) | collective-permute-done | bytes 524320 | tf_op jit(solution)/shard_map/ppermute | solution.py:43
  14.4 3.1 %collective-permute-start.1 = (bf16[128,2048]{1,0:T(8,128)(2,1)S(1)}, bf16[128,2048]{1,0:T(8,128)(2,1)S(1)}, u32[]{:S(2)}, u32[]{:S(2)}) collective-permute-start(bf16[128,2048]{1,0:T(8,128)(2,1)S(1)} %collective-permute-done.refs_0_), channel_id=1, source_target_pairs={{0,32},{1,225},{2,34},{3,227},{4,36},{5,229},{6,38},{7,231},{8,40}... | collective-permute-start | bytes 1572872 | tf_op jit(solution)/shard_map/ppermute | solution.py:43
  17.7 0.9 rotate.2
  18.8 1.3 %collective-permute-done.2.refs_1_ = bf16[128,2048]{1,0:T(8,128)(2,1)S(1)} collective-permute-done((bf16[128,2048]{1,0:T(8,128)(2,1)S(1)}, bf16[128,2048]{1,0:T(8,128)(2,1)S(1)}, u32[]{:S(2)}, u32[]{:S(2)}) %collective-permute-start.2) | collective-permute-done | bytes 524320 | tf_op jit(solution)/shard_map/ppermute | solution.py:43
  20.1 3.1 %collective-permute-start.5 = (bf16[128,2048]{1,0:T(8,128)(2,1)S(1)}, bf16[128,2048]{1,0:T(8,128)(2,1)S(1)}, u32[]{:S(2)}, u32[]{:S(2)}) collective-permute-start(bf16[128,2048]{1,0:T(8,128)(2,1)S(1)} %collective-permute-done.2.refs_1_), channel_id=1, source_target_pairs={{0,32},{1,225},{2,34},{3,227},{4,36},{5,229},{6,38},{7,231},{8,40}... | collective-permute-start | bytes 1572872 | tf_op jit(solution)/shard_map/ppermute | solution.py:43
  23.2 7.8 %collective-permute-done.4.b_ref.refs_5_ = bf16[128,2048]{1,0:T(8,128)(2,1)S(1)} collective-permute-done((bf16[128,2048]{1,0:T(8,128)(2,1)S(1)}, bf16[128,2048]{1,0:T(8,128)(2,1)S(1)}, u32[]{:S(2)}, u32[]{:S(2)}) %collective-permute-start.4) | collective-permute-done | bytes 524320 | tf_op jit(solution)/shard_map/ppermute | solution.py:43
  31.0 0.9 rotate.3
  31.9 4.2 %pairs_0_1.1 = (bf16[2,2,2,32,1536]{4,3,2,1,0:T(8,128)(2,1)S(1)}, bf16[2,2,2,32,1536]{4,3,2,1,0:T(8,128)(2,1)S(1)}) custom-call(s32[2]{0:T(128)S(1)} %pad_add_fusion.1.at_ref, bf16[128,2048]{1,0:T(8,128)(2,1)S(1)} %collective-permute-done.refs_0_, bf16[128,2048]{1,0:T(8,128)(2,1)S(1)} %collective-permute-done.2.refs_1_, ...), custom_call_target="tpu_custom_call" | custom-call | flops 3221225472 | bytes 8388608 | tf_op jit(solution)/shard_map/pairs_0_1/pallas_call | solution.py:147
  36.1 2.6 %collective-permute-start.7 = (bf16[2,2,2,32,1536]{4,3,2,1,0:T(8,128)(2,1)S(1)}, bf16[2,2,2,32,1536]{4,3,2,1,0:T(8,128)(2,1)S(1)}, u32[]{:S(2)}, u32[]{:S(2)}) collective-permute-start(bf16[2,2,2,32,1536]{4,3,2,1,0:T(8,128)(2,1)S(1)} %get-tuple-element.58), channel_id=1, source_target_pairs={{0,2},{1,7},{2,0},{3,5},{4,6},{5,3},{6,4},{7,1},{8,10},{9,15},{10,... | collective-permute-start | bytes 2359304 | tf_op jit(solution)/shard_map/ppermute | solution.py:43
  38.7 2.8 %collective-permute-start.8 = (bf16[128,2048]{1,0:T(8,128)(2,1)S(1)}, bf16[128,2048]{1,0:T(8,128)(2,1)S(1)}, u32[]{:S(2)}, u32[]{:S(2)}) collective-permute-start(bf16[128,2048]{1,0:T(8,128)(2,1)S(1)} %collective-permute-done.1.refs_0_), channel_id=1, source_target_pairs={{0,32},{1,225},{2,34},{3,227},{4,36},{5,229},{6,38},{7,231},{8,40}... | collective-permute-start | bytes 1572872 | tf_op jit(solution)/shard_map/ppermute | solution.py:43
  41.5 3.0 %pairs_2.1 = (bf16[2,2,2,32,1024]{4,3,2,1,0:T(8,128)(2,1)S(1)}, bf16[2,2,2,32,1024]{4,3,2,1,0:T(8,128)(2,1)S(1)}) custom-call(s32[2]{0:T(128)S(1)} %pad_add_fusion.1.at_ref, bf16[128,2048]{1,0:T(8,128)(2,1)S(1)} %collective-permute-done.1.refs_0_, bf16[128,2048]{1,0:T(8,128)(2,1)S(1)} %collective-permute-done.5.refs_1_, ...), custom_call_target="tpu_custom_call" | custom-call | flops 2147483648 | bytes 8388608 | tf_op jit(solution)/shard_map/pairs_2/pallas_call | solution.py:147
  45.0 2.6 %collective-permute-done.8.refs_0_ = bf16[128,2048]{1,0:T(8,128)(2,1)S(1)} collective-permute-done((bf16[128,2048]{1,0:T(8,128)(2,1)S(1)}, bf16[128,2048]{1,0:T(8,128)(2,1)S(1)}, u32[]{:S(2)}, u32[]{:S(2)}) %collective-permute-start.8) | collective-permute-done | bytes 524320 | tf_op jit(solution)/shard_map/ppermute | solution.py:43
  47.6 3.1 %collective-permute-start.10 = (bf16[128,2048]{1,0:T(8,128)(2,1)S(1)}, bf16[128,2048]{1,0:T(8,128)(2,1)S(1)}, u32[]{:S(2)}, u32[]{:S(2)}) collective-permute-start(bf16[128,2048]{1,0:T(8,128)(2,1)S(1)} %collective-permute-done.8.refs_0_), channel_id=1, source_target_pairs={{0,32},{1,225},{2,34},{3,227},{4,36},{5,229},{6,38},{7,231},{8,40}... | collective-permute-start | bytes 1572872 | tf_op jit(solution)/shard_map/ppermute | solution.py:43
  50.7 2.5 %collective-permute-done.6.refs_1_ = bf16[128,2048]{1,0:T(8,128)(2,1)S(1)} collective-permute-done((bf16[128,2048]{1,0:T(8,128)(2,1)S(1)}, bf16[128,2048]{1,0:T(8,128)(2,1)S(1)}, u32[]{:S(2)}, u32[]{:S(2)}) %collective-permute-start.6) | collective-permute-done | bytes 524320 | tf_op jit(solution)/shard_map/ppermute | solution.py:43
  53.2 3.1 %collective-permute-start.11 = (bf16[128,2048]{1,0:T(8,128)(2,1)S(1)}, bf16[128,2048]{1,0:T(8,128)(2,1)S(1)}, u32[]{:S(2)}, u32[]{:S(2)}) collective-permute-start(bf16[128,2048]{1,0:T(8,128)(2,1)S(1)} %collective-permute-done.6.refs_1_), channel_id=1, source_target_pairs={{0,32},{1,225},{2,34},{3,227},{4,36},{5,229},{6,38},{7,231},{8,40}... | collective-permute-start | bytes 1572872 | tf_op jit(solution)/shard_map/ppermute | solution.py:43
  56.3 0.8 sum_1.4
  57.2 3.0 %pairs_3.1 = (bf16[2,2,2,32,1024]{4,3,2,1,0:T(8,128)(2,1)S(1)}, bf16[2,2,2,32,1024]{4,3,2,1,0:T(8,128)(2,1)S(1)}) custom-call(s32[2]{0:T(128)S(1)} %pad_add_fusion.1.at_ref, bf16[128,2048]{1,0:T(8,128)(2,1)S(1)} %collective-permute-done.8.refs_0_, bf16[128,2048]{1,0:T(8,128)(2,1)S(1)} %collective-permute-done.6.refs_1_, ...), custom_call_target="tpu_custom_call" | custom-call | flops 2147483648 | bytes 8388608 | tf_op jit(solution)/shard_map/pairs_3/pallas_call | solution.py:147
  60.5 0.8 sum_1.5
  61.2 1.5 %collective-permute-start.14 = (bf16[2,2,32,1024]{3,2,1,0:T(8,128)(2,1)}, bf16[2,2,32,1024]{3,2,1,0:T(8,128)(2,1)S(1)}, u32[]{:S(2)}, u32[]{:S(2)}) collective-permute-start(bf16[2,2,32,1024]{3,2,1,0:T(8,128)(2,1)} %get-tuple-element.74), channel_id=1, source_target_pairs={{0,6},{1,3},{2,4},{3,1},{4,2},{5,7},{6,0},{7,5},{8,14},{9,11},{10,... | collective-permute-start | bytes 786440 | tf_op jit(solution)/shard_map/ppermute | solution.py:43
  62.7 1.7 %collective-permute-done.11.refs_1_ = bf16[128,2048]{1,0:T(8,128)(2,1)S(1)} collective-permute-done((bf16[128,2048]{1,0:T(8,128)(2,1)S(1)}, bf16[128,2048]{1,0:T(8,128)(2,1)S(1)}, u32[]{:S(2)}, u32[]{:S(2)}) %collective-permute-start.11) | collective-permute-done | bytes 524320 | tf_op jit(solution)/shard_map/ppermute | solution.py:43
  64.4 1.9 %pairs_4.1 = (bf16[2,2,2,32,512]{4,3,2,1,0:T(8,128)(2,1)S(1)}, bf16[2,2,2,32,512]{4,3,2,1,0:T(8,128)(2,1)S(1)}) custom-call(s32[2]{0:T(128)S(1)} %pad_add_fusion.1.at_ref, bf16[128,2048]{1,0:T(8,128)(2,1)S(1)} %collective-permute-done.10.refs_0_, bf16[128,2048]{1,0:T(8,128)(2,1)S(1)} %collective-permute-done.11.refs_1_, ...), custom_call_target="tpu_custom_call" | custom-call | flops 1073741824 | bytes 8388608 | tf_op jit(solution)/shard_map/pairs_4/pallas_call | solution.py:147
  66.4 0.8 collective-permute-start.20
  67.2 8.2 %collective-permute-done.12.recv_ref = bf16[2,2,2,32,1024]{4,3,2,1,0:T(8,128)(2,1)S(1)} collective-permute-done((bf16[2,2,2,32,1024]{4,3,2,1,0:T(8,128)(2,1)S(1)}, bf16[2,2,2,32,1024]{4,3,2,1,0:T(8,128)(2,1)S(1)}, u32[]{:S(2)}, u32[]{:S(2)}) %collective-permute-start.12) | collective-permute-done | bytes 524320 | tf_op jit(solution)/shard_map/ppermute | solution.py:43
  75.4 0.8 sum_1.6
  76.2 0.7 collective-permute-done.14.refs_3_
  77.0 3.0 %collective-permute-start.15 = (bf16[2,32,2560]{2,1,0:T(8,128)(2,1)S(1)}, bf16[2,32,2560]{2,1,0:T(8,128)(2,1)S(1)}, u32[]{:S(2)}, u32[]{:S(2)}) collective-permute-start(bf16[2,32,2560]{2,1,0:T(8,128)(2,1)S(1)} %get-tuple-element.76), channel_id=1, source_target_pairs={{0,8},{1,9},{2,10},{3,11},{4,12},{5,13},{6,14},{7,15},{8,0},{9,1},... | collective-permute-start | bytes 983048 | tf_op jit(solution)/shard_map/ppermute | solution.py:43
  80.0 1.0 collective-permute-done.20.recv_ref
  81.2 4.1 %collective-permute-done.21.refs_3_ = bf16[2,2,32,512]{3,2,1,0:T(8,128)(2,1)S(1)} collective-permute-done((bf16[2,2,32,512]{3,2,1,0:T(8,128)(2,1)S(1)}, bf16[2,2,32,512]{3,2,1,0:T(8,128)(2,1)S(1)}, u32[]{:S(2)}, u32[]{:S(2)}) %collective-permute-start.21) | collective-permute-done | bytes 131104 | tf_op jit(solution)/shard_map/ppermute | solution.py:43
  85.3 3.0 %collective-permute-start.22 = (bf16[2,32,1536]{2,1,0:T(8,128)(2,1)S(1)}, bf16[2,32,1536]{2,1,0:T(8,128)(2,1)S(1)}, u32[]{:S(2)}, u32[]{:S(2)}) collective-permute-start(bf16[2,32,1536]{2,1,0:T(8,128)(2,1)S(1)} %get-tuple-element.86), channel_id=1, source_target_pairs={{0,8},{1,9},{2,10},{3,11},{4,12},{5,13},{6,14},{7,15},{8,0},{9,1},... | collective-permute-start | bytes 589832 | tf_op jit(solution)/shard_map/ppermute | solution.py:43
  88.4 1.0 collective-permute-start.16
  89.4 3.1 %collective-permute-start.25 = (bf16[2,16,1024]{2,1,0:T(8,128)(2,1)S(1)}, bf16[2,16,1024]{2,1,0:T(8,128)(2,1)S(1)}, u32[]{:S(2)}, u32[]{:S(2)}) collective-permute-start(bf16[2,16,1024]{2,1,0:T(8,128)(2,1)S(1)} %get-tuple-element.90), channel_id=1, source_target_pairs={{0,1},{1,0},{2,3},{3,2},{4,5},{5,4},{6,7},{7,6},{8,9},{9,8},{10,11... | collective-permute-start | bytes 196616 | tf_op jit(solution)/shard_map/ppermute | solution.py:43
  92.5 2.2 %collective-permute-done.16.refs_1_ = bf16[2,16,512]{2,1,0:T(8,128)(2,1)S(1)} collective-permute-done((bf16[2,16,512]{2,1,0:T(8,128)(2,1)S(1)}, bf16[2,16,512]{2,1,0:T(8,128)(2,1)S(1)}, u32[]{:S(2)}, u32[]{:S(2)}) %collective-permute-start.16) | collective-permute-done | bytes 32800 | tf_op jit(solution)/shard_map/ppermute | solution.py:43
  95.0 1.5 %collective-permute-start.28 = (bf16[2,16,512]{2,1,0:T(8,128)(2,1)S(1)}, bf16[2,16,512]{2,1,0:T(8,128)(2,1)S(1)}, u32[]{:S(2)}, u32[]{:S(2)}) collective-permute-start(bf16[2,16,512]{2,1,0:T(8,128)(2,1)S(1)} %get-tuple-element.93), channel_id=1, source_target_pairs={{0,193},{1,64},{2,195},{3,66},{4,197},{5,68},{6,199},{7,70},{8,201... | collective-permute-start | bytes 98312 | tf_op jit(solution)/shard_map/ppermute | solution.py:43
  96.5 0.9 collective-permute-done.18.refs_3_
  97.4 0.7 collective-permute-start.23
  98.1 0.4 collective-permute-done.26.refs_8_
  98.5 0.8 collective-permute-start.24
  99.3 1.8 %collective-permute-start.29 = (bf16[2,16,512]{2,1,0:T(8,128)(2,1)S(1)}, bf16[2,16,512]{2,1,0:T(8,128)(2,1)S(1)}, u32[]{:S(2)}, u32[]{:S(2)}) collective-permute-start(bf16[2,16,512]{2,1,0:T(8,128)(2,1)S(1)} %get-tuple-element.94), channel_id=1, source_target_pairs={{0,1},{1,0},{2,3},{3,2},{4,5},{5,4},{6,7},{7,6},{8,9},{9,8},{10,11... | collective-permute-start | bytes 98312 | tf_op jit(solution)/shard_map/ppermute | solution.py:43
  101.1 1.9 %collective-permute-start.30 = (bf16[2,16,512]{2,1,0:T(8,128)(2,1)S(1)}, bf16[2,16,512]{2,1,0:T(8,128)(2,1)S(1)}, u32[]{:S(2)}, u32[]{:S(2)}) collective-permute-start(bf16[2,16,512]{2,1,0:T(8,128)(2,1)S(1)} %get-tuple-element.95), channel_id=1, source_target_pairs={{0,17},{1,16},{2,19},{3,18},{4,21},{5,20},{6,23},{7,22},{8,25},{9,... | collective-permute-start | bytes 98312 | tf_op jit(solution)/shard_map/ppermute | solution.py:43
  103.0 1.5 %collective-permute-start.31 = (bf16[2,16,512]{2,1,0:T(8,128)(2,1)S(1)}, bf16[2,16,512]{2,1,0:T(8,128)(2,1)S(1)}, u32[]{:S(2)}, u32[]{:S(2)}) collective-permute-start(bf16[2,16,512]{2,1,0:T(8,128)(2,1)S(1)} %get-tuple-element.96), channel_id=1, source_target_pairs={{0,161},{1,96},{2,163},{3,98},{4,165},{5,100},{6,167},{7,102},{8,1... | collective-permute-start | bytes 98312 | tf_op jit(solution)/shard_map/ppermute | solution.py:43
  104.9 3.4 %collective-permute-done.31.refs_13_ = bf16[2,16,512]{2,1,0:T(8,128)(2,1)S(1)} collective-permute-done((bf16[2,16,512]{2,1,0:T(8,128)(2,1)S(1)}, bf16[2,16,512]{2,1,0:T(8,128)(2,1)S(1)}, u32[]{:S(2)}, u32[]{:S(2)}) %collective-permute-start.31) | collective-permute-done | bytes 32800 | tf_op jit(solution)/shard_map/ppermute | solution.py:43
  108.3 1.5 %finish.1 = f32[2,16,4096]{2,1,0:T(8,128)} custom-call(s32[3]{0:T(128)S(1)} %pad_add_fusion.place_ref, bf16[2,16,1024]{2,1,0:T(8,128)(2,1)S(1)} %get-tuple-element.77.refs_0_, bf16[2,16,512]{2,1,0:T(8,128)(2,1)S(1)} %collective-permute-done.16.refs_1_, bf16[2,16,512]{2,1,0:T(8,128)(2,1)S(1)} %collective-permute-done.17.refs_2_, ...), custom_call_target="tpu_custom_call" | custom-call | flops 1000 | bytes 1048576 | tf_op jit(solution)/shard_map/finish/pallas_call | solution.py:262
  (42 shorter events, 2.4 us)
Async XLA Ops:
  0.0 1.2 %copy-start = (bf16[2,2,512,256]{3,2,1,0:T(8,128)(2,1)S(1)}, bf16[2,2,512,256]{3,2,1,0:T(8,128)(2,1)}, u32[]{:S(2)}) copy-start(bf16[2,2,512,256]{3,2,1,0:T(8,128)(2,1)} %x_ref.3) | copy-start | bytes 3145732
  1.2 16.3 %copy-start.1 = (s32[512]{0:T(512)S(1)}, s32[512]{0:T(512)}, u32[]{:S(2)}) copy-start(s32[512]{0:T(512)} %param.3) | copy-start | bytes 6148
  1.8 12.6 %collective-permute-start = (bf16[128,2048]{1,0:T(8,128)(2,1)S(1)}, bf16[128,2048]{1,0:T(8,128)(2,1)S(1)}, u32[]{:S(2)}, u32[]{:S(2)}) collective-permute-start(bf16[128,2048]{1,0:T(8,128)(2,1)S(1)} %whiten.2.a_ref.refs_2_), channel_id=1, source_target_pairs={{0,32},{1,225},{2,34},{3,227},{4,36},{5,229},{6,38},{7,231},{8,40}... | collective-permute-start | bytes 1572872 | tf_op jit(solution)/shard_map/ppermute | solution.py:43
  8.3 14.9 %collective-permute-start.3 = (bf16[128,2048]{1,0:T(8,128)(2,1)S(1)}, bf16[128,2048]{1,0:T(8,128)(2,1)S(1)}, u32[]{:S(2)}, u32[]{:S(2)}) collective-permute-start(bf16[128,2048]{1,0:T(8,128)(2,1)S(1)} %whiten.2.a_ref.refs_2_), channel_id=1, source_target_pairs={{0,16},{1,17},{2,18},{3,19},{4,20},{5,21},{6,22},{7,23},{8,24},{9,... | collective-permute-start | bytes 1572872 | tf_op jit(solution)/shard_map/ppermute | solution.py:43
  10.2 20.8 %collective-permute-start.4 = (bf16[128,2048]{1,0:T(8,128)(2,1)S(1)}, bf16[128,2048]{1,0:T(8,128)(2,1)S(1)}, u32[]{:S(2)}, u32[]{:S(2)}) collective-permute-start(bf16[128,2048]{1,0:T(8,128)(2,1)S(1)} %whiten.3.b_ref.refs_3_), channel_id=1, source_target_pairs={{0,16},{1,17},{2,18},{3,19},{4,20},{5,21},{6,22},{7,23},{8,24},{9,... | collective-permute-start | bytes 1572872 | tf_op jit(solution)/shard_map/ppermute | solution.py:43
  10.5 9.6 %collective-permute-start.2 = (bf16[128,2048]{1,0:T(8,128)(2,1)S(1)}, bf16[128,2048]{1,0:T(8,128)(2,1)S(1)}, u32[]{:S(2)}, u32[]{:S(2)}) collective-permute-start(bf16[128,2048]{1,0:T(8,128)(2,1)S(1)} %whiten.3.b_ref.refs_3_), channel_id=1, source_target_pairs={{0,32},{1,225},{2,34},{3,227},{4,36},{5,229},{6,38},{7,231},{8,40}... | collective-permute-start | bytes 1572872 | tf_op jit(solution)/shard_map/ppermute | solution.py:43
  14.4 17.5 %collective-permute-start.1 = (bf16[128,2048]{1,0:T(8,128)(2,1)S(1)}, bf16[128,2048]{1,0:T(8,128)(2,1)S(1)}, u32[]{:S(2)}, u32[]{:S(2)}) collective-permute-start(bf16[128,2048]{1,0:T(8,128)(2,1)S(1)} %collective-permute-done.refs_0_), channel_id=1, source_target_pairs={{0,32},{1,225},{2,34},{3,227},{4,36},{5,229},{6,38},{7,231},{8,40}... | collective-permute-start | bytes 1572872 | tf_op jit(solution)/shard_map/ppermute | solution.py:43
  20.1 21.4 %collective-permute-start.5 = (bf16[128,2048]{1,0:T(8,128)(2,1)S(1)}, bf16[128,2048]{1,0:T(8,128)(2,1)S(1)}, u32[]{:S(2)}, u32[]{:S(2)}) collective-permute-start(bf16[128,2048]{1,0:T(8,128)(2,1)S(1)} %collective-permute-done.2.refs_1_), channel_id=1, source_target_pairs={{0,32},{1,225},{2,34},{3,227},{4,36},{5,229},{6,38},{7,231},{8,40}... | collective-permute-start | bytes 1572872 | tf_op jit(solution)/shard_map/ppermute | solution.py:43
  36.1 20.2 %collective-permute-start.7 = (bf16[2,2,2,32,1536]{4,3,2,1,0:T(8,128)(2,1)S(1)}, bf16[2,2,2,32,1536]{4,3,2,1,0:T(8,128)(2,1)S(1)}, u32[]{:S(2)}, u32[]{:S(2)}) collective-permute-start(bf16[2,2,2,32,1536]{4,3,2,1,0:T(8,128)(2,1)S(1)} %get-tuple-element.58), channel_id=1, source_target_pairs={{0,2},{1,7},{2,0},{3,5},{4,6},{5,3},{6,4},{7,1},{8,10},{9,15},{10,... | collective-permute-start | bytes 2359304 | tf_op jit(solution)/shard_map/ppermute | solution.py:43
  38.7 8.9 %collective-permute-start.8 = (bf16[128,2048]{1,0:T(8,128)(2,1)S(1)}, bf16[128,2048]{1,0:T(8,128)(2,1)S(1)}, u32[]{:S(2)}, u32[]{:S(2)}) collective-permute-start(bf16[128,2048]{1,0:T(8,128)(2,1)S(1)} %collective-permute-done.1.refs_0_), channel_id=1, source_target_pairs={{0,32},{1,225},{2,34},{3,227},{4,36},{5,229},{6,38},{7,231},{8,40}... | collective-permute-start | bytes 1572872 | tf_op jit(solution)/shard_map/ppermute | solution.py:43
  41.5 11.7 %collective-permute-start.6 = (bf16[128,2048]{1,0:T(8,128)(2,1)S(1)}, bf16[128,2048]{1,0:T(8,128)(2,1)S(1)}, u32[]{:S(2)}, u32[]{:S(2)}) collective-permute-start(bf16[128,2048]{1,0:T(8,128)(2,1)S(1)} %collective-permute-done.5.refs_1_), channel_id=1, source_target_pairs={{0,32},{1,225},{2,34},{3,227},{4,36},{5,229},{6,38},{7,231},{8,40}... | collective-permute-start | bytes 1572872 | tf_op jit(solution)/shard_map/ppermute | solution.py:43
  44.5 16.0 %collective-permute-start.9 = (bf16[2,2,2,32,1024]{4,3,2,1,0:T(8,128)(2,1)S(1)}, bf16[2,2,2,32,1024]{4,3,2,1,0:T(8,128)(2,1)S(1)}, u32[]{:S(2)}, u32[]{:S(2)}) collective-permute-start(bf16[2,2,2,32,1024]{4,3,2,1,0:T(8,128)(2,1)S(1)} %get-tuple-element.65), channel_id=1, source_target_pairs={{0,2},{1,7},{2,0},{3,5},{4,6},{5,3},{6,4},{7,1},{8,10},{9,15},{10,... | collective-permute-start | bytes 1572872 | tf_op jit(solution)/shard_map/ppermute | solution.py:43
  47.6 15.1 %collective-permute-start.10 = (bf16[128,2048]{1,0:T(8,128)(2,1)S(1)}, bf16[128,2048]{1,0:T(8,128)(2,1)S(1)}, u32[]{:S(2)}, u32[]{:S(2)}) collective-permute-start(bf16[128,2048]{1,0:T(8,128)(2,1)S(1)} %collective-permute-done.8.refs_0_), channel_id=1, source_target_pairs={{0,32},{1,225},{2,34},{3,227},{4,36},{5,229},{6,38},{7,231},{8,40}... | collective-permute-start | bytes 1572872 | tf_op jit(solution)/shard_map/ppermute | solution.py:43
  53.2 11.2 %collective-permute-start.11 = (bf16[128,2048]{1,0:T(8,128)(2,1)S(1)}, bf16[128,2048]{1,0:T(8,128)(2,1)S(1)}, u32[]{:S(2)}, u32[]{:S(2)}) collective-permute-start(bf16[128,2048]{1,0:T(8,128)(2,1)S(1)} %collective-permute-done.6.refs_1_), channel_id=1, source_target_pairs={{0,32},{1,225},{2,34},{3,227},{4,36},{5,229},{6,38},{7,231},{8,40}... | collective-permute-start | bytes 1572872 | tf_op jit(solution)/shard_map/ppermute | solution.py:43
  60.2 15.2 %collective-permute-start.12 = (bf16[2,2,2,32,1024]{4,3,2,1,0:T(8,128)(2,1)S(1)}, bf16[2,2,2,32,1024]{4,3,2,1,0:T(8,128)(2,1)S(1)}, u32[]{:S(2)}, u32[]{:S(2)}) collective-permute-start(bf16[2,2,2,32,1024]{4,3,2,1,0:T(8,128)(2,1)S(1)} %get-tuple-element.70), channel_id=1, source_target_pairs={{0,2},{1,7},{2,0},{3,5},{4,6},{5,3},{6,4},{7,1},{8,10},{9,15},{10,... | collective-permute-start | bytes 1572872 | tf_op jit(solution)/shard_map/ppermute | solution.py:43
  60.5 16.5 %collective-permute-start.13 = (bf16[2,2,32,1536]{3,2,1,0:T(8,128)(2,1)}, bf16[2,2,32,1536]{3,2,1,0:T(8,128)(2,1)S(1)}, u32[]{:S(2)}, u32[]{:S(2)}) collective-permute-start(bf16[2,2,32,1536]{3,2,1,0:T(8,128)(2,1)} %get-tuple-element.73), channel_id=1, source_target_pairs={{0,6},{1,3},{2,4},{3,1},{4,2},{5,7},{6,0},{7,5},{8,14},{9,11},{10,... | collective-permute-start | bytes 1179656 | tf_op jit(solution)/shard_map/ppermute | solution.py:43
  61.2 15.7 %collective-permute-start.14 = (bf16[2,2,32,1024]{3,2,1,0:T(8,128)(2,1)}, bf16[2,2,32,1024]{3,2,1,0:T(8,128)(2,1)S(1)}, u32[]{:S(2)}, u32[]{:S(2)}) collective-permute-start(bf16[2,2,32,1024]{3,2,1,0:T(8,128)(2,1)} %get-tuple-element.74), channel_id=1, source_target_pairs={{0,6},{1,3},{2,4},{3,1},{4,2},{5,7},{6,0},{7,5},{8,14},{9,11},{10,... | collective-permute-start | bytes 786440 | tf_op jit(solution)/shard_map/ppermute | solution.py:43
  66.4 14.6 %collective-permute-start.20 = (bf16[2,2,2,32,512]{4,3,2,1,0:T(8,128)(2,1)S(1)}, bf16[2,2,2,32,512]{4,3,2,1,0:T(8,128)(2,1)S(1)}, u32[]{:S(2)}, u32[]{:S(2)}) collective-permute-start(bf16[2,2,2,32,512]{4,3,2,1,0:T(8,128)(2,1)S(1)} %get-tuple-element.82), channel_id=1, source_target_pairs={{0,2},{1,7},{2,0},{3,5},{4,6},{5,3},{6,4},{7,1},{8,10},{9,15},{10,... | collective-permute-start | bytes 786440 | tf_op jit(solution)/shard_map/ppermute | solution.py:43
  76.2 9.1 %collective-permute-start.19 = (bf16[2,2,32,1024]{3,2,1,0:T(8,128)(2,1)}, bf16[2,2,32,1024]{3,2,1,0:T(8,128)(2,1)S(1)}, u32[]{:S(2)}, u32[]{:S(2)}) collective-permute-start(bf16[2,2,32,1024]{3,2,1,0:T(8,128)(2,1)} %get-tuple-element.81), channel_id=1, source_target_pairs={{0,6},{1,3},{2,4},{3,1},{4,2},{5,7},{6,0},{7,5},{8,14},{9,11},{10,... | collective-permute-start | bytes 786440 | tf_op jit(solution)/shard_map/ppermute | solution.py:43
  77.0 11.3 %collective-permute-start.15 = (bf16[2,32,2560]{2,1,0:T(8,128)(2,1)S(1)}, bf16[2,32,2560]{2,1,0:T(8,128)(2,1)S(1)}, u32[]{:S(2)}, u32[]{:S(2)}) collective-permute-start(bf16[2,32,2560]{2,1,0:T(8,128)(2,1)S(1)} %get-tuple-element.76), channel_id=1, source_target_pairs={{0,8},{1,9},{2,10},{3,11},{4,12},{5,13},{6,14},{7,15},{8,0},{9,1},... | collective-permute-start | bytes 983048 | tf_op jit(solution)/shard_map/ppermute | solution.py:43
  81.1 4.2 %collective-permute-start.21 = (bf16[2,2,32,512]{3,2,1,0:T(8,128)(2,1)S(1)}, bf16[2,2,32,512]{3,2,1,0:T(8,128)(2,1)S(1)}, u32[]{:S(2)}, u32[]{:S(2)}) collective-permute-start(bf16[2,2,32,512]{3,2,1,0:T(8,128)(2,1)S(1)} %get-tuple-element.84), channel_id=1, source_target_pairs={{0,6},{1,3},{2,4},{3,1},{4,2},{5,7},{6,0},{7,5},{8,14},{9,11},{10,... | collective-permute-start | bytes 393224 | tf_op jit(solution)/shard_map/ppermute | solution.py:43
  85.3 9.6 %collective-permute-start.22 = (bf16[2,32,1536]{2,1,0:T(8,128)(2,1)S(1)}, bf16[2,32,1536]{2,1,0:T(8,128)(2,1)S(1)}, u32[]{:S(2)}, u32[]{:S(2)}) collective-permute-start(bf16[2,32,1536]{2,1,0:T(8,128)(2,1)S(1)} %get-tuple-element.86), channel_id=1, source_target_pairs={{0,8},{1,9},{2,10},{3,11},{4,12},{5,13},{6,14},{7,15},{8,0},{9,1},... | collective-permute-start | bytes 589832 | tf_op jit(solution)/shard_map/ppermute | solution.py:43
  88.4 6.2 %collective-permute-start.16 = (bf16[2,16,512]{2,1,0:T(8,128)(2,1)S(1)}, bf16[2,16,512]{2,1,0:T(8,128)(2,1)S(1)}, u32[]{:S(2)}, u32[]{:S(2)}) collective-permute-start(bf16[2,16,512]{2,1,0:T(8,128)(2,1)S(1)} %get-tuple-element.78), channel_id=1, source_target_pairs={{0,16},{1,17},{2,18},{3,19},{4,20},{5,21},{6,22},{7,23},{8,24},{9,... | collective-permute-start | bytes 98312 | tf_op jit(solution)/shard_map/ppermute | solution.py:43
  89.4 5.6 %collective-permute-start.17 = (bf16[2,16,512]{2,1,0:T(8,128)(2,1)S(1)}, bf16[2,16,512]{2,1,0:T(8,128)(2,1)S(1)}, u32[]{:S(2)}, u32[]{:S(2)}) collective-permute-start(bf16[2,16,512]{2,1,0:T(8,128)(2,1)S(1)} %get-tuple-element.79), channel_id=1, source_target_pairs={{0,224},{1,33},{2,226},{3,35},{4,228},{5,37},{6,230},{7,39},{8,232... | collective-permute-start | bytes 98312 | tf_op jit(solution)/shard_map/ppermute | solution.py:43
  89.4 13.6 %collective-permute-start.25 = (bf16[2,16,1024]{2,1,0:T(8,128)(2,1)S(1)}, bf16[2,16,1024]{2,1,0:T(8,128)(2,1)S(1)}, u32[]{:S(2)}, u32[]{:S(2)}) collective-permute-start(bf16[2,16,1024]{2,1,0:T(8,128)(2,1)S(1)} %get-tuple-element.90), channel_id=1, source_target_pairs={{0,1},{1,0},{2,3},{3,2},{4,5},{5,4},{6,7},{7,6},{8,9},{9,8},{10,11... | collective-permute-start | bytes 196616 | tf_op jit(solution)/shard_map/ppermute | solution.py:43
  92.5 4.9 %collective-permute-start.18 = (bf16[2,16,512]{2,1,0:T(8,128)(2,1)S(1)}, bf16[2,16,512]{2,1,0:T(8,128)(2,1)S(1)}, u32[]{:S(2)}, u32[]{:S(2)}) collective-permute-start(bf16[2,16,512]{2,1,0:T(8,128)(2,1)S(1)} %get-tuple-element.80), channel_id=1, source_target_pairs={{0,192},{1,65},{2,194},{3,67},{4,196},{5,69},{6,198},{7,71},{8,200... | collective-permute-start | bytes 98312 | tf_op jit(solution)/shard_map/ppermute | solution.py:43
  94.7 3.9 %collective-permute-start.26 = (bf16[2,16,512]{2,1,0:T(8,128)(2,1)S(1)}, bf16[2,16,512]{2,1,0:T(8,128)(2,1)S(1)}, u32[]{:S(2)}, u32[]{:S(2)}) collective-permute-start(bf16[2,16,512]{2,1,0:T(8,128)(2,1)S(1)} %get-tuple-element.91), channel_id=1, source_target_pairs={{0,17},{1,16},{2,19},{3,18},{4,21},{5,20},{6,23},{7,22},{8,25},{9,... | collective-permute-start | bytes 98312 | tf_op jit(solution)/shard_map/ppermute | solution.py:43
  95.0 4.4 %collective-permute-start.27 = (bf16[2,16,512]{2,1,0:T(8,128)(2,1)S(1)}, bf16[2,16,512]{2,1,0:T(8,128)(2,1)S(1)}, u32[]{:S(2)}, u32[]{:S(2)}) collective-permute-start(bf16[2,16,512]{2,1,0:T(8,128)(2,1)S(1)} %get-tuple-element.92), channel_id=1, source_target_pairs={{0,225},{1,32},{2,227},{3,34},{4,229},{5,36},{6,231},{7,38},{8,233... | collective-permute-start | bytes 98312 | tf_op jit(solution)/shard_map/ppermute | solution.py:43
  95.0 6.2 %collective-permute-start.28 = (bf16[2,16,512]{2,1,0:T(8,128)(2,1)S(1)}, bf16[2,16,512]{2,1,0:T(8,128)(2,1)S(1)}, u32[]{:S(2)}, u32[]{:S(2)}) collective-permute-start(bf16[2,16,512]{2,1,0:T(8,128)(2,1)S(1)} %get-tuple-element.93), channel_id=1, source_target_pairs={{0,193},{1,64},{2,195},{3,66},{4,197},{5,68},{6,199},{7,70},{8,201... | collective-permute-start | bytes 98312 | tf_op jit(solution)/shard_map/ppermute | solution.py:43
  97.4 7.2 %collective-permute-start.23 = (bf16[2,16,512]{2,1,0:T(8,128)(2,1)S(1)}, bf16[2,16,512]{2,1,0:T(8,128)(2,1)S(1)}, u32[]{:S(2)}, u32[]{:S(2)}) collective-permute-start(bf16[2,16,512]{2,1,0:T(8,128)(2,1)S(1)} %get-tuple-element.88), channel_id=1, source_target_pairs={{0,16},{1,17},{2,18},{3,19},{4,20},{5,21},{6,22},{7,23},{8,24},{9,... | collective-permute-start | bytes 98312 | tf_op jit(solution)/shard_map/ppermute | solution.py:43
  98.5 6.1 %collective-permute-start.24 = (bf16[2,16,512]{2,1,0:T(8,128)(2,1)S(1)}, bf16[2,16,512]{2,1,0:T(8,128)(2,1)S(1)}, u32[]{:S(2)}, u32[]{:S(2)}) collective-permute-start(bf16[2,16,512]{2,1,0:T(8,128)(2,1)S(1)} %get-tuple-element.89), channel_id=1, source_target_pairs={{0,160},{1,97},{2,162},{3,99},{4,164},{5,101},{6,166},{7,103},{8,1... | collective-permute-start | bytes 98312 | tf_op jit(solution)/shard_map/ppermute | solution.py:43
  99.3 5.3 %collective-permute-start.29 = (bf16[2,16,512]{2,1,0:T(8,128)(2,1)S(1)}, bf16[2,16,512]{2,1,0:T(8,128)(2,1)S(1)}, u32[]{:S(2)}, u32[]{:S(2)}) collective-permute-start(bf16[2,16,512]{2,1,0:T(8,128)(2,1)S(1)} %get-tuple-element.94), channel_id=1, source_target_pairs={{0,1},{1,0},{2,3},{3,2},{4,5},{5,4},{6,7},{7,6},{8,9},{9,8},{10,11... | collective-permute-start | bytes 98312 | tf_op jit(solution)/shard_map/ppermute | solution.py:43
  101.1 3.8 %collective-permute-start.30 = (bf16[2,16,512]{2,1,0:T(8,128)(2,1)S(1)}, bf16[2,16,512]{2,1,0:T(8,128)(2,1)S(1)}, u32[]{:S(2)}, u32[]{:S(2)}) collective-permute-start(bf16[2,16,512]{2,1,0:T(8,128)(2,1)S(1)} %get-tuple-element.95), channel_id=1, source_target_pairs={{0,17},{1,16},{2,19},{3,18},{4,21},{5,20},{6,23},{7,22},{8,25},{9,... | collective-permute-start | bytes 98312 | tf_op jit(solution)/shard_map/ppermute | solution.py:43
  103.0 5.3 %collective-permute-start.31 = (bf16[2,16,512]{2,1,0:T(8,128)(2,1)S(1)}, bf16[2,16,512]{2,1,0:T(8,128)(2,1)S(1)}, u32[]{:S(2)}, u32[]{:S(2)}) collective-permute-start(bf16[2,16,512]{2,1,0:T(8,128)(2,1)S(1)} %get-tuple-element.96), channel_id=1, source_target_pairs={{0,161},{1,96},{2,163},{3,98},{4,165},{5,100},{6,167},{7,102},{8,1... | collective-permute-start | bytes 98312 | tf_op jit(solution)/shard_map/ppermute | solution.py:43

commit v3 on v2

v3 whole, which is shorter than its diff:
```python
import math

import jax
import jax.numpy as jnp
import numpy as np
from jax import lax
from jax.experimental import pallas as pl
from jax.experimental.pallas import tpu as pltpu
from jax.sharding import Mesh
from jax.sharding import PartitionSpec as P

NFFT = 8192
LAGS = 2
LAG_STEP = 37
HALF = 64
BINS = 512
BLOCK = 256
DEPTH = 2048
AXES = ("z", "ylo", "yhi", "x", "c")
SIZES = (8, 2, 2, 4, 2)
F32 = jnp.float32
BF16 = jnp.bfloat16
MIB = 1 << 20


def dot_nt(a, b):
    return lax.dot_general(a, b, (((1,), (1,)), ((), ())), preferred_element_type=F32)


def params(mib, **kw):
    return pltpu.CompilerParams(vmem_limit_bytes=mib * MIB, **kw)


def cost(flops, bytes_accessed):
    return pl.CostEstimate(flops=flops, bytes_accessed=bytes_accessed, transcendentals=0)


def move(x, step):
    pairs = []
    for i, at in enumerate(np.ndindex(*SIZES)):
        to = tuple(int(v) % s for v, s in zip(step(*at), SIZES))
        pairs.append((i, int(np.ravel_multi_index(to, SIZES))))
    return lax.ppermute(x, AXES, pairs)


def sign(c):
    return 1 - 2 * c


def whiten_kernel(place_ref, x_ref, o_ref):
    row = lax.broadcasted_iota(jnp.int32, (BINS, BINS), 0)
    col = lax.broadcasted_iota(jnp.int32, (BINS, BINS), 1)
    window = (jnp.abs(row - col) <= HALF).astype(F32).astype(BF16)
    pos = lax.broadcasted_iota(jnp.int32, (1, BINS), 1)
    count = jnp.minimum(pos + HALF, BINS - 1) - jnp.maximum(pos - HALF, 0) + 1
    inverse = 1.0 / count.astype(F32)
    for s in range(2):
        re = x_ref[0, s].astype(F32).T
        im = x_ref[1, s].astype(F32).T
        energy = re * re + im * im
        high = energy.astype(BF16)
        low = (energy - high.astype(F32)).astype(BF16)
        total = jnp.dot(high, window, preferred_element_type=F32)
        total += jnp.dot(low, window, preferred_element_type=F32)
        scale = lax.rsqrt(total * inverse + 1e-06)
        o_ref[:, s * BINS : (s + 1) * BINS] = (re * scale).astype(BF16)
        o_ref[:, (2 + s) * BINS : (3 + s) * BINS] = (im * scale).astype(BF16)


def whiten(place, spectra, half):
    return pl.pallas_call(
        whiten_kernel,
        grid=(1,),
        in_specs=[pl.BlockSpec(memory_space=pltpu.SMEM), pl.BlockSpec((2, 2, BINS, 128), lambda i: (0, 0, 0, half))],
        out_specs=pl.BlockSpec((128, DEPTH), lambda i: (0, 0)),
        out_shape=jax.ShapeDtypeStruct((128, DEPTH), BF16),
        compiler_params=params(12),
        cost_estimate=cost(2 * 4 * 128 * 512 * 512, MIB),
        name="whiten",
    )(place, spectra)


def phases(bin_index):
    lag_samples = (jnp.arange(LAGS, dtype=jnp.int32) + 1) * LAG_STEP
    phase_turn = lag_samples[:, None] * bin_index[None, :] % NFFT
    phase_angle = 2.0 * math.pi / NFFT * phase_turn.astype(F32)
    cosine, sine = jnp.cos(phase_angle), jnp.sin(phase_angle)
    return jnp.concatenate([cosine, cosine], 1), jnp.concatenate([sine, sine], 1)


def rotate_kernel(a_ref, b_ref, cos_ref, sin_ref, plus_ref, minus_ref):
    half = DEPTH // 2
    for n, ref in enumerate((a_ref, b_ref)):

        @pl.loop(0, 8)
        def _(i):
            at = pl.ds(pl.multiple_of(i * 16, 16), 16)
            to = pl.ds(pl.multiple_of(n * 128 + i * 16, 16), 16)
            re = ref[at, :half].astype(F32)
            im = ref[at, half:].astype(F32)
            for m in range(LAGS):
                cosine, sine = cos_ref[m : m + 1, :], sin_ref[m : m + 1, :]
                rc, rs, ic, is_ = re * cosine, re * sine, im * cosine, im * sine
                plus_ref[m, to, :half] = (rc - is_).astype(BF16)
                plus_ref[m, to, half:] = (rs + ic).astype(BF16)
                minus_ref[m, to, :half] = (rc + is_).astype(BF16)
                minus_ref[m, to, half:] = (ic - rs).astype(BF16)


def rotations(chunks, cosine, sine):
    shape = jax.ShapeDtypeStruct((LAGS, BLOCK, DEPTH), BF16)
    return pl.pallas_call(
        rotate_kernel,
        out_shape=(shape, shape),
        compiler_params=params(12),
        cost_estimate=cost(2 * 8 * 256 * 2048, 6 * MIB),
        name="rotate",
    )(*chunks, cosine, sine)


def store_product(acc_ref, m, first, value, scale):
    n = value.shape[1]
    for h in range(2):
        for x in range(4):
            at = h * 128 + x * 32
            acc_ref[m, h, x, :, first : first + n] = (value[at : at + 32] * scale).astype(BF16)


def products(at, parts, chunks, wide, scale, name):
    count = len(chunks)

    def kernel(at_ref, *refs):
        ins, (keep_ref, send_ref), acc_ref = refs[:count], refs[count : count + 2], refs[count + 2]
        x, c = at_ref[3], at_ref[4]
        near, far = 1 + 2 * c, 3 - 2 * c
        for m in range(LAGS):
            for first, value in parts(m, ins):
                store_product(acc_ref, m, first, value, scale)
        slices = ((keep_ref, 0, x), (keep_ref, 1, x ^ far), (send_ref, 0, x ^ near), (send_ref, 1, x ^ 2))
        for out, k, which in slices:
            for m in range(LAGS):
                for h in range(2):
                    out[k, h, m] = acc_ref[m, h, which]

    shape = jax.ShapeDtypeStruct((2, 2, LAGS, 32, wide), BF16)
    whole = pl.BlockSpec(memory_space=pltpu.VMEM)
    return pl.pallas_call(
        kernel,
        in_specs=[pl.BlockSpec(memory_space=pltpu.SMEM)] + [whole] * count,
        out_specs=[whole] * 2,
        out_shape=(shape,) * 2,
        scratch_shapes=[pltpu.VMEM((LAGS, 2, 4, 32, wide), BF16)],
        compiler_params=params(14),
        cost_estimate=cost(2 * 2 * 256 * wide * DEPTH, 8 * MIB),
        name=name,
    )(at, *chunks)


def both(a_ref, b_ref):
    return jnp.concatenate([a_ref[...], b_ref[...]], 0)


def call(kernel, scalars, arrays, shapes, name):
    whole = pl.BlockSpec(memory_space=pltpu.VMEM)
    lead = [] if scalars is None else [scalars]
    return pl.pallas_call(
        kernel,
        in_specs=[pl.BlockSpec(memory_space=pltpu.SMEM)] * len(lead) + [whole] * len(arrays),
        out_specs=[whole] * len(shapes),
        out_shape=tuple(jax.ShapeDtypeStruct(s, t) for s, t in shapes),
        compiler_params=params(12),
        cost_estimate=cost(1000, MIB),
        name=name,
    )(*lead, *arrays)


def sum_1(groups, picks):
    total = sum(n for _, _, n in picks)

    def kernel(*refs):
        kept_ref, send_ref = refs[-2:]
        for h in range(2):
            for m in range(LAGS):
                to = 0
                for g, first, n in picks:
                    cols, out = slice(first, first + n), slice(to, to + n)
                    keep, recv = refs[2 * g], refs[2 * g + 1]
                    kept_ref[h, m, :, out] = keep[0, h, m, :, cols].astype(F32) + recv[0, h, m, :, cols].astype(F32)
                    value = keep[1, h, m, :, cols].astype(F32) + recv[1, h, m, :, cols].astype(F32)
                    send_ref[h, m, :, out] = value.astype(BF16)
                    to += n

    shape = (2, LAGS, 32, total)
    return call(kernel, None, [r for g in groups for r in g], [(shape, F32), (shape, BF16)], "sum_1")


def sum_2(yi, kept, recv):
    n = kept.shape[3]

    def kernel(yi_ref, kept_ref, recv_ref, keep_ref, send_ref):
        mine, other = yi_ref[2], 1 - yi_ref[2]
        for m in range(LAGS):
            keep_ref[m] = kept_ref[mine, m] + recv_ref[mine, m].astype(F32)
            send_ref[m] = (kept_ref[other, m] + recv_ref[other, m].astype(F32)).astype(BF16)

    return call(kernel, yi, [kept, recv], [((LAGS, 32, n), F32), ((LAGS, 32, n), BF16)], "sum_2")


def sum_y(keep, recv, widths, extra=None):
    arrays = [keep, recv] + ([] if extra is None else [extra])
    more = 0 if extra is None else extra.shape[2]

    def kernel(*refs):
        keep_ref, recv_ref, outs = refs[0], refs[1], refs[len(arrays) :]
        for m in range(LAGS):
            first = 0
            for k, (out, n) in enumerate(zip(outs, widths)):
                to = 0
                if k == 1 and more:
                    out[m, :, :more] = refs[2][m]
                    to = more
                cols = slice(first, first + n)
                out[m, :, to : to + n] = (keep_ref[m, :, cols] + recv_ref[m, :, cols].astype(F32)).astype(BF16)
                first += n

    shapes = [((LAGS, 32, n + (more if k == 1 else 0)), BF16) for k, n in enumerate(widths)]
    return call(kernel, None, arrays, shapes, "sum_y")


def sum_last(yi, kept, recv):
    def kernel(yi_ref, kept_ref, recv_ref, keep, send, near_mine, near_other):
        mine, other = yi_ref[2], 1 - yi_ref[2]

        def total(h, m, cols):
            return kept_ref[h, m, :, cols] + recv_ref[h, m, :, cols].astype(F32)

        for m in range(LAGS):
            keep[m] = total(mine, m, slice(0, BLOCK))
            send[m] = total(other, m, slice(0, BLOCK)).astype(BF16)
            near_mine[m] = total(mine, m, slice(BLOCK, 2 * BLOCK)).astype(BF16)
            near_other[m] = total(other, m, slice(BLOCK, 2 * BLOCK)).astype(BF16)

    shape = (LAGS, 32, BLOCK)
    return call(kernel, yi, [kept, recv], [(shape, F32), (shape, BF16), (shape, BF16), (shape, BF16)], "sum_last")


def split_last(ci, keep, recv, near_a, near_b):
    def kernel(ci_ref, keep_ref, recv_ref, a_ref, b_ref, mine_ref, send_ref):
        for out, core in ((mine_ref, ci_ref[4]), (send_ref, 1 - ci_ref[4])):
            at = pl.ds(pl.multiple_of(core * 16, 16), 16)
            for m in range(LAGS):
                own = keep_ref[m, at, :] + recv_ref[m, at, :].astype(F32)
                near = a_ref[m, at, :].astype(F32) + b_ref[m, at, :].astype(F32)
                out[m, :, :BLOCK] = own.astype(out.dtype)
                out[m, :, BLOCK:] = near.astype(out.dtype)

    shape = (LAGS, 16, 2 * BLOCK)
    return call(kernel, ci, [keep, recv, near_a, near_b], [(shape, F32), (shape, BF16)], "split_last")


def split(ci, arrays):
    total = sum(a.shape[2] for a in arrays)

    def kernel(ci_ref, *refs):
        at = pl.ds(pl.multiple_of((1 - ci_ref[4]) * 16, 16), 16)
        first = 0
        for ref in refs[:-1]:
            n = ref.shape[2]
            for m in range(LAGS):
                refs[-1][m, :, first : first + n] = ref[m, at, :]
            first += n

    return call(kernel, ci, arrays, [((LAGS, 16, total), BF16)], "split")[0]


def finish(place, arrays, blocks, recv, last, last_recv, last_blocks):
    def kernel(place_ref, *refs):
        out = refs[-1]
        ins, recv_ref, last_ref, last_recv_ref = refs[:-4], refs[-4], refs[-3], refs[-2]
        z, y, c = place_ref[0], place_ref[1], place_ref[4]
        rows = pl.ds(pl.multiple_of(c * 16, 16), 16)

        def cols(block, way):
            dist, dy = block
            zz = lax.rem(z - way * dist + 16, 8)
            yy = y if dy == 0 else 1 - y
            return pl.ds(pl.multiple_of((zz * 2 + yy) * BLOCK, BLOCK), BLOCK)

        for m in range(LAGS):
            for ref, ids in zip(ins, blocks):
                for n, block in enumerate(ids):
                    out[m, :, cols(block, 1 - 2 * c)] = ref[m, rows, n * BLOCK : (n + 1) * BLOCK].astype(F32)
            for n, block in enumerate(last_blocks):
                out[m, :, cols(block, 1 - 2 * c)] = last_ref[m, :, n * BLOCK : (n + 1) * BLOCK]
            for ref, ids in ((recv_ref, sum(blocks, [])), (last_recv_ref, last_blocks)):
                for n, block in enumerate(ids):
                    out[m, :, cols(block, 2 * c - 1)] += ref[m, :, n * BLOCK : (n + 1) * BLOCK].astype(F32)

    given = list(arrays) + [recv, last, last_recv]
    return call(kernel, place, given, [((LAGS, 16, 4096), F32)], "finish")[0]


def chain_step(z, ylo, yhi, x, c):
    return z + sign(c), ylo, yhi, x, c


def y_step(z, ylo, yhi, x, c):
    return z, 1 - ylo, yhi, x, c


def y_both(z, ylo, yhi, x, c):
    return z, 1 - ylo, 1 - yhi, x, c


def yhi_step(z, ylo, yhi, x, c):
    return z, ylo, 1 - yhi, x, c


def core_step(z, ylo, yhi, x, c):
    return z, ylo, yhi, x, 1 - c


def x_near(z, ylo, yhi, x, c):
    return z, ylo, yhi, x ^ (1 + 2 * c), c


def x_far(z, ylo, yhi, x, c):
    return z, ylo, yhi, x ^ (3 - 2 * c), c


def back(d):
    return lambda z, ylo, yhi, x, c: (z - sign(c) * d, ylo, yhi, x, c)


def after(value, *others):
    return lax.optimization_barrier((value,) + others)[0]


def body(spectra, bin_index):
    scale = 1.0 / math.sqrt(32 * BINS)
    place = jnp.stack([lax.axis_index(a) for a in AXES]).astype(jnp.int32)
    at = yi = ci = place

    own = [whiten(place, spectra, 0), whiten(place, spectra, 1)]
    block = own
    arrived = []
    for _ in range(4):
        block = [move(b, chain_step) for b in block]
        arrived.append(block)
    near = [move(b, y_step) for b in own]

    cosine, sine = phases(bin_index)
    own_plus, own_minus = rotations(own, cosine, sine)
    near_plus, near_minus = rotations(near, cosine, sine)

    def all_pairs(m, ins, at=0):
        b = both(ins[at], ins[at + 1])
        op, om, np_, nm = ins[-4:]
        yield 0, dot_nt(op[m], b)
        yield BLOCK, dot_nt(np_[m], b)
        yield 2 * BLOCK, dot_nt(b, om[m])
        yield 3 * BLOCK, dot_nt(b, nm[m])

    def own_pairs(m, ins):
        op, om = ins[-2:]
        b = both(ins[0], ins[1])
        yield 0, dot_nt(op[m], both(ins[2], ins[3]))
        yield BLOCK, dot_nt(op[m], b)
        yield 2 * BLOCK, dot_nt(b, om[m])

    def near_pairs(m, ins):
        op, np_, nm = ins[-3:]
        b = both(ins[0], ins[1])
        yield 0, dot_nt(op[m], both(ins[2], ins[3]))
        yield BLOCK, dot_nt(np_[m], b)
        yield 2 * BLOCK, dot_nt(b, nm[m])

    def last_pairs(m, ins):
        b = both(ins[0], ins[1])
        yield 0, dot_nt(ins[2][m], b)
        yield BLOCK, dot_nt(ins[3][m], b)

    rotated = [own_plus, own_minus, near_plus, near_minus]
    straight = [(0, 0, 4 * BLOCK)]

    keep_o, send_o = products(at, own_pairs, arrived[0] + own + rotated[:2], 3 * BLOCK, scale, "pairs_own")
    recv_o = move(send_o, x_near)
    at_n = after(at, arrived[1][0], keep_o)
    near_rotated = [own_plus, near_plus, near_minus]
    keep_n, send_n = products(at_n, near_pairs, arrived[0] + near + near_rotated, 3 * BLOCK, scale, "pairs_near")
    recv_n = move(send_n, x_near)
    keep_b, send_b = products(after(at, keep_n), all_pairs, arrived[1] + rotated, 4 * BLOCK, scale, "pairs_2")
    recv_b = move(send_b, x_near)
    picks = [(0, 0, 2 * BLOCK), (1, 0, BLOCK), (1, BLOCK, BLOCK), (0, 2 * BLOCK, BLOCK), (1, 2 * BLOCK, BLOCK)]
    kept_a, send_a = sum_1([(after(keep_o, arrived[2][0], keep_b), recv_o), (keep_n, recv_n)], picks)
    recv_a = move(send_a, x_far)
    keep_c, send_c = products(after(at, kept_a), all_pairs, arrived[2] + rotated, 4 * BLOCK, scale, "pairs_3")
    recv_c = move(send_c, x_near)
    kept_b, send_b = sum_1([(after(keep_b, keep_c, arrived[3][0]), recv_b)], straight)
    recv_b = move(send_b, x_far)
    keep_a, send_a = sum_2(yi, after(kept_a, kept_b), recv_a)
    recv_a = move(send_a, yhi_step)
    kept_c, send_c = sum_1([(after(keep_c, keep_a, arrived[3][1]), recv_c)], straight)
    recv_c = move(send_c, x_far)
    at_d = after(at, kept_c)
    keep_d, send_d = products(at_d, last_pairs, arrived[3] + [own_plus, near_plus], 2 * BLOCK, scale, "pairs_4")
    recv_d = move(send_d, x_near)
    keep_b, send_b = sum_2(yi, after(kept_b, keep_d), recv_b)
    recv_b = move(send_b, yhi_step)
    keep_c, send_c = sum_2(yi, after(kept_c, keep_b), recv_c)
    recv_c = move(send_c, yhi_step)
    own_a, near_a, ret_1 = sum_y(after(keep_a, keep_c), recv_a, [3 * BLOCK, BLOCK, 2 * BLOCK])
    ret_1 = move(ret_1, back(1))
    kept_d, send_d = sum_1([(after(keep_d, own_a), recv_d)], [(0, 0, 2 * BLOCK)])
    recv_d = move(send_d, x_far)
    own_b, near_b, ret_2 = sum_y(after(keep_b, kept_d), recv_b, [BLOCK, BLOCK, 2 * BLOCK], near_a)
    ret_2 = move(ret_2, back(2))
    keep_d, *send_d = sum_last(yi, after(kept_d, own_b), recv_d)
    recv_d = [move(v, step) for v, step in zip(send_d, (yhi_step, y_step, y_both))]
    own_c, near_c, ret_3 = sum_y(after(keep_c, keep_d), recv_c, [BLOCK, BLOCK, 2 * BLOCK], near_b)
    ret_3 = move(ret_3, back(3))
    near_c = move(near_c, y_step)
    mine_d, other_d = split_last(ci, keep_d, *recv_d)
    other_d = move(other_d, core_step)
    arrays = [own_a, own_b, own_c, near_c, ret_1, ret_2, ret_3]
    blocks = [[(0, 0), (1, 0), (0, 1)], [(2, 0)], [(3, 0)], [(1, 1), (2, 1), (3, 1)]]
    blocks += [[(-d, 0), (-d, 1)] for d in (1, 2, 3)]
    others = move(split(ci, arrays), core_step)
    return finish(place, arrays, blocks, others, mine_d, other_d, [(4, 0), (4, 1)])


def solution(mesh):
    torus = Mesh(mesh.devices.reshape(SIZES), AXES)
    placed = (P(None, ("yhi", "x", "c"), None, ("z", "ylo")), P())
    return jax.shard_map(
        body, mesh=torus, in_specs=placed, out_specs=P(None, AXES, None), check_vma=False
    )
```

time: 110 us -> 116 us (1.055)
  starting transfers between devices: 48.3 us -> 56.9 us
  waiting for transfers between devices: 40.5 us -> 34.7 us
  Pallas kernels: 19.3 us -> 22.5 us
    ppermute x32 -> x31, starting transfers between devices: 48.3 us -> 56.9 us  [move(): return lax.ppermute(x, AXES, pairs)]
    ppermute x32 -> x31, waiting for transfers between devices: 40.5 us -> 34.7 us  [move(): return lax.ppermute(x, AXES, pairs)]
    pallas_call x11 -> x16, Pallas kernels: 5.41 us -> 7.83 us  [the longest x14 5.59 us: call(): pl.pallas_call(kernel, in_specs=[pl.BlockSpec(memory_space=pltpu.SMEM)] *...]
    pallas_call x4 -> x5, Pallas kernels: 12 us -> 12.7 us  [products(): pl.pallas_call(kernel, in_specs=[pl.BlockSpec(memory_space=pltpu.SMEM)] +...]
  transfers between devices with their start and end apart: 32 -> 31, of which waited for: 15 -> 16; matrix products, arithmetic and copies ran while one was open for 0% -> 0% of each run, Pallas kernels for 16% -> 16%
where the time goes in v3:
time: 116 us
  starting transfers between devices  56.9 us (49%)
  waiting for transfers between devices  34.7 us (30%)
  Pallas kernels  22.5 us (19%)
  local copies, waits for them, and re-layouts  1.31 us (1%)
    ppermute x31, starting transfers between devices, move(): return lax.ppermute(x, AXES, pairs)  56.9 us
    ppermute x31, waiting for transfers between devices, move(): return lax.ppermute(x, AXES, pairs)  34.7 us
    pallas_call x5, Pallas kernels, products(): pl.pallas_call(kernel, in_specs=[pl.BlockSpec(memory_space=pltpu.SMEM)] +...  12.7 us
    pallas_call x14, Pallas kernels, call(): pl.pallas_call(kernel, in_specs=[pl.BlockSpec(memory_space=pltpu.SMEM)] *...  5.59 us
  transfers between devices with their start and end apart: 31, of which 16 were waited for; matrix products, arithmetic and copies ran while one was open for 0% of the time, Pallas kernels for 16%

profile of v3, /device:TPU:1, one launch (start us, length us, event | category | flops | bytes accessed | tf_op | source)
XLA Modules:
  0.0 115.7 jit_solution(16307008956881659837)
XLA Ops:
  0.1 1.2 %copy-done = bf16[2,2,512,256]{3,2,1,0:T(8,128)(2,1)S(1)} copy-done((bf16[2,2,512,256]{3,2,1,0:T(8,128)(2,1)S(1)}, bf16[2,2,512,256]{3,2,1,0:T(8,128)(2,1)}, u32[]{:S(2)}) %copy-start) | copy-done | bytes 1048600
  1.3 1.1 whiten.2.a_ref.refs_2_
  2.4 6.5 %collective-permute-start = (bf16[128,2048]{1,0:T(8,128)(2,1)S(1)}, bf16[128,2048]{1,0:T(8,128)(2,1)S(1)}, u32[]{:S(2)}, u32[]{:S(2)}) collective-permute-start(bf16[128,2048]{1,0:T(8,128)(2,1)S(1)} %whiten.2.a_ref.refs_2_), channel_id=1, source_target_pairs={{0,32},{1,225},{2,34},{3,227},{4,36},{5,229},{6,38},{7,231},{8,40}... | collective-permute-start | bytes 1572872 | tf_op jit(solution)/shard_map/ppermute | solution.py:43
  8.9 1.1 whiten.3.b_ref.refs_3_
  10.0 0.8 collective-permute-start.1
  10.9 1.3 %collective-permute-start.4 = (bf16[128,2048]{1,0:T(8,128)(2,1)S(1)}, bf16[128,2048]{1,0:T(8,128)(2,1)S(1)}, u32[]{:S(2)}, u32[]{:S(2)}) collective-permute-start(bf16[128,2048]{1,0:T(8,128)(2,1)S(1)} %whiten.2.a_ref.refs_2_), channel_id=1, source_target_pairs={{0,16},{1,17},{2,18},{3,19},{4,20},{5,21},{6,22},{7,23},{8,24},{9,... | collective-permute-start | bytes 1572872 | tf_op jit(solution)/shard_map/ppermute | solution.py:43
  12.3 2.7 %collective-permute-done.refs_0_ = bf16[128,2048]{1,0:T(8,128)(2,1)S(1)} collective-permute-done((bf16[128,2048]{1,0:T(8,128)(2,1)S(1)}, bf16[128,2048]{1,0:T(8,128)(2,1)S(1)}, u32[]{:S(2)}, u32[]{:S(2)}) %collective-permute-start) | collective-permute-done | bytes 524320 | tf_op jit(solution)/shard_map/ppermute | solution.py:43
  15.0 3.1 %collective-permute-start.2 = (bf16[128,2048]{1,0:T(8,128)(2,1)S(1)}, bf16[128,2048]{1,0:T(8,128)(2,1)S(1)}, u32[]{:S(2)}, u32[]{:S(2)}) collective-permute-start(bf16[128,2048]{1,0:T(8,128)(2,1)S(1)} %collective-permute-done.refs_0_), channel_id=1, source_target_pairs={{0,32},{1,225},{2,34},{3,227},{4,36},{5,229},{6,38},{7,231},{8,40}... | collective-permute-start | bytes 1572872 | tf_op jit(solution)/shard_map/ppermute | solution.py:43
  18.2 2.5 %collective-permute-done.1.refs_1_ = bf16[128,2048]{1,0:T(8,128)(2,1)S(1)} collective-permute-done((bf16[128,2048]{1,0:T(8,128)(2,1)S(1)}, bf16[128,2048]{1,0:T(8,128)(2,1)S(1)}, u32[]{:S(2)}, u32[]{:S(2)}) %collective-permute-start.1) | collective-permute-done | bytes 524320 | tf_op jit(solution)/shard_map/ppermute | solution.py:43
  20.7 3.1 %collective-permute-start.6 = (bf16[128,2048]{1,0:T(8,128)(2,1)S(1)}, bf16[128,2048]{1,0:T(8,128)(2,1)S(1)}, u32[]{:S(2)}, u32[]{:S(2)}) collective-permute-start(bf16[128,2048]{1,0:T(8,128)(2,1)S(1)} %collective-permute-done.1.refs_1_), channel_id=1, source_target_pairs={{0,32},{1,225},{2,34},{3,227},{4,36},{5,229},{6,38},{7,231},{8,40}... | collective-permute-start | bytes 1572872 | tf_op jit(solution)/shard_map/ppermute | solution.py:43
  24.0 1.0 rotate.2
  24.9 2.4 %pairs_own.1 = (bf16[2,2,2,32,768]{4,3,2,1,0:T(8,128)(2,1)S(1)}, bf16[2,2,2,32,768]{4,3,2,1,0:T(8,128)(2,1)S(1)}) custom-call(s32[5]{0:T(128)S(1)} %stack.23.place_ref.at_ref.yi_ref.ci_ref, bf16[128,2048]{1,0:T(8,128)(2,1)S(1)} %collective-permute-done.refs_0_, bf16[128,2048]{1,0:T(8,128)(2,1)S(1)} %collective-permute-done.1.refs_1_, ...), custom_call_target="tpu_custom_call" | custom-call | flops 1610612736 | bytes 8388608 | tf_op jit(solution)/shard_map/pairs_own/pallas_call | solution.py:147
  27.4 2.6 %collective-permute-start.7 = (bf16[2,2,2,32,768]{4,3,2,1,0:T(8,128)(2,1)S(1)}, bf16[2,2,2,32,768]{4,3,2,1,0:T(8,128)(2,1)S(1)}, u32[]{:S(2)}, u32[]{:S(2)}) collective-permute-start(bf16[2,2,2,32,768]{4,3,2,1,0:T(8,128)(2,1)S(1)} %get-tuple-element.73), channel_id=1, source_target_pairs={{0,2},{1,7},{2,0},{3,5},{4,6},{5,3},{6,4},{7,1},{8,10},{9,15},{10,... | collective-permute-start | bytes 1179656 | tf_op jit(solution)/shard_map/ppermute | solution.py:43
  29.9 4.5 %collective-permute-done.5.b_ref.refs_3_ = bf16[128,2048]{1,0:T(8,128)(2,1)S(1)} collective-permute-done((bf16[128,2048]{1,0:T(8,128)(2,1)S(1)}, bf16[128,2048]{1,0:T(8,128)(2,1)S(1)}, u32[]{:S(2)}, u32[]{:S(2)}) %collective-permute-start.5) | collective-permute-done | bytes 524320 | tf_op jit(solution)/shard_map/ppermute | solution.py:43
  34.4 1.0 rotate.3
  35.4 2.2 %collective-permute-start.3 = (bf16[128,2048]{1,0:T(8,128)(2,1)S(1)}, bf16[128,2048]{1,0:T(8,128)(2,1)S(1)}, u32[]{:S(2)}, u32[]{:S(2)}) collective-permute-start(bf16[128,2048]{1,0:T(8,128)(2,1)S(1)} %collective-permute-done.2.refs_0_), channel_id=1, source_target_pairs={{0,32},{1,225},{2,34},{3,227},{4,36},{5,229},{6,38},{7,231},{8,40}... | collective-permute-start | bytes 1572872 | tf_op jit(solution)/shard_map/ppermute | solution.py:43
  37.8 2.4 %pairs_near.1 = (bf16[2,2,2,32,768]{4,3,2,1,0:T(8,128)(2,1)S(1)}, bf16[2,2,2,32,768]{4,3,2,1,0:T(8,128)(2,1)S(1)}) custom-call(s32[5]{0:T(128)S(1)} %stack.23.place_ref.at_ref.yi_ref.ci_ref, bf16[128,2048]{1,0:T(8,128)(2,1)S(1)} %collective-permute-done.refs_0_, bf16[128,2048]{1,0:T(8,128)(2,1)S(1)} %collective-permute-done.1.refs_1_, ...), custom_call_target="tpu_custom_call" | custom-call | flops 1610612736 | bytes 8388608 | tf_op jit(solution)/shard_map/pairs_near/pallas_call | solution.py:147
  40.2 2.7 %collective-permute-start.8 = (bf16[2,2,2,32,768]{4,3,2,1,0:T(8,128)(2,1)S(1)}, bf16[2,2,2,32,768]{4,3,2,1,0:T(8,128)(2,1)S(1)}, u32[]{:S(2)}, u32[]{:S(2)}) collective-permute-start(bf16[2,2,2,32,768]{4,3,2,1,0:T(8,128)(2,1)S(1)} %get-tuple-element.74), channel_id=1, source_target_pairs={{0,2},{1,7},{2,0},{3,5},{4,6},{5,3},{6,4},{7,1},{8,10},{9,15},{10,... | collective-permute-start | bytes 1179656 | tf_op jit(solution)/shard_map/ppermute | solution.py:43
  43.0 3.0 %pairs_2.1 = (bf16[2,2,2,32,1024]{4,3,2,1,0:T(8,128)(2,1)S(1)}, bf16[2,2,2,32,1024]{4,3,2,1,0:T(8,128)(2,1)S(1)}) custom-call(s32[5]{0:T(128)S(1)} %stack.23.place_ref.at_ref.yi_ref.ci_ref, bf16[128,2048]{1,0:T(8,128)(2,1)S(1)} %collective-permute-done.2.refs_0_, bf16[128,2048]{1,0:T(8,128)(2,1)S(1)} %collective-permute-done.6.refs_1_, ...), custom_call_target="tpu_custom_call" | custom-call | flops 2147483648 | bytes 8388608 | tf_op jit(solution)/shard_map/pairs_2/pallas_call | solution.py:147
  46.2 2.4 %collective-permute-done.8.refs_3_ = bf16[2,2,2,32,768]{4,3,2,1,0:T(8,128)(2,1)S(1)} collective-permute-done((bf16[2,2,2,32,768]{4,3,2,1,0:T(8,128)(2,1)S(1)}, bf16[2,2,2,32,768]{4,3,2,1,0:T(8,128)(2,1)S(1)}, u32[]{:S(2)}, u32[]{:S(2)}) %collective-permute-start.8) | collective-permute-done | bytes 393248 | tf_op jit(solution)/shard_map/ppermute | solution.py:43
  48.9 0.7 collective-permute-done.9.refs_1_
  49.6 2.9 %collective-permute-start.13 = (bf16[128,2048]{1,0:T(8,128)(2,1)S(1)}, bf16[128,2048]{1,0:T(8,128)(2,1)S(1)}, u32[]{:S(2)}, u32[]{:S(2)}) collective-permute-start(bf16[128,2048]{1,0:T(8,128)(2,1)S(1)} %collective-permute-done.9.refs_1_), channel_id=1, source_target_pairs={{0,32},{1,225},{2,34},{3,227},{4,36},{5,229},{6,38},{7,231},{8,40}... | collective-permute-start | bytes 1572872 | tf_op jit(solution)/shard_map/ppermute | solution.py:43
  52.5 3.0 %pairs_3.1 = (bf16[2,2,2,32,1024]{4,3,2,1,0:T(8,128)(2,1)S(1)}, bf16[2,2,2,32,1024]{4,3,2,1,0:T(8,128)(2,1)S(1)}) custom-call(s32[5]{0:T(128)S(1)} %stack.23.place_ref.at_ref.yi_ref.ci_ref, bf16[128,2048]{1,0:T(8,128)(2,1)S(1)} %collective-permute-done.3.refs_0_, bf16[128,2048]{1,0:T(8,128)(2,1)S(1)} %collective-permute-done.9.refs_1_, ...), custom_call_target="tpu_custom_call" | custom-call | flops 2147483648 | bytes 8388608 | tf_op jit(solution)/shard_map/pairs_3/pallas_call | solution.py:147
  55.5 2.6 %collective-permute-start.14 = (bf16[2,2,2,32,1024]{4,3,2,1,0:T(8,128)(2,1)S(1)}, bf16[2,2,2,32,1024]{4,3,2,1,0:T(8,128)(2,1)S(1)}, u32[]{:S(2)}, u32[]{:S(2)}) collective-permute-start(bf16[2,2,2,32,1024]{4,3,2,1,0:T(8,128)(2,1)S(1)} %get-tuple-element.85), channel_id=1, source_target_pairs={{0,2},{1,7},{2,0},{3,5},{4,6},{5,3},{6,4},{7,1},{8,10},{9,15},{10,... | collective-permute-start | bytes 1572872 | tf_op jit(solution)/shard_map/ppermute | solution.py:43
  58.2 10.4 %collective-permute-done.12.recv_ref = bf16[2,2,32,1536]{3,2,1,0:T(8,128)(2,1)S(1)} collective-permute-done((bf16[2,2,32,1536]{3,2,1,0:T(8,128)(2,1)S(1)}, bf16[2,2,32,1536]{3,2,1,0:T(8,128)(2,1)S(1)}, u32[]{:S(2)}, u32[]{:S(2)}) %collective-permute-start.12) | collective-permute-done | bytes 393248 | tf_op jit(solution)/shard_map/ppermute | solution.py:43
  69.4 0.6 collective-permute-start.15
  70.0 0.9 collective-permute-start.16
  70.9 1.9 %pairs_4.1 = (bf16[2,2,2,32,512]{4,3,2,1,0:T(8,128)(2,1)S(1)}, bf16[2,2,2,32,512]{4,3,2,1,0:T(8,128)(2,1)S(1)}) custom-call(s32[5]{0:T(128)S(1)} %stack.23.place_ref.at_ref.yi_ref.ci_ref, bf16[128,2048]{1,0:T(8,128)(2,1)S(1)} %collective-permute-done.10.refs_0_, bf16[128,2048]{1,0:T(8,128)(2,1)S(1)} %collective-permute-done.13.refs_1_, ...), custom_call_target="tpu_custom_call" | custom-call | flops 1073741824 | bytes 8388608 | tf_op jit(solution)/shard_map/pairs_4/pallas_call | solution.py:147
  72.8 2.6 %collective-permute-start.18 = (bf16[2,2,2,32,512]{4,3,2,1,0:T(8,128)(2,1)S(1)}, bf16[2,2,2,32,512]{4,3,2,1,0:T(8,128)(2,1)S(1)}, u32[]{:S(2)}, u32[]{:S(2)}) collective-permute-start(bf16[2,2,2,32,512]{4,3,2,1,0:T(8,128)(2,1)S(1)} %get-tuple-element.99), channel_id=1, source_target_pairs={{0,2},{1,7},{2,0},{3,5},{4,6},{5,3},{6,4},{7,1},{8,10},{9,15},{10,... | collective-permute-start | bytes 786440 | tf_op jit(solution)/shard_map/ppermute | solution.py:43
  75.4 2.9 %collective-permute-start.17 = (bf16[2,32,1536]{2,1,0:T(8,128)(2,1)S(1)}, bf16[2,32,1536]{2,1,0:T(8,128)(2,1)S(1)}, u32[]{:S(2)}, u32[]{:S(2)}) collective-permute-start(bf16[2,32,1536]{2,1,0:T(8,128)(2,1)S(1)} %get-tuple-element.96), channel_id=1, source_target_pairs={{0,8},{1,9},{2,10},{3,11},{4,12},{5,13},{6,14},{7,15},{8,0},{9,1},... | collective-permute-start | bytes 589832 | tf_op jit(solution)/shard_map/ppermute | solution.py:43
  79.5 1.9 %collective-permute-start.19 = (bf16[2,32,1024]{2,1,0:T(8,128)(2,1)S(1)}, bf16[2,32,1024]{2,1,0:T(8,128)(2,1)S(1)}, u32[]{:S(2)}, u32[]{:S(2)}) collective-permute-start(bf16[2,32,1024]{2,1,0:T(8,128)(2,1)S(1)} %get-tuple-element.102), channel_id=1, source_target_pairs={{0,8},{1,9},{2,10},{3,11},{4,12},{5,13},{6,14},{7,15},{8,0},{9,1},... | collective-permute-start | bytes 393224 | tf_op jit(solution)/shard_map/ppermute | solution.py:43
  81.4 1.5 %collective-permute-done.17.refs_1_ = bf16[2,32,1536]{2,1,0:T(8,128)(2,1)S(1)} collective-permute-done((bf16[2,32,1536]{2,1,0:T(8,128)(2,1)S(1)}, bf16[2,32,1536]{2,1,0:T(8,128)(2,1)S(1)}, u32[]{:S(2)}, u32[]{:S(2)}) %collective-permute-start.17) | collective-permute-done | bytes 196640 | tf_op jit(solution)/shard_map/ppermute | solution.py:43
  83.1 3.2 %collective-permute-start.21 = (bf16[2,32,1024]{2,1,0:T(8,128)(2,1)S(1)}, bf16[2,32,1024]{2,1,0:T(8,128)(2,1)S(1)}, u32[]{:S(2)}, u32[]{:S(2)}) collective-permute-start(bf16[2,32,1024]{2,1,0:T(8,128)(2,1)S(1)} %get-tuple-element.109), channel_id=1, source_target_pairs={{0,8},{1,9},{2,10},{3,11},{4,12},{5,13},{6,14},{7,15},{8,0},{9,1},... | collective-permute-start | bytes 393224 | tf_op jit(solution)/shard_map/ppermute | solution.py:43
  87.5 1.2 %collective-permute-done.21.refs_1_ = bf16[2,32,1024]{2,1,0:T(8,128)(2,1)S(1)} collective-permute-done((bf16[2,32,1024]{2,1,0:T(8,128)(2,1)S(1)}, bf16[2,32,1024]{2,1,0:T(8,128)(2,1)S(1)}, u32[]{:S(2)}, u32[]{:S(2)}) %collective-permute-start.21) | collective-permute-done | bytes 131104 | tf_op jit(solution)/shard_map/ppermute | solution.py:43
  88.8 1.4 %collective-permute-start.22 = (bf16[2,32,768]{2,1,0:T(8,128)(2,1)S(1)}, bf16[2,32,768]{2,1,0:T(8,128)(2,1)S(1)}, u32[]{:S(2)}, u32[]{:S(2)}) collective-permute-start(bf16[2,32,768]{2,1,0:T(8,128)(2,1)S(1)} %get-tuple-element.112), channel_id=1, source_target_pairs={{0,16},{1,17},{2,18},{3,19},{4,20},{5,21},{6,22},{7,23},{8,24},{9,... | collective-permute-start | bytes 294920 | tf_op jit(solution)/shard_map/ppermute | solution.py:43
  90.2 0.6 collective-permute-start.25
  90.8 1.1 collective-permute-start.24
  91.9 2.6 %collective-permute-done.23.refs_4_ = bf16[2,32,512]{2,1,0:T(8,128)(2,1)S(1)} collective-permute-done((bf16[2,32,512]{2,1,0:T(8,128)(2,1)S(1)}, bf16[2,32,512]{2,1,0:T(8,128)(2,1)S(1)}, u32[]{:S(2)}, u32[]{:S(2)}) %collective-permute-start.23) | collective-permute-done | bytes 65568 | tf_op jit(solution)/shard_map/ppermute | solution.py:43
  94.5 1.9 %collective-permute-done.25.refs_6_ = bf16[2,32,512]{2,1,0:T(8,128)(2,1)S(1)} collective-permute-done((bf16[2,32,512]{2,1,0:T(8,128)(2,1)S(1)}, bf16[2,32,512]{2,1,0:T(8,128)(2,1)S(1)}, u32[]{:S(2)}, u32[]{:S(2)}) %collective-permute-start.25) | collective-permute-done | bytes 65568 | tf_op jit(solution)/shard_map/ppermute | solution.py:43
  96.4 0.7 collective-permute-done.24.refs_5_
  97.7 7.9 %collective-permute-start.26 = (bf16[2,16,3584]{2,1,0:T(8,128)(2,1)S(1)}, bf16[2,16,3584]{2,1,0:T(8,128)(2,1)S(1)}, u32[]{:S(2)}, u32[]{:S(2)}) collective-permute-start(bf16[2,16,3584]{2,1,0:T(8,128)(2,1)S(1)} %split.1), channel_id=1, source_target_pairs={{0,1},{1,0},{2,3},{3,2},{4,5},{5,4},{6,7},{7,6},{8,9},{9,8},{10,11... | collective-permute-start | bytes 688136 | tf_op jit(solution)/shard_map/ppermute | solution.py:43
  105.6 1.6 %collective-permute-start.27 = (bf16[2,32,256]{2,1,0:T(8,128)(2,1)S(1)}, bf16[2,32,256]{2,1,0:T(8,128)(2,1)S(1)}, u32[]{:S(2)}, u32[]{:S(2)}) collective-permute-start(bf16[2,32,256]{2,1,0:T(8,128)(2,1)S(1)} %get-tuple-element.116), channel_id=1, source_target_pairs={{0,8},{1,9},{2,10},{3,11},{4,12},{5,13},{6,14},{7,15},{8,0},{9,1},... | collective-permute-start | bytes 98312 | tf_op jit(solution)/shard_map/ppermute | solution.py:43
  107.2 1.9 %collective-permute-start.29 = (bf16[2,32,256]{2,1,0:T(8,128)(2,1)S(1)}, bf16[2,32,256]{2,1,0:T(8,128)(2,1)S(1)}, u32[]{:S(2)}, u32[]{:S(2)}) collective-permute-start(bf16[2,32,256]{2,1,0:T(8,128)(2,1)S(1)} %get-tuple-element.118), channel_id=1, source_target_pairs={{0,24},{1,25},{2,26},{3,27},{4,28},{5,29},{6,30},{7,31},{8,16},{9,... | collective-permute-start | bytes 98312 | tf_op jit(solution)/shard_map/ppermute | solution.py:43
  109.1 0.8 collective-permute-done.27.recv_ref
  110.3 0.9 collective-permute-done.29.b_ref
  111.8 1.6 %collective-permute-start.30 = (bf16[2,16,512]{2,1,0:T(8,128)(2,1)S(1)}, bf16[2,16,512]{2,1,0:T(8,128)(2,1)S(1)}, u32[]{:S(2)}, u32[]{:S(2)}) collective-permute-start(bf16[2,16,512]{2,1,0:T(8,128)(2,1)S(1)} %get-tuple-element.120), channel_id=1, source_target_pairs={{0,1},{1,0},{2,3},{3,2},{4,5},{5,4},{6,7},{7,6},{8,9},{9,8},{10,11... | collective-permute-start | bytes 98312 | tf_op jit(solution)/shard_map/ppermute | solution.py:43
  113.4 0.9 collective-permute-done.30.refs_9_
  114.2 1.5 %finish.1 = f32[2,16,4096]{2,1,0:T(8,128)} custom-call(s32[5]{0:T(128)S(1)} %stack.23.place_ref.at_ref.yi_ref.ci_ref, bf16[2,32,768]{2,1,0:T(8,128)(2,1)S(1)} %get-tuple-element.97.refs_0_, bf16[2,32,256]{2,1,0:T(8,128)(2,1)S(1)} %get-tuple-element.104.refs_1_, bf16[2,32,256]{2,1,0:T(8,128)(2,1)S(1)} %get-tuple-element.111.refs_2_, ...), custom_call_target="tpu_custom_call" | custom-call | flops 1000 | bytes 1048576 | tf_op jit(solution)/shard_map/finish/pallas_call | solution.py:166
  (45 shorter events, 6.0 us)
Async XLA Ops:
  0.0 23.8 %copy-start.1 = (s32[512]{0:T(512)S(1)}, s32[512]{0:T(512)}, u32[]{:S(2)}) copy-start(s32[512]{0:T(512)} %param.3) | copy-start | bytes 6148
  0.1 1.2 %copy-start = (bf16[2,2,512,256]{3,2,1,0:T(8,128)(2,1)S(1)}, bf16[2,2,512,256]{3,2,1,0:T(8,128)(2,1)}, u32[]{:S(2)}) copy-start(bf16[2,2,512,256]{3,2,1,0:T(8,128)(2,1)} %x_ref.3) | copy-start | bytes 3145732
  2.4 12.6 %collective-permute-start = (bf16[128,2048]{1,0:T(8,128)(2,1)S(1)}, bf16[128,2048]{1,0:T(8,128)(2,1)S(1)}, u32[]{:S(2)}, u32[]{:S(2)}) collective-permute-start(bf16[128,2048]{1,0:T(8,128)(2,1)S(1)} %whiten.2.a_ref.refs_2_), channel_id=1, source_target_pairs={{0,32},{1,225},{2,34},{3,227},{4,36},{5,229},{6,38},{7,231},{8,40}... | collective-permute-start | bytes 1572872 | tf_op jit(solution)/shard_map/ppermute | solution.py:43
  10.0 10.6 %collective-permute-start.1 = (bf16[128,2048]{1,0:T(8,128)(2,1)S(1)}, bf16[128,2048]{1,0:T(8,128)(2,1)S(1)}, u32[]{:S(2)}, u32[]{:S(2)}) collective-permute-start(bf16[128,2048]{1,0:T(8,128)(2,1)S(1)} %whiten.3.b_ref.refs_3_), channel_id=1, source_target_pairs={{0,32},{1,225},{2,34},{3,227},{4,36},{5,229},{6,38},{7,231},{8,40}... | collective-permute-start | bytes 1572872 | tf_op jit(solution)/shard_map/ppermute | solution.py:43
  10.9 19.1 %collective-permute-start.4 = (bf16[128,2048]{1,0:T(8,128)(2,1)S(1)}, bf16[128,2048]{1,0:T(8,128)(2,1)S(1)}, u32[]{:S(2)}, u32[]{:S(2)}) collective-permute-start(bf16[128,2048]{1,0:T(8,128)(2,1)S(1)} %whiten.2.a_ref.refs_2_), channel_id=1, source_target_pairs={{0,16},{1,17},{2,18},{3,19},{4,20},{5,21},{6,22},{7,23},{8,24},{9,... | collective-permute-start | bytes 1572872 | tf_op jit(solution)/shard_map/ppermute | solution.py:43
  12.2 22.3 %collective-permute-start.5 = (bf16[128,2048]{1,0:T(8,128)(2,1)S(1)}, bf16[128,2048]{1,0:T(8,128)(2,1)S(1)}, u32[]{:S(2)}, u32[]{:S(2)}) collective-permute-start(bf16[128,2048]{1,0:T(8,128)(2,1)S(1)} %whiten.3.b_ref.refs_3_), channel_id=1, source_target_pairs={{0,16},{1,17},{2,18},{3,19},{4,20},{5,21},{6,22},{7,23},{8,24},{9,... | collective-permute-start | bytes 1572872 | tf_op jit(solution)/shard_map/ppermute | solution.py:43
  15.0 20.3 %collective-permute-start.2 = (bf16[128,2048]{1,0:T(8,128)(2,1)S(1)}, bf16[128,2048]{1,0:T(8,128)(2,1)S(1)}, u32[]{:S(2)}, u32[]{:S(2)}) collective-permute-start(bf16[128,2048]{1,0:T(8,128)(2,1)S(1)} %collective-permute-done.refs_0_), channel_id=1, source_target_pairs={{0,32},{1,225},{2,34},{3,227},{4,36},{5,229},{6,38},{7,231},{8,40}... | collective-permute-start | bytes 1572872 | tf_op jit(solution)/shard_map/ppermute | solution.py:43
  20.7 17.0 %collective-permute-start.6 = (bf16[128,2048]{1,0:T(8,128)(2,1)S(1)}, bf16[128,2048]{1,0:T(8,128)(2,1)S(1)}, u32[]{:S(2)}, u32[]{:S(2)}) collective-permute-start(bf16[128,2048]{1,0:T(8,128)(2,1)S(1)} %collective-permute-done.1.refs_1_), channel_id=1, source_target_pairs={{0,32},{1,225},{2,34},{3,227},{4,36},{5,229},{6,38},{7,231},{8,40}... | collective-permute-start | bytes 1572872 | tf_op jit(solution)/shard_map/ppermute | solution.py:43
  27.4 18.9 %collective-permute-start.7 = (bf16[2,2,2,32,768]{4,3,2,1,0:T(8,128)(2,1)S(1)}, bf16[2,2,2,32,768]{4,3,2,1,0:T(8,128)(2,1)S(1)}, u32[]{:S(2)}, u32[]{:S(2)}) collective-permute-start(bf16[2,2,2,32,768]{4,3,2,1,0:T(8,128)(2,1)S(1)} %get-tuple-element.73), channel_id=1, source_target_pairs={{0,2},{1,7},{2,0},{3,5},{4,6},{5,3},{6,4},{7,1},{8,10},{9,15},{10,... | collective-permute-start | bytes 1179656 | tf_op jit(solution)/shard_map/ppermute | solution.py:43
  35.4 10.9 %collective-permute-start.3 = (bf16[128,2048]{1,0:T(8,128)(2,1)S(1)}, bf16[128,2048]{1,0:T(8,128)(2,1)S(1)}, u32[]{:S(2)}, u32[]{:S(2)}) collective-permute-start(bf16[128,2048]{1,0:T(8,128)(2,1)S(1)} %collective-permute-done.2.refs_0_), channel_id=1, source_target_pairs={{0,32},{1,225},{2,34},{3,227},{4,36},{5,229},{6,38},{7,231},{8,40}... | collective-permute-start | bytes 1572872 | tf_op jit(solution)/shard_map/ppermute | solution.py:43
  37.6 12.0 %collective-permute-start.9 = (bf16[128,2048]{1,0:T(8,128)(2,1)S(1)}, bf16[128,2048]{1,0:T(8,128)(2,1)S(1)}, u32[]{:S(2)}, u32[]{:S(2)}) collective-permute-start(bf16[128,2048]{1,0:T(8,128)(2,1)S(1)} %collective-permute-done.6.refs_1_), channel_id=1, source_target_pairs={{0,32},{1,225},{2,34},{3,227},{4,36},{5,229},{6,38},{7,231},{8,40}... | collective-permute-start | bytes 1572872 | tf_op jit(solution)/shard_map/ppermute | solution.py:43
  40.2 8.4 %collective-permute-start.8 = (bf16[2,2,2,32,768]{4,3,2,1,0:T(8,128)(2,1)S(1)}, bf16[2,2,2,32,768]{4,3,2,1,0:T(8,128)(2,1)S(1)}, u32[]{:S(2)}, u32[]{:S(2)}) collective-permute-start(bf16[2,2,2,32,768]{4,3,2,1,0:T(8,128)(2,1)S(1)} %get-tuple-element.74), channel_id=1, source_target_pairs={{0,2},{1,7},{2,0},{3,5},{4,6},{5,3},{6,4},{7,1},{8,10},{9,15},{10,... | collective-permute-start | bytes 1179656 | tf_op jit(solution)/shard_map/ppermute | solution.py:43
  46.0 12.1 %collective-permute-start.11 = (bf16[2,2,2,32,1024]{4,3,2,1,0:T(8,128)(2,1)S(1)}, bf16[2,2,2,32,1024]{4,3,2,1,0:T(8,128)(2,1)S(1)}, u32[]{:S(2)}, u32[]{:S(2)}) collective-permute-start(bf16[2,2,2,32,1024]{4,3,2,1,0:T(8,128)(2,1)S(1)} %get-tuple-element.79), channel_id=1, source_target_pairs={{0,2},{1,7},{2,0},{3,5},{4,6},{5,3},{6,4},{7,1},{8,10},{9,15},{10,... | collective-permute-start | bytes 1572872 | tf_op jit(solution)/shard_map/ppermute | solution.py:43
  48.8 9.3 %collective-permute-start.10 = (bf16[128,2048]{1,0:T(8,128)(2,1)S(1)}, bf16[128,2048]{1,0:T(8,128)(2,1)S(1)}, u32[]{:S(2)}, u32[]{:S(2)}) collective-permute-start(bf16[128,2048]{1,0:T(8,128)(2,1)S(1)} %collective-permute-done.3.refs_0_), channel_id=1, source_target_pairs={{0,32},{1,225},{2,34},{3,227},{4,36},{5,229},{6,38},{7,231},{8,40}... | collective-permute-start | bytes 1572872 | tf_op jit(solution)/shard_map/ppermute | solution.py:43
  49.6 19.6 %collective-permute-start.13 = (bf16[128,2048]{1,0:T(8,128)(2,1)S(1)}, bf16[128,2048]{1,0:T(8,128)(2,1)S(1)}, u32[]{:S(2)}, u32[]{:S(2)}) collective-permute-start(bf16[128,2048]{1,0:T(8,128)(2,1)S(1)} %collective-permute-done.9.refs_1_), channel_id=1, source_target_pairs={{0,32},{1,225},{2,34},{3,227},{4,36},{5,229},{6,38},{7,231},{8,40}... | collective-permute-start | bytes 1572872 | tf_op jit(solution)/shard_map/ppermute | solution.py:43
  55.5 13.8 %collective-permute-start.14 = (bf16[2,2,2,32,1024]{4,3,2,1,0:T(8,128)(2,1)S(1)}, bf16[2,2,2,32,1024]{4,3,2,1,0:T(8,128)(2,1)S(1)}, u32[]{:S(2)}, u32[]{:S(2)}) collective-permute-start(bf16[2,2,2,32,1024]{4,3,2,1,0:T(8,128)(2,1)S(1)} %get-tuple-element.85), channel_id=1, source_target_pairs={{0,2},{1,7},{2,0},{3,5},{4,6},{5,3},{6,4},{7,1},{8,10},{9,15},{10,... | collective-permute-start | bytes 1572872 | tf_op jit(solution)/shard_map/ppermute | solution.py:43
  58.0 10.6 %collective-permute-start.12 = (bf16[2,2,32,1536]{3,2,1,0:T(8,128)(2,1)S(1)}, bf16[2,2,32,1536]{3,2,1,0:T(8,128)(2,1)S(1)}, u32[]{:S(2)}, u32[]{:S(2)}) collective-permute-start(bf16[2,2,32,1536]{3,2,1,0:T(8,128)(2,1)S(1)} %get-tuple-element.82), channel_id=1, source_target_pairs={{0,6},{1,3},{2,4},{3,1},{4,2},{5,7},{6,0},{7,5},{8,14},{9,11},{10,... | collective-permute-start | bytes 1179656 | tf_op jit(solution)/shard_map/ppermute | solution.py:43
  69.4 8.9 %collective-permute-start.15 = (bf16[2,2,32,1024]{3,2,1,0:T(8,128)(2,1)S(1)}, bf16[2,2,32,1024]{3,2,1,0:T(8,128)(2,1)S(1)}, u32[]{:S(2)}, u32[]{:S(2)}) collective-permute-start(bf16[2,2,32,1024]{3,2,1,0:T(8,128)(2,1)S(1)} %get-tuple-element.90), channel_id=1, source_target_pairs={{0,6},{1,3},{2,4},{3,1},{4,2},{5,7},{6,0},{7,5},{8,14},{9,11},{10,... | collective-permute-start | bytes 786440 | tf_op jit(solution)/shard_map/ppermute | solution.py:43
  70.0 8.9 %collective-permute-start.16 = (bf16[2,2,32,1024]{3,2,1,0:T(8,128)(2,1)S(1)}, bf16[2,2,32,1024]{3,2,1,0:T(8,128)(2,1)S(1)}, u32[]{:S(2)}, u32[]{:S(2)}) collective-permute-start(bf16[2,2,32,1024]{3,2,1,0:T(8,128)(2,1)S(1)} %get-tuple-element.93), channel_id=1, source_target_pairs={{0,6},{1,3},{2,4},{3,1},{4,2},{5,7},{6,0},{7,5},{8,14},{9,11},{10,... | collective-permute-start | bytes 786440 | tf_op jit(solution)/shard_map/ppermute | solution.py:43
  72.8 10.1 %collective-permute-start.18 = (bf16[2,2,2,32,512]{4,3,2,1,0:T(8,128)(2,1)S(1)}, bf16[2,2,2,32,512]{4,3,2,1,0:T(8,128)(2,1)S(1)}, u32[]{:S(2)}, u32[]{:S(2)}) collective-permute-start(bf16[2,2,2,32,512]{4,3,2,1,0:T(8,128)(2,1)S(1)} %get-tuple-element.99), channel_id=1, source_target_pairs={{0,2},{1,7},{2,0},{3,5},{4,6},{5,3},{6,4},{7,1},{8,10},{9,15},{10,... | collective-permute-start | bytes 786440 | tf_op jit(solution)/shard_map/ppermute | solution.py:43
  75.4 7.5 %collective-permute-start.17 = (bf16[2,32,1536]{2,1,0:T(8,128)(2,1)S(1)}, bf16[2,32,1536]{2,1,0:T(8,128)(2,1)S(1)}, u32[]{:S(2)}, u32[]{:S(2)}) collective-permute-start(bf16[2,32,1536]{2,1,0:T(8,128)(2,1)S(1)} %get-tuple-element.96), channel_id=1, source_target_pairs={{0,8},{1,9},{2,10},{3,11},{4,12},{5,13},{6,14},{7,15},{8,0},{9,1},... | collective-permute-start | bytes 589832 | tf_op jit(solution)/shard_map/ppermute | solution.py:43
  79.5 6.8 %collective-permute-start.19 = (bf16[2,32,1024]{2,1,0:T(8,128)(2,1)S(1)}, bf16[2,32,1024]{2,1,0:T(8,128)(2,1)S(1)}, u32[]{:S(2)}, u32[]{:S(2)}) collective-permute-start(bf16[2,32,1024]{2,1,0:T(8,128)(2,1)S(1)} %get-tuple-element.102), channel_id=1, source_target_pairs={{0,8},{1,9},{2,10},{3,11},{4,12},{5,13},{6,14},{7,15},{8,0},{9,1},... | collective-permute-start | bytes 393224 | tf_op jit(solution)/shard_map/ppermute | solution.py:43
  83.0 3.9 %collective-permute-start.20 = (bf16[2,2,32,512]{3,2,1,0:T(8,128)(2,1)S(1)}, bf16[2,2,32,512]{3,2,1,0:T(8,128)(2,1)S(1)}, u32[]{:S(2)}, u32[]{:S(2)}) collective-permute-start(bf16[2,2,32,512]{3,2,1,0:T(8,128)(2,1)S(1)} %get-tuple-element.106), channel_id=1, source_target_pairs={{0,6},{1,3},{2,4},{3,1},{4,2},{5,7},{6,0},{7,5},{8,14},{9,11},{10,... | collective-permute-start | bytes 393224 | tf_op jit(solution)/shard_map/ppermute | solution.py:43
  83.1 5.6 %collective-permute-start.21 = (bf16[2,32,1024]{2,1,0:T(8,128)(2,1)S(1)}, bf16[2,32,1024]{2,1,0:T(8,128)(2,1)S(1)}, u32[]{:S(2)}, u32[]{:S(2)}) collective-permute-start(bf16[2,32,1024]{2,1,0:T(8,128)(2,1)S(1)} %get-tuple-element.109), channel_id=1, source_target_pairs={{0,8},{1,9},{2,10},{3,11},{4,12},{5,13},{6,14},{7,15},{8,0},{9,1},... | collective-permute-start | bytes 393224 | tf_op jit(solution)/shard_map/ppermute | solution.py:43
  88.8 8.4 %collective-permute-start.22 = (bf16[2,32,768]{2,1,0:T(8,128)(2,1)S(1)}, bf16[2,32,768]{2,1,0:T(8,128)(2,1)S(1)}, u32[]{:S(2)}, u32[]{:S(2)}) collective-permute-start(bf16[2,32,768]{2,1,0:T(8,128)(2,1)S(1)} %get-tuple-element.112), channel_id=1, source_target_pairs={{0,16},{1,17},{2,18},{3,19},{4,20},{5,21},{6,22},{7,23},{8,24},{9,... | collective-permute-start | bytes 294920 | tf_op jit(solution)/shard_map/ppermute | solution.py:43
  90.2 4.3 %collective-permute-start.23 = (bf16[2,32,512]{2,1,0:T(8,128)(2,1)S(1)}, bf16[2,32,512]{2,1,0:T(8,128)(2,1)S(1)}, u32[]{:S(2)}, u32[]{:S(2)}) collective-permute-start(bf16[2,32,512]{2,1,0:T(8,128)(2,1)S(1)} %get-tuple-element.113), channel_id=1, source_target_pairs={{0,224},{1,33},{2,226},{3,35},{4,228},{5,37},{6,230},{7,39},{8,232... | collective-permute-start | bytes 196616 | tf_op jit(solution)/shard_map/ppermute | solution.py:43
  90.2 6.2 %collective-permute-start.25 = (bf16[2,32,512]{2,1,0:T(8,128)(2,1)S(1)}, bf16[2,32,512]{2,1,0:T(8,128)(2,1)S(1)}, u32[]{:S(2)}, u32[]{:S(2)}) collective-permute-start(bf16[2,32,512]{2,1,0:T(8,128)(2,1)S(1)} %get-tuple-element.115), channel_id=1, source_target_pairs={{0,160},{1,97},{2,162},{3,99},{4,164},{5,101},{6,166},{7,103},{8,1... | collective-permute-start | bytes 196616 | tf_op jit(solution)/shard_map/ppermute | solution.py:43
  90.8 6.3 %collective-permute-start.24 = (bf16[2,32,512]{2,1,0:T(8,128)(2,1)S(1)}, bf16[2,32,512]{2,1,0:T(8,128)(2,1)S(1)}, u32[]{:S(2)}, u32[]{:S(2)}) collective-permute-start(bf16[2,32,512]{2,1,0:T(8,128)(2,1)S(1)} %get-tuple-element.114), channel_id=1, source_target_pairs={{0,192},{1,65},{2,194},{3,67},{4,196},{5,69},{6,198},{7,71},{8,200... | collective-permute-start | bytes 196616 | tf_op jit(solution)/shard_map/ppermute | solution.py:43
  97.7 16.5 %collective-permute-start.26 = (bf16[2,16,3584]{2,1,0:T(8,128)(2,1)S(1)}, bf16[2,16,3584]{2,1,0:T(8,128)(2,1)S(1)}, u32[]{:S(2)}, u32[]{:S(2)}) collective-permute-start(bf16[2,16,3584]{2,1,0:T(8,128)(2,1)S(1)} %split.1), channel_id=1, source_target_pairs={{0,1},{1,0},{2,3},{3,2},{4,5},{5,4},{6,7},{7,6},{8,9},{9,8},{10,11... | collective-permute-start | bytes 688136 | tf_op jit(solution)/shard_map/ppermute | solution.py:43
  105.6 4.3 %collective-permute-start.27 = (bf16[2,32,256]{2,1,0:T(8,128)(2,1)S(1)}, bf16[2,32,256]{2,1,0:T(8,128)(2,1)S(1)}, u32[]{:S(2)}, u32[]{:S(2)}) collective-permute-start(bf16[2,32,256]{2,1,0:T(8,128)(2,1)S(1)} %get-tuple-element.116), channel_id=1, source_target_pairs={{0,8},{1,9},{2,10},{3,11},{4,12},{5,13},{6,14},{7,15},{8,0},{9,1},... | collective-permute-start | bytes 98312 | tf_op jit(solution)/shard_map/ppermute | solution.py:43
  107.2 3.1 %collective-permute-start.28 = (bf16[2,32,256]{2,1,0:T(8,128)(2,1)S(1)}, bf16[2,32,256]{2,1,0:T(8,128)(2,1)S(1)}, u32[]{:S(2)}, u32[]{:S(2)}) collective-permute-start(bf16[2,32,256]{2,1,0:T(8,128)(2,1)S(1)} %get-tuple-element.117), channel_id=1, source_target_pairs={{0,16},{1,17},{2,18},{3,19},{4,20},{5,21},{6,22},{7,23},{8,24},{9,... | collective-permute-start | bytes 98312 | tf_op jit(solution)/shard_map/ppermute | solution.py:43
  107.2 4.0 %collective-permute-start.29 = (bf16[2,32,256]{2,1,0:T(8,128)(2,1)S(1)}, bf16[2,32,256]{2,1,0:T(8,128)(2,1)S(1)}, u32[]{:S(2)}, u32[]{:S(2)}) collective-permute-start(bf16[2,32,256]{2,1,0:T(8,128)(2,1)S(1)} %get-tuple-element.118), channel_id=1, source_target_pairs={{0,24},{1,25},{2,26},{3,27},{4,28},{5,29},{6,30},{7,31},{8,16},{9,... | collective-permute-start | bytes 98312 | tf_op jit(solution)/shard_map/ppermute | solution.py:43
  111.8 2.5 %collective-permute-start.30 = (bf16[2,16,512]{2,1,0:T(8,128)(2,1)S(1)}, bf16[2,16,512]{2,1,0:T(8,128)(2,1)S(1)}, u32[]{:S(2)}, u32[]{:S(2)}) collective-permute-start(bf16[2,16,512]{2,1,0:T(8,128)(2,1)S(1)} %get-tuple-element.120), channel_id=1, source_target_pairs={{0,1},{1,0},{2,3},{3,2},{4,5},{5,4},{6,7},{7,6},{8,9},{9,8},{10,11... | collective-permute-start | bytes 98312 | tf_op jit(solution)/shard_map/ppermute | solution.py:43

commit v4 on v3

--- a/solution.py
+++ b/solution.py
@@ -47,7 +47,7 @@
     return 1 - 2 * c
 
 
-def whiten_kernel(place_ref, x_ref, o_ref):
+def whiten_kernel(x_ref, o_ref):
     row = lax.broadcasted_iota(jnp.int32, (BINS, BINS), 0)
     col = lax.broadcasted_iota(jnp.int32, (BINS, BINS), 1)
     window = (jnp.abs(row - col) <= HALF).astype(F32).astype(BF16)
@@ -67,17 +67,17 @@
         o_ref[:, (2 + s) * BINS : (3 + s) * BINS] = (im * scale).astype(BF16)
 
 
-def whiten(place, spectra, half):
+def whiten(spectra, half):
     return pl.pallas_call(
         whiten_kernel,
         grid=(1,),
-        in_specs=[pl.BlockSpec(memory_space=pltpu.SMEM), pl.BlockSpec((2, 2, BINS, 128), lambda i: (0, 0, 0, half))],
+        in_specs=[pl.BlockSpec((2, 2, BINS, 128), lambda i: (0, 0, 0, half))],
         out_specs=pl.BlockSpec((128, DEPTH), lambda i: (0, 0)),
         out_shape=jax.ShapeDtypeStruct((128, DEPTH), BF16),
         compiler_params=params(12),
         cost_estimate=cost(2 * 4 * 128 * 512 * 512, MIB),
         name="whiten",
-    )(place, spectra)
+    )(spectra)
 
 
 def phases(bin_index):
@@ -194,75 +194,50 @@
     return call(kernel, None, [r for g in groups for r in g], [(shape, F32), (shape, BF16)], "sum_1")
 
 
-def sum_2(yi, kept, recv):
-    n = kept.shape[3]
-
-    def kernel(yi_ref, kept_ref, recv_ref, keep_ref, send_ref):
-        mine, other = yi_ref[2], 1 - yi_ref[2]
-        for m in range(LAGS):
-            keep_ref[m] = kept_ref[mine, m] + recv_ref[mine, m].astype(F32)
-            send_ref[m] = (kept_ref[other, m] + recv_ref[other, m].astype(F32)).astype(BF16)
-
-    return call(kernel, yi, [kept, recv], [((LAGS, 32, n), F32), ((LAGS, 32, n), BF16)], "sum_2")
-
-
-def sum_y(keep, recv, widths, extra=None):
+def sum_2(place, groups):
+    widths = [g[0].shape[3] for g in groups]
+
+    def kernel(place_ref, *refs):
+        keep_ref, send_ref = refs[-2:]
+        mine, other = place_ref[2], 1 - place_ref[2]
+        first = 0
+        for k, n in enumerate(widths):
+            kept, recv, cols = refs[2 * k], refs[2 * k + 1], slice(first, first + n)
+            for m in range(LAGS):
+                keep_ref[m, :, cols] = kept[mine, m] + recv[mine, m].astype(F32)
+                send_ref[m, :, cols] = (kept[other, m] + recv[other, m].astype(F32)).astype(BF16)
+            first += n
+
+    shape = (LAGS, 32, sum(widths))
+    return call(kernel, place, [r for g in groups for r in g], [(shape, F32), (shape, BF16)], "sum_2")
+
+
+def sum_y(keep, recv, outputs, extra=None):
     arrays = [keep, recv] + ([] if extra is None else [extra])
     more = 0 if extra is None else extra.shape[2]
 
     def kernel(*refs):
         keep_ref, recv_ref, outs = refs[0], refs[1], refs[len(arrays) :]
         for m in range(LAGS):
-            first = 0
-            for k, (out, n) in enumerate(zip(outs, widths)):
+            for k, (out, picks) in enumerate(zip(outs, outputs)):
                 to = 0
                 if k == 1 and more:
                     out[m, :, :more] = refs[2][m]
                     to = more
-                cols = slice(first, first + n)
-                out[m, :, to : to + n] = (keep_ref[m, :, cols] + recv_ref[m, :, cols].astype(F32)).astype(BF16)
-                first += n
-
-    shapes = [((LAGS, 32, n + (more if k == 1 else 0)), BF16) for k, n in enumerate(widths)]
+                for first, n in picks:
+                    cols = slice(first, first + n)
+                    out[m, :, to : to + n] = (keep_ref[m, :, cols] + recv_ref[m, :, cols].astype(F32)).astype(BF16)
+                    to += n
+
+    shapes = [((LAGS, 32, sum(n for _, n in p) + (more if k == 1 else 0)), BF16) for k, p in enumerate(outputs)]
     return call(kernel, None, arrays, shapes, "sum_y")
 
 
-def sum_last(yi, kept, recv):
-    def kernel(yi_ref, kept_ref, recv_ref, keep, send, near_mine, near_other):
-        mine, other = yi_ref[2], 1 - yi_ref[2]
-
-        def total(h, m, cols):
-            return kept_ref[h, m, :, cols] + recv_ref[h, m, :, cols].astype(F32)
-
-        for m in range(LAGS):
-            keep[m] = total(mine, m, slice(0, BLOCK))
-            send[m] = total(other, m, slice(0, BLOCK)).astype(BF16)
-            near_mine[m] = total(mine, m, slice(BLOCK, 2 * BLOCK)).astype(BF16)
-            near_other[m] = total(other, m, slice(BLOCK, 2 * BLOCK)).astype(BF16)
-
-    shape = (LAGS, 32, BLOCK)
-    return call(kernel, yi, [kept, recv], [(shape, F32), (shape, BF16), (shape, BF16), (shape, BF16)], "sum_last")
-
-
-def split_last(ci, keep, recv, near_a, near_b):
-    def kernel(ci_ref, keep_ref, recv_ref, a_ref, b_ref, mine_ref, send_ref):
-        for out, core in ((mine_ref, ci_ref[4]), (send_ref, 1 - ci_ref[4])):
-            at = pl.ds(pl.multiple_of(core * 16, 16), 16)
-            for m in range(LAGS):
-                own = keep_ref[m, at, :] + recv_ref[m, at, :].astype(F32)
-                near = a_ref[m, at, :].astype(F32) + b_ref[m, at, :].astype(F32)
-                out[m, :, :BLOCK] = own.astype(out.dtype)
-                out[m, :, BLOCK:] = near.astype(out.dtype)
-
-    shape = (LAGS, 16, 2 * BLOCK)
-    return call(kernel, ci, [keep, recv, near_a, near_b], [(shape, F32), (shape, BF16)], "split_last")
-
-
-def split(ci, arrays):
+def split(place, arrays):
     total = sum(a.shape[2] for a in arrays)
 
-    def kernel(ci_ref, *refs):
-        at = pl.ds(pl.multiple_of((1 - ci_ref[4]) * 16, 16), 16)
+    def kernel(place_ref, *refs):
+        at = pl.ds(pl.multiple_of((1 - place_ref[4]) * 16, 16), 16)
         first = 0
         for ref in refs[:-1]:
             n = ref.shape[2]
@@ -270,13 +245,12 @@
                 refs[-1][m, :, first : first + n] = ref[m, at, :]
             first += n
 
-    return call(kernel, ci, arrays, [((LAGS, 16, total), BF16)], "split")[0]
-
-
-def finish(place, arrays, blocks, recv, last, last_recv, last_blocks):
+    return call(kernel, place, arrays, [((LAGS, 16, total), BF16)], "split")[0]
+
+
+def finish(place, arrays, blocks, recv):
     def kernel(place_ref, *refs):
-        out = refs[-1]
-        ins, recv_ref, last_ref, last_recv_ref = refs[:-4], refs[-4], refs[-3], refs[-2]
+        ins, recv_ref, out = refs[:-2], refs[-2], refs[-1]
         z, y, c = place_ref[0], place_ref[1], place_ref[4]
         rows = pl.ds(pl.multiple_of(c * 16, 16), 16)
 
@@ -290,14 +264,10 @@
             for ref, ids in zip(ins, blocks):
                 for n, block in enumerate(ids):
                     out[m, :, cols(block, 1 - 2 * c)] = ref[m, rows, n * BLOCK : (n + 1) * BLOCK].astype(F32)
-            for n, block in enumerate(last_blocks):
-                out[m, :, cols(block, 1 - 2 * c)] = last_ref[m, :, n * BLOCK : (n + 1) * BLOCK]
-            for ref, ids in ((recv_ref, sum(blocks, [])), (last_recv_ref, last_blocks)):
-                for n, block in enumerate(ids):
-                    out[m, :, cols(block, 2 * c - 1)] += ref[m, :, n * BLOCK : (n + 1) * BLOCK].astype(F32)
-
-    given = list(arrays) + [recv, last, last_recv]
-    return call(kernel, place, given, [((LAGS, 16, 4096), F32)], "finish")[0]
+            for n, block in enumerate(sum(blocks, [])):
+                out[m, :, cols(block, 2 * c - 1)] += recv_ref[m, :, n * BLOCK : (n + 1) * BLOCK].astype(F32)
+
+    return call(kernel, place, list(arrays) + [recv], [((LAGS, 16, 4096), F32)], "finish")[0]
 
 
 def chain_step(z, ylo, yhi, x, c):
@@ -306,10 +276,6 @@
 
 def y_step(z, ylo, yhi, x, c):
     return z, 1 - ylo, yhi, x, c
-
-
-def y_both(z, ylo, yhi, x, c):
-    return z, 1 - ylo, 1 - yhi, x, c
 
 
 def yhi_step(z, ylo, yhi, x, c):
@@ -339,15 +305,13 @@
 def body(spectra, bin_index):
     scale = 1.0 / math.sqrt(32 * BINS)
     place = jnp.stack([lax.axis_index(a) for a in AXES]).astype(jnp.int32)
-    at = yi = ci = place
-
-    own = [whiten(place, spectra, 0), whiten(place, spectra, 1)]
-    block = own
-    arrived = []
-    for _ in range(4):
-        block = [move(b, chain_step) for b in block]
-        arrived.append(block)
+
+    spectra = after(spectra, place)
+    own = [whiten(spectra, 0), whiten(spectra, 1)]
     near = [move(b, y_step) for b in own]
+    first = [move(b, chain_step) for b in own]
+    first[0] = after(first[0], near[0])
+    second = [move(b, chain_step) for b in first]
 
     cosine, sine = phases(bin_index)
     own_plus, own_minus = rotations(own, cosine, sine)
@@ -383,50 +347,48 @@
     rotated = [own_plus, own_minus, near_plus, near_minus]
     straight = [(0, 0, 4 * BLOCK)]
 
-    keep_o, send_o = products(at, own_pairs, arrived[0] + own + rotated[:2], 3 * BLOCK, scale, "pairs_own")
+    keep_o, send_o = products(place, own_pairs, first + own + rotated[:2], 3 * BLOCK, scale, "pairs_own")
     recv_o = move(send_o, x_near)
-    at_n = after(at, arrived[1][0], keep_o)
+    third = [move(b, chain_step) for b in (after(second[0], near[1], keep_o), second[1])]
+    fourth = [move(b, chain_step) for b in third]
+    at = after(place, second[1], keep_o)
     near_rotated = [own_plus, near_plus, near_minus]
-    keep_n, send_n = products(at_n, near_pairs, arrived[0] + near + near_rotated, 3 * BLOCK, scale, "pairs_near")
+    keep_n, send_n = products(at, near_pairs, first + near + near_rotated, 3 * BLOCK, scale, "pairs_near")
     recv_n = move(send_n, x_near)
-    keep_b, send_b = products(after(at, keep_n), all_pairs, arrived[1] + rotated, 4 * BLOCK, scale, "pairs_2")
+    at = after(place, keep_n, third[0])
+    keep_b, send_b = products(at, all_pairs, second + rotated, 4 * BLOCK, scale, "pairs_2")
     recv_b = move(send_b, x_near)
     picks = [(0, 0, 2 * BLOCK), (1, 0, BLOCK), (1, BLOCK, BLOCK), (0, 2 * BLOCK, BLOCK), (1, 2 * BLOCK, BLOCK)]
-    kept_a, send_a = sum_1([(after(keep_o, arrived[2][0], keep_b), recv_o), (keep_n, recv_n)], picks)
+    kept_a, send_a = sum_1([(after(keep_o, keep_b), recv_o), (keep_n, recv_n)], picks)
     recv_a = move(send_a, x_far)
-    keep_c, send_c = products(after(at, kept_a), all_pairs, arrived[2] + rotated, 4 * BLOCK, scale, "pairs_3")
+    at = after(place, kept_a)
+    keep_c, send_c = products(at, all_pairs, third + rotated, 4 * BLOCK, scale, "pairs_3")
     recv_c = move(send_c, x_near)
-    kept_b, send_b = sum_1([(after(keep_b, keep_c, arrived[3][0]), recv_b)], straight)
+    kept_b, send_b = sum_1([(after(keep_b, keep_c, fourth[0]), recv_b)], straight)
     recv_b = move(send_b, x_far)
-    keep_a, send_a = sum_2(yi, after(kept_a, kept_b), recv_a)
-    recv_a = move(send_a, yhi_step)
-    kept_c, send_c = sum_1([(after(keep_c, keep_a, arrived[3][1]), recv_c)], straight)
+    at = after(place, kept_b)
+    keep_d, send_d = products(at, last_pairs, fourth + [own_plus, near_plus], 2 * BLOCK, scale, "pairs_4")
+    recv_d = move(send_d, x_near)
+    kept_c, send_c = sum_1([(after(keep_c, keep_d), recv_c)], straight)
     recv_c = move(send_c, x_far)
-    at_d = after(at, kept_c)
-    keep_d, send_d = products(at_d, last_pairs, arrived[3] + [own_plus, near_plus], 2 * BLOCK, scale, "pairs_4")
-    recv_d = move(send_d, x_near)
-    keep_b, send_b = sum_2(yi, after(kept_b, keep_d), recv_b)
-    recv_b = move(send_b, yhi_step)
-    keep_c, send_c = sum_2(yi, after(kept_c, keep_b), recv_c)
-    recv_c = move(send_c, yhi_step)
-    own_a, near_a, ret_1 = sum_y(after(keep_a, keep_c), recv_a, [3 * BLOCK, BLOCK, 2 * BLOCK])
-    ret_1 = move(ret_1, back(1))
-    kept_d, send_d = sum_1([(after(keep_d, own_a), recv_d)], [(0, 0, 2 * BLOCK)])
+    keep_ab, send_ab = sum_2(place, [(after(kept_a, kept_c), recv_a), (kept_b, recv_b)])
+    recv_ab = move(send_ab, yhi_step)
+    kept_d, send_d = sum_1([(after(keep_d, keep_ab), recv_d)], [(0, 0, 2 * BLOCK)])
     recv_d = move(send_d, x_far)
-    own_b, near_b, ret_2 = sum_y(after(keep_b, kept_d), recv_b, [BLOCK, BLOCK, 2 * BLOCK], near_a)
-    ret_2 = move(ret_2, back(2))
-    keep_d, *send_d = sum_last(yi, after(kept_d, own_b), recv_d)
-    recv_d = [move(v, step) for v, step in zip(send_d, (yhi_step, y_step, y_both))]
-    own_c, near_c, ret_3 = sum_y(after(keep_c, keep_d), recv_c, [BLOCK, BLOCK, 2 * BLOCK], near_b)
+    keep_cd, send_cd = sum_2(place, [(kept_c, recv_c), (kept_d, recv_d)])
+    recv_cd = move(send_cd, yhi_step)
+    outputs = [[(0, 768), (1536, 256)], [(768, 256), (1792, 256)], [(1024, 512)], [(2048, 512)]]
+    own_ab, near_ab, ret_1, ret_2 = sum_y(after(keep_ab, keep_cd), recv_ab, outputs)
+    ret_1, ret_2 = move(ret_1, back(1)), move(ret_2, back(2))
+    outputs = [[(0, 256), (1024, 256)], [(256, 256), (1280, 256)], [(512, 512)]]
+    own_cd, near_all, ret_3 = sum_y(after(keep_cd, own_ab), recv_cd, outputs, near_ab)
     ret_3 = move(ret_3, back(3))
-    near_c = move(near_c, y_step)
-    mine_d, other_d = split_last(ci, keep_d, *recv_d)
-    other_d = move(other_d, core_step)
-    arrays = [own_a, own_b, own_c, near_c, ret_1, ret_2, ret_3]
-    blocks = [[(0, 0), (1, 0), (0, 1)], [(2, 0)], [(3, 0)], [(1, 1), (2, 1), (3, 1)]]
+    near_all = move(near_all, y_step)
+    arrays = [own_ab, own_cd, near_all, ret_1, ret_2, ret_3]
+    blocks = [[(0, 0), (1, 0), (0, 1), (2, 0)], [(3, 0), (4, 0)], [(1, 1), (2, 1), (3, 1), (4, 1)]]
     blocks += [[(-d, 0), (-d, 1)] for d in (1, 2, 3)]
-    others = move(split(ci, arrays), core_step)
-    return finish(place, arrays, blocks, others, mine_d, other_d, [(4, 0), (4, 1)])
+    others = move(split(place, arrays), core_step)
+    return finish(place, arrays, blocks, others)
 
 
 def solution(mesh):

time: 116 us -> 108 us (0.931)
  starting transfers between devices: 56.9 us -> 51.3 us
  Pallas kernels: 22.5 us -> 19.8 us
    ppermute x31 -> x26, starting transfers between devices: 56.9 us -> 51.3 us  [move(): return lax.ppermute(x, AXES, pairs)]
    pallas_call x14 -> x10, Pallas kernels: 5.59 us -> 3.91 us  [call(): pl.pallas_call(kernel, in_specs=[pl.BlockSpec(memory_space=pltpu.SMEM)] *...]
    ppermute x31 -> x26, waiting for transfers between devices: 34.7 us -> 34.8 us  [move(): return lax.ppermute(x, AXES, pairs)]
  transfers between devices with their start and end apart: 31 -> 26, of which waited for: 16 -> 15; matrix products, arithmetic and copies ran while one was open for 0% -> 0% of each run, Pallas kernels for 16% -> 16%
where the time goes in v4:
time: 108 us
  starting transfers between devices  51.3 us (48%)
  waiting for transfers between devices  34.8 us (32%)
  Pallas kernels  19.8 us (18%)
  local copies, waits for them, and re-layouts  1.31 us (1%)
    ppermute x26, starting transfers between devices, move(): return lax.ppermute(x, AXES, pairs)  51.3 us
    ppermute x26, waiting for transfers between devices, move(): return lax.ppermute(x, AXES, pairs)  34.8 us
    pallas_call x5, Pallas kernels, products(): pl.pallas_call(kernel, in_specs=[pl.BlockSpec(memory_space=pltpu.SMEM)] +...  12.7 us
    pallas_call x10, Pallas kernels, call(): pl.pallas_call(kernel, in_specs=[pl.BlockSpec(memory_space=pltpu.SMEM)] *...  3.91 us
  transfers between devices with their start and end apart: 26, of which 15 were waited for; matrix products, arithmetic and copies ran while one was open for 0% of the time, Pallas kernels for 16%

profile of v4, /device:TPU:1, one launch (start us, length us, event | category | flops | bytes accessed | tf_op | source)
XLA Modules:
  0.0 107.5 jit_solution(4913952994177589333)
XLA Ops:
  0.1 1.2 %copy-done = bf16[2,2,512,256]{3,2,1,0:T(8,128)(2,1)S(1)} copy-done((bf16[2,2,512,256]{3,2,1,0:T(8,128)(2,1)S(1)}, bf16[2,2,512,256]{3,2,1,0:T(8,128)(2,1)}, u32[]{:S(2)}) %copy-start) | copy-done | bytes 1048600
  1.3 0.6 whiten.2.a_ref.refs_2_
  1.9 2.2 %collective-permute-start.1 = (bf16[128,2048]{1,0:T(8,128)(2,1)S(1)}, bf16[128,2048]{1,0:T(8,128)(2,1)S(1)}, u32[]{:S(2)}, u32[]{:S(2)}) collective-permute-start(bf16[128,2048]{1,0:T(8,128)(2,1)S(1)} %whiten.2.a_ref.refs_2_), channel_id=1, source_target_pairs={{0,16},{1,17},{2,18},{3,19},{4,20},{5,21},{6,22},{7,23},{8,24},{9,... | collective-permute-start | bytes 1572872 | tf_op jit(solution)/shard_map/ppermute | solution.py:43
  4.1 5.6 %collective-permute-start = (bf16[128,2048]{1,0:T(8,128)(2,1)S(1)}, bf16[128,2048]{1,0:T(8,128)(2,1)S(1)}, u32[]{:S(2)}, u32[]{:S(2)}) collective-permute-start(bf16[128,2048]{1,0:T(8,128)(2,1)S(1)} %whiten.2.a_ref.refs_2_), channel_id=1, source_target_pairs={{0,32},{1,225},{2,34},{3,227},{4,36},{5,229},{6,38},{7,231},{8,40}... | collective-permute-start | bytes 1572872 | tf_op jit(solution)/shard_map/ppermute | solution.py:43
  9.7 0.6 whiten.3.b_ref.refs_3_
  10.3 0.8 collective-permute-start.2
  11.1 0.2 collective-permute-start.4
  11.3 3.2 %collective-permute-done.1.a_ref.refs_2_ = bf16[128,2048]{1,0:T(8,128)(2,1)S(1)} collective-permute-done((bf16[128,2048]{1,0:T(8,128)(2,1)S(1)}, bf16[128,2048]{1,0:T(8,128)(2,1)S(1)}, u32[]{:S(2)}, u32[]{:S(2)}) %collective-permute-start.1) | collective-permute-done | bytes 524320 | tf_op jit(solution)/shard_map/ppermute | solution.py:43
  14.5 1.3 %collective-permute-done.refs_0_ = bf16[128,2048]{1,0:T(8,128)(2,1)S(1)} collective-permute-done((bf16[128,2048]{1,0:T(8,128)(2,1)S(1)}, bf16[128,2048]{1,0:T(8,128)(2,1)S(1)}, u32[]{:S(2)}, u32[]{:S(2)}) %collective-permute-start) | collective-permute-done | bytes 524320 | tf_op jit(solution)/shard_map/ppermute | solution.py:43
  15.8 5.4 %collective-permute-start.5 = (bf16[128,2048]{1,0:T(8,128)(2,1)S(1)}, bf16[128,2048]{1,0:T(8,128)(2,1)S(1)}, u32[]{:S(2)}, u32[]{:S(2)}) collective-permute-start(bf16[128,2048]{1,0:T(8,128)(2,1)S(1)} %collective-permute-done.refs_0_), channel_id=1, source_target_pairs={{0,32},{1,225},{2,34},{3,227},{4,36},{5,229},{6,38},{7,231},{8,40}... | collective-permute-start | bytes 1572872 | tf_op jit(solution)/shard_map/ppermute | solution.py:43
  21.2 0.2 collective-permute-done.2.refs_1_
  21.5 3.1 %collective-permute-start.3 = (bf16[128,2048]{1,0:T(8,128)(2,1)S(1)}, bf16[128,2048]{1,0:T(8,128)(2,1)S(1)}, u32[]{:S(2)}, u32[]{:S(2)}) collective-permute-start(bf16[128,2048]{1,0:T(8,128)(2,1)S(1)} %collective-permute-done.2.refs_1_), channel_id=1, source_target_pairs={{0,32},{1,225},{2,34},{3,227},{4,36},{5,229},{6,38},{7,231},{8,40}... | collective-permute-start | bytes 1572872 | tf_op jit(solution)/shard_map/ppermute | solution.py:43
  24.7 1.0 rotate.2
  25.7 2.4 %pairs_own.1 = (bf16[2,2,2,32,768]{4,3,2,1,0:T(8,128)(2,1)S(1)}, bf16[2,2,2,32,768]{4,3,2,1,0:T(8,128)(2,1)S(1)}) custom-call(s32[5]{0:T(128)S(1)} %stack.23.at_ref.place_ref, bf16[128,2048]{1,0:T(8,128)(2,1)S(1)} %collective-permute-done.refs_0_, bf16[128,2048]{1,0:T(8,128)(2,1)S(1)} %collective-permute-done.2.refs_1_, ...), custom_call_target="tpu_custom_call" | custom-call | flops 1610612736 | bytes 8388608 | tf_op jit(solution)/shard_map/pairs_own/pallas_call | solution.py:147
  28.2 4.3 %collective-permute-start.6 = (bf16[128,2048]{1,0:T(8,128)(2,1)S(1)}, bf16[128,2048]{1,0:T(8,128)(2,1)S(1)}, u32[]{:S(2)}, u32[]{:S(2)}) collective-permute-start(bf16[128,2048]{1,0:T(8,128)(2,1)S(1)} %collective-permute-done.5.refs_0_), channel_id=1, source_target_pairs={{0,32},{1,225},{2,34},{3,227},{4,36},{5,229},{6,38},{7,231},{8,40}... | collective-permute-start | bytes 1572872 | tf_op jit(solution)/shard_map/ppermute | solution.py:43
  32.4 0.5 collective-permute-done.3.refs_1_
  33.0 3.1 %collective-permute-start.9 = (bf16[128,2048]{1,0:T(8,128)(2,1)S(1)}, bf16[128,2048]{1,0:T(8,128)(2,1)S(1)}, u32[]{:S(2)}, u32[]{:S(2)}) collective-permute-start(bf16[128,2048]{1,0:T(8,128)(2,1)S(1)} %collective-permute-done.3.refs_1_), channel_id=1, source_target_pairs={{0,32},{1,225},{2,34},{3,227},{4,36},{5,229},{6,38},{7,231},{8,40}... | collective-permute-start | bytes 1572872 | tf_op jit(solution)/shard_map/ppermute | solution.py:43
  36.1 2.5 %collective-permute-start.7 = (bf16[2,2,2,32,768]{4,3,2,1,0:T(8,128)(2,1)S(1)}, bf16[2,2,2,32,768]{4,3,2,1,0:T(8,128)(2,1)S(1)}, u32[]{:S(2)}, u32[]{:S(2)}) collective-permute-start(bf16[2,2,2,32,768]{4,3,2,1,0:T(8,128)(2,1)S(1)} %get-tuple-element.65), channel_id=1, source_target_pairs={{0,2},{1,7},{2,0},{3,5},{4,6},{5,3},{6,4},{7,1},{8,10},{9,15},{10,... | collective-permute-start | bytes 1179656 | tf_op jit(solution)/shard_map/ppermute | solution.py:43
  38.5 1.0 rotate.3
  39.5 2.4 %pairs_near.1 = (bf16[2,2,2,32,768]{4,3,2,1,0:T(8,128)(2,1)S(1)}, bf16[2,2,2,32,768]{4,3,2,1,0:T(8,128)(2,1)S(1)}) custom-call(s32[5]{0:T(128)S(1)} %stack.23.at_ref.place_ref, bf16[128,2048]{1,0:T(8,128)(2,1)S(1)} %collective-permute-done.refs_0_, bf16[128,2048]{1,0:T(8,128)(2,1)S(1)} %collective-permute-done.2.refs_1_, ...), custom_call_target="tpu_custom_call" | custom-call | flops 1610612736 | bytes 8388608 | tf_op jit(solution)/shard_map/pairs_near/pallas_call | solution.py:147
  42.0 0.3 collective-permute-start.8
  42.3 3.0 %pairs_2.1 = (bf16[2,2,2,32,1024]{4,3,2,1,0:T(8,128)(2,1)S(1)}, bf16[2,2,2,32,1024]{4,3,2,1,0:T(8,128)(2,1)S(1)}) custom-call(s32[5]{0:T(128)S(1)} %stack.23.at_ref.place_ref, bf16[128,2048]{1,0:T(8,128)(2,1)S(1)} %collective-permute-done.5.refs_0_, bf16[128,2048]{1,0:T(8,128)(2,1)S(1)} %collective-permute-done.3.refs_1_, ...), custom_call_target="tpu_custom_call" | custom-call | flops 2147483648 | bytes 8388608 | tf_op jit(solution)/shard_map/pairs_2/pallas_call | solution.py:147
  45.3 2.5 %collective-permute-start.11 = (bf16[2,2,2,32,1024]{4,3,2,1,0:T(8,128)(2,1)S(1)}, bf16[2,2,2,32,1024]{4,3,2,1,0:T(8,128)(2,1)S(1)}, u32[]{:S(2)}, u32[]{:S(2)}) collective-permute-start(bf16[2,2,2,32,1024]{4,3,2,1,0:T(8,128)(2,1)S(1)} %get-tuple-element.71), channel_id=1, source_target_pairs={{0,2},{1,7},{2,0},{3,5},{4,6},{5,3},{6,4},{7,1},{8,10},{9,15},{10,... | collective-permute-start | bytes 1572872 | tf_op jit(solution)/shard_map/ppermute | solution.py:43
  47.8 0.5 collective-permute-start.12
  48.4 1.8 %collective-permute-done.8.refs_3_ = bf16[2,2,2,32,768]{4,3,2,1,0:T(8,128)(2,1)S(1)} collective-permute-done((bf16[2,2,2,32,768]{4,3,2,1,0:T(8,128)(2,1)S(1)}, bf16[2,2,2,32,768]{4,3,2,1,0:T(8,128)(2,1)S(1)}, u32[]{:S(2)}, u32[]{:S(2)}) %collective-permute-start.8) | collective-permute-done | bytes 393248 | tf_op jit(solution)/shard_map/ppermute | solution.py:43
  50.3 3.0 %pairs_3.1 = (bf16[2,2,2,32,1024]{4,3,2,1,0:T(8,128)(2,1)S(1)}, bf16[2,2,2,32,1024]{4,3,2,1,0:T(8,128)(2,1)S(1)}) custom-call(s32[5]{0:T(128)S(1)} %stack.23.at_ref.place_ref, bf16[128,2048]{1,0:T(8,128)(2,1)S(1)} %collective-permute-done.6.refs_0_, bf16[128,2048]{1,0:T(8,128)(2,1)S(1)} %collective-permute-done.9.refs_1_, ...), custom_call_target="tpu_custom_call" | custom-call | flops 2147483648 | bytes 8388608 | tf_op jit(solution)/shard_map/pairs_3/pallas_call | solution.py:147
  53.3 0.8 collective-permute-start.13
  54.1 1.6 %collective-permute-done.11.refs_1_ = bf16[2,2,2,32,1024]{4,3,2,1,0:T(8,128)(2,1)S(1)} collective-permute-done((bf16[2,2,2,32,1024]{4,3,2,1,0:T(8,128)(2,1)S(1)}, bf16[2,2,2,32,1024]{4,3,2,1,0:T(8,128)(2,1)S(1)}, u32[]{:S(2)}, u32[]{:S(2)}) %collective-permute-start.11) | collective-permute-done | bytes 524320 | tf_op jit(solution)/shard_map/ppermute | solution.py:43
  56.0 0.3 collective-permute-done.12.refs_1_
  56.3 1.9 %pairs_4.1 = (bf16[2,2,2,32,512]{4,3,2,1,0:T(8,128)(2,1)S(1)}, bf16[2,2,2,32,512]{4,3,2,1,0:T(8,128)(2,1)S(1)}) custom-call(s32[5]{0:T(128)S(1)} %stack.23.at_ref.place_ref, bf16[128,2048]{1,0:T(8,128)(2,1)S(1)} %collective-permute-done.10.refs_0_, bf16[128,2048]{1,0:T(8,128)(2,1)S(1)} %collective-permute-done.12.refs_1_, ...), custom_call_target="tpu_custom_call" | custom-call | flops 1073741824 | bytes 8388608 | tf_op jit(solution)/shard_map/pairs_4/pallas_call | solution.py:147
  58.1 2.5 %collective-permute-start.17 = (bf16[2,2,2,32,512]{4,3,2,1,0:T(8,128)(2,1)S(1)}, bf16[2,2,2,32,512]{4,3,2,1,0:T(8,128)(2,1)S(1)}, u32[]{:S(2)}, u32[]{:S(2)}) collective-permute-start(bf16[2,2,2,32,512]{4,3,2,1,0:T(8,128)(2,1)S(1)} %get-tuple-element.84), channel_id=1, source_target_pairs={{0,2},{1,7},{2,0},{3,5},{4,6},{5,3},{6,4},{7,1},{8,10},{9,15},{10,... | collective-permute-start | bytes 786440 | tf_op jit(solution)/shard_map/ppermute | solution.py:43
  60.6 7.2 %collective-permute-done.13.refs_1_ = bf16[2,2,2,32,1024]{4,3,2,1,0:T(8,128)(2,1)S(1)} collective-permute-done((bf16[2,2,2,32,1024]{4,3,2,1,0:T(8,128)(2,1)S(1)}, bf16[2,2,2,32,1024]{4,3,2,1,0:T(8,128)(2,1)S(1)}, u32[]{:S(2)}, u32[]{:S(2)}) %collective-permute-start.13) | collective-permute-done | bytes 524320 | tf_op jit(solution)/shard_map/ppermute | solution.py:43
  68.1 2.7 %collective-permute-done.15.refs_3_ = bf16[2,2,32,1024]{3,2,1,0:T(8,128)(2,1)S(1)} collective-permute-done((bf16[2,2,32,1024]{3,2,1,0:T(8,128)(2,1)S(1)}, bf16[2,2,32,1024]{3,2,1,0:T(8,128)(2,1)S(1)}, u32[]{:S(2)}, u32[]{:S(2)}) %collective-permute-start.15) | collective-permute-done | bytes 262176 | tf_op jit(solution)/shard_map/ppermute | solution.py:43
  70.8 0.6 sum_2.2
  71.5 3.0 %collective-permute-start.19 = (bf16[2,32,2560]{2,1,0:T(8,128)(2,1)S(1)}, bf16[2,32,2560]{2,1,0:T(8,128)(2,1)S(1)}, u32[]{:S(2)}, u32[]{:S(2)}) collective-permute-start(bf16[2,32,2560]{2,1,0:T(8,128)(2,1)S(1)} %get-tuple-element.89), channel_id=1, source_target_pairs={{0,8},{1,9},{2,10},{3,11},{4,12},{5,13},{6,14},{7,15},{8,0},{9,1},... | collective-permute-start | bytes 983048 | tf_op jit(solution)/shard_map/ppermute | solution.py:43
  74.7 4.1 %collective-permute-done.18.refs_3_ = bf16[2,2,32,512]{3,2,1,0:T(8,128)(2,1)S(1)} collective-permute-done((bf16[2,2,32,512]{3,2,1,0:T(8,128)(2,1)S(1)}, bf16[2,2,32,512]{3,2,1,0:T(8,128)(2,1)S(1)}, u32[]{:S(2)}, u32[]{:S(2)}) %collective-permute-start.18) | collective-permute-done | bytes 131104 | tf_op jit(solution)/shard_map/ppermute | solution.py:43
  78.8 0.6 sum_2.3
  79.4 1.7 %collective-permute-start.20 = (bf16[2,32,1536]{2,1,0:T(8,128)(2,1)S(1)}, bf16[2,32,1536]{2,1,0:T(8,128)(2,1)S(1)}, u32[]{:S(2)}, u32[]{:S(2)}) collective-permute-start(bf16[2,32,1536]{2,1,0:T(8,128)(2,1)S(1)} %get-tuple-element.92), channel_id=1, source_target_pairs={{0,8},{1,9},{2,10},{3,11},{4,12},{5,13},{6,14},{7,15},{8,0},{9,1},... | collective-permute-start | bytes 589832 | tf_op jit(solution)/shard_map/ppermute | solution.py:43
  81.2 4.3 %collective-permute-done.20.refs_1_ = bf16[2,32,1536]{2,1,0:T(8,128)(2,1)S(1)} collective-permute-done((bf16[2,32,1536]{2,1,0:T(8,128)(2,1)S(1)}, bf16[2,32,1536]{2,1,0:T(8,128)(2,1)S(1)}, u32[]{:S(2)}, u32[]{:S(2)}) %collective-permute-start.20) | collective-permute-done | bytes 196640 | tf_op jit(solution)/shard_map/ppermute | solution.py:43
  85.5 0.5 collective-permute-start.21
  86.1 3.8 %collective-permute-start.23 = (bf16[2,32,512]{2,1,0:T(8,128)(2,1)S(1)}, bf16[2,32,512]{2,1,0:T(8,128)(2,1)S(1)}, u32[]{:S(2)}, u32[]{:S(2)}) collective-permute-start(bf16[2,32,512]{2,1,0:T(8,128)(2,1)S(1)} %get-tuple-element.97), channel_id=1, source_target_pairs={{0,192},{1,65},{2,194},{3,67},{4,196},{5,69},{6,198},{7,71},{8,200... | collective-permute-start | bytes 196616 | tf_op jit(solution)/shard_map/ppermute | solution.py:43
  89.8 0.5 collective-permute-start.24
  90.4 0.9 collective-permute-done.23.refs_4_
  91.3 5.3 %collective-permute-done.24.refs_5_ = bf16[2,32,512]{2,1,0:T(8,128)(2,1)S(1)} collective-permute-done((bf16[2,32,512]{2,1,0:T(8,128)(2,1)S(1)}, bf16[2,32,512]{2,1,0:T(8,128)(2,1)S(1)}, u32[]{:S(2)}, u32[]{:S(2)}) %collective-permute-start.24) | collective-permute-done | bytes 65568 | tf_op jit(solution)/shard_map/ppermute | solution.py:43
  96.6 0.6 split.1
  97.2 7.6 %collective-permute-start.25 = (bf16[2,16,4096]{2,1,0:T(8,128)(2,1)S(1)}, bf16[2,16,4096]{2,1,0:T(8,128)(2,1)S(1)}, u32[]{:S(2)}, u32[]{:S(2)}) collective-permute-start(bf16[2,16,4096]{2,1,0:T(8,128)(2,1)S(1)} %split.1), channel_id=1, source_target_pairs={{0,1},{1,0},{2,3},{3,2},{4,5},{5,4},{6,7},{7,6},{8,9},{9,8},{10,11... | collective-permute-start | bytes 786440 | tf_op jit(solution)/shard_map/ppermute | solution.py:43
  104.8 1.2 %collective-permute-done.25.refs_6_ = bf16[2,16,4096]{2,1,0:T(8,128)(2,1)S(1)} collective-permute-done((bf16[2,16,4096]{2,1,0:T(8,128)(2,1)S(1)}, bf16[2,16,4096]{2,1,0:T(8,128)(2,1)S(1)}, u32[]{:S(2)}, u32[]{:S(2)}) %collective-permute-start.25) | collective-permute-done | bytes 262176 | tf_op jit(solution)/shard_map/ppermute | solution.py:43
  106.0 1.5 %finish.1 = f32[2,16,4096]{2,1,0:T(8,128)} custom-call(s32[5]{0:T(128)S(1)} %stack.23.at_ref.place_ref, bf16[2,32,1024]{2,1,0:T(8,128)(2,1)S(1)} %get-tuple-element.90.refs_0_, bf16[2,32,512]{2,1,0:T(8,128)(2,1)S(1)} %get-tuple-element.94.refs_1_, bf16[2,32,1024]{2,1,0:T(8,128)(2,1)S(1)} %collective-permute-done.21.refs_2_, ...), custom_call_target="tpu_custom_call" | custom-call | flops 1000 | bytes 1048576 | tf_op jit(solution)/shard_map/finish/pallas_call | solution.py:166
  (31 shorter events, 1.3 us)
Async XLA Ops:
  0.0 24.6 %copy-start.1 = (s32[512]{0:T(512)S(1)}, s32[512]{0:T(512)}, u32[]{:S(2)}) copy-start(s32[512]{0:T(512)} %param.3) | copy-start | bytes 6148
  0.1 1.2 %copy-start = (bf16[2,2,512,256]{3,2,1,0:T(8,128)(2,1)S(1)}, bf16[2,2,512,256]{3,2,1,0:T(8,128)(2,1)}, u32[]{:S(2)}) copy-start(bf16[2,2,512,256]{3,2,1,0:T(8,128)(2,1)} %x_ref.1) | copy-start | bytes 3145732
  1.9 12.6 %collective-permute-start.1 = (bf16[128,2048]{1,0:T(8,128)(2,1)S(1)}, bf16[128,2048]{1,0:T(8,128)(2,1)S(1)}, u32[]{:S(2)}, u32[]{:S(2)}) collective-permute-start(bf16[128,2048]{1,0:T(8,128)(2,1)S(1)} %whiten.2.a_ref.refs_2_), channel_id=1, source_target_pairs={{0,16},{1,17},{2,18},{3,19},{4,20},{5,21},{6,22},{7,23},{8,24},{9,... | collective-permute-start | bytes 1572872 | tf_op jit(solution)/shard_map/ppermute | solution.py:43
  4.1 11.7 %collective-permute-start = (bf16[128,2048]{1,0:T(8,128)(2,1)S(1)}, bf16[128,2048]{1,0:T(8,128)(2,1)S(1)}, u32[]{:S(2)}, u32[]{:S(2)}) collective-permute-start(bf16[128,2048]{1,0:T(8,128)(2,1)S(1)} %whiten.2.a_ref.refs_2_), channel_id=1, source_target_pairs={{0,32},{1,225},{2,34},{3,227},{4,36},{5,229},{6,38},{7,231},{8,40}... | collective-permute-start | bytes 1572872 | tf_op jit(solution)/shard_map/ppermute | solution.py:43
  10.3 11.1 %collective-permute-start.2 = (bf16[128,2048]{1,0:T(8,128)(2,1)S(1)}, bf16[128,2048]{1,0:T(8,128)(2,1)S(1)}, u32[]{:S(2)}, u32[]{:S(2)}) collective-permute-start(bf16[128,2048]{1,0:T(8,128)(2,1)S(1)} %whiten.3.b_ref.refs_3_), channel_id=1, source_target_pairs={{0,32},{1,225},{2,34},{3,227},{4,36},{5,229},{6,38},{7,231},{8,40}... | collective-permute-start | bytes 1572872 | tf_op jit(solution)/shard_map/ppermute | solution.py:43
  11.1 17.0 %collective-permute-start.4 = (bf16[128,2048]{1,0:T(8,128)(2,1)S(1)}, bf16[128,2048]{1,0:T(8,128)(2,1)S(1)}, u32[]{:S(2)}, u32[]{:S(2)}) collective-permute-start(bf16[128,2048]{1,0:T(8,128)(2,1)S(1)} %whiten.3.b_ref.refs_3_), channel_id=1, source_target_pairs={{0,16},{1,17},{2,18},{3,19},{4,20},{5,21},{6,22},{7,23},{8,24},{9,... | collective-permute-start | bytes 1572872 | tf_op jit(solution)/shard_map/ppermute | solution.py:43
  15.8 12.3 %collective-permute-start.5 = (bf16[128,2048]{1,0:T(8,128)(2,1)S(1)}, bf16[128,2048]{1,0:T(8,128)(2,1)S(1)}, u32[]{:S(2)}, u32[]{:S(2)}) collective-permute-start(bf16[128,2048]{1,0:T(8,128)(2,1)S(1)} %collective-permute-done.refs_0_), channel_id=1, source_target_pairs={{0,32},{1,225},{2,34},{3,227},{4,36},{5,229},{6,38},{7,231},{8,40}... | collective-permute-start | bytes 1572872 | tf_op jit(solution)/shard_map/ppermute | solution.py:43
  21.5 11.5 %collective-permute-start.3 = (bf16[128,2048]{1,0:T(8,128)(2,1)S(1)}, bf16[128,2048]{1,0:T(8,128)(2,1)S(1)}, u32[]{:S(2)}, u32[]{:S(2)}) collective-permute-start(bf16[128,2048]{1,0:T(8,128)(2,1)S(1)} %collective-permute-done.2.refs_1_), channel_id=1, source_target_pairs={{0,32},{1,225},{2,34},{3,227},{4,36},{5,229},{6,38},{7,231},{8,40}... | collective-permute-start | bytes 1572872 | tf_op jit(solution)/shard_map/ppermute | solution.py:43
  28.2 14.1 %collective-permute-start.6 = (bf16[128,2048]{1,0:T(8,128)(2,1)S(1)}, bf16[128,2048]{1,0:T(8,128)(2,1)S(1)}, u32[]{:S(2)}, u32[]{:S(2)}) collective-permute-start(bf16[128,2048]{1,0:T(8,128)(2,1)S(1)} %collective-permute-done.5.refs_0_), channel_id=1, source_target_pairs={{0,32},{1,225},{2,34},{3,227},{4,36},{5,229},{6,38},{7,231},{8,40}... | collective-permute-start | bytes 1572872 | tf_op jit(solution)/shard_map/ppermute | solution.py:43
  33.0 14.9 %collective-permute-start.9 = (bf16[128,2048]{1,0:T(8,128)(2,1)S(1)}, bf16[128,2048]{1,0:T(8,128)(2,1)S(1)}, u32[]{:S(2)}, u32[]{:S(2)}) collective-permute-start(bf16[128,2048]{1,0:T(8,128)(2,1)S(1)} %collective-permute-done.3.refs_1_), channel_id=1, source_target_pairs={{0,32},{1,225},{2,34},{3,227},{4,36},{5,229},{6,38},{7,231},{8,40}... | collective-permute-start | bytes 1572872 | tf_op jit(solution)/shard_map/ppermute | solution.py:43
  36.1 12.3 %collective-permute-start.7 = (bf16[2,2,2,32,768]{4,3,2,1,0:T(8,128)(2,1)S(1)}, bf16[2,2,2,32,768]{4,3,2,1,0:T(8,128)(2,1)S(1)}, u32[]{:S(2)}, u32[]{:S(2)}) collective-permute-start(bf16[2,2,2,32,768]{4,3,2,1,0:T(8,128)(2,1)S(1)} %get-tuple-element.65), channel_id=1, source_target_pairs={{0,2},{1,7},{2,0},{3,5},{4,6},{5,3},{6,4},{7,1},{8,10},{9,15},{10,... | collective-permute-start | bytes 1179656 | tf_op jit(solution)/shard_map/ppermute | solution.py:43
  42.0 8.2 %collective-permute-start.8 = (bf16[2,2,2,32,768]{4,3,2,1,0:T(8,128)(2,1)S(1)}, bf16[2,2,2,32,768]{4,3,2,1,0:T(8,128)(2,1)S(1)}, u32[]{:S(2)}, u32[]{:S(2)}) collective-permute-start(bf16[2,2,2,32,768]{4,3,2,1,0:T(8,128)(2,1)S(1)} %get-tuple-element.66), channel_id=1, source_target_pairs={{0,2},{1,7},{2,0},{3,5},{4,6},{5,3},{6,4},{7,1},{8,10},{9,15},{10,... | collective-permute-start | bytes 1179656 | tf_op jit(solution)/shard_map/ppermute | solution.py:43
  42.2 11.9 %collective-permute-start.10 = (bf16[128,2048]{1,0:T(8,128)(2,1)S(1)}, bf16[128,2048]{1,0:T(8,128)(2,1)S(1)}, u32[]{:S(2)}, u32[]{:S(2)}) collective-permute-start(bf16[128,2048]{1,0:T(8,128)(2,1)S(1)} %collective-permute-done.6.refs_0_), channel_id=1, source_target_pairs={{0,32},{1,225},{2,34},{3,227},{4,36},{5,229},{6,38},{7,231},{8,40}... | collective-permute-start | bytes 1572872 | tf_op jit(solution)/shard_map/ppermute | solution.py:43
  45.3 10.5 %collective-permute-start.11 = (bf16[2,2,2,32,1024]{4,3,2,1,0:T(8,128)(2,1)S(1)}, bf16[2,2,2,32,1024]{4,3,2,1,0:T(8,128)(2,1)S(1)}, u32[]{:S(2)}, u32[]{:S(2)}) collective-permute-start(bf16[2,2,2,32,1024]{4,3,2,1,0:T(8,128)(2,1)S(1)} %get-tuple-element.71), channel_id=1, source_target_pairs={{0,2},{1,7},{2,0},{3,5},{4,6},{5,3},{6,4},{7,1},{8,10},{9,15},{10,... | collective-permute-start | bytes 1572872 | tf_op jit(solution)/shard_map/ppermute | solution.py:43
  47.8 8.4 %collective-permute-start.12 = (bf16[128,2048]{1,0:T(8,128)(2,1)S(1)}, bf16[128,2048]{1,0:T(8,128)(2,1)S(1)}, u32[]{:S(2)}, u32[]{:S(2)}) collective-permute-start(bf16[128,2048]{1,0:T(8,128)(2,1)S(1)} %collective-permute-done.9.refs_1_), channel_id=1, source_target_pairs={{0,32},{1,225},{2,34},{3,227},{4,36},{5,229},{6,38},{7,231},{8,40}... | collective-permute-start | bytes 1572872 | tf_op jit(solution)/shard_map/ppermute | solution.py:43
  53.3 14.5 %collective-permute-start.13 = (bf16[2,2,2,32,1024]{4,3,2,1,0:T(8,128)(2,1)S(1)}, bf16[2,2,2,32,1024]{4,3,2,1,0:T(8,128)(2,1)S(1)}, u32[]{:S(2)}, u32[]{:S(2)}) collective-permute-start(bf16[2,2,2,32,1024]{4,3,2,1,0:T(8,128)(2,1)S(1)} %get-tuple-element.76), channel_id=1, source_target_pairs={{0,2},{1,7},{2,0},{3,5},{4,6},{5,3},{6,4},{7,1},{8,10},{9,15},{10,... | collective-permute-start | bytes 1572872 | tf_op jit(solution)/shard_map/ppermute | solution.py:43
  54.1 14.0 %collective-permute-start.14 = (bf16[2,2,32,1536]{3,2,1,0:T(8,128)(2,1)S(1)}, bf16[2,2,32,1536]{3,2,1,0:T(8,128)(2,1)S(1)}, u32[]{:S(2)}, u32[]{:S(2)}) collective-permute-start(bf16[2,2,32,1536]{3,2,1,0:T(8,128)(2,1)S(1)} %get-tuple-element.79), channel_id=1, source_target_pairs={{0,6},{1,3},{2,4},{3,1},{4,2},{5,7},{6,0},{7,5},{8,14},{9,11},{10,... | collective-permute-start | bytes 1179656 | tf_op jit(solution)/shard_map/ppermute | solution.py:43
  55.9 14.9 %collective-permute-start.15 = (bf16[2,2,32,1024]{3,2,1,0:T(8,128)(2,1)S(1)}, bf16[2,2,32,1024]{3,2,1,0:T(8,128)(2,1)S(1)}, u32[]{:S(2)}, u32[]{:S(2)}) collective-permute-start(bf16[2,2,32,1024]{3,2,1,0:T(8,128)(2,1)S(1)} %get-tuple-element.80), channel_id=1, source_target_pairs={{0,6},{1,3},{2,4},{3,1},{4,2},{5,7},{6,0},{7,5},{8,14},{9,11},{10,... | collective-permute-start | bytes 786440 | tf_op jit(solution)/shard_map/ppermute | solution.py:43
  58.1 16.4 %collective-permute-start.17 = (bf16[2,2,2,32,512]{4,3,2,1,0:T(8,128)(2,1)S(1)}, bf16[2,2,2,32,512]{4,3,2,1,0:T(8,128)(2,1)S(1)}, u32[]{:S(2)}, u32[]{:S(2)}) collective-permute-start(bf16[2,2,2,32,512]{4,3,2,1,0:T(8,128)(2,1)S(1)} %get-tuple-element.84), channel_id=1, source_target_pairs={{0,2},{1,7},{2,0},{3,5},{4,6},{5,3},{6,4},{7,1},{8,10},{9,15},{10,... | collective-permute-start | bytes 786440 | tf_op jit(solution)/shard_map/ppermute | solution.py:43
  68.0 6.7 %collective-permute-start.16 = (bf16[2,2,32,1024]{3,2,1,0:T(8,128)(2,1)S(1)}, bf16[2,2,32,1024]{3,2,1,0:T(8,128)(2,1)S(1)}, u32[]{:S(2)}, u32[]{:S(2)}) collective-permute-start(bf16[2,2,32,1024]{3,2,1,0:T(8,128)(2,1)S(1)} %get-tuple-element.82), channel_id=1, source_target_pairs={{0,6},{1,3},{2,4},{3,1},{4,2},{5,7},{6,0},{7,5},{8,14},{9,11},{10,... | collective-permute-start | bytes 786440 | tf_op jit(solution)/shard_map/ppermute | solution.py:43
  71.5 9.6 %collective-permute-start.19 = (bf16[2,32,2560]{2,1,0:T(8,128)(2,1)S(1)}, bf16[2,32,2560]{2,1,0:T(8,128)(2,1)S(1)}, u32[]{:S(2)}, u32[]{:S(2)}) collective-permute-start(bf16[2,32,2560]{2,1,0:T(8,128)(2,1)S(1)} %get-tuple-element.89), channel_id=1, source_target_pairs={{0,8},{1,9},{2,10},{3,11},{4,12},{5,13},{6,14},{7,15},{8,0},{9,1},... | collective-permute-start | bytes 983048 | tf_op jit(solution)/shard_map/ppermute | solution.py:43
  74.6 4.2 %collective-permute-start.18 = (bf16[2,2,32,512]{3,2,1,0:T(8,128)(2,1)S(1)}, bf16[2,2,32,512]{3,2,1,0:T(8,128)(2,1)S(1)}, u32[]{:S(2)}, u32[]{:S(2)}) collective-permute-start(bf16[2,2,32,512]{3,2,1,0:T(8,128)(2,1)S(1)} %get-tuple-element.86), channel_id=1, source_target_pairs={{0,6},{1,3},{2,4},{3,1},{4,2},{5,7},{6,0},{7,5},{8,14},{9,11},{10,... | collective-permute-start | bytes 393224 | tf_op jit(solution)/shard_map/ppermute | solution.py:43
  79.4 6.1 %collective-permute-start.20 = (bf16[2,32,1536]{2,1,0:T(8,128)(2,1)S(1)}, bf16[2,32,1536]{2,1,0:T(8,128)(2,1)S(1)}, u32[]{:S(2)}, u32[]{:S(2)}) collective-permute-start(bf16[2,32,1536]{2,1,0:T(8,128)(2,1)S(1)} %get-tuple-element.92), channel_id=1, source_target_pairs={{0,8},{1,9},{2,10},{3,11},{4,12},{5,13},{6,14},{7,15},{8,0},{9,1},... | collective-permute-start | bytes 589832 | tf_op jit(solution)/shard_map/ppermute | solution.py:43
  85.5 11.1 %collective-permute-start.21 = (bf16[2,32,1024]{2,1,0:T(8,128)(2,1)S(1)}, bf16[2,32,1024]{2,1,0:T(8,128)(2,1)S(1)}, u32[]{:S(2)}, u32[]{:S(2)}) collective-permute-start(bf16[2,32,1024]{2,1,0:T(8,128)(2,1)S(1)} %get-tuple-element.95), channel_id=1, source_target_pairs={{0,16},{1,17},{2,18},{3,19},{4,20},{5,21},{6,22},{7,23},{8,24},{9,... | collective-permute-start | bytes 393224 | tf_op jit(solution)/shard_map/ppermute | solution.py:43
  86.1 4.4 %collective-permute-start.22 = (bf16[2,32,512]{2,1,0:T(8,128)(2,1)S(1)}, bf16[2,32,512]{2,1,0:T(8,128)(2,1)S(1)}, u32[]{:S(2)}, u32[]{:S(2)}) collective-permute-start(bf16[2,32,512]{2,1,0:T(8,128)(2,1)S(1)} %get-tuple-element.96), channel_id=1, source_target_pairs={{0,224},{1,33},{2,226},{3,35},{4,228},{5,37},{6,230},{7,39},{8,232... | collective-permute-start | bytes 196616 | tf_op jit(solution)/shard_map/ppermute | solution.py:43
  86.1 5.2 %collective-permute-start.23 = (bf16[2,32,512]{2,1,0:T(8,128)(2,1)S(1)}, bf16[2,32,512]{2,1,0:T(8,128)(2,1)S(1)}, u32[]{:S(2)}, u32[]{:S(2)}) collective-permute-start(bf16[2,32,512]{2,1,0:T(8,128)(2,1)S(1)} %get-tuple-element.97), channel_id=1, source_target_pairs={{0,192},{1,65},{2,194},{3,67},{4,196},{5,69},{6,198},{7,71},{8,200... | collective-permute-start | bytes 196616 | tf_op jit(solution)/shard_map/ppermute | solution.py:43
  89.8 6.8 %collective-permute-start.24 = (bf16[2,32,512]{2,1,0:T(8,128)(2,1)S(1)}, bf16[2,32,512]{2,1,0:T(8,128)(2,1)S(1)}, u32[]{:S(2)}, u32[]{:S(2)}) collective-permute-start(bf16[2,32,512]{2,1,0:T(8,128)(2,1)S(1)} %get-tuple-element.98), channel_id=1, source_target_pairs={{0,160},{1,97},{2,162},{3,99},{4,164},{5,101},{6,166},{7,103},{8,1... | collective-permute-start | bytes 196616 | tf_op jit(solution)/shard_map/ppermute | solution.py:43
  97.2 8.8 %collective-permute-start.25 = (bf16[2,16,4096]{2,1,0:T(8,128)(2,1)S(1)}, bf16[2,16,4096]{2,1,0:T(8,128)(2,1)S(1)}, u32[]{:S(2)}, u32[]{:S(2)}) collective-permute-start(bf16[2,16,4096]{2,1,0:T(8,128)(2,1)S(1)} %split.1), channel_id=1, source_target_pairs={{0,1},{1,0},{2,3},{3,2},{4,5},{5,4},{6,7},{7,6},{8,9},{9,8},{10,11... | collective-permute-start | bytes 786440 | tf_op jit(solution)/shard_map/ppermute | solution.py:43

commit v5 on v4

--- a/solution.py
+++ b/solution.py
@@ -32,7 +32,7 @@
 
 
 def cost(flops, bytes_accessed):
-    return pl.CostEstimate(flops=flops, bytes_accessed=bytes_accessed, transcendentals=0)
+    return pl.CostEstimate(flops=flops // 10, bytes_accessed=bytes_accessed // 10, transcendentals=0)
 
 
 def move(x, step):
@@ -169,7 +169,7 @@
         out_specs=[whole] * len(shapes),
         out_shape=tuple(jax.ShapeDtypeStruct(s, t) for s, t in shapes),
         compiler_params=params(12),
-        cost_estimate=cost(1000, MIB),
+        cost_estimate=cost(1000, 80 * MIB),
         name=name,
     )(*lead, *arrays)
 
@@ -351,37 +351,37 @@
     recv_o = move(send_o, x_near)
     third = [move(b, chain_step) for b in (after(second[0], near[1], keep_o), second[1])]
     fourth = [move(b, chain_step) for b in third]
-    at = after(place, second[1], keep_o)
+    at = after(place, recv_o)
     near_rotated = [own_plus, near_plus, near_minus]
     keep_n, send_n = products(at, near_pairs, first + near + near_rotated, 3 * BLOCK, scale, "pairs_near")
     recv_n = move(send_n, x_near)
-    at = after(place, keep_n, third[0])
+    at = after(place, recv_n)
     keep_b, send_b = products(at, all_pairs, second + rotated, 4 * BLOCK, scale, "pairs_2")
     recv_b = move(send_b, x_near)
     picks = [(0, 0, 2 * BLOCK), (1, 0, BLOCK), (1, BLOCK, BLOCK), (0, 2 * BLOCK, BLOCK), (1, 2 * BLOCK, BLOCK)]
-    kept_a, send_a = sum_1([(after(keep_o, keep_b), recv_o), (keep_n, recv_n)], picks)
+    kept_a, send_a = sum_1([(after(keep_o, keep_b, third[0]), recv_o), (keep_n, recv_n)], picks)
     recv_a = move(send_a, x_far)
-    at = after(place, kept_a)
+    kept_b, send_b = sum_1([(after(keep_b, kept_a, third[1]), recv_b)], straight)
+    recv_b = move(send_b, x_far)
+    at = after(place, kept_b)
     keep_c, send_c = products(at, all_pairs, third + rotated, 4 * BLOCK, scale, "pairs_3")
     recv_c = move(send_c, x_near)
-    kept_b, send_b = sum_1([(after(keep_b, keep_c, fourth[0]), recv_b)], straight)
-    recv_b = move(send_b, x_far)
-    at = after(place, kept_b)
+    keep_ab, send_ab = sum_2(place, [(after(kept_a, keep_c), recv_a), (kept_b, recv_b)])
+    recv_ab = move(send_ab, yhi_step)
+    kept_c, send_c = sum_1([(after(keep_c, keep_ab, fourth[1]), recv_c)], straight)
+    recv_c = move(send_c, x_far)
+    at = after(place, kept_c)
     keep_d, send_d = products(at, last_pairs, fourth + [own_plus, near_plus], 2 * BLOCK, scale, "pairs_4")
     recv_d = move(send_d, x_near)
-    kept_c, send_c = sum_1([(after(keep_c, keep_d), recv_c)], straight)
-    recv_c = move(send_c, x_far)
-    keep_ab, send_ab = sum_2(place, [(after(kept_a, kept_c), recv_a), (kept_b, recv_b)])
-    recv_ab = move(send_ab, yhi_step)
-    kept_d, send_d = sum_1([(after(keep_d, keep_ab), recv_d)], [(0, 0, 2 * BLOCK)])
+    outputs = [[(0, 768), (1536, 256)], [(768, 256), (1792, 256)], [(1024, 512)], [(2048, 512)]]
+    own_ab, near_ab, ret_1, ret_2 = sum_y(after(keep_ab, keep_d), recv_ab, outputs)
+    ret_1, ret_2 = move(ret_1, back(1)), move(ret_2, back(2))
+    kept_d, send_d = sum_1([(after(keep_d, own_ab), recv_d)], [(0, 0, 2 * BLOCK)])
     recv_d = move(send_d, x_far)
-    keep_cd, send_cd = sum_2(place, [(kept_c, recv_c), (kept_d, recv_d)])
+    keep_cd, send_cd = sum_2(place, [(after(kept_c, kept_d), recv_c), (kept_d, recv_d)])
     recv_cd = move(send_cd, yhi_step)
-    outputs = [[(0, 768), (1536, 256)], [(768, 256), (1792, 256)], [(1024, 512)], [(2048, 512)]]
-    own_ab, near_ab, ret_1, ret_2 = sum_y(after(keep_ab, keep_cd), recv_ab, outputs)
-    ret_1, ret_2 = move(ret_1, back(1)), move(ret_2, back(2))
     outputs = [[(0, 256), (1024, 256)], [(256, 256), (1280, 256)], [(512, 512)]]
-    own_cd, near_all, ret_3 = sum_y(after(keep_cd, own_ab), recv_cd, outputs, near_ab)
+    own_cd, near_all, ret_3 = sum_y(after(keep_cd, ret_1, ret_2), recv_cd, outputs, near_ab)
     ret_3 = move(ret_3, back(3))
     near_all = move(near_all, y_step)
     arrays = [own_ab, own_cd, near_all, ret_1, ret_2, ret_3]

time: 108 us -> 116 us (1.074)
  waiting for transfers between devices: 34.8 us -> 47.2 us
  starting transfers between devices: 51.3 us -> 47.1 us
    ppermute x26, waiting for transfers between devices: 34.8 us -> 47.2 us  [move(): return lax.ppermute(x, AXES, pairs)]
    ppermute x26, starting transfers between devices: 51.3 us -> 47.1 us  [move(): return lax.ppermute(x, AXES, pairs)]
  transfers between devices with their start and end apart: 26 -> 26, of which waited for: 15 -> 17; matrix products, arithmetic and copies ran while one was open for 0% -> 0% of each run, Pallas kernels for 16% -> 14%
where the time goes in v5:
time: 116 us
  waiting for transfers between devices  47.2 us (41%)
  starting transfers between devices  47.1 us (41%)
  Pallas kernels  19.8 us (17%)
  local copies, waits for them, and re-layouts  1.31 us (1%)
    ppermute x26, waiting for transfers between devices, move(): return lax.ppermute(x, AXES, pairs)  47.2 us
    ppermute x26, starting transfers between devices, move(): return lax.ppermute(x, AXES, pairs)  47.1 us
    pallas_call x5, Pallas kernels, products(): pl.pallas_call(kernel, in_specs=[pl.BlockSpec(memory_space=pltpu.SMEM)] +...  12.7 us
    pallas_call x10, Pallas kernels, call(): pl.pallas_call(kernel, in_specs=[pl.BlockSpec(memory_space=pltpu.SMEM)] *...  3.93 us
  transfers between devices with their start and end apart: 26, of which 17 were waited for; matrix products, arithmetic and copies ran while one was open for 0% of the time, Pallas kernels for 14%

profile of v5, /device:TPU:1, one launch (start us, length us, event | category | flops | bytes accessed | tf_op | source)
XLA Modules:
  0.0 115.7 jit_solution(9777171189631429928)
XLA Ops:
  0.1 1.2 %copy-done = bf16[2,2,512,256]{3,2,1,0:T(8,128)(2,1)S(1)} copy-done((bf16[2,2,512,256]{3,2,1,0:T(8,128)(2,1)S(1)}, bf16[2,2,512,256]{3,2,1,0:T(8,128)(2,1)}, u32[]{:S(2)}) %copy-start) | copy-done | bytes 1048600
  1.3 0.6 whiten.2.a_ref.refs_2_
  1.9 2.2 %collective-permute-start.1 = (bf16[128,2048]{1,0:T(8,128)(2,1)S(1)}, bf16[128,2048]{1,0:T(8,128)(2,1)S(1)}, u32[]{:S(2)}, u32[]{:S(2)}) collective-permute-start(bf16[128,2048]{1,0:T(8,128)(2,1)S(1)} %whiten.2.a_ref.refs_2_), channel_id=1, source_target_pairs={{0,16},{1,17},{2,18},{3,19},{4,20},{5,21},{6,22},{7,23},{8,24},{9,... | collective-permute-start | bytes 1572872 | tf_op jit(solution)/shard_map/ppermute | solution.py:43
  4.1 5.6 %collective-permute-start = (bf16[128,2048]{1,0:T(8,128)(2,1)S(1)}, bf16[128,2048]{1,0:T(8,128)(2,1)S(1)}, u32[]{:S(2)}, u32[]{:S(2)}) collective-permute-start(bf16[128,2048]{1,0:T(8,128)(2,1)S(1)} %whiten.2.a_ref.refs_2_), channel_id=1, source_target_pairs={{0,32},{1,225},{2,34},{3,227},{4,36},{5,229},{6,38},{7,231},{8,40}... | collective-permute-start | bytes 1572872 | tf_op jit(solution)/shard_map/ppermute | solution.py:43
  9.7 0.6 whiten.3.b_ref.refs_3_
  10.3 0.8 collective-permute-start.2
  11.5 1.0 rotate.2
  12.5 2.1 %collective-permute-done.1.a_ref.refs_2_ = bf16[128,2048]{1,0:T(8,128)(2,1)S(1)} collective-permute-done((bf16[128,2048]{1,0:T(8,128)(2,1)S(1)}, bf16[128,2048]{1,0:T(8,128)(2,1)S(1)}, u32[]{:S(2)}, u32[]{:S(2)}) %collective-permute-start.1) | collective-permute-done | bytes 524320 | tf_op jit(solution)/shard_map/ppermute | solution.py:43
  14.5 1.3 %collective-permute-done.refs_0_ = bf16[128,2048]{1,0:T(8,128)(2,1)S(1)} collective-permute-done((bf16[128,2048]{1,0:T(8,128)(2,1)S(1)}, bf16[128,2048]{1,0:T(8,128)(2,1)S(1)}, u32[]{:S(2)}, u32[]{:S(2)}) %collective-permute-start) | collective-permute-done | bytes 524320 | tf_op jit(solution)/shard_map/ppermute | solution.py:43
  15.8 5.6 %collective-permute-done.2.refs_1_ = bf16[128,2048]{1,0:T(8,128)(2,1)S(1)} collective-permute-done((bf16[128,2048]{1,0:T(8,128)(2,1)S(1)}, bf16[128,2048]{1,0:T(8,128)(2,1)S(1)}, u32[]{:S(2)}, u32[]{:S(2)}) %collective-permute-start.2) | collective-permute-done | bytes 524320 | tf_op jit(solution)/shard_map/ppermute | solution.py:43
  21.5 2.4 %pairs_own.1 = (bf16[2,2,2,32,768]{4,3,2,1,0:T(8,128)(2,1)S(1)}, bf16[2,2,2,32,768]{4,3,2,1,0:T(8,128)(2,1)S(1)}) custom-call(s32[5]{0:T(128)S(1)} %stack.23.at_ref.place_ref, bf16[128,2048]{1,0:T(8,128)(2,1)S(1)} %collective-permute-done.refs_0_, bf16[128,2048]{1,0:T(8,128)(2,1)S(1)} %collective-permute-done.2.refs_1_, ...), custom_call_target="tpu_custom_call" | custom-call | flops 161061280 | bytes 838860 | tf_op jit(solution)/shard_map/pairs_own/pallas_call | solution.py:147
  23.9 2.6 %collective-permute-start.3 = (bf16[2,2,2,32,768]{4,3,2,1,0:T(8,128)(2,1)S(1)}, bf16[2,2,2,32,768]{4,3,2,1,0:T(8,128)(2,1)S(1)}, u32[]{:S(2)}, u32[]{:S(2)}) collective-permute-start(bf16[2,2,2,32,768]{4,3,2,1,0:T(8,128)(2,1)S(1)} %get-tuple-element.58), channel_id=1, source_target_pairs={{0,2},{1,7},{2,0},{3,5},{4,6},{5,3},{6,4},{7,1},{8,10},{9,15},{10,... | collective-permute-start | bytes 1179656 | tf_op jit(solution)/shard_map/ppermute | solution.py:43
  26.5 3.1 %collective-permute-start.6 = (bf16[128,2048]{1,0:T(8,128)(2,1)S(1)}, bf16[128,2048]{1,0:T(8,128)(2,1)S(1)}, u32[]{:S(2)}, u32[]{:S(2)}) collective-permute-start(bf16[128,2048]{1,0:T(8,128)(2,1)S(1)} %collective-permute-done.refs_0_), channel_id=1, source_target_pairs={{0,32},{1,225},{2,34},{3,227},{4,36},{5,229},{6,38},{7,231},{8,40}... | collective-permute-start | bytes 1572872 | tf_op jit(solution)/shard_map/ppermute | solution.py:43
  29.6 1.0 rotate.3
  30.6 1.2 %collective-permute-done.3.refs_1_ = bf16[2,2,2,32,768]{4,3,2,1,0:T(8,128)(2,1)S(1)} collective-permute-done((bf16[2,2,2,32,768]{4,3,2,1,0:T(8,128)(2,1)S(1)}, bf16[2,2,2,32,768]{4,3,2,1,0:T(8,128)(2,1)S(1)}, u32[]{:S(2)}, u32[]{:S(2)}) %collective-permute-start.3) | collective-permute-done | bytes 393248 | tf_op jit(solution)/shard_map/ppermute | solution.py:43
  31.8 2.4 %pairs_near.1 = (bf16[2,2,2,32,768]{4,3,2,1,0:T(8,128)(2,1)S(1)}, bf16[2,2,2,32,768]{4,3,2,1,0:T(8,128)(2,1)S(1)}) custom-call(s32[5]{0:T(128)S(1)} %stack.23.at_ref.place_ref, bf16[128,2048]{1,0:T(8,128)(2,1)S(1)} %collective-permute-done.refs_0_, bf16[128,2048]{1,0:T(8,128)(2,1)S(1)} %collective-permute-done.2.refs_1_, ...), custom_call_target="tpu_custom_call" | custom-call | flops 161061280 | bytes 838860 | tf_op jit(solution)/shard_map/pairs_near/pallas_call | solution.py:147
  34.2 2.9 %collective-permute-start.5 = (bf16[2,2,2,32,768]{4,3,2,1,0:T(8,128)(2,1)S(1)}, bf16[2,2,2,32,768]{4,3,2,1,0:T(8,128)(2,1)S(1)}, u32[]{:S(2)}, u32[]{:S(2)}) collective-permute-start(bf16[2,2,2,32,768]{4,3,2,1,0:T(8,128)(2,1)S(1)} %get-tuple-element.62), channel_id=1, source_target_pairs={{0,2},{1,7},{2,0},{3,5},{4,6},{5,3},{6,4},{7,1},{8,10},{9,15},{10,... | collective-permute-start | bytes 1179656 | tf_op jit(solution)/shard_map/ppermute | solution.py:43
  37.1 2.8 %collective-permute-start.8 = (bf16[128,2048]{1,0:T(8,128)(2,1)S(1)}, bf16[128,2048]{1,0:T(8,128)(2,1)S(1)}, u32[]{:S(2)}, u32[]{:S(2)}) collective-permute-start(bf16[128,2048]{1,0:T(8,128)(2,1)S(1)} %collective-permute-done.6.refs_0_), channel_id=1, source_target_pairs={{0,32},{1,225},{2,34},{3,227},{4,36},{5,229},{6,38},{7,231},{8,40}... | collective-permute-start | bytes 1572872 | tf_op jit(solution)/shard_map/ppermute | solution.py:43
  39.9 1.4 %collective-permute-done.7.refs_1_ = bf16[128,2048]{1,0:T(8,128)(2,1)S(1)} collective-permute-done((bf16[128,2048]{1,0:T(8,128)(2,1)S(1)}, bf16[128,2048]{1,0:T(8,128)(2,1)S(1)}, u32[]{:S(2)}, u32[]{:S(2)}) %collective-permute-start.7) | collective-permute-done | bytes 524320 | tf_op jit(solution)/shard_map/ppermute | solution.py:43
  41.3 3.1 %collective-permute-start.9 = (bf16[128,2048]{1,0:T(8,128)(2,1)S(1)}, bf16[128,2048]{1,0:T(8,128)(2,1)S(1)}, u32[]{:S(2)}, u32[]{:S(2)}) collective-permute-start(bf16[128,2048]{1,0:T(8,128)(2,1)S(1)} %collective-permute-done.7.refs_1_), channel_id=1, source_target_pairs={{0,32},{1,225},{2,34},{3,227},{4,36},{5,229},{6,38},{7,231},{8,40}... | collective-permute-start | bytes 1572872 | tf_op jit(solution)/shard_map/ppermute | solution.py:43
  44.4 3.0 %pairs_2.1 = (bf16[2,2,2,32,1024]{4,3,2,1,0:T(8,128)(2,1)S(1)}, bf16[2,2,2,32,1024]{4,3,2,1,0:T(8,128)(2,1)S(1)}) custom-call(s32[5]{0:T(128)S(1)} %stack.23.at_ref.place_ref, bf16[128,2048]{1,0:T(8,128)(2,1)S(1)} %collective-permute-done.6.refs_0_, bf16[128,2048]{1,0:T(8,128)(2,1)S(1)} %collective-permute-done.7.refs_1_, ...), custom_call_target="tpu_custom_call" | custom-call | flops 214748368 | bytes 838860 | tf_op jit(solution)/shard_map/pairs_2/pallas_call | solution.py:147
  47.4 0.9 collective-permute-start.10
  48.5 4.0 %collective-permute-done.9.refs_1_ = bf16[128,2048]{1,0:T(8,128)(2,1)S(1)} collective-permute-done((bf16[128,2048]{1,0:T(8,128)(2,1)S(1)}, bf16[128,2048]{1,0:T(8,128)(2,1)S(1)}, u32[]{:S(2)}, u32[]{:S(2)}) %collective-permute-start.9) | collective-permute-done | bytes 524320 | tf_op jit(solution)/shard_map/ppermute | solution.py:43
  52.5 3.1 %collective-permute-start.13 = (bf16[128,2048]{1,0:T(8,128)(2,1)S(1)}, bf16[128,2048]{1,0:T(8,128)(2,1)S(1)}, u32[]{:S(2)}, u32[]{:S(2)}) collective-permute-start(bf16[128,2048]{1,0:T(8,128)(2,1)S(1)} %collective-permute-done.9.refs_1_), channel_id=1, source_target_pairs={{0,32},{1,225},{2,34},{3,227},{4,36},{5,229},{6,38},{7,231},{8,40}... | collective-permute-start | bytes 1572872 | tf_op jit(solution)/shard_map/ppermute | solution.py:43
  55.7 1.1 collective-permute-done.10.refs_1_
  56.9 3.0 %pairs_3.1 = (bf16[2,2,2,32,1024]{4,3,2,1,0:T(8,128)(2,1)S(1)}, bf16[2,2,2,32,1024]{4,3,2,1,0:T(8,128)(2,1)S(1)}) custom-call(s32[5]{0:T(128)S(1)} %stack.23.at_ref.place_ref, bf16[128,2048]{1,0:T(8,128)(2,1)S(1)} %collective-permute-done.8.refs_0_, bf16[128,2048]{1,0:T(8,128)(2,1)S(1)} %collective-permute-done.9.refs_1_, ...), custom_call_target="tpu_custom_call" | custom-call | flops 214748368 | bytes 838860 | tf_op jit(solution)/shard_map/pairs_3/pallas_call | solution.py:147
  59.9 0.9 collective-permute-start.14
  60.8 2.5 %collective-permute-start.15 = (bf16[128,2048]{1,0:T(8,128)(2,1)S(1)}, bf16[128,2048]{1,0:T(8,128)(2,1)S(1)}, u32[]{:S(2)}, u32[]{:S(2)}) collective-permute-start(bf16[128,2048]{1,0:T(8,128)(2,1)S(1)} %collective-permute-done.8.refs_0_), channel_id=1, source_target_pairs={{0,32},{1,225},{2,34},{3,227},{4,36},{5,229},{6,38},{7,231},{8,40}... | collective-permute-start | bytes 1572872 | tf_op jit(solution)/shard_map/ppermute | solution.py:43
  63.3 1.5 %collective-permute-start.12 = (bf16[2,2,32,1024]{3,2,1,0:T(8,128)(2,1)S(1)}, bf16[2,2,32,1024]{3,2,1,0:T(8,128)(2,1)S(1)}, u32[]{:S(2)}, u32[]{:S(2)}) collective-permute-start(bf16[2,2,32,1024]{3,2,1,0:T(8,128)(2,1)S(1)} %get-tuple-element.76), channel_id=1, source_target_pairs={{0,6},{1,3},{2,4},{3,1},{4,2},{5,7},{6,0},{7,5},{8,14},{9,11},{10,... | collective-permute-start | bytes 786440 | tf_op jit(solution)/shard_map/ppermute | solution.py:43
  64.8 8.0 %collective-permute-done.11.refs_1_ = bf16[2,2,32,1536]{3,2,1,0:T(8,128)(2,1)S(1)} collective-permute-done((bf16[2,2,32,1536]{3,2,1,0:T(8,128)(2,1)S(1)}, bf16[2,2,32,1536]{3,2,1,0:T(8,128)(2,1)S(1)}, u32[]{:S(2)}, u32[]{:S(2)}) %collective-permute-start.11) | collective-permute-done | bytes 393248 | tf_op jit(solution)/shard_map/ppermute | solution.py:43
  72.8 2.8 %collective-permute-done.12.refs_3_ = bf16[2,2,32,1024]{3,2,1,0:T(8,128)(2,1)S(1)} collective-permute-done((bf16[2,2,32,1024]{3,2,1,0:T(8,128)(2,1)S(1)}, bf16[2,2,32,1024]{3,2,1,0:T(8,128)(2,1)S(1)}, u32[]{:S(2)}, u32[]{:S(2)}) %collective-permute-start.12) | collective-permute-done | bytes 262176 | tf_op jit(solution)/shard_map/ppermute | solution.py:43
  75.6 0.7 sum_2.2
  76.3 2.7 %collective-permute-start.16 = (bf16[2,32,2560]{2,1,0:T(8,128)(2,1)S(1)}, bf16[2,32,2560]{2,1,0:T(8,128)(2,1)S(1)}, u32[]{:S(2)}, u32[]{:S(2)}) collective-permute-start(bf16[2,32,2560]{2,1,0:T(8,128)(2,1)S(1)} %get-tuple-element.84), channel_id=1, source_target_pairs={{0,8},{1,9},{2,10},{3,11},{4,12},{5,13},{6,14},{7,15},{8,0},{9,1},... | collective-permute-start | bytes 983048 | tf_op jit(solution)/shard_map/ppermute | solution.py:43
  79.1 1.9 %pairs_4.1 = (bf16[2,2,2,32,512]{4,3,2,1,0:T(8,128)(2,1)S(1)}, bf16[2,2,2,32,512]{4,3,2,1,0:T(8,128)(2,1)S(1)}) custom-call(s32[5]{0:T(128)S(1)} %stack.23.at_ref.place_ref, bf16[128,2048]{1,0:T(8,128)(2,1)S(1)} %collective-permute-done.15.refs_0_, bf16[128,2048]{1,0:T(8,128)(2,1)S(1)} %collective-permute-done.13.refs_1_, ...), custom_call_target="tpu_custom_call" | custom-call | flops 107374184 | bytes 838860 | tf_op jit(solution)/shard_map/pairs_4/pallas_call | solution.py:147
  81.0 2.3 %collective-permute-start.17 = (bf16[2,2,2,32,512]{4,3,2,1,0:T(8,128)(2,1)S(1)}, bf16[2,2,2,32,512]{4,3,2,1,0:T(8,128)(2,1)S(1)}, u32[]{:S(2)}, u32[]{:S(2)}) collective-permute-start(bf16[2,2,2,32,512]{4,3,2,1,0:T(8,128)(2,1)S(1)} %get-tuple-element.87), channel_id=1, source_target_pairs={{0,2},{1,7},{2,0},{3,5},{4,6},{5,3},{6,4},{7,1},{8,10},{9,15},{10,... | collective-permute-start | bytes 786440 | tf_op jit(solution)/shard_map/ppermute | solution.py:43
  83.3 2.5 %collective-permute-done.16.refs_1_ = bf16[2,32,2560]{2,1,0:T(8,128)(2,1)S(1)} collective-permute-done((bf16[2,32,2560]{2,1,0:T(8,128)(2,1)S(1)}, bf16[2,32,2560]{2,1,0:T(8,128)(2,1)S(1)}, u32[]{:S(2)}, u32[]{:S(2)}) %collective-permute-start.16) | collective-permute-done | bytes 327712 | tf_op jit(solution)/shard_map/ppermute | solution.py:43
  85.8 2.9 %collective-permute-done.17.refs_1_ = bf16[2,2,2,32,512]{4,3,2,1,0:T(8,128)(2,1)S(1)} collective-permute-done((bf16[2,2,2,32,512]{4,3,2,1,0:T(8,128)(2,1)S(1)}, bf16[2,2,2,32,512]{4,3,2,1,0:T(8,128)(2,1)S(1)}, u32[]{:S(2)}, u32[]{:S(2)}) %collective-permute-start.17) | collective-permute-done | bytes 262176 | tf_op jit(solution)/shard_map/ppermute | solution.py:43
  88.8 2.5 %collective-permute-done.18.refs_1_ = bf16[2,2,32,1024]{3,2,1,0:T(8,128)(2,1)S(1)} collective-permute-done((bf16[2,2,32,1024]{3,2,1,0:T(8,128)(2,1)S(1)}, bf16[2,2,32,1024]{3,2,1,0:T(8,128)(2,1)S(1)}, u32[]{:S(2)}, u32[]{:S(2)}) %collective-permute-start.18) | collective-permute-done | bytes 262176 | tf_op jit(solution)/shard_map/ppermute | solution.py:43
  91.3 1.3 %collective-permute-done.19.refs_3_ = bf16[2,2,32,512]{3,2,1,0:T(8,128)(2,1)S(1)} collective-permute-done((bf16[2,2,32,512]{3,2,1,0:T(8,128)(2,1)S(1)}, bf16[2,2,32,512]{3,2,1,0:T(8,128)(2,1)S(1)}, u32[]{:S(2)}, u32[]{:S(2)}) %collective-permute-start.19) | collective-permute-done | bytes 131104 | tf_op jit(solution)/shard_map/ppermute | solution.py:43
  92.6 0.6 sum_2.3
  93.7 1.1 collective-permute-start.21
  94.7 3.7 %collective-permute-done.20.refs_3_ = bf16[2,32,512]{2,1,0:T(8,128)(2,1)S(1)} collective-permute-done((bf16[2,32,512]{2,1,0:T(8,128)(2,1)S(1)}, bf16[2,32,512]{2,1,0:T(8,128)(2,1)S(1)}, u32[]{:S(2)}, u32[]{:S(2)}) %collective-permute-start.20) | collective-permute-done | bytes 65568 | tf_op jit(solution)/shard_map/ppermute | solution.py:43
  98.5 2.6 %collective-permute-done.21.refs_4_ = bf16[2,32,512]{2,1,0:T(8,128)(2,1)S(1)} collective-permute-done((bf16[2,32,512]{2,1,0:T(8,128)(2,1)S(1)}, bf16[2,32,512]{2,1,0:T(8,128)(2,1)S(1)}, u32[]{:S(2)}, u32[]{:S(2)}) %collective-permute-start.21) | collective-permute-done | bytes 65568 | tf_op jit(solution)/shard_map/ppermute | solution.py:43
  101.4 3.3 %collective-permute-start.24 = (bf16[2,32,512]{2,1,0:T(8,128)(2,1)S(1)}, bf16[2,32,512]{2,1,0:T(8,128)(2,1)S(1)}, u32[]{:S(2)}, u32[]{:S(2)}) collective-permute-start(bf16[2,32,512]{2,1,0:T(8,128)(2,1)S(1)} %get-tuple-element.100), channel_id=1, source_target_pairs={{0,160},{1,97},{2,162},{3,99},{4,164},{5,101},{6,166},{7,103},{8,1... | collective-permute-start | bytes 196616 | tf_op jit(solution)/shard_map/ppermute | solution.py:43
  104.7 3.0 %collective-permute-done.24.refs_5_ = bf16[2,32,512]{2,1,0:T(8,128)(2,1)S(1)} collective-permute-done((bf16[2,32,512]{2,1,0:T(8,128)(2,1)S(1)}, bf16[2,32,512]{2,1,0:T(8,128)(2,1)S(1)}, u32[]{:S(2)}, u32[]{:S(2)}) %collective-permute-start.24) | collective-permute-done | bytes 65568 | tf_op jit(solution)/shard_map/ppermute | solution.py:43
  108.2 4.8 %collective-permute-start.25 = (bf16[2,16,4096]{2,1,0:T(8,128)(2,1)S(1)}, bf16[2,16,4096]{2,1,0:T(8,128)(2,1)S(1)}, u32[]{:S(2)}, u32[]{:S(2)}) collective-permute-start(bf16[2,16,4096]{2,1,0:T(8,128)(2,1)S(1)} %split.1), channel_id=1, source_target_pairs={{0,1},{1,0},{2,3},{3,2},{4,5},{5,4},{6,7},{7,6},{8,9},{9,8},{10,11... | collective-permute-start | bytes 786440 | tf_op jit(solution)/shard_map/ppermute | solution.py:43
  113.0 1.2 %collective-permute-done.25.refs_6_ = bf16[2,16,4096]{2,1,0:T(8,128)(2,1)S(1)} collective-permute-done((bf16[2,16,4096]{2,1,0:T(8,128)(2,1)S(1)}, bf16[2,16,4096]{2,1,0:T(8,128)(2,1)S(1)}, u32[]{:S(2)}, u32[]{:S(2)}) %collective-permute-start.25) | collective-permute-done | bytes 262176 | tf_op jit(solution)/shard_map/ppermute | solution.py:43
  114.2 1.5 %finish.1 = f32[2,16,4096]{2,1,0:T(8,128)} custom-call(s32[5]{0:T(128)S(1)} %stack.23.at_ref.place_ref, bf16[2,32,1024]{2,1,0:T(8,128)(2,1)S(1)} %get-tuple-element.85.refs_0_, bf16[2,32,512]{2,1,0:T(8,128)(2,1)S(1)} %get-tuple-element.98.refs_1_, bf16[2,32,1024]{2,1,0:T(8,128)(2,1)S(1)} %collective-permute-done.23.refs_2_, ...), custom_call_target="tpu_custom_call" | custom-call | flops 100 | bytes 8388608 | tf_op jit(solution)/shard_map/finish/pallas_call | solution.py:166
  (31 shorter events, 2.4 us)
Async XLA Ops:
  0.0 11.3 %copy-start.1 = (s32[512]{0:T(512)S(1)}, s32[512]{0:T(512)}, u32[]{:S(2)}) copy-start(s32[512]{0:T(512)} %param.3) | copy-start | bytes 6148
  0.1 1.2 %copy-start = (bf16[2,2,512,256]{3,2,1,0:T(8,128)(2,1)S(1)}, bf16[2,2,512,256]{3,2,1,0:T(8,128)(2,1)}, u32[]{:S(2)}) copy-start(bf16[2,2,512,256]{3,2,1,0:T(8,128)(2,1)} %x_ref.1) | copy-start | bytes 3145732
  1.9 12.6 %collective-permute-start.1 = (bf16[128,2048]{1,0:T(8,128)(2,1)S(1)}, bf16[128,2048]{1,0:T(8,128)(2,1)S(1)}, u32[]{:S(2)}, u32[]{:S(2)}) collective-permute-start(bf16[128,2048]{1,0:T(8,128)(2,1)S(1)} %whiten.2.a_ref.refs_2_), channel_id=1, source_target_pairs={{0,16},{1,17},{2,18},{3,19},{4,20},{5,21},{6,22},{7,23},{8,24},{9,... | collective-permute-start | bytes 1572872 | tf_op jit(solution)/shard_map/ppermute | solution.py:43
  4.1 11.7 %collective-permute-start = (bf16[128,2048]{1,0:T(8,128)(2,1)S(1)}, bf16[128,2048]{1,0:T(8,128)(2,1)S(1)}, u32[]{:S(2)}, u32[]{:S(2)}) collective-permute-start(bf16[128,2048]{1,0:T(8,128)(2,1)S(1)} %whiten.2.a_ref.refs_2_), channel_id=1, source_target_pairs={{0,32},{1,225},{2,34},{3,227},{4,36},{5,229},{6,38},{7,231},{8,40}... | collective-permute-start | bytes 1572872 | tf_op jit(solution)/shard_map/ppermute | solution.py:43
  10.3 11.1 %collective-permute-start.2 = (bf16[128,2048]{1,0:T(8,128)(2,1)S(1)}, bf16[128,2048]{1,0:T(8,128)(2,1)S(1)}, u32[]{:S(2)}, u32[]{:S(2)}) collective-permute-start(bf16[128,2048]{1,0:T(8,128)(2,1)S(1)} %whiten.3.b_ref.refs_3_), channel_id=1, source_target_pairs={{0,32},{1,225},{2,34},{3,227},{4,36},{5,229},{6,38},{7,231},{8,40}... | collective-permute-start | bytes 1572872 | tf_op jit(solution)/shard_map/ppermute | solution.py:43
  11.1 18.5 %collective-permute-start.4 = (bf16[128,2048]{1,0:T(8,128)(2,1)S(1)}, bf16[128,2048]{1,0:T(8,128)(2,1)S(1)}, u32[]{:S(2)}, u32[]{:S(2)}) collective-permute-start(bf16[128,2048]{1,0:T(8,128)(2,1)S(1)} %whiten.3.b_ref.refs_3_), channel_id=1, source_target_pairs={{0,16},{1,17},{2,18},{3,19},{4,20},{5,21},{6,22},{7,23},{8,24},{9,... | collective-permute-start | bytes 1572872 | tf_op jit(solution)/shard_map/ppermute | solution.py:43
  23.9 7.9 %collective-permute-start.3 = (bf16[2,2,2,32,768]{4,3,2,1,0:T(8,128)(2,1)S(1)}, bf16[2,2,2,32,768]{4,3,2,1,0:T(8,128)(2,1)S(1)}, u32[]{:S(2)}, u32[]{:S(2)}) collective-permute-start(bf16[2,2,2,32,768]{4,3,2,1,0:T(8,128)(2,1)S(1)} %get-tuple-element.58), channel_id=1, source_target_pairs={{0,2},{1,7},{2,0},{3,5},{4,6},{5,3},{6,4},{7,1},{8,10},{9,15},{10,... | collective-permute-start | bytes 1179656 | tf_op jit(solution)/shard_map/ppermute | solution.py:43
  26.5 10.7 %collective-permute-start.6 = (bf16[128,2048]{1,0:T(8,128)(2,1)S(1)}, bf16[128,2048]{1,0:T(8,128)(2,1)S(1)}, u32[]{:S(2)}, u32[]{:S(2)}) collective-permute-start(bf16[128,2048]{1,0:T(8,128)(2,1)S(1)} %collective-permute-done.refs_0_), channel_id=1, source_target_pairs={{0,32},{1,225},{2,34},{3,227},{4,36},{5,229},{6,38},{7,231},{8,40}... | collective-permute-start | bytes 1572872 | tf_op jit(solution)/shard_map/ppermute | solution.py:43
  29.6 11.7 %collective-permute-start.7 = (bf16[128,2048]{1,0:T(8,128)(2,1)S(1)}, bf16[128,2048]{1,0:T(8,128)(2,1)S(1)}, u32[]{:S(2)}, u32[]{:S(2)}) collective-permute-start(bf16[128,2048]{1,0:T(8,128)(2,1)S(1)} %collective-permute-done.2.refs_1_), channel_id=1, source_target_pairs={{0,32},{1,225},{2,34},{3,227},{4,36},{5,229},{6,38},{7,231},{8,40}... | collective-permute-start | bytes 1572872 | tf_op jit(solution)/shard_map/ppermute | solution.py:43
  34.2 10.2 %collective-permute-start.5 = (bf16[2,2,2,32,768]{4,3,2,1,0:T(8,128)(2,1)S(1)}, bf16[2,2,2,32,768]{4,3,2,1,0:T(8,128)(2,1)S(1)}, u32[]{:S(2)}, u32[]{:S(2)}) collective-permute-start(bf16[2,2,2,32,768]{4,3,2,1,0:T(8,128)(2,1)S(1)} %get-tuple-element.62), channel_id=1, source_target_pairs={{0,2},{1,7},{2,0},{3,5},{4,6},{5,3},{6,4},{7,1},{8,10},{9,15},{10,... | collective-permute-start | bytes 1179656 | tf_op jit(solution)/shard_map/ppermute | solution.py:43
  37.1 11.2 %collective-permute-start.8 = (bf16[128,2048]{1,0:T(8,128)(2,1)S(1)}, bf16[128,2048]{1,0:T(8,128)(2,1)S(1)}, u32[]{:S(2)}, u32[]{:S(2)}) collective-permute-start(bf16[128,2048]{1,0:T(8,128)(2,1)S(1)} %collective-permute-done.6.refs_0_), channel_id=1, source_target_pairs={{0,32},{1,225},{2,34},{3,227},{4,36},{5,229},{6,38},{7,231},{8,40}... | collective-permute-start | bytes 1572872 | tf_op jit(solution)/shard_map/ppermute | solution.py:43
  41.3 11.2 %collective-permute-start.9 = (bf16[128,2048]{1,0:T(8,128)(2,1)S(1)}, bf16[128,2048]{1,0:T(8,128)(2,1)S(1)}, u32[]{:S(2)}, u32[]{:S(2)}) collective-permute-start(bf16[128,2048]{1,0:T(8,128)(2,1)S(1)} %collective-permute-done.7.refs_1_), channel_id=1, source_target_pairs={{0,32},{1,225},{2,34},{3,227},{4,36},{5,229},{6,38},{7,231},{8,40}... | collective-permute-start | bytes 1572872 | tf_op jit(solution)/shard_map/ppermute | solution.py:43
  47.4 9.3 %collective-permute-start.10 = (bf16[2,2,2,32,1024]{4,3,2,1,0:T(8,128)(2,1)S(1)}, bf16[2,2,2,32,1024]{4,3,2,1,0:T(8,128)(2,1)S(1)}, u32[]{:S(2)}, u32[]{:S(2)}) collective-permute-start(bf16[2,2,2,32,1024]{4,3,2,1,0:T(8,128)(2,1)S(1)} %get-tuple-element.70), channel_id=1, source_target_pairs={{0,2},{1,7},{2,0},{3,5},{4,6},{5,3},{6,4},{7,1},{8,10},{9,15},{10,... | collective-permute-start | bytes 1572872 | tf_op jit(solution)/shard_map/ppermute | solution.py:43
  52.5 26.4 %collective-permute-start.13 = (bf16[128,2048]{1,0:T(8,128)(2,1)S(1)}, bf16[128,2048]{1,0:T(8,128)(2,1)S(1)}, u32[]{:S(2)}, u32[]{:S(2)}) collective-permute-start(bf16[128,2048]{1,0:T(8,128)(2,1)S(1)} %collective-permute-done.9.refs_1_), channel_id=1, source_target_pairs={{0,32},{1,225},{2,34},{3,227},{4,36},{5,229},{6,38},{7,231},{8,40}... | collective-permute-start | bytes 1572872 | tf_op jit(solution)/shard_map/ppermute | solution.py:43
  59.9 19.1 %collective-permute-start.14 = (bf16[2,2,2,32,1024]{4,3,2,1,0:T(8,128)(2,1)S(1)}, bf16[2,2,2,32,1024]{4,3,2,1,0:T(8,128)(2,1)S(1)}, u32[]{:S(2)}, u32[]{:S(2)}) collective-permute-start(bf16[2,2,2,32,1024]{4,3,2,1,0:T(8,128)(2,1)S(1)} %get-tuple-element.79), channel_id=1, source_target_pairs={{0,2},{1,7},{2,0},{3,5},{4,6},{5,3},{6,4},{7,1},{8,10},{9,15},{10,... | collective-permute-start | bytes 1572872 | tf_op jit(solution)/shard_map/ppermute | solution.py:43
  60.8 18.3 %collective-permute-start.15 = (bf16[128,2048]{1,0:T(8,128)(2,1)S(1)}, bf16[128,2048]{1,0:T(8,128)(2,1)S(1)}, u32[]{:S(2)}, u32[]{:S(2)}) collective-permute-start(bf16[128,2048]{1,0:T(8,128)(2,1)S(1)} %collective-permute-done.8.refs_0_), channel_id=1, source_target_pairs={{0,32},{1,225},{2,34},{3,227},{4,36},{5,229},{6,38},{7,231},{8,40}... | collective-permute-start | bytes 1572872 | tf_op jit(solution)/shard_map/ppermute | solution.py:43
  63.3 9.5 %collective-permute-start.11 = (bf16[2,2,32,1536]{3,2,1,0:T(8,128)(2,1)S(1)}, bf16[2,2,32,1536]{3,2,1,0:T(8,128)(2,1)S(1)}, u32[]{:S(2)}, u32[]{:S(2)}) collective-permute-start(bf16[2,2,32,1536]{3,2,1,0:T(8,128)(2,1)S(1)} %get-tuple-element.75), channel_id=1, source_target_pairs={{0,6},{1,3},{2,4},{3,1},{4,2},{5,7},{6,0},{7,5},{8,14},{9,11},{10,... | collective-permute-start | bytes 1179656 | tf_op jit(solution)/shard_map/ppermute | solution.py:43
  63.3 12.3 %collective-permute-start.12 = (bf16[2,2,32,1024]{3,2,1,0:T(8,128)(2,1)S(1)}, bf16[2,2,32,1024]{3,2,1,0:T(8,128)(2,1)S(1)}, u32[]{:S(2)}, u32[]{:S(2)}) collective-permute-start(bf16[2,2,32,1024]{3,2,1,0:T(8,128)(2,1)S(1)} %get-tuple-element.76), channel_id=1, source_target_pairs={{0,6},{1,3},{2,4},{3,1},{4,2},{5,7},{6,0},{7,5},{8,14},{9,11},{10,... | collective-permute-start | bytes 786440 | tf_op jit(solution)/shard_map/ppermute | solution.py:43
  76.3 9.5 %collective-permute-start.16 = (bf16[2,32,2560]{2,1,0:T(8,128)(2,1)S(1)}, bf16[2,32,2560]{2,1,0:T(8,128)(2,1)S(1)}, u32[]{:S(2)}, u32[]{:S(2)}) collective-permute-start(bf16[2,32,2560]{2,1,0:T(8,128)(2,1)S(1)} %get-tuple-element.84), channel_id=1, source_target_pairs={{0,8},{1,9},{2,10},{3,11},{4,12},{5,13},{6,14},{7,15},{8,0},{9,1},... | collective-permute-start | bytes 983048 | tf_op jit(solution)/shard_map/ppermute | solution.py:43
  81.0 7.7 %collective-permute-start.17 = (bf16[2,2,2,32,512]{4,3,2,1,0:T(8,128)(2,1)S(1)}, bf16[2,2,2,32,512]{4,3,2,1,0:T(8,128)(2,1)S(1)}, u32[]{:S(2)}, u32[]{:S(2)}) collective-permute-start(bf16[2,2,2,32,512]{4,3,2,1,0:T(8,128)(2,1)S(1)} %get-tuple-element.87), channel_id=1, source_target_pairs={{0,2},{1,7},{2,0},{3,5},{4,6},{5,3},{6,4},{7,1},{8,10},{9,15},{10,... | collective-permute-start | bytes 786440 | tf_op jit(solution)/shard_map/ppermute | solution.py:43
  83.3 8.1 %collective-permute-start.18 = (bf16[2,2,32,1024]{3,2,1,0:T(8,128)(2,1)S(1)}, bf16[2,2,32,1024]{3,2,1,0:T(8,128)(2,1)S(1)}, u32[]{:S(2)}, u32[]{:S(2)}) collective-permute-start(bf16[2,2,32,1024]{3,2,1,0:T(8,128)(2,1)S(1)} %get-tuple-element.90), channel_id=1, source_target_pairs={{0,6},{1,3},{2,4},{3,1},{4,2},{5,7},{6,0},{7,5},{8,14},{9,11},{10,... | collective-permute-start | bytes 786440 | tf_op jit(solution)/shard_map/ppermute | solution.py:43
  88.7 3.9 %collective-permute-start.19 = (bf16[2,2,32,512]{3,2,1,0:T(8,128)(2,1)S(1)}, bf16[2,2,32,512]{3,2,1,0:T(8,128)(2,1)S(1)}, u32[]{:S(2)}, u32[]{:S(2)}) collective-permute-start(bf16[2,2,32,512]{3,2,1,0:T(8,128)(2,1)S(1)} %get-tuple-element.91), channel_id=1, source_target_pairs={{0,6},{1,3},{2,4},{3,1},{4,2},{5,7},{6,0},{7,5},{8,14},{9,11},{10,... | collective-permute-start | bytes 393224 | tf_op jit(solution)/shard_map/ppermute | solution.py:43
  93.3 7.8 %collective-permute-start.22 = (bf16[2,32,1536]{2,1,0:T(8,128)(2,1)S(1)}, bf16[2,32,1536]{2,1,0:T(8,128)(2,1)S(1)}, u32[]{:S(2)}, u32[]{:S(2)}) collective-permute-start(bf16[2,32,1536]{2,1,0:T(8,128)(2,1)S(1)} %get-tuple-element.96), channel_id=1, source_target_pairs={{0,8},{1,9},{2,10},{3,11},{4,12},{5,13},{6,14},{7,15},{8,0},{9,1},... | collective-permute-start | bytes 589832 | tf_op jit(solution)/shard_map/ppermute | solution.py:43
  93.6 4.9 %collective-permute-start.20 = (bf16[2,32,512]{2,1,0:T(8,128)(2,1)S(1)}, bf16[2,32,512]{2,1,0:T(8,128)(2,1)S(1)}, u32[]{:S(2)}, u32[]{:S(2)}) collective-permute-start(bf16[2,32,512]{2,1,0:T(8,128)(2,1)S(1)} %get-tuple-element.93), channel_id=1, source_target_pairs={{0,224},{1,33},{2,226},{3,35},{4,228},{5,37},{6,230},{7,39},{8,232... | collective-permute-start | bytes 196616 | tf_op jit(solution)/shard_map/ppermute | solution.py:43
  93.7 7.4 %collective-permute-start.21 = (bf16[2,32,512]{2,1,0:T(8,128)(2,1)S(1)}, bf16[2,32,512]{2,1,0:T(8,128)(2,1)S(1)}, u32[]{:S(2)}, u32[]{:S(2)}) collective-permute-start(bf16[2,32,512]{2,1,0:T(8,128)(2,1)S(1)} %get-tuple-element.94), channel_id=1, source_target_pairs={{0,192},{1,65},{2,194},{3,67},{4,196},{5,69},{6,198},{7,71},{8,200... | collective-permute-start | bytes 196616 | tf_op jit(solution)/shard_map/ppermute | solution.py:43
  101.1 6.5 %collective-permute-start.23 = (bf16[2,32,1024]{2,1,0:T(8,128)(2,1)S(1)}, bf16[2,32,1024]{2,1,0:T(8,128)(2,1)S(1)}, u32[]{:S(2)}, u32[]{:S(2)}) collective-permute-start(bf16[2,32,1024]{2,1,0:T(8,128)(2,1)S(1)} %get-tuple-element.99), channel_id=1, source_target_pairs={{0,16},{1,17},{2,18},{3,19},{4,20},{5,21},{6,22},{7,23},{8,24},{9,... | collective-permute-start | bytes 393224 | tf_op jit(solution)/shard_map/ppermute | solution.py:43
  101.4 6.3 %collective-permute-start.24 = (bf16[2,32,512]{2,1,0:T(8,128)(2,1)S(1)}, bf16[2,32,512]{2,1,0:T(8,128)(2,1)S(1)}, u32[]{:S(2)}, u32[]{:S(2)}) collective-permute-start(bf16[2,32,512]{2,1,0:T(8,128)(2,1)S(1)} %get-tuple-element.100), channel_id=1, source_target_pairs={{0,160},{1,97},{2,162},{3,99},{4,164},{5,101},{6,166},{7,103},{8,1... | collective-permute-start | bytes 196616 | tf_op jit(solution)/shard_map/ppermute | solution.py:43
  108.2 6.0 %collective-permute-start.25 = (bf16[2,16,4096]{2,1,0:T(8,128)(2,1)S(1)}, bf16[2,16,4096]{2,1,0:T(8,128)(2,1)S(1)}, u32[]{:S(2)}, u32[]{:S(2)}) collective-permute-start(bf16[2,16,4096]{2,1,0:T(8,128)(2,1)S(1)} %split.1), channel_id=1, source_target_pairs={{0,1},{1,0},{2,3},{3,2},{4,5},{5,4},{6,7},{7,6},{8,9},{9,8},{10,11... | collective-permute-start | bytes 786440 | tf_op jit(solution)/shard_map/ppermute | solution.py:43

commit v6 on v4

--- a/solution.py
+++ b/solution.py
@@ -169,7 +169,7 @@
         out_specs=[whole] * len(shapes),
         out_shape=tuple(jax.ShapeDtypeStruct(s, t) for s, t in shapes),
         compiler_params=params(12),
-        cost_estimate=cost(1000, MIB),
+        cost_estimate=cost(1000, 10 * MIB),
         name=name,
     )(*lead, *arrays)
 
@@ -351,15 +351,15 @@
     recv_o = move(send_o, x_near)
     third = [move(b, chain_step) for b in (after(second[0], near[1], keep_o), second[1])]
     fourth = [move(b, chain_step) for b in third]
-    at = after(place, second[1], keep_o)
+    at = after(place, recv_o)
     near_rotated = [own_plus, near_plus, near_minus]
     keep_n, send_n = products(at, near_pairs, first + near + near_rotated, 3 * BLOCK, scale, "pairs_near")
     recv_n = move(send_n, x_near)
-    at = after(place, keep_n, third[0])
+    at = after(place, keep_n)
     keep_b, send_b = products(at, all_pairs, second + rotated, 4 * BLOCK, scale, "pairs_2")
     recv_b = move(send_b, x_near)
     picks = [(0, 0, 2 * BLOCK), (1, 0, BLOCK), (1, BLOCK, BLOCK), (0, 2 * BLOCK, BLOCK), (1, 2 * BLOCK, BLOCK)]
-    kept_a, send_a = sum_1([(after(keep_o, keep_b), recv_o), (keep_n, recv_n)], picks)
+    kept_a, send_a = sum_1([(after(keep_o, keep_b, third[0]), recv_o), (keep_n, recv_n)], picks)
     recv_a = move(send_a, x_far)
     at = after(place, kept_a)
     keep_c, send_c = products(at, all_pairs, third + rotated, 4 * BLOCK, scale, "pairs_3")
@@ -381,7 +381,7 @@
     own_ab, near_ab, ret_1, ret_2 = sum_y(after(keep_ab, keep_cd), recv_ab, outputs)
     ret_1, ret_2 = move(ret_1, back(1)), move(ret_2, back(2))
     outputs = [[(0, 256), (1024, 256)], [(256, 256), (1280, 256)], [(512, 512)]]
-    own_cd, near_all, ret_3 = sum_y(after(keep_cd, own_ab), recv_cd, outputs, near_ab)
+    own_cd, near_all, ret_3 = sum_y(after(keep_cd, ret_1, ret_2), recv_cd, outputs, near_ab)
     ret_3 = move(ret_3, back(3))
     near_all = move(near_all, y_step)
     arrays = [own_ab, own_cd, near_all, ret_1, ret_2, ret_3]

time: 108 us -> 106 us (0.981)
  starting transfers between devices: 51.3 us -> 48.9 us
    ppermute x26, starting transfers between devices: 51.3 us -> 48.9 us  [move(): return lax.ppermute(x, AXES, pairs)]
where the time goes in v6:
time: 106 us; the launch traced here: 105 us
  starting transfers between devices  48.9 us (46%)
  waiting for transfers between devices  34.4 us (32%)
  Pallas kernels  19.7 us (19%)
  local copies, waits for them, and re-layouts  1.31 us (1%)
    ppermute x26, starting transfers between devices, move(): return lax.ppermute(x, AXES, pairs)  48.9 us
    ppermute x26, waiting for transfers between devices, move(): return lax.ppermute(x, AXES, pairs)  34.4 us
    pallas_call x5, Pallas kernels, products(): pl.pallas_call(kernel, in_specs=[pl.BlockSpec(memory_space=pltpu.SMEM)] +...  12.7 us
    pallas_call x10, Pallas kernels, call(): pl.pallas_call(kernel, in_specs=[pl.BlockSpec(memory_space=pltpu.SMEM)] *...  3.91 us
  transfers between devices with their start and end apart: 26, of which 15 were waited for; matrix products, arithmetic and copies ran while one was open for 0% of the time, Pallas kernels for 16%

profile of v6, /device:TPU:1, one launch (start us, length us, event | category | flops | bytes accessed | tf_op | source)
XLA Modules:
  0.0 104.7 jit_solution(3611418835897500379)
XLA Ops:
  0.1 1.2 %copy-done = bf16[2,2,512,256]{3,2,1,0:T(8,128)(2,1)S(1)} copy-done((bf16[2,2,512,256]{3,2,1,0:T(8,128)(2,1)S(1)}, bf16[2,2,512,256]{3,2,1,0:T(8,128)(2,1)}, u32[]{:S(2)}) %copy-start) | copy-done | bytes 1048600
  1.3 0.6 whiten.2.a_ref.refs_2_
  1.9 2.2 %collective-permute-start.1 = (bf16[128,2048]{1,0:T(8,128)(2,1)S(1)}, bf16[128,2048]{1,0:T(8,128)(2,1)S(1)}, u32[]{:S(2)}, u32[]{:S(2)}) collective-permute-start(bf16[128,2048]{1,0:T(8,128)(2,1)S(1)} %whiten.2.a_ref.refs_2_), channel_id=1, source_target_pairs={{0,16},{1,17},{2,18},{3,19},{4,20},{5,21},{6,22},{7,23},{8,24},{9,... | collective-permute-start | bytes 1572872 | tf_op jit(solution)/shard_map/ppermute | solution.py:43
  4.1 5.6 %collective-permute-start = (bf16[128,2048]{1,0:T(8,128)(2,1)S(1)}, bf16[128,2048]{1,0:T(8,128)(2,1)S(1)}, u32[]{:S(2)}, u32[]{:S(2)}) collective-permute-start(bf16[128,2048]{1,0:T(8,128)(2,1)S(1)} %whiten.2.a_ref.refs_2_), channel_id=1, source_target_pairs={{0,32},{1,225},{2,34},{3,227},{4,36},{5,229},{6,38},{7,231},{8,40}... | collective-permute-start | bytes 1572872 | tf_op jit(solution)/shard_map/ppermute | solution.py:43
  9.7 0.6 whiten.3.b_ref.refs_3_
  10.3 0.8 collective-permute-start.2
  11.3 3.2 %collective-permute-done.1.a_ref.refs_2_ = bf16[128,2048]{1,0:T(8,128)(2,1)S(1)} collective-permute-done((bf16[128,2048]{1,0:T(8,128)(2,1)S(1)}, bf16[128,2048]{1,0:T(8,128)(2,1)S(1)}, u32[]{:S(2)}, u32[]{:S(2)}) %collective-permute-start.1) | collective-permute-done | bytes 524320 | tf_op jit(solution)/shard_map/ppermute | solution.py:43
  14.5 1.3 %collective-permute-done.refs_0_ = bf16[128,2048]{1,0:T(8,128)(2,1)S(1)} collective-permute-done((bf16[128,2048]{1,0:T(8,128)(2,1)S(1)}, bf16[128,2048]{1,0:T(8,128)(2,1)S(1)}, u32[]{:S(2)}, u32[]{:S(2)}) %collective-permute-start) | collective-permute-done | bytes 524320 | tf_op jit(solution)/shard_map/ppermute | solution.py:43
  15.8 5.4 %collective-permute-start.5 = (bf16[128,2048]{1,0:T(8,128)(2,1)S(1)}, bf16[128,2048]{1,0:T(8,128)(2,1)S(1)}, u32[]{:S(2)}, u32[]{:S(2)}) collective-permute-start(bf16[128,2048]{1,0:T(8,128)(2,1)S(1)} %collective-permute-done.refs_0_), channel_id=1, source_target_pairs={{0,32},{1,225},{2,34},{3,227},{4,36},{5,229},{6,38},{7,231},{8,40}... | collective-permute-start | bytes 1572872 | tf_op jit(solution)/shard_map/ppermute | solution.py:43
  21.4 1.0 rotate.2
  22.4 2.2 %collective-permute-start.6 = (bf16[128,2048]{1,0:T(8,128)(2,1)S(1)}, bf16[128,2048]{1,0:T(8,128)(2,1)S(1)}, u32[]{:S(2)}, u32[]{:S(2)}) collective-permute-start(bf16[128,2048]{1,0:T(8,128)(2,1)S(1)} %collective-permute-done.2.refs_1_), channel_id=1, source_target_pairs={{0,32},{1,225},{2,34},{3,227},{4,36},{5,229},{6,38},{7,231},{8,40}... | collective-permute-start | bytes 1572872 | tf_op jit(solution)/shard_map/ppermute | solution.py:43
  24.6 2.4 %pairs_own.1 = (bf16[2,2,2,32,768]{4,3,2,1,0:T(8,128)(2,1)S(1)}, bf16[2,2,2,32,768]{4,3,2,1,0:T(8,128)(2,1)S(1)}) custom-call(s32[5]{0:T(128)S(1)} %stack.23.at_ref.place_ref, bf16[128,2048]{1,0:T(8,128)(2,1)S(1)} %collective-permute-done.refs_0_, bf16[128,2048]{1,0:T(8,128)(2,1)S(1)} %collective-permute-done.2.refs_1_, ...), custom_call_target="tpu_custom_call" | custom-call | flops 1610612736 | bytes 8388608 | tf_op jit(solution)/shard_map/pairs_own/pallas_call | solution.py:147
  27.0 2.6 %collective-permute-start.3 = (bf16[2,2,2,32,768]{4,3,2,1,0:T(8,128)(2,1)S(1)}, bf16[2,2,2,32,768]{4,3,2,1,0:T(8,128)(2,1)S(1)}, u32[]{:S(2)}, u32[]{:S(2)}) collective-permute-start(bf16[2,2,2,32,768]{4,3,2,1,0:T(8,128)(2,1)S(1)} %get-tuple-element.57), channel_id=1, source_target_pairs={{0,2},{1,7},{2,0},{3,5},{4,6},{5,3},{6,4},{7,1},{8,10},{9,15},{10,... | collective-permute-start | bytes 1179656 | tf_op jit(solution)/shard_map/ppermute | solution.py:43
  29.6 2.9 %collective-permute-start.7 = (bf16[128,2048]{1,0:T(8,128)(2,1)S(1)}, bf16[128,2048]{1,0:T(8,128)(2,1)S(1)}, u32[]{:S(2)}, u32[]{:S(2)}) collective-permute-start(bf16[128,2048]{1,0:T(8,128)(2,1)S(1)} %collective-permute-done.5.refs_0_), channel_id=1, source_target_pairs={{0,32},{1,225},{2,34},{3,227},{4,36},{5,229},{6,38},{7,231},{8,40}... | collective-permute-start | bytes 1572872 | tf_op jit(solution)/shard_map/ppermute | solution.py:43
  32.4 0.5 collective-permute-done.6.refs_1_
  33.0 3.1 %collective-permute-start.9 = (bf16[128,2048]{1,0:T(8,128)(2,1)S(1)}, bf16[128,2048]{1,0:T(8,128)(2,1)S(1)}, u32[]{:S(2)}, u32[]{:S(2)}) collective-permute-start(bf16[128,2048]{1,0:T(8,128)(2,1)S(1)} %collective-permute-done.6.refs_1_), channel_id=1, source_target_pairs={{0,32},{1,225},{2,34},{3,227},{4,36},{5,229},{6,38},{7,231},{8,40}... | collective-permute-start | bytes 1572872 | tf_op jit(solution)/shard_map/ppermute | solution.py:43
  36.1 1.0 rotate.3
  37.1 2.4 %pairs_near.1 = (bf16[2,2,2,32,768]{4,3,2,1,0:T(8,128)(2,1)S(1)}, bf16[2,2,2,32,768]{4,3,2,1,0:T(8,128)(2,1)S(1)}) custom-call(s32[5]{0:T(128)S(1)} %stack.23.at_ref.place_ref, bf16[128,2048]{1,0:T(8,128)(2,1)S(1)} %collective-permute-done.refs_0_, bf16[128,2048]{1,0:T(8,128)(2,1)S(1)} %collective-permute-done.2.refs_1_, ...), custom_call_target="tpu_custom_call" | custom-call | flops 1610612736 | bytes 8388608 | tf_op jit(solution)/shard_map/pairs_near/pallas_call | solution.py:147
  39.5 2.6 %collective-permute-start.8 = (bf16[2,2,2,32,768]{4,3,2,1,0:T(8,128)(2,1)S(1)}, bf16[2,2,2,32,768]{4,3,2,1,0:T(8,128)(2,1)S(1)}, u32[]{:S(2)}, u32[]{:S(2)}) collective-permute-start(bf16[2,2,2,32,768]{4,3,2,1,0:T(8,128)(2,1)S(1)} %get-tuple-element.66), channel_id=1, source_target_pairs={{0,2},{1,7},{2,0},{3,5},{4,6},{5,3},{6,4},{7,1},{8,10},{9,15},{10,... | collective-permute-start | bytes 1179656 | tf_op jit(solution)/shard_map/ppermute | solution.py:43
  42.1 3.0 %pairs_2.1 = (bf16[2,2,2,32,1024]{4,3,2,1,0:T(8,128)(2,1)S(1)}, bf16[2,2,2,32,1024]{4,3,2,1,0:T(8,128)(2,1)S(1)}) custom-call(s32[5]{0:T(128)S(1)} %stack.23.at_ref.place_ref, bf16[128,2048]{1,0:T(8,128)(2,1)S(1)} %collective-permute-done.5.refs_0_, bf16[128,2048]{1,0:T(8,128)(2,1)S(1)} %collective-permute-done.6.refs_1_, ...), custom_call_target="tpu_custom_call" | custom-call | flops 2147483648 | bytes 8388608 | tf_op jit(solution)/shard_map/pairs_2/pallas_call | solution.py:147
  45.1 2.2 %collective-permute-start.11 = (bf16[2,2,2,32,1024]{4,3,2,1,0:T(8,128)(2,1)S(1)}, bf16[2,2,2,32,1024]{4,3,2,1,0:T(8,128)(2,1)S(1)}, u32[]{:S(2)}, u32[]{:S(2)}) collective-permute-start(bf16[2,2,2,32,1024]{4,3,2,1,0:T(8,128)(2,1)S(1)} %get-tuple-element.71), channel_id=1, source_target_pairs={{0,2},{1,7},{2,0},{3,5},{4,6},{5,3},{6,4},{7,1},{8,10},{9,15},{10,... | collective-permute-start | bytes 1572872 | tf_op jit(solution)/shard_map/ppermute | solution.py:43
  47.3 0.4 collective-permute-done.8.refs_3_
  47.9 3.0 %pairs_3.1 = (bf16[2,2,2,32,1024]{4,3,2,1,0:T(8,128)(2,1)S(1)}, bf16[2,2,2,32,1024]{4,3,2,1,0:T(8,128)(2,1)S(1)}) custom-call(s32[5]{0:T(128)S(1)} %stack.23.at_ref.place_ref, bf16[128,2048]{1,0:T(8,128)(2,1)S(1)} %collective-permute-done.7.refs_0_, bf16[128,2048]{1,0:T(8,128)(2,1)S(1)} %collective-permute-done.9.refs_1_, ...), custom_call_target="tpu_custom_call" | custom-call | flops 2147483648 | bytes 8388608 | tf_op jit(solution)/shard_map/pairs_3/pallas_call | solution.py:147
  50.9 2.6 %collective-permute-start.13 = (bf16[2,2,2,32,1024]{4,3,2,1,0:T(8,128)(2,1)S(1)}, bf16[2,2,2,32,1024]{4,3,2,1,0:T(8,128)(2,1)S(1)}, u32[]{:S(2)}, u32[]{:S(2)}) collective-permute-start(bf16[2,2,2,32,1024]{4,3,2,1,0:T(8,128)(2,1)S(1)} %get-tuple-element.76), channel_id=1, source_target_pairs={{0,2},{1,7},{2,0},{3,5},{4,6},{5,3},{6,4},{7,1},{8,10},{9,15},{10,... | collective-permute-start | bytes 1572872 | tf_op jit(solution)/shard_map/ppermute | solution.py:43
  53.4 1.2 %collective-permute-done.11.refs_1_ = bf16[2,2,2,32,1024]{4,3,2,1,0:T(8,128)(2,1)S(1)} collective-permute-done((bf16[2,2,2,32,1024]{4,3,2,1,0:T(8,128)(2,1)S(1)}, bf16[2,2,2,32,1024]{4,3,2,1,0:T(8,128)(2,1)S(1)}, u32[]{:S(2)}, u32[]{:S(2)}) %collective-permute-start.11) | collective-permute-done | bytes 524320 | tf_op jit(solution)/shard_map/ppermute | solution.py:43
  54.8 0.3 collective-permute-start.15
  55.1 0.9 collective-permute-done.12.refs_1_
  56.0 1.9 %pairs_4.1 = (bf16[2,2,2,32,512]{4,3,2,1,0:T(8,128)(2,1)S(1)}, bf16[2,2,2,32,512]{4,3,2,1,0:T(8,128)(2,1)S(1)}) custom-call(s32[5]{0:T(128)S(1)} %stack.23.at_ref.place_ref, bf16[128,2048]{1,0:T(8,128)(2,1)S(1)} %collective-permute-done.10.refs_0_, bf16[128,2048]{1,0:T(8,128)(2,1)S(1)} %collective-permute-done.12.refs_1_, ...), custom_call_target="tpu_custom_call" | custom-call | flops 1073741824 | bytes 8388608 | tf_op jit(solution)/shard_map/pairs_4/pallas_call | solution.py:147
  57.9 2.0 %collective-permute-start.17 = (bf16[2,2,2,32,512]{4,3,2,1,0:T(8,128)(2,1)S(1)}, bf16[2,2,2,32,512]{4,3,2,1,0:T(8,128)(2,1)S(1)}, u32[]{:S(2)}, u32[]{:S(2)}) collective-permute-start(bf16[2,2,2,32,512]{4,3,2,1,0:T(8,128)(2,1)S(1)} %get-tuple-element.84), channel_id=1, source_target_pairs={{0,2},{1,7},{2,0},{3,5},{4,6},{5,3},{6,4},{7,1},{8,10},{9,15},{10,... | collective-permute-start | bytes 786440 | tf_op jit(solution)/shard_map/ppermute | solution.py:43
  59.9 3.7 %collective-permute-done.13.refs_1_ = bf16[2,2,2,32,1024]{4,3,2,1,0:T(8,128)(2,1)S(1)} collective-permute-done((bf16[2,2,2,32,1024]{4,3,2,1,0:T(8,128)(2,1)S(1)}, bf16[2,2,2,32,1024]{4,3,2,1,0:T(8,128)(2,1)S(1)}, u32[]{:S(2)}, u32[]{:S(2)}) %collective-permute-start.13) | collective-permute-done | bytes 524320 | tf_op jit(solution)/shard_map/ppermute | solution.py:43
  63.8 0.7 collective-permute-done.14.refs_1_
  64.5 5.5 %collective-permute-done.15.refs_3_ = bf16[2,2,32,1024]{3,2,1,0:T(8,128)(2,1)S(1)} collective-permute-done((bf16[2,2,32,1024]{3,2,1,0:T(8,128)(2,1)S(1)}, bf16[2,2,32,1024]{3,2,1,0:T(8,128)(2,1)S(1)}, u32[]{:S(2)}, u32[]{:S(2)}) %collective-permute-start.15) | collective-permute-done | bytes 262176 | tf_op jit(solution)/shard_map/ppermute | solution.py:43
  70.0 0.6 sum_2.2
  70.6 3.0 %collective-permute-start.19 = (bf16[2,32,2560]{2,1,0:T(8,128)(2,1)S(1)}, bf16[2,32,2560]{2,1,0:T(8,128)(2,1)S(1)}, u32[]{:S(2)}, u32[]{:S(2)}) collective-permute-start(bf16[2,32,2560]{2,1,0:T(8,128)(2,1)S(1)} %get-tuple-element.89), channel_id=1, source_target_pairs={{0,8},{1,9},{2,10},{3,11},{4,12},{5,13},{6,14},{7,15},{8,0},{9,1},... | collective-permute-start | bytes 983048 | tf_op jit(solution)/shard_map/ppermute | solution.py:43
  73.7 0.3 collective-permute-start.18
  74.0 3.9 %collective-permute-done.18.refs_3_ = bf16[2,2,32,512]{3,2,1,0:T(8,128)(2,1)S(1)} collective-permute-done((bf16[2,2,32,512]{3,2,1,0:T(8,128)(2,1)S(1)}, bf16[2,2,32,512]{3,2,1,0:T(8,128)(2,1)S(1)}, u32[]{:S(2)}, u32[]{:S(2)}) %collective-permute-start.18) | collective-permute-done | bytes 131104 | tf_op jit(solution)/shard_map/ppermute | solution.py:43
  77.9 0.6 sum_2.3
  78.6 2.1 %collective-permute-done.19.refs_1_ = bf16[2,32,2560]{2,1,0:T(8,128)(2,1)S(1)} collective-permute-done((bf16[2,32,2560]{2,1,0:T(8,128)(2,1)S(1)}, bf16[2,32,2560]{2,1,0:T(8,128)(2,1)S(1)}, u32[]{:S(2)}, u32[]{:S(2)}) %collective-permute-start.19) | collective-permute-done | bytes 327712 | tf_op jit(solution)/shard_map/ppermute | solution.py:43
  80.9 2.1 %collective-permute-start.21 = (bf16[2,32,512]{2,1,0:T(8,128)(2,1)S(1)}, bf16[2,32,512]{2,1,0:T(8,128)(2,1)S(1)}, u32[]{:S(2)}, u32[]{:S(2)}) collective-permute-start(bf16[2,32,512]{2,1,0:T(8,128)(2,1)S(1)} %get-tuple-element.92), channel_id=1, source_target_pairs={{0,192},{1,65},{2,194},{3,67},{4,196},{5,69},{6,198},{7,71},{8,200... | collective-permute-start | bytes 196616 | tf_op jit(solution)/shard_map/ppermute | solution.py:43
  83.0 2.2 %collective-permute-done.20.refs_3_ = bf16[2,32,512]{2,1,0:T(8,128)(2,1)S(1)} collective-permute-done((bf16[2,32,512]{2,1,0:T(8,128)(2,1)S(1)}, bf16[2,32,512]{2,1,0:T(8,128)(2,1)S(1)}, u32[]{:S(2)}, u32[]{:S(2)}) %collective-permute-start.20) | collective-permute-done | bytes 65568 | tf_op jit(solution)/shard_map/ppermute | solution.py:43
  85.2 1.5 %collective-permute-done.21.refs_4_ = bf16[2,32,512]{2,1,0:T(8,128)(2,1)S(1)} collective-permute-done((bf16[2,32,512]{2,1,0:T(8,128)(2,1)S(1)}, bf16[2,32,512]{2,1,0:T(8,128)(2,1)S(1)}, u32[]{:S(2)}, u32[]{:S(2)}) %collective-permute-start.21) | collective-permute-done | bytes 65568 | tf_op jit(solution)/shard_map/ppermute | solution.py:43
  86.7 1.2 %collective-permute-start.23 = (bf16[2,32,1024]{2,1,0:T(8,128)(2,1)S(1)}, bf16[2,32,1024]{2,1,0:T(8,128)(2,1)S(1)}, u32[]{:S(2)}, u32[]{:S(2)}) collective-permute-start(bf16[2,32,1024]{2,1,0:T(8,128)(2,1)S(1)} %get-tuple-element.97), channel_id=1, source_target_pairs={{0,16},{1,17},{2,18},{3,19},{4,20},{5,21},{6,22},{7,23},{8,24},{9,... | collective-permute-start | bytes 393224 | tf_op jit(solution)/shard_map/ppermute | solution.py:43
  87.9 1.0 collective-permute-start.24
  88.9 6.1 %collective-permute-done.24.refs_5_ = bf16[2,32,512]{2,1,0:T(8,128)(2,1)S(1)} collective-permute-done((bf16[2,32,512]{2,1,0:T(8,128)(2,1)S(1)}, bf16[2,32,512]{2,1,0:T(8,128)(2,1)S(1)}, u32[]{:S(2)}, u32[]{:S(2)}) %collective-permute-start.24) | collective-permute-done | bytes 65568 | tf_op jit(solution)/shard_map/ppermute | solution.py:43
  95.0 0.6 split.1
  95.5 6.5 %collective-permute-start.25 = (bf16[2,16,4096]{2,1,0:T(8,128)(2,1)S(1)}, bf16[2,16,4096]{2,1,0:T(8,128)(2,1)S(1)}, u32[]{:S(2)}, u32[]{:S(2)}) collective-permute-start(bf16[2,16,4096]{2,1,0:T(8,128)(2,1)S(1)} %split.1), channel_id=1, source_target_pairs={{0,1},{1,0},{2,3},{3,2},{4,5},{5,4},{6,7},{7,6},{8,9},{9,8},{10,11... | collective-permute-start | bytes 786440 | tf_op jit(solution)/shard_map/ppermute | solution.py:43
  102.0 1.2 %collective-permute-done.25.refs_6_ = bf16[2,16,4096]{2,1,0:T(8,128)(2,1)S(1)} collective-permute-done((bf16[2,16,4096]{2,1,0:T(8,128)(2,1)S(1)}, bf16[2,16,4096]{2,1,0:T(8,128)(2,1)S(1)}, u32[]{:S(2)}, u32[]{:S(2)}) %collective-permute-start.25) | collective-permute-done | bytes 262176 | tf_op jit(solution)/shard_map/ppermute | solution.py:43
  103.2 1.5 %finish.1 = f32[2,16,4096]{2,1,0:T(8,128)} custom-call(s32[5]{0:T(128)S(1)} %stack.23.at_ref.place_ref, bf16[2,32,1024]{2,1,0:T(8,128)(2,1)S(1)} %get-tuple-element.90.refs_0_, bf16[2,32,512]{2,1,0:T(8,128)(2,1)S(1)} %get-tuple-element.96.refs_1_, bf16[2,32,1024]{2,1,0:T(8,128)(2,1)S(1)} %collective-permute-done.23.refs_2_, ...), custom_call_target="tpu_custom_call" | custom-call | flops 1000 | bytes 10485760 | tf_op jit(solution)/shard_map/finish/pallas_call | solution.py:166
  (31 shorter events, 1.4 us)
Async XLA Ops:
  0.0 21.2 %copy-start.1 = (s32[512]{0:T(512)S(1)}, s32[512]{0:T(512)}, u32[]{:S(2)}) copy-start(s32[512]{0:T(512)} %param.3) | copy-start | bytes 6148
  0.1 1.2 %copy-start = (bf16[2,2,512,256]{3,2,1,0:T(8,128)(2,1)S(1)}, bf16[2,2,512,256]{3,2,1,0:T(8,128)(2,1)}, u32[]{:S(2)}) copy-start(bf16[2,2,512,256]{3,2,1,0:T(8,128)(2,1)} %x_ref.1) | copy-start | bytes 3145732
  1.9 12.6 %collective-permute-start.1 = (bf16[128,2048]{1,0:T(8,128)(2,1)S(1)}, bf16[128,2048]{1,0:T(8,128)(2,1)S(1)}, u32[]{:S(2)}, u32[]{:S(2)}) collective-permute-start(bf16[128,2048]{1,0:T(8,128)(2,1)S(1)} %whiten.2.a_ref.refs_2_), channel_id=1, source_target_pairs={{0,16},{1,17},{2,18},{3,19},{4,20},{5,21},{6,22},{7,23},{8,24},{9,... | collective-permute-start | bytes 1572872 | tf_op jit(solution)/shard_map/ppermute | solution.py:43
  4.1 11.7 %collective-permute-start = (bf16[128,2048]{1,0:T(8,128)(2,1)S(1)}, bf16[128,2048]{1,0:T(8,128)(2,1)S(1)}, u32[]{:S(2)}, u32[]{:S(2)}) collective-permute-start(bf16[128,2048]{1,0:T(8,128)(2,1)S(1)} %whiten.2.a_ref.refs_2_), channel_id=1, source_target_pairs={{0,32},{1,225},{2,34},{3,227},{4,36},{5,229},{6,38},{7,231},{8,40}... | collective-permute-start | bytes 1572872 | tf_op jit(solution)/shard_map/ppermute | solution.py:43
  10.3 12.0 %collective-permute-start.2 = (bf16[128,2048]{1,0:T(8,128)(2,1)S(1)}, bf16[128,2048]{1,0:T(8,128)(2,1)S(1)}, u32[]{:S(2)}, u32[]{:S(2)}) collective-permute-start(bf16[128,2048]{1,0:T(8,128)(2,1)S(1)} %whiten.3.b_ref.refs_3_), channel_id=1, source_target_pairs={{0,32},{1,225},{2,34},{3,227},{4,36},{5,229},{6,38},{7,231},{8,40}... | collective-permute-start | bytes 1572872 | tf_op jit(solution)/shard_map/ppermute | solution.py:43
  11.1 18.4 %collective-permute-start.4 = (bf16[128,2048]{1,0:T(8,128)(2,1)S(1)}, bf16[128,2048]{1,0:T(8,128)(2,1)S(1)}, u32[]{:S(2)}, u32[]{:S(2)}) collective-permute-start(bf16[128,2048]{1,0:T(8,128)(2,1)S(1)} %whiten.3.b_ref.refs_3_), channel_id=1, source_target_pairs={{0,16},{1,17},{2,18},{3,19},{4,20},{5,21},{6,22},{7,23},{8,24},{9,... | collective-permute-start | bytes 1572872 | tf_op jit(solution)/shard_map/ppermute | solution.py:43
  15.8 13.7 %collective-permute-start.5 = (bf16[128,2048]{1,0:T(8,128)(2,1)S(1)}, bf16[128,2048]{1,0:T(8,128)(2,1)S(1)}, u32[]{:S(2)}, u32[]{:S(2)}) collective-permute-start(bf16[128,2048]{1,0:T(8,128)(2,1)S(1)} %collective-permute-done.refs_0_), channel_id=1, source_target_pairs={{0,32},{1,225},{2,34},{3,227},{4,36},{5,229},{6,38},{7,231},{8,40}... | collective-permute-start | bytes 1572872 | tf_op jit(solution)/shard_map/ppermute | solution.py:43
  22.4 10.6 %collective-permute-start.6 = (bf16[128,2048]{1,0:T(8,128)(2,1)S(1)}, bf16[128,2048]{1,0:T(8,128)(2,1)S(1)}, u32[]{:S(2)}, u32[]{:S(2)}) collective-permute-start(bf16[128,2048]{1,0:T(8,128)(2,1)S(1)} %collective-permute-done.2.refs_1_), channel_id=1, source_target_pairs={{0,32},{1,225},{2,34},{3,227},{4,36},{5,229},{6,38},{7,231},{8,40}... | collective-permute-start | bytes 1572872 | tf_op jit(solution)/shard_map/ppermute | solution.py:43
  27.0 10.0 %collective-permute-start.3 = (bf16[2,2,2,32,768]{4,3,2,1,0:T(8,128)(2,1)S(1)}, bf16[2,2,2,32,768]{4,3,2,1,0:T(8,128)(2,1)S(1)}, u32[]{:S(2)}, u32[]{:S(2)}) collective-permute-start(bf16[2,2,2,32,768]{4,3,2,1,0:T(8,128)(2,1)S(1)} %get-tuple-element.57), channel_id=1, source_target_pairs={{0,2},{1,7},{2,0},{3,5},{4,6},{5,3},{6,4},{7,1},{8,10},{9,15},{10,... | collective-permute-start | bytes 1179656 | tf_op jit(solution)/shard_map/ppermute | solution.py:43
  29.6 12.5 %collective-permute-start.7 = (bf16[128,2048]{1,0:T(8,128)(2,1)S(1)}, bf16[128,2048]{1,0:T(8,128)(2,1)S(1)}, u32[]{:S(2)}, u32[]{:S(2)}) collective-permute-start(bf16[128,2048]{1,0:T(8,128)(2,1)S(1)} %collective-permute-done.5.refs_0_), channel_id=1, source_target_pairs={{0,32},{1,225},{2,34},{3,227},{4,36},{5,229},{6,38},{7,231},{8,40}... | collective-permute-start | bytes 1572872 | tf_op jit(solution)/shard_map/ppermute | solution.py:43
  33.0 14.3 %collective-permute-start.9 = (bf16[128,2048]{1,0:T(8,128)(2,1)S(1)}, bf16[128,2048]{1,0:T(8,128)(2,1)S(1)}, u32[]{:S(2)}, u32[]{:S(2)}) collective-permute-start(bf16[128,2048]{1,0:T(8,128)(2,1)S(1)} %collective-permute-done.6.refs_1_), channel_id=1, source_target_pairs={{0,32},{1,225},{2,34},{3,227},{4,36},{5,229},{6,38},{7,231},{8,40}... | collective-permute-start | bytes 1572872 | tf_op jit(solution)/shard_map/ppermute | solution.py:43
  39.5 8.2 %collective-permute-start.8 = (bf16[2,2,2,32,768]{4,3,2,1,0:T(8,128)(2,1)S(1)}, bf16[2,2,2,32,768]{4,3,2,1,0:T(8,128)(2,1)S(1)}, u32[]{:S(2)}, u32[]{:S(2)}) collective-permute-start(bf16[2,2,2,32,768]{4,3,2,1,0:T(8,128)(2,1)S(1)} %get-tuple-element.66), channel_id=1, source_target_pairs={{0,2},{1,7},{2,0},{3,5},{4,6},{5,3},{6,4},{7,1},{8,10},{9,15},{10,... | collective-permute-start | bytes 1179656 | tf_op jit(solution)/shard_map/ppermute | solution.py:43
  42.1 11.4 %collective-permute-start.10 = (bf16[128,2048]{1,0:T(8,128)(2,1)S(1)}, bf16[128,2048]{1,0:T(8,128)(2,1)S(1)}, u32[]{:S(2)}, u32[]{:S(2)}) collective-permute-start(bf16[128,2048]{1,0:T(8,128)(2,1)S(1)} %collective-permute-done.7.refs_0_), channel_id=1, source_target_pairs={{0,32},{1,225},{2,34},{3,227},{4,36},{5,229},{6,38},{7,231},{8,40}... | collective-permute-start | bytes 1572872 | tf_op jit(solution)/shard_map/ppermute | solution.py:43
  45.1 9.6 %collective-permute-start.11 = (bf16[2,2,2,32,1024]{4,3,2,1,0:T(8,128)(2,1)S(1)}, bf16[2,2,2,32,1024]{4,3,2,1,0:T(8,128)(2,1)S(1)}, u32[]{:S(2)}, u32[]{:S(2)}) collective-permute-start(bf16[2,2,2,32,1024]{4,3,2,1,0:T(8,128)(2,1)S(1)} %get-tuple-element.71), channel_id=1, source_target_pairs={{0,2},{1,7},{2,0},{3,5},{4,6},{5,3},{6,4},{7,1},{8,10},{9,15},{10,... | collective-permute-start | bytes 1572872 | tf_op jit(solution)/shard_map/ppermute | solution.py:43
  47.2 8.8 %collective-permute-start.12 = (bf16[128,2048]{1,0:T(8,128)(2,1)S(1)}, bf16[128,2048]{1,0:T(8,128)(2,1)S(1)}, u32[]{:S(2)}, u32[]{:S(2)}) collective-permute-start(bf16[128,2048]{1,0:T(8,128)(2,1)S(1)} %collective-permute-done.9.refs_1_), channel_id=1, source_target_pairs={{0,32},{1,225},{2,34},{3,227},{4,36},{5,229},{6,38},{7,231},{8,40}... | collective-permute-start | bytes 1572872 | tf_op jit(solution)/shard_map/ppermute | solution.py:43
  50.9 12.7 %collective-permute-start.13 = (bf16[2,2,2,32,1024]{4,3,2,1,0:T(8,128)(2,1)S(1)}, bf16[2,2,2,32,1024]{4,3,2,1,0:T(8,128)(2,1)S(1)}, u32[]{:S(2)}, u32[]{:S(2)}) collective-permute-start(bf16[2,2,2,32,1024]{4,3,2,1,0:T(8,128)(2,1)S(1)} %get-tuple-element.76), channel_id=1, source_target_pairs={{0,2},{1,7},{2,0},{3,5},{4,6},{5,3},{6,4},{7,1},{8,10},{9,15},{10,... | collective-permute-start | bytes 1572872 | tf_op jit(solution)/shard_map/ppermute | solution.py:43
  53.4 11.1 %collective-permute-start.14 = (bf16[2,2,32,1536]{3,2,1,0:T(8,128)(2,1)S(1)}, bf16[2,2,32,1536]{3,2,1,0:T(8,128)(2,1)S(1)}, u32[]{:S(2)}, u32[]{:S(2)}) collective-permute-start(bf16[2,2,32,1536]{3,2,1,0:T(8,128)(2,1)S(1)} %get-tuple-element.79), channel_id=1, source_target_pairs={{0,6},{1,3},{2,4},{3,1},{4,2},{5,7},{6,0},{7,5},{8,14},{9,11},{10,... | collective-permute-start | bytes 1179656 | tf_op jit(solution)/shard_map/ppermute | solution.py:43
  54.8 15.2 %collective-permute-start.15 = (bf16[2,2,32,1024]{3,2,1,0:T(8,128)(2,1)S(1)}, bf16[2,2,32,1024]{3,2,1,0:T(8,128)(2,1)S(1)}, u32[]{:S(2)}, u32[]{:S(2)}) collective-permute-start(bf16[2,2,32,1024]{3,2,1,0:T(8,128)(2,1)S(1)} %get-tuple-element.80), channel_id=1, source_target_pairs={{0,6},{1,3},{2,4},{3,1},{4,2},{5,7},{6,0},{7,5},{8,14},{9,11},{10,... | collective-permute-start | bytes 786440 | tf_op jit(solution)/shard_map/ppermute | solution.py:43
  57.9 15.8 %collective-permute-start.17 = (bf16[2,2,2,32,512]{4,3,2,1,0:T(8,128)(2,1)S(1)}, bf16[2,2,2,32,512]{4,3,2,1,0:T(8,128)(2,1)S(1)}, u32[]{:S(2)}, u32[]{:S(2)}) collective-permute-start(bf16[2,2,2,32,512]{4,3,2,1,0:T(8,128)(2,1)S(1)} %get-tuple-element.84), channel_id=1, source_target_pairs={{0,2},{1,7},{2,0},{3,5},{4,6},{5,3},{6,4},{7,1},{8,10},{9,15},{10,... | collective-permute-start | bytes 786440 | tf_op jit(solution)/shard_map/ppermute | solution.py:43
  63.7 10.3 %collective-permute-start.16 = (bf16[2,2,32,1024]{3,2,1,0:T(8,128)(2,1)S(1)}, bf16[2,2,32,1024]{3,2,1,0:T(8,128)(2,1)S(1)}, u32[]{:S(2)}, u32[]{:S(2)}) collective-permute-start(bf16[2,2,32,1024]{3,2,1,0:T(8,128)(2,1)S(1)} %get-tuple-element.82), channel_id=1, source_target_pairs={{0,6},{1,3},{2,4},{3,1},{4,2},{5,7},{6,0},{7,5},{8,14},{9,11},{10,... | collective-permute-start | bytes 786440 | tf_op jit(solution)/shard_map/ppermute | solution.py:43
  70.6 10.1 %collective-permute-start.19 = (bf16[2,32,2560]{2,1,0:T(8,128)(2,1)S(1)}, bf16[2,32,2560]{2,1,0:T(8,128)(2,1)S(1)}, u32[]{:S(2)}, u32[]{:S(2)}) collective-permute-start(bf16[2,32,2560]{2,1,0:T(8,128)(2,1)S(1)} %get-tuple-element.89), channel_id=1, source_target_pairs={{0,8},{1,9},{2,10},{3,11},{4,12},{5,13},{6,14},{7,15},{8,0},{9,1},... | collective-permute-start | bytes 983048 | tf_op jit(solution)/shard_map/ppermute | solution.py:43
  73.7 4.2 %collective-permute-start.18 = (bf16[2,2,32,512]{3,2,1,0:T(8,128)(2,1)S(1)}, bf16[2,2,32,512]{3,2,1,0:T(8,128)(2,1)S(1)}, u32[]{:S(2)}, u32[]{:S(2)}) collective-permute-start(bf16[2,2,32,512]{3,2,1,0:T(8,128)(2,1)S(1)} %get-tuple-element.86), channel_id=1, source_target_pairs={{0,6},{1,3},{2,4},{3,1},{4,2},{5,7},{6,0},{7,5},{8,14},{9,11},{10,... | collective-permute-start | bytes 393224 | tf_op jit(solution)/shard_map/ppermute | solution.py:43
  78.5 8.2 %collective-permute-start.22 = (bf16[2,32,1536]{2,1,0:T(8,128)(2,1)S(1)}, bf16[2,32,1536]{2,1,0:T(8,128)(2,1)S(1)}, u32[]{:S(2)}, u32[]{:S(2)}) collective-permute-start(bf16[2,32,1536]{2,1,0:T(8,128)(2,1)S(1)} %get-tuple-element.94), channel_id=1, source_target_pairs={{0,8},{1,9},{2,10},{3,11},{4,12},{5,13},{6,14},{7,15},{8,0},{9,1},... | collective-permute-start | bytes 589832 | tf_op jit(solution)/shard_map/ppermute | solution.py:43
  80.8 4.4 %collective-permute-start.20 = (bf16[2,32,512]{2,1,0:T(8,128)(2,1)S(1)}, bf16[2,32,512]{2,1,0:T(8,128)(2,1)S(1)}, u32[]{:S(2)}, u32[]{:S(2)}) collective-permute-start(bf16[2,32,512]{2,1,0:T(8,128)(2,1)S(1)} %get-tuple-element.91), channel_id=1, source_target_pairs={{0,224},{1,33},{2,226},{3,35},{4,228},{5,37},{6,230},{7,39},{8,232... | collective-permute-start | bytes 196616 | tf_op jit(solution)/shard_map/ppermute | solution.py:43
  80.9 5.8 %collective-permute-start.21 = (bf16[2,32,512]{2,1,0:T(8,128)(2,1)S(1)}, bf16[2,32,512]{2,1,0:T(8,128)(2,1)S(1)}, u32[]{:S(2)}, u32[]{:S(2)}) collective-permute-start(bf16[2,32,512]{2,1,0:T(8,128)(2,1)S(1)} %get-tuple-element.92), channel_id=1, source_target_pairs={{0,192},{1,65},{2,194},{3,67},{4,196},{5,69},{6,198},{7,71},{8,200... | collective-permute-start | bytes 196616 | tf_op jit(solution)/shard_map/ppermute | solution.py:43
  86.7 8.2 %collective-permute-start.23 = (bf16[2,32,1024]{2,1,0:T(8,128)(2,1)S(1)}, bf16[2,32,1024]{2,1,0:T(8,128)(2,1)S(1)}, u32[]{:S(2)}, u32[]{:S(2)}) collective-permute-start(bf16[2,32,1024]{2,1,0:T(8,128)(2,1)S(1)} %get-tuple-element.97), channel_id=1, source_target_pairs={{0,16},{1,17},{2,18},{3,19},{4,20},{5,21},{6,22},{7,23},{8,24},{9,... | collective-permute-start | bytes 393224 | tf_op jit(solution)/shard_map/ppermute | solution.py:43
  87.9 7.0 %collective-permute-start.24 = (bf16[2,32,512]{2,1,0:T(8,128)(2,1)S(1)}, bf16[2,32,512]{2,1,0:T(8,128)(2,1)S(1)}, u32[]{:S(2)}, u32[]{:S(2)}) collective-permute-start(bf16[2,32,512]{2,1,0:T(8,128)(2,1)S(1)} %get-tuple-element.98), channel_id=1, source_target_pairs={{0,160},{1,97},{2,162},{3,99},{4,164},{5,101},{6,166},{7,103},{8,1... | collective-permute-start | bytes 196616 | tf_op jit(solution)/shard_map/ppermute | solution.py:43
  95.5 7.6 %collective-permute-start.25 = (bf16[2,16,4096]{2,1,0:T(8,128)(2,1)S(1)}, bf16[2,16,4096]{2,1,0:T(8,128)(2,1)S(1)}, u32[]{:S(2)}, u32[]{:S(2)}) collective-permute-start(bf16[2,16,4096]{2,1,0:T(8,128)(2,1)S(1)} %split.1), channel_id=1, source_target_pairs={{0,1},{1,0},{2,3},{3,2},{4,5},{5,4},{6,7},{7,6},{8,9},{9,8},{10,11... | collective-permute-start | bytes 786440 | tf_op jit(solution)/shard_map/ppermute | solution.py:43

commit v7 on v6

--- a/solution.py
+++ b/solution.py
@@ -349,29 +349,29 @@
 
     keep_o, send_o = products(place, own_pairs, first + own + rotated[:2], 3 * BLOCK, scale, "pairs_own")
     recv_o = move(send_o, x_near)
-    third = [move(b, chain_step) for b in (after(second[0], near[1], keep_o), second[1])]
-    fourth = [move(b, chain_step) for b in third]
+    third = [move(after(second[0], near[1], keep_o), chain_step)]
     at = after(place, recv_o)
     near_rotated = [own_plus, near_plus, near_minus]
     keep_n, send_n = products(at, near_pairs, first + near + near_rotated, 3 * BLOCK, scale, "pairs_near")
     recv_n = move(send_n, x_near)
+    third.append(move(after(second[1], keep_n), chain_step))
     at = after(place, keep_n)
     keep_b, send_b = products(at, all_pairs, second + rotated, 4 * BLOCK, scale, "pairs_2")
     recv_b = move(send_b, x_near)
-    picks = [(0, 0, 2 * BLOCK), (1, 0, BLOCK), (1, BLOCK, BLOCK), (0, 2 * BLOCK, BLOCK), (1, 2 * BLOCK, BLOCK)]
-    kept_a, send_a = sum_1([(after(keep_o, keep_b, third[0]), recv_o), (keep_n, recv_n)], picks)
-    recv_a = move(send_a, x_far)
-    at = after(place, kept_a)
+    fourth = [move(b, chain_step) for b in (after(third[0], keep_b), third[1])]
+    at = after(place, keep_b, recv_n)
     keep_c, send_c = products(at, all_pairs, third + rotated, 4 * BLOCK, scale, "pairs_3")
     recv_c = move(send_c, x_near)
-    kept_b, send_b = sum_1([(after(keep_b, keep_c, fourth[0]), recv_b)], straight)
-    recv_b = move(send_b, x_far)
-    at = after(place, kept_b)
+    picks = [(0, 0, 2 * BLOCK), (1, 0, BLOCK), (1, BLOCK, BLOCK), (0, 2 * BLOCK, BLOCK), (1, 2 * BLOCK, BLOCK)]
+    keep_o = after(keep_o, keep_c, fourth[0])
+    kept_ab, send_ab = sum_1([(keep_o, recv_o), (keep_n, recv_n), (keep_b, recv_b)], picks + [(2, 0, 4 * BLOCK)])
+    recv_ab = move(send_ab, x_far)
+    kept_c, send_c = sum_1([(after(keep_c, kept_ab), recv_c)], straight)
+    recv_c = move(send_c, x_far)
+    at = after(place, kept_c)
     keep_d, send_d = products(at, last_pairs, fourth + [own_plus, near_plus], 2 * BLOCK, scale, "pairs_4")
     recv_d = move(send_d, x_near)
-    kept_c, send_c = sum_1([(after(keep_c, keep_d), recv_c)], straight)
-    recv_c = move(send_c, x_far)
-    keep_ab, send_ab = sum_2(place, [(after(kept_a, kept_c), recv_a), (kept_b, recv_b)])
+    keep_ab, send_ab = sum_2(place, [(after(kept_ab, keep_d), recv_ab)])
     recv_ab = move(send_ab, yhi_step)
     kept_d, send_d = sum_1([(after(keep_d, keep_ab), recv_d)], [(0, 0, 2 * BLOCK)])
     recv_d = move(send_d, x_far)

time: 106 us -> 105 us (level)
  the two profiles are of different devices: /device:TPU:1 before, /device:TPU:65 now
where the time goes in v7:
time: 105 us
  starting transfers between devices  45.6 us (43%)
  waiting for transfers between devices  38.3 us (36%)
  Pallas kernels  19.8 us (19%)
  local copies, waits for them, and re-layouts  1.31 us (1%)
    ppermute x25, starting transfers between devices, move(): return lax.ppermute(x, AXES, pairs)  45.6 us
    ppermute x25, waiting for transfers between devices, move(): return lax.ppermute(x, AXES, pairs)  38.3 us
    pallas_call x5, Pallas kernels, products(): pl.pallas_call(kernel, in_specs=[pl.BlockSpec(memory_space=pltpu.SMEM)] +...  12.7 us
    pallas_call x9, Pallas kernels, call(): pl.pallas_call(kernel, in_specs=[pl.BlockSpec(memory_space=pltpu.SMEM)] *...  3.94 us
  transfers between devices with their start and end apart: 25, of which 14 were waited for; matrix products, arithmetic and copies ran while one was open for 0% of the time, Pallas kernels for 16%

profile of v7, /device:TPU:65, one launch (start us, length us, event | category | flops | bytes accessed | tf_op | source)
XLA Modules:
  0.0 105.4 jit_solution(11014344742071157843)
XLA Ops:
  0.1 1.2 %copy-done = bf16[2,2,512,256]{3,2,1,0:T(8,128)(2,1)S(1)} copy-done((bf16[2,2,512,256]{3,2,1,0:T(8,128)(2,1)S(1)}, bf16[2,2,512,256]{3,2,1,0:T(8,128)(2,1)}, u32[]{:S(2)}) %copy-start) | copy-done | bytes 1048600
  1.3 0.6 whiten.2.a_ref.refs_2_
  2.0 1.4 %collective-permute-start.1 = (bf16[128,2048]{1,0:T(8,128)(2,1)S(1)}, bf16[128,2048]{1,0:T(8,128)(2,1)S(1)}, u32[]{:S(2)}, u32[]{:S(2)}) collective-permute-start(bf16[128,2048]{1,0:T(8,128)(2,1)S(1)} %whiten.2.a_ref.refs_2_), channel_id=1, source_target_pairs={{0,16},{1,17},{2,18},{3,19},{4,20},{5,21},{6,22},{7,23},{8,24},{9,... | collective-permute-start | bytes 1572872 | tf_op jit(solution)/shard_map/ppermute | solution.py:43
  3.4 0.6 whiten.3.b_ref.refs_3_
  4.1 0.3 collective-permute-start.4
  4.5 1.0 rotate.2
  5.5 5.0 %collective-permute-done.refs_0_ = bf16[128,2048]{1,0:T(8,128)(2,1)S(1)} collective-permute-done((bf16[128,2048]{1,0:T(8,128)(2,1)S(1)}, bf16[128,2048]{1,0:T(8,128)(2,1)S(1)}, u32[]{:S(2)}, u32[]{:S(2)}) %collective-permute-start) | collective-permute-done | bytes 524320 | tf_op jit(solution)/shard_map/ppermute | solution.py:43
  10.5 2.5 %collective-permute-done.1.a_ref.refs_2_ = bf16[128,2048]{1,0:T(8,128)(2,1)S(1)} collective-permute-done((bf16[128,2048]{1,0:T(8,128)(2,1)S(1)}, bf16[128,2048]{1,0:T(8,128)(2,1)S(1)}, u32[]{:S(2)}, u32[]{:S(2)}) %collective-permute-start.1) | collective-permute-done | bytes 524320 | tf_op jit(solution)/shard_map/ppermute | solution.py:43
  13.0 3.1 %collective-permute-done.2.refs_1_ = bf16[128,2048]{1,0:T(8,128)(2,1)S(1)} collective-permute-done((bf16[128,2048]{1,0:T(8,128)(2,1)S(1)}, bf16[128,2048]{1,0:T(8,128)(2,1)S(1)}, u32[]{:S(2)}, u32[]{:S(2)}) %collective-permute-start.2) | collective-permute-done | bytes 524320 | tf_op jit(solution)/shard_map/ppermute | solution.py:43
  16.1 2.4 %pairs_own.1 = (bf16[2,2,2,32,768]{4,3,2,1,0:T(8,128)(2,1)S(1)}, bf16[2,2,2,32,768]{4,3,2,1,0:T(8,128)(2,1)S(1)}) custom-call(s32[5]{0:T(128)S(1)} %stack.23.at_ref.place_ref, bf16[128,2048]{1,0:T(8,128)(2,1)S(1)} %collective-permute-done.refs_0_, bf16[128,2048]{1,0:T(8,128)(2,1)S(1)} %collective-permute-done.2.refs_1_, ...), custom_call_target="tpu_custom_call" | custom-call | flops 1610612736 | bytes 8388608 | tf_op jit(solution)/shard_map/pairs_own/pallas_call | solution.py:147
  18.6 2.6 %collective-permute-start.3 = (bf16[2,2,2,32,768]{4,3,2,1,0:T(8,128)(2,1)S(1)}, bf16[2,2,2,32,768]{4,3,2,1,0:T(8,128)(2,1)S(1)}, u32[]{:S(2)}, u32[]{:S(2)}) collective-permute-start(bf16[2,2,2,32,768]{4,3,2,1,0:T(8,128)(2,1)S(1)} %get-tuple-element.56), channel_id=1, source_target_pairs={{0,2},{1,7},{2,0},{3,5},{4,6},{5,3},{6,4},{7,1},{8,10},{9,15},{10,... | collective-permute-start | bytes 1179656 | tf_op jit(solution)/shard_map/ppermute | solution.py:43
  21.1 5.1 %collective-permute-start.6 = (bf16[128,2048]{1,0:T(8,128)(2,1)S(1)}, bf16[128,2048]{1,0:T(8,128)(2,1)S(1)}, u32[]{:S(2)}, u32[]{:S(2)}) collective-permute-start(bf16[128,2048]{1,0:T(8,128)(2,1)S(1)} %collective-permute-done.2.refs_1_), channel_id=1, source_target_pairs={{0,32},{1,225},{2,34},{3,227},{4,36},{5,229},{6,38},{7,231},{8,40}... | collective-permute-start | bytes 1572872 | tf_op jit(solution)/shard_map/ppermute | solution.py:43
  26.3 1.1 %collective-permute-start.8 = (bf16[128,2048]{1,0:T(8,128)(2,1)S(1)}, bf16[128,2048]{1,0:T(8,128)(2,1)S(1)}, u32[]{:S(2)}, u32[]{:S(2)}) collective-permute-start(bf16[128,2048]{1,0:T(8,128)(2,1)S(1)} %collective-permute-done.5.refs_0_), channel_id=1, source_target_pairs={{0,32},{1,225},{2,34},{3,227},{4,36},{5,229},{6,38},{7,231},{8,40}... | collective-permute-start | bytes 1572872 | tf_op jit(solution)/shard_map/ppermute | solution.py:43
  27.4 1.0 rotate.3
  28.4 2.4 %pairs_near.1 = (bf16[2,2,2,32,768]{4,3,2,1,0:T(8,128)(2,1)S(1)}, bf16[2,2,2,32,768]{4,3,2,1,0:T(8,128)(2,1)S(1)}) custom-call(s32[5]{0:T(128)S(1)} %stack.23.at_ref.place_ref, bf16[128,2048]{1,0:T(8,128)(2,1)S(1)} %collective-permute-done.refs_0_, bf16[128,2048]{1,0:T(8,128)(2,1)S(1)} %collective-permute-done.2.refs_1_, ...), custom_call_target="tpu_custom_call" | custom-call | flops 1610612736 | bytes 8388608 | tf_op jit(solution)/shard_map/pairs_near/pallas_call | solution.py:147
  30.8 1.6 %collective-permute-done.6.refs_1_ = bf16[128,2048]{1,0:T(8,128)(2,1)S(1)} collective-permute-done((bf16[128,2048]{1,0:T(8,128)(2,1)S(1)}, bf16[128,2048]{1,0:T(8,128)(2,1)S(1)}, u32[]{:S(2)}, u32[]{:S(2)}) %collective-permute-start.6) | collective-permute-done | bytes 524320 | tf_op jit(solution)/shard_map/ppermute | solution.py:43
  32.4 2.2 %collective-permute-start.9 = (bf16[128,2048]{1,0:T(8,128)(2,1)S(1)}, bf16[128,2048]{1,0:T(8,128)(2,1)S(1)}, u32[]{:S(2)}, u32[]{:S(2)}) collective-permute-start(bf16[128,2048]{1,0:T(8,128)(2,1)S(1)} %collective-permute-done.6.refs_1_), channel_id=1, source_target_pairs={{0,32},{1,225},{2,34},{3,227},{4,36},{5,229},{6,38},{7,231},{8,40}... | collective-permute-start | bytes 1572872 | tf_op jit(solution)/shard_map/ppermute | solution.py:43
  34.6 2.0 %collective-permute-start.7 = (bf16[2,2,2,32,768]{4,3,2,1,0:T(8,128)(2,1)S(1)}, bf16[2,2,2,32,768]{4,3,2,1,0:T(8,128)(2,1)S(1)}, u32[]{:S(2)}, u32[]{:S(2)}) collective-permute-start(bf16[2,2,2,32,768]{4,3,2,1,0:T(8,128)(2,1)S(1)} %get-tuple-element.63), channel_id=1, source_target_pairs={{0,2},{1,7},{2,0},{3,5},{4,6},{5,3},{6,4},{7,1},{8,10},{9,15},{10,... | collective-permute-start | bytes 1179656 | tf_op jit(solution)/shard_map/ppermute | solution.py:43
  36.6 3.0 %pairs_2.1 = (bf16[2,2,2,32,1024]{4,3,2,1,0:T(8,128)(2,1)S(1)}, bf16[2,2,2,32,1024]{4,3,2,1,0:T(8,128)(2,1)S(1)}) custom-call(s32[5]{0:T(128)S(1)} %stack.23.at_ref.place_ref, bf16[128,2048]{1,0:T(8,128)(2,1)S(1)} %collective-permute-done.5.refs_0_, bf16[128,2048]{1,0:T(8,128)(2,1)S(1)} %collective-permute-done.6.refs_1_, ...), custom_call_target="tpu_custom_call" | custom-call | flops 2147483648 | bytes 8388608 | tf_op jit(solution)/shard_map/pairs_2/pallas_call | solution.py:147
  39.6 2.2 %collective-permute-start.10 = (bf16[128,2048]{1,0:T(8,128)(2,1)S(1)}, bf16[128,2048]{1,0:T(8,128)(2,1)S(1)}, u32[]{:S(2)}, u32[]{:S(2)}) collective-permute-start(bf16[128,2048]{1,0:T(8,128)(2,1)S(1)} %collective-permute-done.8.refs_0_), channel_id=1, source_target_pairs={{0,32},{1,225},{2,34},{3,227},{4,36},{5,229},{6,38},{7,231},{8,40}... | collective-permute-start | bytes 1572872 | tf_op jit(solution)/shard_map/ppermute | solution.py:43
  42.0 0.4 collective-permute-done.7.refs_3_
  42.4 1.2 %collective-permute-done.9.refs_1_ = bf16[128,2048]{1,0:T(8,128)(2,1)S(1)} collective-permute-done((bf16[128,2048]{1,0:T(8,128)(2,1)S(1)}, bf16[128,2048]{1,0:T(8,128)(2,1)S(1)}, u32[]{:S(2)}, u32[]{:S(2)}) %collective-permute-start.9) | collective-permute-done | bytes 524320 | tf_op jit(solution)/shard_map/ppermute | solution.py:43
  43.6 3.0 %pairs_3.1 = (bf16[2,2,2,32,1024]{4,3,2,1,0:T(8,128)(2,1)S(1)}, bf16[2,2,2,32,1024]{4,3,2,1,0:T(8,128)(2,1)S(1)}) custom-call(s32[5]{0:T(128)S(1)} %stack.23.at_ref.place_ref, bf16[128,2048]{1,0:T(8,128)(2,1)S(1)} %collective-permute-done.8.refs_0_, bf16[128,2048]{1,0:T(8,128)(2,1)S(1)} %collective-permute-done.9.refs_1_, ...), custom_call_target="tpu_custom_call" | custom-call | flops 2147483648 | bytes 8388608 | tf_op jit(solution)/shard_map/pairs_3/pallas_call | solution.py:147
  46.6 0.9 collective-permute-start.12
  47.5 2.2 %collective-permute-start.13 = (bf16[128,2048]{1,0:T(8,128)(2,1)S(1)}, bf16[128,2048]{1,0:T(8,128)(2,1)S(1)}, u32[]{:S(2)}, u32[]{:S(2)}) collective-permute-start(bf16[128,2048]{1,0:T(8,128)(2,1)S(1)} %collective-permute-done.9.refs_1_), channel_id=1, source_target_pairs={{0,32},{1,225},{2,34},{3,227},{4,36},{5,229},{6,38},{7,231},{8,40}... | collective-permute-start | bytes 1572872 | tf_op jit(solution)/shard_map/ppermute | solution.py:43
  49.8 1.3 %collective-permute-done.11.refs_5_ = bf16[2,2,2,32,1024]{4,3,2,1,0:T(8,128)(2,1)S(1)} collective-permute-done((bf16[2,2,2,32,1024]{4,3,2,1,0:T(8,128)(2,1)S(1)}, bf16[2,2,2,32,1024]{4,3,2,1,0:T(8,128)(2,1)S(1)}, u32[]{:S(2)}, u32[]{:S(2)}) %collective-permute-start.11) | collective-permute-done | bytes 524320 | tf_op jit(solution)/shard_map/ppermute | solution.py:43
  51.0 0.3 sum_1.3
  51.4 5.2 %collective-permute-done.12.refs_1_ = bf16[2,2,2,32,1024]{4,3,2,1,0:T(8,128)(2,1)S(1)} collective-permute-done((bf16[2,2,2,32,1024]{4,3,2,1,0:T(8,128)(2,1)S(1)}, bf16[2,2,2,32,1024]{4,3,2,1,0:T(8,128)(2,1)S(1)}, u32[]{:S(2)}, u32[]{:S(2)}) %collective-permute-start.12) | collective-permute-done | bytes 524320 | tf_op jit(solution)/shard_map/ppermute | solution.py:43
  56.8 1.9 %pairs_4.1 = (bf16[2,2,2,32,512]{4,3,2,1,0:T(8,128)(2,1)S(1)}, bf16[2,2,2,32,512]{4,3,2,1,0:T(8,128)(2,1)S(1)}) custom-call(s32[5]{0:T(128)S(1)} %stack.23.at_ref.place_ref, bf16[128,2048]{1,0:T(8,128)(2,1)S(1)} %collective-permute-done.10.refs_0_, bf16[128,2048]{1,0:T(8,128)(2,1)S(1)} %collective-permute-done.13.refs_1_, ...), custom_call_target="tpu_custom_call" | custom-call | flops 1073741824 | bytes 8388608 | tf_op jit(solution)/shard_map/pairs_4/pallas_call | solution.py:147
  58.6 1.0 collective-permute-start.16
  59.6 6.2 %collective-permute-done.14.refs_1_ = bf16[2,2,32,2560]{3,2,1,0:T(8,128)(2,1)S(1)} collective-permute-done((bf16[2,2,32,2560]{3,2,1,0:T(8,128)(2,1)S(1)}, bf16[2,2,32,2560]{3,2,1,0:T(8,128)(2,1)S(1)}, u32[]{:S(2)}, u32[]{:S(2)}) %collective-permute-start.14) | collective-permute-done | bytes 655392 | tf_op jit(solution)/shard_map/ppermute | solution.py:43
  65.9 0.7 sum_2.2
  66.6 3.0 %collective-permute-start.18 = (bf16[2,32,2560]{2,1,0:T(8,128)(2,1)S(1)}, bf16[2,32,2560]{2,1,0:T(8,128)(2,1)S(1)}, u32[]{:S(2)}, u32[]{:S(2)}) collective-permute-start(bf16[2,32,2560]{2,1,0:T(8,128)(2,1)S(1)} %get-tuple-element.87), channel_id=1, source_target_pairs={{0,8},{1,9},{2,10},{3,11},{4,12},{5,13},{6,14},{7,15},{8,0},{9,1},... | collective-permute-start | bytes 983048 | tf_op jit(solution)/shard_map/ppermute | solution.py:43
  69.7 0.4 collective-permute-start.17
  70.1 3.8 %collective-permute-done.17.refs_3_ = bf16[2,2,32,512]{3,2,1,0:T(8,128)(2,1)S(1)} collective-permute-done((bf16[2,2,32,512]{3,2,1,0:T(8,128)(2,1)S(1)}, bf16[2,2,32,512]{3,2,1,0:T(8,128)(2,1)S(1)}, u32[]{:S(2)}, u32[]{:S(2)}) %collective-permute-start.17) | collective-permute-done | bytes 131104 | tf_op jit(solution)/shard_map/ppermute | solution.py:43
  73.9 0.6 sum_2.3
  74.5 2.5 %collective-permute-start.21 = (bf16[2,32,1536]{2,1,0:T(8,128)(2,1)S(1)}, bf16[2,32,1536]{2,1,0:T(8,128)(2,1)S(1)}, u32[]{:S(2)}, u32[]{:S(2)}) collective-permute-start(bf16[2,32,1536]{2,1,0:T(8,128)(2,1)S(1)} %get-tuple-element.92), channel_id=1, source_target_pairs={{0,8},{1,9},{2,10},{3,11},{4,12},{5,13},{6,14},{7,15},{8,0},{9,1},... | collective-permute-start | bytes 589832 | tf_op jit(solution)/shard_map/ppermute | solution.py:43
  77.0 0.6 collective-permute-start.19
  77.6 1.2 %collective-permute-start.20 = (bf16[2,32,512]{2,1,0:T(8,128)(2,1)S(1)}, bf16[2,32,512]{2,1,0:T(8,128)(2,1)S(1)}, u32[]{:S(2)}, u32[]{:S(2)}) collective-permute-start(bf16[2,32,512]{2,1,0:T(8,128)(2,1)S(1)} %get-tuple-element.90), channel_id=1, source_target_pairs={{0,192},{1,65},{2,194},{3,67},{4,196},{5,69},{6,198},{7,71},{8,200... | collective-permute-start | bytes 196616 | tf_op jit(solution)/shard_map/ppermute | solution.py:43
  78.7 2.0 %collective-permute-done.19.refs_3_ = bf16[2,32,512]{2,1,0:T(8,128)(2,1)S(1)} collective-permute-done((bf16[2,32,512]{2,1,0:T(8,128)(2,1)S(1)}, bf16[2,32,512]{2,1,0:T(8,128)(2,1)S(1)}, u32[]{:S(2)}, u32[]{:S(2)}) %collective-permute-start.19) | collective-permute-done | bytes 65568 | tf_op jit(solution)/shard_map/ppermute | solution.py:43
  80.7 1.0 collective-permute-done.20.refs_4_
  81.8 1.4 %collective-permute-start.22 = (bf16[2,32,1024]{2,1,0:T(8,128)(2,1)S(1)}, bf16[2,32,1024]{2,1,0:T(8,128)(2,1)S(1)}, u32[]{:S(2)}, u32[]{:S(2)}) collective-permute-start(bf16[2,32,1024]{2,1,0:T(8,128)(2,1)S(1)} %get-tuple-element.95), channel_id=1, source_target_pairs={{0,16},{1,17},{2,18},{3,19},{4,20},{5,21},{6,22},{7,23},{8,24},{9,... | collective-permute-start | bytes 393224 | tf_op jit(solution)/shard_map/ppermute | solution.py:43
  83.2 2.4 %collective-permute-start.23 = (bf16[2,32,512]{2,1,0:T(8,128)(2,1)S(1)}, bf16[2,32,512]{2,1,0:T(8,128)(2,1)S(1)}, u32[]{:S(2)}, u32[]{:S(2)}) collective-permute-start(bf16[2,32,512]{2,1,0:T(8,128)(2,1)S(1)} %get-tuple-element.96), channel_id=1, source_target_pairs={{0,160},{1,97},{2,162},{3,99},{4,164},{5,101},{6,166},{7,103},{8,1... | collective-permute-start | bytes 196616 | tf_op jit(solution)/shard_map/ppermute | solution.py:43
  85.6 3.8 %collective-permute-done.23.refs_5_ = bf16[2,32,512]{2,1,0:T(8,128)(2,1)S(1)} collective-permute-done((bf16[2,32,512]{2,1,0:T(8,128)(2,1)S(1)}, bf16[2,32,512]{2,1,0:T(8,128)(2,1)S(1)}, u32[]{:S(2)}, u32[]{:S(2)}) %collective-permute-start.23) | collective-permute-done | bytes 65568 | tf_op jit(solution)/shard_map/ppermute | solution.py:43
  89.4 0.6 split.1
  90.0 12.7 %collective-permute-start.24 = (bf16[2,16,4096]{2,1,0:T(8,128)(2,1)S(1)}, bf16[2,16,4096]{2,1,0:T(8,128)(2,1)S(1)}, u32[]{:S(2)}, u32[]{:S(2)}) collective-permute-start(bf16[2,16,4096]{2,1,0:T(8,128)(2,1)S(1)} %split.1), channel_id=1, source_target_pairs={{0,1},{1,0},{2,3},{3,2},{4,5},{5,4},{6,7},{7,6},{8,9},{9,8},{10,11... | collective-permute-start | bytes 786440 | tf_op jit(solution)/shard_map/ppermute | solution.py:43
  102.7 1.2 %collective-permute-done.24.refs_6_ = bf16[2,16,4096]{2,1,0:T(8,128)(2,1)S(1)} collective-permute-done((bf16[2,16,4096]{2,1,0:T(8,128)(2,1)S(1)}, bf16[2,16,4096]{2,1,0:T(8,128)(2,1)S(1)}, u32[]{:S(2)}, u32[]{:S(2)}) %collective-permute-start.24) | collective-permute-done | bytes 262176 | tf_op jit(solution)/shard_map/ppermute | solution.py:43
  103.8 1.5 %finish.1 = f32[2,16,4096]{2,1,0:T(8,128)} custom-call(s32[5]{0:T(128)S(1)} %stack.23.at_ref.place_ref, bf16[2,32,1024]{2,1,0:T(8,128)(2,1)S(1)} %get-tuple-element.88.refs_0_, bf16[2,32,512]{2,1,0:T(8,128)(2,1)S(1)} %get-tuple-element.94.refs_1_, bf16[2,32,1024]{2,1,0:T(8,128)(2,1)S(1)} %collective-permute-done.22.refs_2_, ...), custom_call_target="tpu_custom_call" | custom-call | flops 1000 | bytes 10485760 | tf_op jit(solution)/shard_map/finish/pallas_call | solution.py:166
  (28 shorter events, 1.1 us)
Async XLA Ops:
  0.0 4.4 %copy-start.1 = (s32[512]{0:T(512)S(1)}, s32[512]{0:T(512)}, u32[]{:S(2)}) copy-start(s32[512]{0:T(512)} %param.3) | copy-start | bytes 6148
  0.1 1.2 %copy-start = (bf16[2,2,512,256]{3,2,1,0:T(8,128)(2,1)S(1)}, bf16[2,2,512,256]{3,2,1,0:T(8,128)(2,1)}, u32[]{:S(2)}) copy-start(bf16[2,2,512,256]{3,2,1,0:T(8,128)(2,1)} %x_ref.1) | copy-start | bytes 3145732
  1.9 8.6 %collective-permute-start = (bf16[128,2048]{1,0:T(8,128)(2,1)S(1)}, bf16[128,2048]{1,0:T(8,128)(2,1)S(1)}, u32[]{:S(2)}, u32[]{:S(2)}) collective-permute-start(bf16[128,2048]{1,0:T(8,128)(2,1)S(1)} %whiten.2.a_ref.refs_2_), channel_id=1, source_target_pairs={{0,32},{1,225},{2,34},{3,227},{4,36},{5,229},{6,38},{7,231},{8,40}... | collective-permute-start | bytes 1572872 | tf_op jit(solution)/shard_map/ppermute | solution.py:43
  2.0 11.0 %collective-permute-start.1 = (bf16[128,2048]{1,0:T(8,128)(2,1)S(1)}, bf16[128,2048]{1,0:T(8,128)(2,1)S(1)}, u32[]{:S(2)}, u32[]{:S(2)}) collective-permute-start(bf16[128,2048]{1,0:T(8,128)(2,1)S(1)} %whiten.2.a_ref.refs_2_), channel_id=1, source_target_pairs={{0,16},{1,17},{2,18},{3,19},{4,20},{5,21},{6,22},{7,23},{8,24},{9,... | collective-permute-start | bytes 1572872 | tf_op jit(solution)/shard_map/ppermute | solution.py:43
  4.0 12.1 %collective-permute-start.2 = (bf16[128,2048]{1,0:T(8,128)(2,1)S(1)}, bf16[128,2048]{1,0:T(8,128)(2,1)S(1)}, u32[]{:S(2)}, u32[]{:S(2)}) collective-permute-start(bf16[128,2048]{1,0:T(8,128)(2,1)S(1)} %whiten.3.b_ref.refs_3_), channel_id=1, source_target_pairs={{0,32},{1,225},{2,34},{3,227},{4,36},{5,229},{6,38},{7,231},{8,40}... | collective-permute-start | bytes 1572872 | tf_op jit(solution)/shard_map/ppermute | solution.py:43
  4.1 22.2 %collective-permute-start.4 = (bf16[128,2048]{1,0:T(8,128)(2,1)S(1)}, bf16[128,2048]{1,0:T(8,128)(2,1)S(1)}, u32[]{:S(2)}, u32[]{:S(2)}) collective-permute-start(bf16[128,2048]{1,0:T(8,128)(2,1)S(1)} %whiten.3.b_ref.refs_3_), channel_id=1, source_target_pairs={{0,16},{1,17},{2,18},{3,19},{4,20},{5,21},{6,22},{7,23},{8,24},{9,... | collective-permute-start | bytes 1572872 | tf_op jit(solution)/shard_map/ppermute | solution.py:43
  13.0 13.2 %collective-permute-start.5 = (bf16[128,2048]{1,0:T(8,128)(2,1)S(1)}, bf16[128,2048]{1,0:T(8,128)(2,1)S(1)}, u32[]{:S(2)}, u32[]{:S(2)}) collective-permute-start(bf16[128,2048]{1,0:T(8,128)(2,1)S(1)} %collective-permute-done.refs_0_), channel_id=1, source_target_pairs={{0,32},{1,225},{2,34},{3,227},{4,36},{5,229},{6,38},{7,231},{8,40}... | collective-permute-start | bytes 1572872 | tf_op jit(solution)/shard_map/ppermute | solution.py:43
  18.6 9.8 %collective-permute-start.3 = (bf16[2,2,2,32,768]{4,3,2,1,0:T(8,128)(2,1)S(1)}, bf16[2,2,2,32,768]{4,3,2,1,0:T(8,128)(2,1)S(1)}, u32[]{:S(2)}, u32[]{:S(2)}) collective-permute-start(bf16[2,2,2,32,768]{4,3,2,1,0:T(8,128)(2,1)S(1)} %get-tuple-element.56), channel_id=1, source_target_pairs={{0,2},{1,7},{2,0},{3,5},{4,6},{5,3},{6,4},{7,1},{8,10},{9,15},{10,... | collective-permute-start | bytes 1179656 | tf_op jit(solution)/shard_map/ppermute | solution.py:43
  21.1 11.3 %collective-permute-start.6 = (bf16[128,2048]{1,0:T(8,128)(2,1)S(1)}, bf16[128,2048]{1,0:T(8,128)(2,1)S(1)}, u32[]{:S(2)}, u32[]{:S(2)}) collective-permute-start(bf16[128,2048]{1,0:T(8,128)(2,1)S(1)} %collective-permute-done.2.refs_1_), channel_id=1, source_target_pairs={{0,32},{1,225},{2,34},{3,227},{4,36},{5,229},{6,38},{7,231},{8,40}... | collective-permute-start | bytes 1572872 | tf_op jit(solution)/shard_map/ppermute | solution.py:43
  26.3 13.4 %collective-permute-start.8 = (bf16[128,2048]{1,0:T(8,128)(2,1)S(1)}, bf16[128,2048]{1,0:T(8,128)(2,1)S(1)}, u32[]{:S(2)}, u32[]{:S(2)}) collective-permute-start(bf16[128,2048]{1,0:T(8,128)(2,1)S(1)} %collective-permute-done.5.refs_0_), channel_id=1, source_target_pairs={{0,32},{1,225},{2,34},{3,227},{4,36},{5,229},{6,38},{7,231},{8,40}... | collective-permute-start | bytes 1572872 | tf_op jit(solution)/shard_map/ppermute | solution.py:43
  32.4 11.2 %collective-permute-start.9 = (bf16[128,2048]{1,0:T(8,128)(2,1)S(1)}, bf16[128,2048]{1,0:T(8,128)(2,1)S(1)}, u32[]{:S(2)}, u32[]{:S(2)}) collective-permute-start(bf16[128,2048]{1,0:T(8,128)(2,1)S(1)} %collective-permute-done.6.refs_1_), channel_id=1, source_target_pairs={{0,32},{1,225},{2,34},{3,227},{4,36},{5,229},{6,38},{7,231},{8,40}... | collective-permute-start | bytes 1572872 | tf_op jit(solution)/shard_map/ppermute | solution.py:43
  34.6 7.8 %collective-permute-start.7 = (bf16[2,2,2,32,768]{4,3,2,1,0:T(8,128)(2,1)S(1)}, bf16[2,2,2,32,768]{4,3,2,1,0:T(8,128)(2,1)S(1)}, u32[]{:S(2)}, u32[]{:S(2)}) collective-permute-start(bf16[2,2,2,32,768]{4,3,2,1,0:T(8,128)(2,1)S(1)} %get-tuple-element.63), channel_id=1, source_target_pairs={{0,2},{1,7},{2,0},{3,5},{4,6},{5,3},{6,4},{7,1},{8,10},{9,15},{10,... | collective-permute-start | bytes 1179656 | tf_op jit(solution)/shard_map/ppermute | solution.py:43
  39.6 10.2 %collective-permute-start.10 = (bf16[128,2048]{1,0:T(8,128)(2,1)S(1)}, bf16[128,2048]{1,0:T(8,128)(2,1)S(1)}, u32[]{:S(2)}, u32[]{:S(2)}) collective-permute-start(bf16[128,2048]{1,0:T(8,128)(2,1)S(1)} %collective-permute-done.8.refs_0_), channel_id=1, source_target_pairs={{0,32},{1,225},{2,34},{3,227},{4,36},{5,229},{6,38},{7,231},{8,40}... | collective-permute-start | bytes 1572872 | tf_op jit(solution)/shard_map/ppermute | solution.py:43
  41.8 9.2 %collective-permute-start.11 = (bf16[2,2,2,32,1024]{4,3,2,1,0:T(8,128)(2,1)S(1)}, bf16[2,2,2,32,1024]{4,3,2,1,0:T(8,128)(2,1)S(1)}, u32[]{:S(2)}, u32[]{:S(2)}) collective-permute-start(bf16[2,2,2,32,1024]{4,3,2,1,0:T(8,128)(2,1)S(1)} %get-tuple-element.70), channel_id=1, source_target_pairs={{0,2},{1,7},{2,0},{3,5},{4,6},{5,3},{6,4},{7,1},{8,10},{9,15},{10,... | collective-permute-start | bytes 1572872 | tf_op jit(solution)/shard_map/ppermute | solution.py:43
  46.6 10.1 %collective-permute-start.12 = (bf16[2,2,2,32,1024]{4,3,2,1,0:T(8,128)(2,1)S(1)}, bf16[2,2,2,32,1024]{4,3,2,1,0:T(8,128)(2,1)S(1)}, u32[]{:S(2)}, u32[]{:S(2)}) collective-permute-start(bf16[2,2,2,32,1024]{4,3,2,1,0:T(8,128)(2,1)S(1)} %get-tuple-element.73), channel_id=1, source_target_pairs={{0,2},{1,7},{2,0},{3,5},{4,6},{5,3},{6,4},{7,1},{8,10},{9,15},{10,... | collective-permute-start | bytes 1572872 | tf_op jit(solution)/shard_map/ppermute | solution.py:43
  47.5 9.2 %collective-permute-start.13 = (bf16[128,2048]{1,0:T(8,128)(2,1)S(1)}, bf16[128,2048]{1,0:T(8,128)(2,1)S(1)}, u32[]{:S(2)}, u32[]{:S(2)}) collective-permute-start(bf16[128,2048]{1,0:T(8,128)(2,1)S(1)} %collective-permute-done.9.refs_1_), channel_id=1, source_target_pairs={{0,32},{1,225},{2,34},{3,227},{4,36},{5,229},{6,38},{7,231},{8,40}... | collective-permute-start | bytes 1572872 | tf_op jit(solution)/shard_map/ppermute | solution.py:43
  51.3 14.6 %collective-permute-start.14 = (bf16[2,2,32,2560]{3,2,1,0:T(8,128)(2,1)S(1)}, bf16[2,2,32,2560]{3,2,1,0:T(8,128)(2,1)S(1)}, u32[]{:S(2)}, u32[]{:S(2)}) collective-permute-start(bf16[2,2,32,2560]{3,2,1,0:T(8,128)(2,1)S(1)} %get-tuple-element.78), channel_id=1, source_target_pairs={{0,6},{1,3},{2,4},{3,1},{4,2},{5,7},{6,0},{7,5},{8,14},{9,11},{10,... | collective-permute-start | bytes 1966088 | tf_op jit(solution)/shard_map/ppermute | solution.py:43
  58.6 11.0 %collective-permute-start.16 = (bf16[2,2,2,32,512]{4,3,2,1,0:T(8,128)(2,1)S(1)}, bf16[2,2,2,32,512]{4,3,2,1,0:T(8,128)(2,1)S(1)}, u32[]{:S(2)}, u32[]{:S(2)}) collective-permute-start(bf16[2,2,2,32,512]{4,3,2,1,0:T(8,128)(2,1)S(1)} %get-tuple-element.82), channel_id=1, source_target_pairs={{0,2},{1,7},{2,0},{3,5},{4,6},{5,3},{6,4},{7,1},{8,10},{9,15},{10,... | collective-permute-start | bytes 786440 | tf_op jit(solution)/shard_map/ppermute | solution.py:43
  59.6 10.4 %collective-permute-start.15 = (bf16[2,2,32,1024]{3,2,1,0:T(8,128)(2,1)S(1)}, bf16[2,2,32,1024]{3,2,1,0:T(8,128)(2,1)S(1)}, u32[]{:S(2)}, u32[]{:S(2)}) collective-permute-start(bf16[2,2,32,1024]{3,2,1,0:T(8,128)(2,1)S(1)} %get-tuple-element.80), channel_id=1, source_target_pairs={{0,6},{1,3},{2,4},{3,1},{4,2},{5,7},{6,0},{7,5},{8,14},{9,11},{10,... | collective-permute-start | bytes 786440 | tf_op jit(solution)/shard_map/ppermute | solution.py:43
  66.6 10.4 %collective-permute-start.18 = (bf16[2,32,2560]{2,1,0:T(8,128)(2,1)S(1)}, bf16[2,32,2560]{2,1,0:T(8,128)(2,1)S(1)}, u32[]{:S(2)}, u32[]{:S(2)}) collective-permute-start(bf16[2,32,2560]{2,1,0:T(8,128)(2,1)S(1)} %get-tuple-element.87), channel_id=1, source_target_pairs={{0,8},{1,9},{2,10},{3,11},{4,12},{5,13},{6,14},{7,15},{8,0},{9,1},... | collective-permute-start | bytes 983048 | tf_op jit(solution)/shard_map/ppermute | solution.py:43
  69.7 4.2 %collective-permute-start.17 = (bf16[2,2,32,512]{3,2,1,0:T(8,128)(2,1)S(1)}, bf16[2,2,32,512]{3,2,1,0:T(8,128)(2,1)S(1)}, u32[]{:S(2)}, u32[]{:S(2)}) collective-permute-start(bf16[2,2,32,512]{3,2,1,0:T(8,128)(2,1)S(1)} %get-tuple-element.84), channel_id=1, source_target_pairs={{0,6},{1,3},{2,4},{3,1},{4,2},{5,7},{6,0},{7,5},{8,14},{9,11},{10,... | collective-permute-start | bytes 393224 | tf_op jit(solution)/shard_map/ppermute | solution.py:43
  74.5 7.2 %collective-permute-start.21 = (bf16[2,32,1536]{2,1,0:T(8,128)(2,1)S(1)}, bf16[2,32,1536]{2,1,0:T(8,128)(2,1)S(1)}, u32[]{:S(2)}, u32[]{:S(2)}) collective-permute-start(bf16[2,32,1536]{2,1,0:T(8,128)(2,1)S(1)} %get-tuple-element.92), channel_id=1, source_target_pairs={{0,8},{1,9},{2,10},{3,11},{4,12},{5,13},{6,14},{7,15},{8,0},{9,1},... | collective-permute-start | bytes 589832 | tf_op jit(solution)/shard_map/ppermute | solution.py:43
  77.0 3.7 %collective-permute-start.19 = (bf16[2,32,512]{2,1,0:T(8,128)(2,1)S(1)}, bf16[2,32,512]{2,1,0:T(8,128)(2,1)S(1)}, u32[]{:S(2)}, u32[]{:S(2)}) collective-permute-start(bf16[2,32,512]{2,1,0:T(8,128)(2,1)S(1)} %get-tuple-element.89), channel_id=1, source_target_pairs={{0,224},{1,33},{2,226},{3,35},{4,228},{5,37},{6,230},{7,39},{8,232... | collective-permute-start | bytes 196616 | tf_op jit(solution)/shard_map/ppermute | solution.py:43
  77.6 4.1 %collective-permute-start.20 = (bf16[2,32,512]{2,1,0:T(8,128)(2,1)S(1)}, bf16[2,32,512]{2,1,0:T(8,128)(2,1)S(1)}, u32[]{:S(2)}, u32[]{:S(2)}) collective-permute-start(bf16[2,32,512]{2,1,0:T(8,128)(2,1)S(1)} %get-tuple-element.90), channel_id=1, source_target_pairs={{0,192},{1,65},{2,194},{3,67},{4,196},{5,69},{6,198},{7,71},{8,200... | collective-permute-start | bytes 196616 | tf_op jit(solution)/shard_map/ppermute | solution.py:43
  81.8 7.6 %collective-permute-start.22 = (bf16[2,32,1024]{2,1,0:T(8,128)(2,1)S(1)}, bf16[2,32,1024]{2,1,0:T(8,128)(2,1)S(1)}, u32[]{:S(2)}, u32[]{:S(2)}) collective-permute-start(bf16[2,32,1024]{2,1,0:T(8,128)(2,1)S(1)} %get-tuple-element.95), channel_id=1, source_target_pairs={{0,16},{1,17},{2,18},{3,19},{4,20},{5,21},{6,22},{7,23},{8,24},{9,... | collective-permute-start | bytes 393224 | tf_op jit(solution)/shard_map/ppermute | solution.py:43
  83.2 6.2 %collective-permute-start.23 = (bf16[2,32,512]{2,1,0:T(8,128)(2,1)S(1)}, bf16[2,32,512]{2,1,0:T(8,128)(2,1)S(1)}, u32[]{:S(2)}, u32[]{:S(2)}) collective-permute-start(bf16[2,32,512]{2,1,0:T(8,128)(2,1)S(1)} %get-tuple-element.96), channel_id=1, source_target_pairs={{0,160},{1,97},{2,162},{3,99},{4,164},{5,101},{6,166},{7,103},{8,1... | collective-permute-start | bytes 196616 | tf_op jit(solution)/shard_map/ppermute | solution.py:43
  90.0 13.9 %collective-permute-start.24 = (bf16[2,16,4096]{2,1,0:T(8,128)(2,1)S(1)}, bf16[2,16,4096]{2,1,0:T(8,128)(2,1)S(1)}, u32[]{:S(2)}, u32[]{:S(2)}) collective-permute-start(bf16[2,16,4096]{2,1,0:T(8,128)(2,1)S(1)} %split.1), channel_id=1, source_target_pairs={{0,1},{1,0},{2,3},{3,2},{4,5},{5,4},{6,7},{7,6},{8,9},{9,8},{10,11... | collective-permute-start | bytes 786440 | tf_op jit(solution)/shard_map/ppermute | solution.py:43

commit v8 on v7

--- a/solution.py
+++ b/solution.py
@@ -126,7 +126,7 @@
             acc_ref[m, h, x, :, first : first + n] = (value[at : at + 32] * scale).astype(BF16)
 
 
-def products(at, parts, chunks, wide, scale, name):
+def products(at, parts, chunks, wide, scale, name, yhi_first=False):
     count = len(chunks)
 
     def kernel(at_ref, *refs):
@@ -136,13 +136,19 @@
         for m in range(LAGS):
             for first, value in parts(m, ins):
                 store_product(acc_ref, m, first, value, scale)
+        if yhi_first:
+            for out, h in ((keep_ref, at_ref[2]), (send_ref, 1 - at_ref[2])):
+                for k, which in enumerate((x, x ^ far, x ^ near, x ^ 2)):
+                    for m in range(LAGS):
+                        out[k, m] = acc_ref[m, h, which]
+            return
         slices = ((keep_ref, 0, x), (keep_ref, 1, x ^ far), (send_ref, 0, x ^ near), (send_ref, 1, x ^ 2))
         for out, k, which in slices:
             for m in range(LAGS):
                 for h in range(2):
                     out[k, h, m] = acc_ref[m, h, which]
 
-    shape = jax.ShapeDtypeStruct((2, 2, LAGS, 32, wide), BF16)
+    shape = jax.ShapeDtypeStruct((4, LAGS, 32, wide) if yhi_first else (2, 2, LAGS, 32, wide), BF16)
     whole = pl.BlockSpec(memory_space=pltpu.VMEM)
     return pl.pallas_call(
         kernel,
@@ -192,6 +198,34 @@
 
     shape = (2, LAGS, 32, total)
     return call(kernel, None, [r for g in groups for r in g], [(shape, F32), (shape, BF16)], "sum_1")
+
+
+def sum_h(groups):
+    widths = [g[0].shape[3] for g in groups]
+
+    def kernel(*refs):
+        keep_ref, send_ref = refs[-2:]
+        for k in range(2):
+            for m in range(LAGS):
+                first = 0
+                for g, n in enumerate(widths):
+                    keep, recv, cols = refs[2 * g], refs[2 * g + 1], slice(first, first + n)
+                    keep_ref[k, m, :, cols] = keep[k, m].astype(F32) + recv[k, m].astype(F32)
+                    send_ref[k, m, :, cols] = (keep[2 + k, m].astype(F32) + recv[2 + k, m].astype(F32)).astype(BF16)
+                    first += n
+
+    shape = (2, LAGS, 32, sum(widths))
+    return call(kernel, None, [r for g in groups for r in g], [(shape, F32), (shape, BF16)], "sum_h")
+
+
+def sum_n(kept, recv):
+    def kernel(kept_ref, recv_ref, keep_ref, send_ref):
+        for m in range(LAGS):
+            keep_ref[m] = kept_ref[0, m] + recv_ref[0, m].astype(F32)
+            send_ref[m] = (kept_ref[1, m] + recv_ref[1, m].astype(F32)).astype(BF16)
+
+    shape = kept.shape[1:]
+    return call(kernel, None, [kept, recv], [(shape, F32), (shape, BF16)], "sum_n")
 
 
 def sum_2(place, groups):
@@ -360,28 +394,26 @@
     recv_b = move(send_b, x_near)
     fourth = [move(b, chain_step) for b in (after(third[0], keep_b), third[1])]
     at = after(place, keep_b, recv_n)
-    keep_c, send_c = products(at, all_pairs, third + rotated, 4 * BLOCK, scale, "pairs_3")
-    recv_c = move(send_c, x_near)
+    keep_c, send_c = products(at, all_pairs, third + rotated, 4 * BLOCK, scale, "pairs_3", True)
+    recv_c = move(send_c, yhi_step)
     picks = [(0, 0, 2 * BLOCK), (1, 0, BLOCK), (1, BLOCK, BLOCK), (0, 2 * BLOCK, BLOCK), (1, 2 * BLOCK, BLOCK)]
     keep_o = after(keep_o, keep_c, fourth[0])
     kept_ab, send_ab = sum_1([(keep_o, recv_o), (keep_n, recv_n), (keep_b, recv_b)], picks + [(2, 0, 4 * BLOCK)])
     recv_ab = move(send_ab, x_far)
-    kept_c, send_c = sum_1([(after(keep_c, kept_ab), recv_c)], straight)
-    recv_c = move(send_c, x_far)
-    at = after(place, kept_c)
-    keep_d, send_d = products(at, last_pairs, fourth + [own_plus, near_plus], 2 * BLOCK, scale, "pairs_4")
-    recv_d = move(send_d, x_near)
+    at = after(place, kept_ab)
+    keep_d, send_d = products(at, last_pairs, fourth + [own_plus, near_plus], 2 * BLOCK, scale, "pairs_4", True)
+    recv_d = move(send_d, yhi_step)
     keep_ab, send_ab = sum_2(place, [(after(kept_ab, keep_d), recv_ab)])
     recv_ab = move(send_ab, yhi_step)
-    kept_d, send_d = sum_1([(after(keep_d, keep_ab), recv_d)], [(0, 0, 2 * BLOCK)])
-    recv_d = move(send_d, x_far)
-    keep_cd, send_cd = sum_2(place, [(kept_c, recv_c), (kept_d, recv_d)])
-    recv_cd = move(send_cd, yhi_step)
+    kept_cd, send_cd = sum_h([(after(keep_c, keep_ab), recv_c), (keep_d, recv_d)])
+    recv_cd = move(send_cd, x_near)
+    keep_cd, send_cd = sum_n(kept_cd, recv_cd)
+    recv_cd = move(send_cd, x_far)
     outputs = [[(0, 768), (1536, 256)], [(768, 256), (1792, 256)], [(1024, 512)], [(2048, 512)]]
     own_ab, near_ab, ret_1, ret_2 = sum_y(after(keep_ab, keep_cd), recv_ab, outputs)
     ret_1, ret_2 = move(ret_1, back(1)), move(ret_2, back(2))
     outputs = [[(0, 256), (1024, 256)], [(256, 256), (1280, 256)], [(512, 512)]]
-    own_cd, near_all, ret_3 = sum_y(after(keep_cd, ret_1, ret_2), recv_cd, outputs, near_ab)
+    own_cd, near_all, ret_3 = sum_y(after(keep_cd, ret_1), recv_cd, outputs, near_ab)
     ret_3 = move(ret_3, back(3))
     near_all = move(near_all, y_step)
     arrays = [own_ab, own_cd, near_all, ret_1, ret_2, ret_3]

time: 105 us -> 107 us (1.019)
  the two profiles are of different devices: /device:TPU:65 before, /device:TPU:1 now
where the time goes in v8:
time: 107 us; the launch traced here: 106 us
  waiting for transfers between devices  44 us (41%)
  starting transfers between devices  40.8 us (38%)
  Pallas kernels  19.3 us (18%)
  local copies, waits for them, and re-layouts  1.31 us (1%)
    ppermute x24, waiting for transfers between devices, move(): return lax.ppermute(x, AXES, pairs)  44 us
    ppermute x24, starting transfers between devices, move(): return lax.ppermute(x, AXES, pairs)  40.8 us
    pallas_call x5, Pallas kernels, products(): pl.pallas_call(kernel, in_specs=[pl.BlockSpec(memory_space=pltpu.SMEM)] +...  12.7 us
    pallas_call x8, Pallas kernels, call(): pl.pallas_call(kernel, in_specs=[pl.BlockSpec(memory_space=pltpu.SMEM)] *...  3.42 us
  transfers between devices with their start and end apart: 24, of which 13 were waited for; matrix products, arithmetic and copies ran while one was open for 0% of the time, Pallas kernels for 15%

profile of v8, /device:TPU:1, one launch (start us, length us, event | category | flops | bytes accessed | tf_op | source)
XLA Modules:
  0.0 105.7 jit_solution(9537384805056584392)
XLA Ops:
  0.1 1.2 %copy-done = bf16[2,2,512,256]{3,2,1,0:T(8,128)(2,1)S(1)} copy-done((bf16[2,2,512,256]{3,2,1,0:T(8,128)(2,1)S(1)}, bf16[2,2,512,256]{3,2,1,0:T(8,128)(2,1)}, u32[]{:S(2)}) %copy-start) | copy-done | bytes 1048600
  1.3 0.6 whiten.2.a_ref.refs_2_
  1.9 6.5 %collective-permute-start = (bf16[128,2048]{1,0:T(8,128)(2,1)S(1)}, bf16[128,2048]{1,0:T(8,128)(2,1)S(1)}, u32[]{:S(2)}, u32[]{:S(2)}) collective-permute-start(bf16[128,2048]{1,0:T(8,128)(2,1)S(1)} %whiten.2.a_ref.refs_2_), channel_id=1, source_target_pairs={{0,32},{1,225},{2,34},{3,227},{4,36},{5,229},{6,38},{7,231},{8,40}... | collective-permute-start | bytes 1572872 | tf_op jit(solution)/shard_map/ppermute | solution.py:43
  8.4 1.3 %collective-permute-start.1 = (bf16[128,2048]{1,0:T(8,128)(2,1)S(1)}, bf16[128,2048]{1,0:T(8,128)(2,1)S(1)}, u32[]{:S(2)}, u32[]{:S(2)}) collective-permute-start(bf16[128,2048]{1,0:T(8,128)(2,1)S(1)} %whiten.2.a_ref.refs_2_), channel_id=1, source_target_pairs={{0,16},{1,17},{2,18},{3,19},{4,20},{5,21},{6,22},{7,23},{8,24},{9,... | collective-permute-start | bytes 1572872 | tf_op jit(solution)/shard_map/ppermute | solution.py:43
  9.7 0.6 whiten.3.b_ref.refs_3_
  10.3 0.8 collective-permute-start.2
  11.1 0.2 collective-permute-start.4
  11.3 3.2 %collective-permute-done.refs_0_ = bf16[128,2048]{1,0:T(8,128)(2,1)S(1)} collective-permute-done((bf16[128,2048]{1,0:T(8,128)(2,1)S(1)}, bf16[128,2048]{1,0:T(8,128)(2,1)S(1)}, u32[]{:S(2)}, u32[]{:S(2)}) %collective-permute-start) | collective-permute-done | bytes 524320 | tf_op jit(solution)/shard_map/ppermute | solution.py:43
  14.5 7.9 %collective-permute-done.1.a_ref.refs_2_ = bf16[128,2048]{1,0:T(8,128)(2,1)S(1)} collective-permute-done((bf16[128,2048]{1,0:T(8,128)(2,1)S(1)}, bf16[128,2048]{1,0:T(8,128)(2,1)S(1)}, u32[]{:S(2)}, u32[]{:S(2)}) %collective-permute-start.1) | collective-permute-done | bytes 524320 | tf_op jit(solution)/shard_map/ppermute | solution.py:43
  22.4 0.2 collective-permute-start.5
  22.8 1.0 rotate.2
  23.8 2.4 %pairs_own.1 = (bf16[2,2,2,32,768]{4,3,2,1,0:T(8,128)(2,1)S(1)}, bf16[2,2,2,32,768]{4,3,2,1,0:T(8,128)(2,1)S(1)}) custom-call(s32[5]{0:T(128)S(1)} %stack.23.at_ref.place_ref, bf16[128,2048]{1,0:T(8,128)(2,1)S(1)} %collective-permute-done.refs_0_, bf16[128,2048]{1,0:T(8,128)(2,1)S(1)} %collective-permute-done.2.refs_1_, ...), custom_call_target="tpu_custom_call" | custom-call | flops 1610612736 | bytes 8388608 | tf_op jit(solution)/shard_map/pairs_own/pallas_call | solution.py:153
  26.2 2.6 %collective-permute-start.3 = (bf16[2,2,2,32,768]{4,3,2,1,0:T(8,128)(2,1)S(1)}, bf16[2,2,2,32,768]{4,3,2,1,0:T(8,128)(2,1)S(1)}, u32[]{:S(2)}, u32[]{:S(2)}) collective-permute-start(bf16[2,2,2,32,768]{4,3,2,1,0:T(8,128)(2,1)S(1)} %get-tuple-element.53), channel_id=1, source_target_pairs={{0,2},{1,7},{2,0},{3,5},{4,6},{5,3},{6,4},{7,1},{8,10},{9,15},{10,... | collective-permute-start | bytes 1179656 | tf_op jit(solution)/shard_map/ppermute | solution.py:43
  28.8 2.2 %collective-permute-done.4.b_ref.refs_3_ = bf16[128,2048]{1,0:T(8,128)(2,1)S(1)} collective-permute-done((bf16[128,2048]{1,0:T(8,128)(2,1)S(1)}, bf16[128,2048]{1,0:T(8,128)(2,1)S(1)}, u32[]{:S(2)}, u32[]{:S(2)}) %collective-permute-start.4) | collective-permute-done | bytes 524320 | tf_op jit(solution)/shard_map/ppermute | solution.py:43
  31.1 2.8 %collective-permute-start.8 = (bf16[128,2048]{1,0:T(8,128)(2,1)S(1)}, bf16[128,2048]{1,0:T(8,128)(2,1)S(1)}, u32[]{:S(2)}, u32[]{:S(2)}) collective-permute-start(bf16[128,2048]{1,0:T(8,128)(2,1)S(1)} %collective-permute-done.5.refs_0_), channel_id=1, source_target_pairs={{0,32},{1,225},{2,34},{3,227},{4,36},{5,229},{6,38},{7,231},{8,40}... | collective-permute-start | bytes 1572872 | tf_op jit(solution)/shard_map/ppermute | solution.py:43
  33.9 1.0 rotate.3
  34.9 2.4 %pairs_near.1 = (bf16[2,2,2,32,768]{4,3,2,1,0:T(8,128)(2,1)S(1)}, bf16[2,2,2,32,768]{4,3,2,1,0:T(8,128)(2,1)S(1)}) custom-call(s32[5]{0:T(128)S(1)} %stack.23.at_ref.place_ref, bf16[128,2048]{1,0:T(8,128)(2,1)S(1)} %collective-permute-done.refs_0_, bf16[128,2048]{1,0:T(8,128)(2,1)S(1)} %collective-permute-done.2.refs_1_, ...), custom_call_target="tpu_custom_call" | custom-call | flops 1610612736 | bytes 8388608 | tf_op jit(solution)/shard_map/pairs_near/pallas_call | solution.py:153
  37.3 0.7 collective-permute-start.9
  38.1 2.1 %collective-permute-start.7 = (bf16[2,2,2,32,768]{4,3,2,1,0:T(8,128)(2,1)S(1)}, bf16[2,2,2,32,768]{4,3,2,1,0:T(8,128)(2,1)S(1)}, u32[]{:S(2)}, u32[]{:S(2)}) collective-permute-start(bf16[2,2,2,32,768]{4,3,2,1,0:T(8,128)(2,1)S(1)} %get-tuple-element.60), channel_id=1, source_target_pairs={{0,2},{1,7},{2,0},{3,5},{4,6},{5,3},{6,4},{7,1},{8,10},{9,15},{10,... | collective-permute-start | bytes 1179656 | tf_op jit(solution)/shard_map/ppermute | solution.py:43
  40.2 3.0 %pairs_2.1 = (bf16[2,2,2,32,1024]{4,3,2,1,0:T(8,128)(2,1)S(1)}, bf16[2,2,2,32,1024]{4,3,2,1,0:T(8,128)(2,1)S(1)}) custom-call(s32[5]{0:T(128)S(1)} %stack.23.at_ref.place_ref, bf16[128,2048]{1,0:T(8,128)(2,1)S(1)} %collective-permute-done.5.refs_0_, bf16[128,2048]{1,0:T(8,128)(2,1)S(1)} %collective-permute-done.6.refs_1_, ...), custom_call_target="tpu_custom_call" | custom-call | flops 2147483648 | bytes 8388608 | tf_op jit(solution)/shard_map/pairs_2/pallas_call | solution.py:153
  43.2 0.5 collective-permute-start.10
  43.7 1.9 %collective-permute-start.11 = (bf16[2,2,2,32,1024]{4,3,2,1,0:T(8,128)(2,1)S(1)}, bf16[2,2,2,32,1024]{4,3,2,1,0:T(8,128)(2,1)S(1)}, u32[]{:S(2)}, u32[]{:S(2)}) collective-permute-start(bf16[2,2,2,32,1024]{4,3,2,1,0:T(8,128)(2,1)S(1)} %get-tuple-element.67), channel_id=1, source_target_pairs={{0,2},{1,7},{2,0},{3,5},{4,6},{5,3},{6,4},{7,1},{8,10},{9,15},{10,... | collective-permute-start | bytes 1572872 | tf_op jit(solution)/shard_map/ppermute | solution.py:43
  45.6 2.8 %collective-permute-done.9.refs_1_ = bf16[128,2048]{1,0:T(8,128)(2,1)S(1)} collective-permute-done((bf16[128,2048]{1,0:T(8,128)(2,1)S(1)}, bf16[128,2048]{1,0:T(8,128)(2,1)S(1)}, u32[]{:S(2)}, u32[]{:S(2)}) %collective-permute-start.9) | collective-permute-done | bytes 524320 | tf_op jit(solution)/shard_map/ppermute | solution.py:43
  48.4 0.9 collective-permute-start.12
  49.3 3.0 %pairs_3.1 = (bf16[4,2,32,1024]{3,2,1,0:T(8,128)(2,1)S(1)}, bf16[4,2,32,1024]{3,2,1,0:T(8,128)(2,1)S(1)}) custom-call(s32[5]{0:T(128)S(1)} %stack.23.at_ref.place_ref, bf16[128,2048]{1,0:T(8,128)(2,1)S(1)} %collective-permute-done.8.refs_0_, bf16[128,2048]{1,0:T(8,128)(2,1)S(1)} %collective-permute-done.9.refs_1_, ...), custom_call_target="tpu_custom_call" | custom-call | flops 2147483648 | bytes 8388608 | tf_op jit(solution)/shard_map/pairs_3/pallas_call | solution.py:153
  52.3 1.7 %collective-permute-done.10.refs_0_ = bf16[128,2048]{1,0:T(8,128)(2,1)S(1)} collective-permute-done((bf16[128,2048]{1,0:T(8,128)(2,1)S(1)}, bf16[128,2048]{1,0:T(8,128)(2,1)S(1)}, u32[]{:S(2)}, u32[]{:S(2)}) %collective-permute-start.10) | collective-permute-done | bytes 524320 | tf_op jit(solution)/shard_map/ppermute | solution.py:43
  54.0 0.3 sum_1.1
  54.3 0.5 collective-permute-start.13
  54.8 2.9 %collective-permute-start.14 = (bf16[4,2,32,1024]{3,2,1,0:T(8,128)(2,1)S(1)}, bf16[4,2,32,1024]{3,2,1,0:T(8,128)(2,1)S(1)}, u32[]{:S(2)}, u32[]{:S(2)}) collective-permute-start(bf16[4,2,32,1024]{3,2,1,0:T(8,128)(2,1)S(1)} %get-tuple-element.75), channel_id=1, source_target_pairs={{0,8},{1,9},{2,10},{3,11},{4,12},{5,13},{6,14},{7,15},{8,0},{9,1},... | collective-permute-start | bytes 1572872 | tf_op jit(solution)/shard_map/ppermute | solution.py:43
  57.7 1.9 %collective-permute-done.12.refs_1_ = bf16[128,2048]{1,0:T(8,128)(2,1)S(1)} collective-permute-done((bf16[128,2048]{1,0:T(8,128)(2,1)S(1)}, bf16[128,2048]{1,0:T(8,128)(2,1)S(1)}, u32[]{:S(2)}, u32[]{:S(2)}) %collective-permute-start.12) | collective-permute-done | bytes 524320 | tf_op jit(solution)/shard_map/ppermute | solution.py:43
  59.6 1.9 %pairs_4.1 = (bf16[4,2,32,512]{3,2,1,0:T(8,128)(2,1)S(1)}, bf16[4,2,32,512]{3,2,1,0:T(8,128)(2,1)S(1)}) custom-call(s32[5]{0:T(128)S(1)} %stack.23.at_ref.place_ref, bf16[128,2048]{1,0:T(8,128)(2,1)S(1)} %collective-permute-done.10.refs_0_, bf16[128,2048]{1,0:T(8,128)(2,1)S(1)} %collective-permute-done.12.refs_1_, ...), custom_call_target="tpu_custom_call" | custom-call | flops 1073741824 | bytes 8388608 | tf_op jit(solution)/shard_map/pairs_4/pallas_call | solution.py:153
  61.5 3.0 %collective-permute-start.15 = (bf16[4,2,32,512]{3,2,1,0:T(8,128)(2,1)S(1)}, bf16[4,2,32,512]{3,2,1,0:T(8,128)(2,1)S(1)}, u32[]{:S(2)}, u32[]{:S(2)}) collective-permute-start(bf16[4,2,32,512]{3,2,1,0:T(8,128)(2,1)S(1)} %get-tuple-element.76), channel_id=1, source_target_pairs={{0,8},{1,9},{2,10},{3,11},{4,12},{5,13},{6,14},{7,15},{8,0},{9,1},... | collective-permute-start | bytes 786440 | tf_op jit(solution)/shard_map/ppermute | solution.py:43
  64.5 0.7 sum_2.1
  65.2 1.8 %collective-permute-done.14.refs_1_ = bf16[4,2,32,1024]{3,2,1,0:T(8,128)(2,1)S(1)} collective-permute-done((bf16[4,2,32,1024]{3,2,1,0:T(8,128)(2,1)S(1)}, bf16[4,2,32,1024]{3,2,1,0:T(8,128)(2,1)S(1)}, u32[]{:S(2)}, u32[]{:S(2)}) %collective-permute-start.14) | collective-permute-done | bytes 524320 | tf_op jit(solution)/shard_map/ppermute | solution.py:43
  67.0 5.6 %collective-permute-done.15.refs_3_ = bf16[4,2,32,512]{3,2,1,0:T(8,128)(2,1)S(1)} collective-permute-done((bf16[4,2,32,512]{3,2,1,0:T(8,128)(2,1)S(1)}, bf16[4,2,32,512]{3,2,1,0:T(8,128)(2,1)S(1)}, u32[]{:S(2)}, u32[]{:S(2)}) %collective-permute-start.15) | collective-permute-done | bytes 262176 | tf_op jit(solution)/shard_map/ppermute | solution.py:43
  72.6 0.2 sum_h.1
  72.8 2.9 %collective-permute-start.16 = (bf16[2,2,32,1536]{3,2,1,0:T(8,128)(2,1)S(1)}, bf16[2,2,32,1536]{3,2,1,0:T(8,128)(2,1)S(1)}, u32[]{:S(2)}, u32[]{:S(2)}) collective-permute-start(bf16[2,2,32,1536]{3,2,1,0:T(8,128)(2,1)S(1)} %get-tuple-element.78), channel_id=1, source_target_pairs={{0,2},{1,7},{2,0},{3,5},{4,6},{5,3},{6,4},{7,1},{8,10},{9,15},{10,... | collective-permute-start | bytes 1179656 | tf_op jit(solution)/shard_map/ppermute | solution.py:43
  75.7 2.9 %collective-permute-start.17 = (bf16[2,32,2560]{2,1,0:T(8,128)(2,1)S(1)}, bf16[2,32,2560]{2,1,0:T(8,128)(2,1)S(1)}, u32[]{:S(2)}, u32[]{:S(2)}) collective-permute-start(bf16[2,32,2560]{2,1,0:T(8,128)(2,1)S(1)} %get-tuple-element.81), channel_id=1, source_target_pairs={{0,8},{1,9},{2,10},{3,11},{4,12},{5,13},{6,14},{7,15},{8,0},{9,1},... | collective-permute-start | bytes 983048 | tf_op jit(solution)/shard_map/ppermute | solution.py:43
  78.6 2.2 %collective-permute-done.16.recv_ref = bf16[2,2,32,1536]{3,2,1,0:T(8,128)(2,1)S(1)} collective-permute-done((bf16[2,2,32,1536]{3,2,1,0:T(8,128)(2,1)S(1)}, bf16[2,2,32,1536]{3,2,1,0:T(8,128)(2,1)S(1)}, u32[]{:S(2)}, u32[]{:S(2)}) %collective-permute-start.16) | collective-permute-done | bytes 393248 | tf_op jit(solution)/shard_map/ppermute | solution.py:43
  80.9 1.6 %collective-permute-start.19 = (bf16[2,32,1536]{2,1,0:T(8,128)(2,1)S(1)}, bf16[2,32,1536]{2,1,0:T(8,128)(2,1)S(1)}, u32[]{:S(2)}, u32[]{:S(2)}) collective-permute-start(bf16[2,32,1536]{2,1,0:T(8,128)(2,1)S(1)} %get-tuple-element.85), channel_id=1, source_target_pairs={{0,6},{1,3},{2,4},{3,1},{4,2},{5,7},{6,0},{7,5},{8,14},{9,11},{10,... | collective-permute-start | bytes 589832 | tf_op jit(solution)/shard_map/ppermute | solution.py:43
  82.6 1.7 %collective-permute-done.17.refs_1_ = bf16[2,32,2560]{2,1,0:T(8,128)(2,1)S(1)} collective-permute-done((bf16[2,32,2560]{2,1,0:T(8,128)(2,1)S(1)}, bf16[2,32,2560]{2,1,0:T(8,128)(2,1)S(1)}, u32[]{:S(2)}, u32[]{:S(2)}) %collective-permute-start.17) | collective-permute-done | bytes 327712 | tf_op jit(solution)/shard_map/ppermute | solution.py:43
  84.5 4.6 %collective-permute-done.18.refs_3_ = bf16[2,32,512]{2,1,0:T(8,128)(2,1)S(1)} collective-permute-done((bf16[2,32,512]{2,1,0:T(8,128)(2,1)S(1)}, bf16[2,32,512]{2,1,0:T(8,128)(2,1)S(1)}, u32[]{:S(2)}, u32[]{:S(2)}) %collective-permute-start.18) | collective-permute-done | bytes 65568 | tf_op jit(solution)/shard_map/ppermute | solution.py:43
  89.1 1.4 %collective-permute-start.20 = (bf16[2,32,1024]{2,1,0:T(8,128)(2,1)S(1)}, bf16[2,32,1024]{2,1,0:T(8,128)(2,1)S(1)}, u32[]{:S(2)}, u32[]{:S(2)}) collective-permute-start(bf16[2,32,1024]{2,1,0:T(8,128)(2,1)S(1)} %get-tuple-element.88), channel_id=1, source_target_pairs={{0,16},{1,17},{2,18},{3,19},{4,20},{5,21},{6,22},{7,23},{8,24},{9,... | collective-permute-start | bytes 393224 | tf_op jit(solution)/shard_map/ppermute | solution.py:43
  90.5 7.1 %collective-permute-done.21.refs_4_ = bf16[2,32,512]{2,1,0:T(8,128)(2,1)S(1)} collective-permute-done((bf16[2,32,512]{2,1,0:T(8,128)(2,1)S(1)}, bf16[2,32,512]{2,1,0:T(8,128)(2,1)S(1)}, u32[]{:S(2)}, u32[]{:S(2)}) %collective-permute-start.21) | collective-permute-done | bytes 65568 | tf_op jit(solution)/shard_map/ppermute | solution.py:43
  97.6 0.6 split.1
  98.2 4.8 %collective-permute-start.23 = (bf16[2,16,4096]{2,1,0:T(8,128)(2,1)S(1)}, bf16[2,16,4096]{2,1,0:T(8,128)(2,1)S(1)}, u32[]{:S(2)}, u32[]{:S(2)}) collective-permute-start(bf16[2,16,4096]{2,1,0:T(8,128)(2,1)S(1)} %split.1), channel_id=1, source_target_pairs={{0,1},{1,0},{2,3},{3,2},{4,5},{5,4},{6,7},{7,6},{8,9},{9,8},{10,11... | collective-permute-start | bytes 786440 | tf_op jit(solution)/shard_map/ppermute | solution.py:43
  103.0 1.2 %collective-permute-done.23.refs_6_ = bf16[2,16,4096]{2,1,0:T(8,128)(2,1)S(1)} collective-permute-done((bf16[2,16,4096]{2,1,0:T(8,128)(2,1)S(1)}, bf16[2,16,4096]{2,1,0:T(8,128)(2,1)S(1)}, u32[]{:S(2)}, u32[]{:S(2)}) %collective-permute-start.23) | collective-permute-done | bytes 262176 | tf_op jit(solution)/shard_map/ppermute | solution.py:43
  104.1 1.5 %finish.1 = f32[2,16,4096]{2,1,0:T(8,128)} custom-call(s32[5]{0:T(128)S(1)} %stack.23.at_ref.place_ref, bf16[2,32,1024]{2,1,0:T(8,128)(2,1)S(1)} %get-tuple-element.82.refs_0_, bf16[2,32,512]{2,1,0:T(8,128)(2,1)S(1)} %get-tuple-element.87.refs_1_, bf16[2,32,1024]{2,1,0:T(8,128)(2,1)S(1)} %collective-permute-done.20.refs_2_, ...), custom_call_target="tpu_custom_call" | custom-call | flops 1000 | bytes 10485760 | tf_op jit(solution)/shard_map/finish/pallas_call | solution.py:172
  (25 shorter events, 0.6 us)
Async XLA Ops:
  0.0 22.6 %copy-start.1 = (s32[512]{0:T(512)S(1)}, s32[512]{0:T(512)}, u32[]{:S(2)}) copy-start(s32[512]{0:T(512)} %param.3) | copy-start | bytes 6148
  0.1 1.2 %copy-start = (bf16[2,2,512,256]{3,2,1,0:T(8,128)(2,1)S(1)}, bf16[2,2,512,256]{3,2,1,0:T(8,128)(2,1)}, u32[]{:S(2)}) copy-start(bf16[2,2,512,256]{3,2,1,0:T(8,128)(2,1)} %x_ref.1) | copy-start | bytes 3145732
  1.9 12.6 %collective-permute-start = (bf16[128,2048]{1,0:T(8,128)(2,1)S(1)}, bf16[128,2048]{1,0:T(8,128)(2,1)S(1)}, u32[]{:S(2)}, u32[]{:S(2)}) collective-permute-start(bf16[128,2048]{1,0:T(8,128)(2,1)S(1)} %whiten.2.a_ref.refs_2_), channel_id=1, source_target_pairs={{0,32},{1,225},{2,34},{3,227},{4,36},{5,229},{6,38},{7,231},{8,40}... | collective-permute-start | bytes 1572872 | tf_op jit(solution)/shard_map/ppermute | solution.py:43
  8.4 14.0 %collective-permute-start.1 = (bf16[128,2048]{1,0:T(8,128)(2,1)S(1)}, bf16[128,2048]{1,0:T(8,128)(2,1)S(1)}, u32[]{:S(2)}, u32[]{:S(2)}) collective-permute-start(bf16[128,2048]{1,0:T(8,128)(2,1)S(1)} %whiten.2.a_ref.refs_2_), channel_id=1, source_target_pairs={{0,16},{1,17},{2,18},{3,19},{4,20},{5,21},{6,22},{7,23},{8,24},{9,... | collective-permute-start | bytes 1572872 | tf_op jit(solution)/shard_map/ppermute | solution.py:43
  10.3 13.5 %collective-permute-start.2 = (bf16[128,2048]{1,0:T(8,128)(2,1)S(1)}, bf16[128,2048]{1,0:T(8,128)(2,1)S(1)}, u32[]{:S(2)}, u32[]{:S(2)}) collective-permute-start(bf16[128,2048]{1,0:T(8,128)(2,1)S(1)} %whiten.3.b_ref.refs_3_), channel_id=1, source_target_pairs={{0,32},{1,225},{2,34},{3,227},{4,36},{5,229},{6,38},{7,231},{8,40}... | collective-permute-start | bytes 1572872 | tf_op jit(solution)/shard_map/ppermute | solution.py:43
  11.1 19.9 %collective-permute-start.4 = (bf16[128,2048]{1,0:T(8,128)(2,1)S(1)}, bf16[128,2048]{1,0:T(8,128)(2,1)S(1)}, u32[]{:S(2)}, u32[]{:S(2)}) collective-permute-start(bf16[128,2048]{1,0:T(8,128)(2,1)S(1)} %whiten.3.b_ref.refs_3_), channel_id=1, source_target_pairs={{0,16},{1,17},{2,18},{3,19},{4,20},{5,21},{6,22},{7,23},{8,24},{9,... | collective-permute-start | bytes 1572872 | tf_op jit(solution)/shard_map/ppermute | solution.py:43
  22.4 8.6 %collective-permute-start.5 = (bf16[128,2048]{1,0:T(8,128)(2,1)S(1)}, bf16[128,2048]{1,0:T(8,128)(2,1)S(1)}, u32[]{:S(2)}, u32[]{:S(2)}) collective-permute-start(bf16[128,2048]{1,0:T(8,128)(2,1)S(1)} %collective-permute-done.refs_0_), channel_id=1, source_target_pairs={{0,32},{1,225},{2,34},{3,227},{4,36},{5,229},{6,38},{7,231},{8,40}... | collective-permute-start | bytes 1572872 | tf_op jit(solution)/shard_map/ppermute | solution.py:43
  26.2 8.6 %collective-permute-start.3 = (bf16[2,2,2,32,768]{4,3,2,1,0:T(8,128)(2,1)S(1)}, bf16[2,2,2,32,768]{4,3,2,1,0:T(8,128)(2,1)S(1)}, u32[]{:S(2)}, u32[]{:S(2)}) collective-permute-start(bf16[2,2,2,32,768]{4,3,2,1,0:T(8,128)(2,1)S(1)} %get-tuple-element.53), channel_id=1, source_target_pairs={{0,2},{1,7},{2,0},{3,5},{4,6},{5,3},{6,4},{7,1},{8,10},{9,15},{10,... | collective-permute-start | bytes 1179656 | tf_op jit(solution)/shard_map/ppermute | solution.py:43
  28.8 8.5 %collective-permute-start.6 = (bf16[128,2048]{1,0:T(8,128)(2,1)S(1)}, bf16[128,2048]{1,0:T(8,128)(2,1)S(1)}, u32[]{:S(2)}, u32[]{:S(2)}) collective-permute-start(bf16[128,2048]{1,0:T(8,128)(2,1)S(1)} %collective-permute-done.2.refs_1_), channel_id=1, source_target_pairs={{0,32},{1,225},{2,34},{3,227},{4,36},{5,229},{6,38},{7,231},{8,40}... | collective-permute-start | bytes 1572872 | tf_op jit(solution)/shard_map/ppermute | solution.py:43
  31.1 12.1 %collective-permute-start.8 = (bf16[128,2048]{1,0:T(8,128)(2,1)S(1)}, bf16[128,2048]{1,0:T(8,128)(2,1)S(1)}, u32[]{:S(2)}, u32[]{:S(2)}) collective-permute-start(bf16[128,2048]{1,0:T(8,128)(2,1)S(1)} %collective-permute-done.5.refs_0_), channel_id=1, source_target_pairs={{0,32},{1,225},{2,34},{3,227},{4,36},{5,229},{6,38},{7,231},{8,40}... | collective-permute-start | bytes 1572872 | tf_op jit(solution)/shard_map/ppermute | solution.py:43
  37.3 11.0 %collective-permute-start.9 = (bf16[128,2048]{1,0:T(8,128)(2,1)S(1)}, bf16[128,2048]{1,0:T(8,128)(2,1)S(1)}, u32[]{:S(2)}, u32[]{:S(2)}) collective-permute-start(bf16[128,2048]{1,0:T(8,128)(2,1)S(1)} %collective-permute-done.6.refs_1_), channel_id=1, source_target_pairs={{0,32},{1,225},{2,34},{3,227},{4,36},{5,229},{6,38},{7,231},{8,40}... | collective-permute-start | bytes 1572872 | tf_op jit(solution)/shard_map/ppermute | solution.py:43
  38.1 11.2 %collective-permute-start.7 = (bf16[2,2,2,32,768]{4,3,2,1,0:T(8,128)(2,1)S(1)}, bf16[2,2,2,32,768]{4,3,2,1,0:T(8,128)(2,1)S(1)}, u32[]{:S(2)}, u32[]{:S(2)}) collective-permute-start(bf16[2,2,2,32,768]{4,3,2,1,0:T(8,128)(2,1)S(1)} %get-tuple-element.60), channel_id=1, source_target_pairs={{0,2},{1,7},{2,0},{3,5},{4,6},{5,3},{6,4},{7,1},{8,10},{9,15},{10,... | collective-permute-start | bytes 1179656 | tf_op jit(solution)/shard_map/ppermute | solution.py:43
  43.2 10.8 %collective-permute-start.10 = (bf16[128,2048]{1,0:T(8,128)(2,1)S(1)}, bf16[128,2048]{1,0:T(8,128)(2,1)S(1)}, u32[]{:S(2)}, u32[]{:S(2)}) collective-permute-start(bf16[128,2048]{1,0:T(8,128)(2,1)S(1)} %collective-permute-done.8.refs_0_), channel_id=1, source_target_pairs={{0,32},{1,225},{2,34},{3,227},{4,36},{5,229},{6,38},{7,231},{8,40}... | collective-permute-start | bytes 1572872 | tf_op jit(solution)/shard_map/ppermute | solution.py:43
  43.7 10.3 %collective-permute-start.11 = (bf16[2,2,2,32,1024]{4,3,2,1,0:T(8,128)(2,1)S(1)}, bf16[2,2,2,32,1024]{4,3,2,1,0:T(8,128)(2,1)S(1)}, u32[]{:S(2)}, u32[]{:S(2)}) collective-permute-start(bf16[2,2,2,32,1024]{4,3,2,1,0:T(8,128)(2,1)S(1)} %get-tuple-element.67), channel_id=1, source_target_pairs={{0,2},{1,7},{2,0},{3,5},{4,6},{5,3},{6,4},{7,1},{8,10},{9,15},{10,... | collective-permute-start | bytes 1572872 | tf_op jit(solution)/shard_map/ppermute | solution.py:43
  48.4 11.2 %collective-permute-start.12 = (bf16[128,2048]{1,0:T(8,128)(2,1)S(1)}, bf16[128,2048]{1,0:T(8,128)(2,1)S(1)}, u32[]{:S(2)}, u32[]{:S(2)}) collective-permute-start(bf16[128,2048]{1,0:T(8,128)(2,1)S(1)} %collective-permute-done.9.refs_1_), channel_id=1, source_target_pairs={{0,32},{1,225},{2,34},{3,227},{4,36},{5,229},{6,38},{7,231},{8,40}... | collective-permute-start | bytes 1572872 | tf_op jit(solution)/shard_map/ppermute | solution.py:43
  54.3 10.2 %collective-permute-start.13 = (bf16[2,2,32,2560]{3,2,1,0:T(8,128)(2,1)S(1)}, bf16[2,2,32,2560]{3,2,1,0:T(8,128)(2,1)S(1)}, u32[]{:S(2)}, u32[]{:S(2)}) collective-permute-start(bf16[2,2,32,2560]{3,2,1,0:T(8,128)(2,1)S(1)} %get-tuple-element.72), channel_id=1, source_target_pairs={{0,6},{1,3},{2,4},{3,1},{4,2},{5,7},{6,0},{7,5},{8,14},{9,11},{10,... | collective-permute-start | bytes 1966088 | tf_op jit(solution)/shard_map/ppermute | solution.py:43
  54.8 12.2 %collective-permute-start.14 = (bf16[4,2,32,1024]{3,2,1,0:T(8,128)(2,1)S(1)}, bf16[4,2,32,1024]{3,2,1,0:T(8,128)(2,1)S(1)}, u32[]{:S(2)}, u32[]{:S(2)}) collective-permute-start(bf16[4,2,32,1024]{3,2,1,0:T(8,128)(2,1)S(1)} %get-tuple-element.75), channel_id=1, source_target_pairs={{0,8},{1,9},{2,10},{3,11},{4,12},{5,13},{6,14},{7,15},{8,0},{9,1},... | collective-permute-start | bytes 1572872 | tf_op jit(solution)/shard_map/ppermute | solution.py:43
  61.5 11.1 %collective-permute-start.15 = (bf16[4,2,32,512]{3,2,1,0:T(8,128)(2,1)S(1)}, bf16[4,2,32,512]{3,2,1,0:T(8,128)(2,1)S(1)}, u32[]{:S(2)}, u32[]{:S(2)}) collective-permute-start(bf16[4,2,32,512]{3,2,1,0:T(8,128)(2,1)S(1)} %get-tuple-element.76), channel_id=1, source_target_pairs={{0,8},{1,9},{2,10},{3,11},{4,12},{5,13},{6,14},{7,15},{8,0},{9,1},... | collective-permute-start | bytes 786440 | tf_op jit(solution)/shard_map/ppermute | solution.py:43
  72.8 8.1 %collective-permute-start.16 = (bf16[2,2,32,1536]{3,2,1,0:T(8,128)(2,1)S(1)}, bf16[2,2,32,1536]{3,2,1,0:T(8,128)(2,1)S(1)}, u32[]{:S(2)}, u32[]{:S(2)}) collective-permute-start(bf16[2,2,32,1536]{3,2,1,0:T(8,128)(2,1)S(1)} %get-tuple-element.78), channel_id=1, source_target_pairs={{0,2},{1,7},{2,0},{3,5},{4,6},{5,3},{6,4},{7,1},{8,10},{9,15},{10,... | collective-permute-start | bytes 1179656 | tf_op jit(solution)/shard_map/ppermute | solution.py:43
  75.7 8.6 %collective-permute-start.17 = (bf16[2,32,2560]{2,1,0:T(8,128)(2,1)S(1)}, bf16[2,32,2560]{2,1,0:T(8,128)(2,1)S(1)}, u32[]{:S(2)}, u32[]{:S(2)}) collective-permute-start(bf16[2,32,2560]{2,1,0:T(8,128)(2,1)S(1)} %get-tuple-element.81), channel_id=1, source_target_pairs={{0,8},{1,9},{2,10},{3,11},{4,12},{5,13},{6,14},{7,15},{8,0},{9,1},... | collective-permute-start | bytes 983048 | tf_op jit(solution)/shard_map/ppermute | solution.py:43
  80.9 8.1 %collective-permute-start.19 = (bf16[2,32,1536]{2,1,0:T(8,128)(2,1)S(1)}, bf16[2,32,1536]{2,1,0:T(8,128)(2,1)S(1)}, u32[]{:S(2)}, u32[]{:S(2)}) collective-permute-start(bf16[2,32,1536]{2,1,0:T(8,128)(2,1)S(1)} %get-tuple-element.85), channel_id=1, source_target_pairs={{0,6},{1,3},{2,4},{3,1},{4,2},{5,7},{6,0},{7,5},{8,14},{9,11},{10,... | collective-permute-start | bytes 589832 | tf_op jit(solution)/shard_map/ppermute | solution.py:43
  84.4 4.7 %collective-permute-start.18 = (bf16[2,32,512]{2,1,0:T(8,128)(2,1)S(1)}, bf16[2,32,512]{2,1,0:T(8,128)(2,1)S(1)}, u32[]{:S(2)}, u32[]{:S(2)}) collective-permute-start(bf16[2,32,512]{2,1,0:T(8,128)(2,1)S(1)} %get-tuple-element.83), channel_id=1, source_target_pairs={{0,224},{1,33},{2,226},{3,35},{4,228},{5,37},{6,230},{7,39},{8,232... | collective-permute-start | bytes 196616 | tf_op jit(solution)/shard_map/ppermute | solution.py:43
  89.1 8.5 %collective-permute-start.20 = (bf16[2,32,1024]{2,1,0:T(8,128)(2,1)S(1)}, bf16[2,32,1024]{2,1,0:T(8,128)(2,1)S(1)}, u32[]{:S(2)}, u32[]{:S(2)}) collective-permute-start(bf16[2,32,1024]{2,1,0:T(8,128)(2,1)S(1)} %get-tuple-element.88), channel_id=1, source_target_pairs={{0,16},{1,17},{2,18},{3,19},{4,20},{5,21},{6,22},{7,23},{8,24},{9,... | collective-permute-start | bytes 393224 | tf_op jit(solution)/shard_map/ppermute | solution.py:43
  90.5 7.1 %collective-permute-start.21 = (bf16[2,32,512]{2,1,0:T(8,128)(2,1)S(1)}, bf16[2,32,512]{2,1,0:T(8,128)(2,1)S(1)}, u32[]{:S(2)}, u32[]{:S(2)}) collective-permute-start(bf16[2,32,512]{2,1,0:T(8,128)(2,1)S(1)} %get-tuple-element.89), channel_id=1, source_target_pairs={{0,192},{1,65},{2,194},{3,67},{4,196},{5,69},{6,198},{7,71},{8,200... | collective-permute-start | bytes 196616 | tf_op jit(solution)/shard_map/ppermute | solution.py:43
  90.5 7.1 %collective-permute-start.22 = (bf16[2,32,512]{2,1,0:T(8,128)(2,1)S(1)}, bf16[2,32,512]{2,1,0:T(8,128)(2,1)S(1)}, u32[]{:S(2)}, u32[]{:S(2)}) collective-permute-start(bf16[2,32,512]{2,1,0:T(8,128)(2,1)S(1)} %get-tuple-element.90), channel_id=1, source_target_pairs={{0,160},{1,97},{2,162},{3,99},{4,164},{5,101},{6,166},{7,103},{8,1... | collective-permute-start | bytes 196616 | tf_op jit(solution)/shard_map/ppermute | solution.py:43
  98.2 6.0 %collective-permute-start.23 = (bf16[2,16,4096]{2,1,0:T(8,128)(2,1)S(1)}, bf16[2,16,4096]{2,1,0:T(8,128)(2,1)S(1)}, u32[]{:S(2)}, u32[]{:S(2)}) collective-permute-start(bf16[2,16,4096]{2,1,0:T(8,128)(2,1)S(1)} %split.1), channel_id=1, source_target_pairs={{0,1},{1,0},{2,3},{3,2},{4,5},{5,4},{6,7},{7,6},{8,9},{9,8},{10,11... | collective-permute-start | bytes 786440 | tf_op jit(solution)/shard_map/ppermute | solution.py:43

commit v9 on v7

--- a/solution.py
+++ b/solution.py
@@ -126,7 +126,7 @@
             acc_ref[m, h, x, :, first : first + n] = (value[at : at + 32] * scale).astype(BF16)
 
 
-def products(at, parts, chunks, wide, scale, name):
+def products(at, parts, chunks, wide, scale, name, stage="near"):
     count = len(chunks)
 
     def kernel(at_ref, *refs):
@@ -136,13 +136,21 @@
         for m in range(LAGS):
             for first, value in parts(m, ins):
                 store_product(acc_ref, m, first, value, scale)
+        if stage == "yhi":
+            for out, h in ((keep_ref, at_ref[2]), (send_ref, 1 - at_ref[2])):
+                for k, which in enumerate((x, x ^ far, x ^ near, x ^ 2)):
+                    for m in range(LAGS):
+                        out[k, m] = acc_ref[m, h, which]
+            return
+        if stage == "far":
+            near, far = far, near
         slices = ((keep_ref, 0, x), (keep_ref, 1, x ^ far), (send_ref, 0, x ^ near), (send_ref, 1, x ^ 2))
         for out, k, which in slices:
             for m in range(LAGS):
                 for h in range(2):
                     out[k, h, m] = acc_ref[m, h, which]
 
-    shape = jax.ShapeDtypeStruct((2, 2, LAGS, 32, wide), BF16)
+    shape = jax.ShapeDtypeStruct((4, LAGS, 32, wide) if stage == "yhi" else (2, 2, LAGS, 32, wide), BF16)
     whole = pl.BlockSpec(memory_space=pltpu.VMEM)
     return pl.pallas_call(
         kernel,
@@ -194,6 +202,37 @@
     return call(kernel, None, [r for g in groups for r in g], [(shape, F32), (shape, BF16)], "sum_1")
 
 
+def sum_h(keep_c, recv_c, keep_d, recv_d):
+    nc, nd = keep_c.shape[3], keep_d.shape[4]
+
+    def kernel(c_ref, rc_ref, d_ref, rd_ref, keep_ref, send_ref):
+        for k in range(2):
+            for m in range(LAGS):
+                keep_ref[k, m, :, :nc] = c_ref[k, m].astype(F32) + rc_ref[k, m].astype(F32)
+                send_ref[k, m, :, :nc] = (c_ref[2 + k, m].astype(F32) + rc_ref[2 + k, m].astype(F32)).astype(BF16)
+                keep_ref[k, m, :, nc:] = d_ref[0, k, m].astype(F32) + rd_ref[0, k, m].astype(F32)
+                send_ref[k, m, :, nc:] = (d_ref[1, k, m].astype(F32) + rd_ref[1, k, m].astype(F32)).astype(BF16)
+
+    shape = (2, LAGS, 32, nc + nd)
+    return call(kernel, None, [keep_c, recv_c, keep_d, recv_d], [(shape, F32), (shape, BF16)], "sum_h")
+
+
+def sum_n(place, kept, recv, nc):
+    n = kept.shape[3]
+
+    def kernel(place_ref, kept_ref, recv_ref, keep_ref, send_c_ref, send_d_ref):
+        mine, other = place_ref[2], 1 - place_ref[2]
+        c, d = slice(0, nc), slice(nc, n)
+        for m in range(LAGS):
+            keep_ref[m, :, c] = kept_ref[0, m, :, c] + recv_ref[0, m, :, c].astype(F32)
+            send_c_ref[m] = (kept_ref[1, m, :, c] + recv_ref[1, m, :, c].astype(F32)).astype(BF16)
+            keep_ref[m, :, d] = kept_ref[mine, m, :, d] + recv_ref[mine, m, :, d].astype(F32)
+            send_d_ref[m] = (kept_ref[other, m, :, d] + recv_ref[other, m, :, d].astype(F32)).astype(BF16)
+
+    shapes = [((LAGS, 32, n), F32), ((LAGS, 32, nc), BF16), ((LAGS, 32, n - nc), BF16)]
+    return call(kernel, place, [kept, recv], shapes, "sum_n")
+
+
 def sum_2(place, groups):
     widths = [g[0].shape[3] for g in groups]
 
@@ -212,21 +251,23 @@
     return call(kernel, place, [r for g in groups for r in g], [(shape, F32), (shape, BF16)], "sum_2")
 
 
-def sum_y(keep, recv, outputs, extra=None):
-    arrays = [keep, recv] + ([] if extra is None else [extra])
+def sum_y(keep, recvs, outputs, extra=None):
+    arrays = [keep] + list(recvs) + ([] if extra is None else [extra])
     more = 0 if extra is None else extra.shape[2]
+    split_at = recvs[0].shape[2]
 
     def kernel(*refs):
-        keep_ref, recv_ref, outs = refs[0], refs[1], refs[len(arrays) :]
+        keep_ref, outs = refs[0], refs[len(arrays) :]
         for m in range(LAGS):
             for k, (out, picks) in enumerate(zip(outs, outputs)):
                 to = 0
                 if k == 1 and more:
-                    out[m, :, :more] = refs[2][m]
+                    out[m, :, :more] = refs[len(arrays) - 1][m]
                     to = more
                 for first, n in picks:
-                    cols = slice(first, first + n)
-                    out[m, :, to : to + n] = (keep_ref[m, :, cols] + recv_ref[m, :, cols].astype(F32)).astype(BF16)
+                    recv_ref, at = (refs[1], first) if first < split_at else (refs[2], first - split_at)
+                    value = keep_ref[m, :, first : first + n] + recv_ref[m, :, at : at + n].astype(F32)
+                    out[m, :, to : to + n] = value.astype(BF16)
                     to += n
 
     shapes = [((LAGS, 32, sum(n for _, n in p) + (more if k == 1 else 0)), BF16) for k, p in enumerate(outputs)]
@@ -360,25 +401,23 @@
     recv_b = move(send_b, x_near)
     fourth = [move(b, chain_step) for b in (after(third[0], keep_b), third[1])]
     at = after(place, keep_b, recv_n)
-    keep_c, send_c = products(at, all_pairs, third + rotated, 4 * BLOCK, scale, "pairs_3")
-    recv_c = move(send_c, x_near)
+    keep_c, send_c = products(at, all_pairs, third + rotated, 4 * BLOCK, scale, "pairs_3", "yhi")
+    recv_c = move(send_c, yhi_step)
     picks = [(0, 0, 2 * BLOCK), (1, 0, BLOCK), (1, BLOCK, BLOCK), (0, 2 * BLOCK, BLOCK), (1, 2 * BLOCK, BLOCK)]
     keep_o = after(keep_o, keep_c, fourth[0])
     kept_ab, send_ab = sum_1([(keep_o, recv_o), (keep_n, recv_n), (keep_b, recv_b)], picks + [(2, 0, 4 * BLOCK)])
     recv_ab = move(send_ab, x_far)
-    kept_c, send_c = sum_1([(after(keep_c, kept_ab), recv_c)], straight)
-    recv_c = move(send_c, x_far)
-    at = after(place, kept_c)
-    keep_d, send_d = products(at, last_pairs, fourth + [own_plus, near_plus], 2 * BLOCK, scale, "pairs_4")
-    recv_d = move(send_d, x_near)
+    at = after(place, kept_ab)
+    keep_d, send_d = products(at, last_pairs, fourth + [own_plus, near_plus], 2 * BLOCK, scale, "pairs_4", "far")
+    recv_d = move(send_d, x_far)
     keep_ab, send_ab = sum_2(place, [(after(kept_ab, keep_d), recv_ab)])
     recv_ab = move(send_ab, yhi_step)
-    kept_d, send_d = sum_1([(after(keep_d, keep_ab), recv_d)], [(0, 0, 2 * BLOCK)])
-    recv_d = move(send_d, x_far)
-    keep_cd, send_cd = sum_2(place, [(kept_c, recv_c), (kept_d, recv_d)])
-    recv_cd = move(send_cd, yhi_step)
+    kept_cd, send_cd = sum_h(after(keep_c, keep_ab), recv_c, keep_d, recv_d)
+    recv_cd = move(send_cd, x_near)
+    keep_cd, send_c, send_d = sum_n(place, kept_cd, recv_cd, 4 * BLOCK)
+    recv_cd = [move(send_c, x_far), move(send_d, yhi_step)]
     outputs = [[(0, 768), (1536, 256)], [(768, 256), (1792, 256)], [(1024, 512)], [(2048, 512)]]
-    own_ab, near_ab, ret_1, ret_2 = sum_y(after(keep_ab, keep_cd), recv_ab, outputs)
+    own_ab, near_ab, ret_1, ret_2 = sum_y(after(keep_ab, keep_cd), [recv_ab], outputs)
     ret_1, ret_2 = move(ret_1, back(1)), move(ret_2, back(2))
     outputs = [[(0, 256), (1024, 256)], [(256, 256), (1280, 256)], [(512, 512)]]
     own_cd, near_all, ret_3 = sum_y(after(keep_cd, ret_1, ret_2), recv_cd, outputs, near_ab)

time: 105 us -> 105 us (level)
  the two profiles are of different devices: /device:TPU:65 before, /device:TPU:1 now
where the time goes in v9:
time: 105 us
  starting transfers between devices  45.5 us (43%)
  waiting for transfers between devices  38.2 us (36%)
  Pallas kernels  19.8 us (19%)
  local copies, waits for them, and re-layouts  1.31 us (1%)
    ppermute x25, starting transfers between devices, move(): return lax.ppermute(x, AXES, pairs)  45.5 us
    ppermute x25, waiting for transfers between devices, move(): return lax.ppermute(x, AXES, pairs)  38.2 us
    pallas_call x5, Pallas kernels, products(): pl.pallas_call(kernel, in_specs=[pl.BlockSpec(memory_space=pltpu.SMEM)] +...  12.7 us
    pallas_call x8, Pallas kernels, call(): pl.pallas_call(kernel, in_specs=[pl.BlockSpec(memory_space=pltpu.SMEM)] *...  3.96 us
  transfers between devices with their start and end apart: 25, of which 15 were waited for; matrix products, arithmetic and copies ran while one was open for 0% of the time, Pallas kernels for 16%

profile of v9, /device:TPU:1, one launch (start us, length us, event | category | flops | bytes accessed | tf_op | source)
XLA Modules:
  0.0 105.1 jit_solution(15678312185098755258)
XLA Ops:
  0.1 1.2 %copy-done = bf16[2,2,512,256]{3,2,1,0:T(8,128)(2,1)S(1)} copy-done((bf16[2,2,512,256]{3,2,1,0:T(8,128)(2,1)S(1)}, bf16[2,2,512,256]{3,2,1,0:T(8,128)(2,1)}, u32[]{:S(2)}) %copy-start) | copy-done | bytes 1048600
  1.3 0.6 whiten.2.a_ref.refs_2_
  1.9 6.5 %collective-permute-start = (bf16[128,2048]{1,0:T(8,128)(2,1)S(1)}, bf16[128,2048]{1,0:T(8,128)(2,1)S(1)}, u32[]{:S(2)}, u32[]{:S(2)}) collective-permute-start(bf16[128,2048]{1,0:T(8,128)(2,1)S(1)} %whiten.2.a_ref.refs_2_), channel_id=1, source_target_pairs={{0,32},{1,225},{2,34},{3,227},{4,36},{5,229},{6,38},{7,231},{8,40}... | collective-permute-start | bytes 1572872 | tf_op jit(solution)/shard_map/ppermute | solution.py:43
  8.4 1.3 %collective-permute-start.1 = (bf16[128,2048]{1,0:T(8,128)(2,1)S(1)}, bf16[128,2048]{1,0:T(8,128)(2,1)S(1)}, u32[]{:S(2)}, u32[]{:S(2)}) collective-permute-start(bf16[128,2048]{1,0:T(8,128)(2,1)S(1)} %whiten.2.a_ref.refs_2_), channel_id=1, source_target_pairs={{0,16},{1,17},{2,18},{3,19},{4,20},{5,21},{6,22},{7,23},{8,24},{9,... | collective-permute-start | bytes 1572872 | tf_op jit(solution)/shard_map/ppermute | solution.py:43
  9.7 0.6 whiten.3.b_ref.refs_3_
  10.3 0.8 collective-permute-start.2
  11.3 3.2 %collective-permute-done.refs_0_ = bf16[128,2048]{1,0:T(8,128)(2,1)S(1)} collective-permute-done((bf16[128,2048]{1,0:T(8,128)(2,1)S(1)}, bf16[128,2048]{1,0:T(8,128)(2,1)S(1)}, u32[]{:S(2)}, u32[]{:S(2)}) %collective-permute-start) | collective-permute-done | bytes 524320 | tf_op jit(solution)/shard_map/ppermute | solution.py:43
  14.5 7.9 %collective-permute-done.1.a_ref.refs_2_ = bf16[128,2048]{1,0:T(8,128)(2,1)S(1)} collective-permute-done((bf16[128,2048]{1,0:T(8,128)(2,1)S(1)}, bf16[128,2048]{1,0:T(8,128)(2,1)S(1)}, u32[]{:S(2)}, u32[]{:S(2)}) %collective-permute-start.1) | collective-permute-done | bytes 524320 | tf_op jit(solution)/shard_map/ppermute | solution.py:43
  22.8 1.0 rotate.2
  23.8 2.4 %pairs_own.1 = (bf16[2,2,2,32,768]{4,3,2,1,0:T(8,128)(2,1)S(1)}, bf16[2,2,2,32,768]{4,3,2,1,0:T(8,128)(2,1)S(1)}) custom-call(s32[5]{0:T(128)S(1)} %stack.23.at_ref.place_ref, bf16[128,2048]{1,0:T(8,128)(2,1)S(1)} %collective-permute-done.refs_0_, bf16[128,2048]{1,0:T(8,128)(2,1)S(1)} %collective-permute-done.2.refs_1_, ...), custom_call_target="tpu_custom_call" | custom-call | flops 1610612736 | bytes 8388608 | tf_op jit(solution)/shard_map/pairs_own/pallas_call | solution.py:155
  26.2 2.6 %collective-permute-start.3 = (bf16[2,2,2,32,768]{4,3,2,1,0:T(8,128)(2,1)S(1)}, bf16[2,2,2,32,768]{4,3,2,1,0:T(8,128)(2,1)S(1)}, u32[]{:S(2)}, u32[]{:S(2)}) collective-permute-start(bf16[2,2,2,32,768]{4,3,2,1,0:T(8,128)(2,1)S(1)} %get-tuple-element.54), channel_id=1, source_target_pairs={{0,2},{1,7},{2,0},{3,5},{4,6},{5,3},{6,4},{7,1},{8,10},{9,15},{10,... | collective-permute-start | bytes 1179656 | tf_op jit(solution)/shard_map/ppermute | solution.py:43
  28.8 2.2 %collective-permute-done.4.b_ref.refs_3_ = bf16[128,2048]{1,0:T(8,128)(2,1)S(1)} collective-permute-done((bf16[128,2048]{1,0:T(8,128)(2,1)S(1)}, bf16[128,2048]{1,0:T(8,128)(2,1)S(1)}, u32[]{:S(2)}, u32[]{:S(2)}) %collective-permute-start.4) | collective-permute-done | bytes 524320 | tf_op jit(solution)/shard_map/ppermute | solution.py:43
  31.1 2.8 %collective-permute-start.8 = (bf16[128,2048]{1,0:T(8,128)(2,1)S(1)}, bf16[128,2048]{1,0:T(8,128)(2,1)S(1)}, u32[]{:S(2)}, u32[]{:S(2)}) collective-permute-start(bf16[128,2048]{1,0:T(8,128)(2,1)S(1)} %collective-permute-done.5.refs_0_), channel_id=1, source_target_pairs={{0,32},{1,225},{2,34},{3,227},{4,36},{5,229},{6,38},{7,231},{8,40}... | collective-permute-start | bytes 1572872 | tf_op jit(solution)/shard_map/ppermute | solution.py:43
  33.9 1.0 rotate.3
  34.9 2.4 %pairs_near.1 = (bf16[2,2,2,32,768]{4,3,2,1,0:T(8,128)(2,1)S(1)}, bf16[2,2,2,32,768]{4,3,2,1,0:T(8,128)(2,1)S(1)}) custom-call(s32[5]{0:T(128)S(1)} %stack.23.at_ref.place_ref, bf16[128,2048]{1,0:T(8,128)(2,1)S(1)} %collective-permute-done.refs_0_, bf16[128,2048]{1,0:T(8,128)(2,1)S(1)} %collective-permute-done.2.refs_1_, ...), custom_call_target="tpu_custom_call" | custom-call | flops 1610612736 | bytes 8388608 | tf_op jit(solution)/shard_map/pairs_near/pallas_call | solution.py:155
  37.3 0.7 collective-permute-start.9
  38.1 2.1 %collective-permute-start.7 = (bf16[2,2,2,32,768]{4,3,2,1,0:T(8,128)(2,1)S(1)}, bf16[2,2,2,32,768]{4,3,2,1,0:T(8,128)(2,1)S(1)}, u32[]{:S(2)}, u32[]{:S(2)}) collective-permute-start(bf16[2,2,2,32,768]{4,3,2,1,0:T(8,128)(2,1)S(1)} %get-tuple-element.61), channel_id=1, source_target_pairs={{0,2},{1,7},{2,0},{3,5},{4,6},{5,3},{6,4},{7,1},{8,10},{9,15},{10,... | collective-permute-start | bytes 1179656 | tf_op jit(solution)/shard_map/ppermute | solution.py:43
  40.2 3.0 %pairs_2.1 = (bf16[2,2,2,32,1024]{4,3,2,1,0:T(8,128)(2,1)S(1)}, bf16[2,2,2,32,1024]{4,3,2,1,0:T(8,128)(2,1)S(1)}) custom-call(s32[5]{0:T(128)S(1)} %stack.23.at_ref.place_ref, bf16[128,2048]{1,0:T(8,128)(2,1)S(1)} %collective-permute-done.5.refs_0_, bf16[128,2048]{1,0:T(8,128)(2,1)S(1)} %collective-permute-done.6.refs_1_, ...), custom_call_target="tpu_custom_call" | custom-call | flops 2147483648 | bytes 8388608 | tf_op jit(solution)/shard_map/pairs_2/pallas_call | solution.py:155
  43.2 0.5 collective-permute-start.10
  43.7 1.9 %collective-permute-start.11 = (bf16[2,2,2,32,1024]{4,3,2,1,0:T(8,128)(2,1)S(1)}, bf16[2,2,2,32,1024]{4,3,2,1,0:T(8,128)(2,1)S(1)}, u32[]{:S(2)}, u32[]{:S(2)}) collective-permute-start(bf16[2,2,2,32,1024]{4,3,2,1,0:T(8,128)(2,1)S(1)} %get-tuple-element.68), channel_id=1, source_target_pairs={{0,2},{1,7},{2,0},{3,5},{4,6},{5,3},{6,4},{7,1},{8,10},{9,15},{10,... | collective-permute-start | bytes 1572872 | tf_op jit(solution)/shard_map/ppermute | solution.py:43
  45.6 2.8 %collective-permute-done.9.refs_1_ = bf16[128,2048]{1,0:T(8,128)(2,1)S(1)} collective-permute-done((bf16[128,2048]{1,0:T(8,128)(2,1)S(1)}, bf16[128,2048]{1,0:T(8,128)(2,1)S(1)}, u32[]{:S(2)}, u32[]{:S(2)}) %collective-permute-start.9) | collective-permute-done | bytes 524320 | tf_op jit(solution)/shard_map/ppermute | solution.py:43
  48.4 0.9 collective-permute-start.12
  49.3 3.0 %pairs_3.1 = (bf16[4,2,32,1024]{3,2,1,0:T(8,128)(2,1)S(1)}, bf16[4,2,32,1024]{3,2,1,0:T(8,128)(2,1)S(1)}) custom-call(s32[5]{0:T(128)S(1)} %stack.23.at_ref.place_ref, bf16[128,2048]{1,0:T(8,128)(2,1)S(1)} %collective-permute-done.8.refs_0_, bf16[128,2048]{1,0:T(8,128)(2,1)S(1)} %collective-permute-done.9.refs_1_, ...), custom_call_target="tpu_custom_call" | custom-call | flops 2147483648 | bytes 8388608 | tf_op jit(solution)/shard_map/pairs_3/pallas_call | solution.py:155
  52.3 1.7 %collective-permute-done.10.refs_0_ = bf16[128,2048]{1,0:T(8,128)(2,1)S(1)} collective-permute-done((bf16[128,2048]{1,0:T(8,128)(2,1)S(1)}, bf16[128,2048]{1,0:T(8,128)(2,1)S(1)}, u32[]{:S(2)}, u32[]{:S(2)}) %collective-permute-start.10) | collective-permute-done | bytes 524320 | tf_op jit(solution)/shard_map/ppermute | solution.py:43
  54.3 0.5 collective-permute-start.13
  54.8 2.9 %collective-permute-start.14 = (bf16[4,2,32,1024]{3,2,1,0:T(8,128)(2,1)S(1)}, bf16[4,2,32,1024]{3,2,1,0:T(8,128)(2,1)S(1)}, u32[]{:S(2)}, u32[]{:S(2)}) collective-permute-start(bf16[4,2,32,1024]{3,2,1,0:T(8,128)(2,1)S(1)} %get-tuple-element.76), channel_id=1, source_target_pairs={{0,8},{1,9},{2,10},{3,11},{4,12},{5,13},{6,14},{7,15},{8,0},{9,1},... | collective-permute-start | bytes 1572872 | tf_op jit(solution)/shard_map/ppermute | solution.py:43
  57.7 1.9 %collective-permute-done.12.refs_1_ = bf16[128,2048]{1,0:T(8,128)(2,1)S(1)} collective-permute-done((bf16[128,2048]{1,0:T(8,128)(2,1)S(1)}, bf16[128,2048]{1,0:T(8,128)(2,1)S(1)}, u32[]{:S(2)}, u32[]{:S(2)}) %collective-permute-start.12) | collective-permute-done | bytes 524320 | tf_op jit(solution)/shard_map/ppermute | solution.py:43
  59.6 1.9 %pairs_4.1 = (bf16[2,2,2,32,512]{4,3,2,1,0:T(8,128)(2,1)S(1)}, bf16[2,2,2,32,512]{4,3,2,1,0:T(8,128)(2,1)S(1)}) custom-call(s32[5]{0:T(128)S(1)} %stack.23.at_ref.place_ref, bf16[128,2048]{1,0:T(8,128)(2,1)S(1)} %collective-permute-done.10.refs_0_, bf16[128,2048]{1,0:T(8,128)(2,1)S(1)} %collective-permute-done.12.refs_1_, ...), custom_call_target="tpu_custom_call" | custom-call | flops 1073741824 | bytes 8388608 | tf_op jit(solution)/shard_map/pairs_4/pallas_call | solution.py:155
  61.5 0.5 collective-permute-start.15
  62.0 2.1 %collective-permute-done.13.refs_1_ = bf16[2,2,32,2560]{3,2,1,0:T(8,128)(2,1)S(1)} collective-permute-done((bf16[2,2,32,2560]{3,2,1,0:T(8,128)(2,1)S(1)}, bf16[2,2,32,2560]{3,2,1,0:T(8,128)(2,1)S(1)}, u32[]{:S(2)}, u32[]{:S(2)}) %collective-permute-start.13) | collective-permute-done | bytes 655392 | tf_op jit(solution)/shard_map/ppermute | solution.py:43
  64.1 0.7 sum_2.1
  64.8 2.2 %collective-permute-done.14.rc_ref = bf16[4,2,32,1024]{3,2,1,0:T(8,128)(2,1)S(1)} collective-permute-done((bf16[4,2,32,1024]{3,2,1,0:T(8,128)(2,1)S(1)}, bf16[4,2,32,1024]{3,2,1,0:T(8,128)(2,1)S(1)}, u32[]{:S(2)}, u32[]{:S(2)}) %collective-permute-start.14) | collective-permute-done | bytes 524320 | tf_op jit(solution)/shard_map/ppermute | solution.py:43
  67.3 2.8 %collective-permute-start.16 = (bf16[2,2,32,1536]{3,2,1,0:T(8,128)(2,1)S(1)}, bf16[2,2,32,1536]{3,2,1,0:T(8,128)(2,1)S(1)}, u32[]{:S(2)}, u32[]{:S(2)}) collective-permute-start(bf16[2,2,32,1536]{3,2,1,0:T(8,128)(2,1)S(1)} %get-tuple-element.79), channel_id=1, source_target_pairs={{0,2},{1,7},{2,0},{3,5},{4,6},{5,3},{6,4},{7,1},{8,10},{9,15},{10,... | collective-permute-start | bytes 1179656 | tf_op jit(solution)/shard_map/ppermute | solution.py:43
  70.1 2.9 %collective-permute-start.17 = (bf16[2,32,2560]{2,1,0:T(8,128)(2,1)S(1)}, bf16[2,32,2560]{2,1,0:T(8,128)(2,1)S(1)}, u32[]{:S(2)}, u32[]{:S(2)}) collective-permute-start(bf16[2,32,2560]{2,1,0:T(8,128)(2,1)S(1)} %get-tuple-element.82), channel_id=1, source_target_pairs={{0,8},{1,9},{2,10},{3,11},{4,12},{5,13},{6,14},{7,15},{8,0},{9,1},... | collective-permute-start | bytes 983048 | tf_op jit(solution)/shard_map/ppermute | solution.py:43
  73.0 2.2 %collective-permute-done.16.recv_ref = bf16[2,2,32,1536]{3,2,1,0:T(8,128)(2,1)S(1)} collective-permute-done((bf16[2,2,32,1536]{3,2,1,0:T(8,128)(2,1)S(1)}, bf16[2,2,32,1536]{3,2,1,0:T(8,128)(2,1)S(1)}, u32[]{:S(2)}, u32[]{:S(2)}) %collective-permute-start.16) | collective-permute-done | bytes 393248 | tf_op jit(solution)/shard_map/ppermute | solution.py:43
  75.3 0.6 sum_n.1
  75.9 1.6 %collective-permute-start.20 = (bf16[2,32,1024]{2,1,0:T(8,128)(2,1)S(1)}, bf16[2,32,1024]{2,1,0:T(8,128)(2,1)S(1)}, u32[]{:S(2)}, u32[]{:S(2)}) collective-permute-start(bf16[2,32,1024]{2,1,0:T(8,128)(2,1)S(1)} %get-tuple-element.87), channel_id=1, source_target_pairs={{0,6},{1,3},{2,4},{3,1},{4,2},{5,7},{6,0},{7,5},{8,14},{9,11},{10,... | collective-permute-start | bytes 393224 | tf_op jit(solution)/shard_map/ppermute | solution.py:43
  77.5 1.1 %collective-permute-done.17.refs_1_ = bf16[2,32,2560]{2,1,0:T(8,128)(2,1)S(1)} collective-permute-done((bf16[2,32,2560]{2,1,0:T(8,128)(2,1)S(1)}, bf16[2,32,2560]{2,1,0:T(8,128)(2,1)S(1)}, u32[]{:S(2)}, u32[]{:S(2)}) %collective-permute-start.17) | collective-permute-done | bytes 327712 | tf_op jit(solution)/shard_map/ppermute | solution.py:43
  78.8 0.3 collective-permute-start.19
  79.1 3.0 %collective-permute-start.21 = (bf16[2,32,512]{2,1,0:T(8,128)(2,1)S(1)}, bf16[2,32,512]{2,1,0:T(8,128)(2,1)S(1)}, u32[]{:S(2)}, u32[]{:S(2)}) collective-permute-start(bf16[2,32,512]{2,1,0:T(8,128)(2,1)S(1)} %get-tuple-element.88), channel_id=1, source_target_pairs={{0,8},{1,9},{2,10},{3,11},{4,12},{5,13},{6,14},{7,15},{8,0},{9,1},... | collective-permute-start | bytes 196616 | tf_op jit(solution)/shard_map/ppermute | solution.py:43
  82.2 1.0 collective-permute-done.18.refs_3_
  83.1 2.4 %collective-permute-done.19.refs_4_ = bf16[2,32,512]{2,1,0:T(8,128)(2,1)S(1)} collective-permute-done((bf16[2,32,512]{2,1,0:T(8,128)(2,1)S(1)}, bf16[2,32,512]{2,1,0:T(8,128)(2,1)S(1)}, u32[]{:S(2)}, u32[]{:S(2)}) %collective-permute-start.19) | collective-permute-done | bytes 65568 | tf_op jit(solution)/shard_map/ppermute | solution.py:43
  85.6 1.4 %collective-permute-start.22 = (bf16[2,32,1024]{2,1,0:T(8,128)(2,1)S(1)}, bf16[2,32,1024]{2,1,0:T(8,128)(2,1)S(1)}, u32[]{:S(2)}, u32[]{:S(2)}) collective-permute-start(bf16[2,32,1024]{2,1,0:T(8,128)(2,1)S(1)} %get-tuple-element.91), channel_id=1, source_target_pairs={{0,16},{1,17},{2,18},{3,19},{4,20},{5,21},{6,22},{7,23},{8,24},{9,... | collective-permute-start | bytes 393224 | tf_op jit(solution)/shard_map/ppermute | solution.py:43
  87.0 6.1 %collective-permute-done.23.refs_5_ = bf16[2,32,512]{2,1,0:T(8,128)(2,1)S(1)} collective-permute-done((bf16[2,32,512]{2,1,0:T(8,128)(2,1)S(1)}, bf16[2,32,512]{2,1,0:T(8,128)(2,1)S(1)}, u32[]{:S(2)}, u32[]{:S(2)}) %collective-permute-start.23) | collective-permute-done | bytes 65568 | tf_op jit(solution)/shard_map/ppermute | solution.py:43
  93.1 0.6 split.1
  93.7 8.8 %collective-permute-start.24 = (bf16[2,16,4096]{2,1,0:T(8,128)(2,1)S(1)}, bf16[2,16,4096]{2,1,0:T(8,128)(2,1)S(1)}, u32[]{:S(2)}, u32[]{:S(2)}) collective-permute-start(bf16[2,16,4096]{2,1,0:T(8,128)(2,1)S(1)} %split.1), channel_id=1, source_target_pairs={{0,1},{1,0},{2,3},{3,2},{4,5},{5,4},{6,7},{7,6},{8,9},{9,8},{10,11... | collective-permute-start | bytes 786440 | tf_op jit(solution)/shard_map/ppermute | solution.py:43
  102.4 1.2 %collective-permute-done.24.refs_6_ = bf16[2,16,4096]{2,1,0:T(8,128)(2,1)S(1)} collective-permute-done((bf16[2,16,4096]{2,1,0:T(8,128)(2,1)S(1)}, bf16[2,16,4096]{2,1,0:T(8,128)(2,1)S(1)}, u32[]{:S(2)}, u32[]{:S(2)}) %collective-permute-start.24) | collective-permute-done | bytes 262176 | tf_op jit(solution)/shard_map/ppermute | solution.py:43
  103.6 1.5 %finish.1 = f32[2,16,4096]{2,1,0:T(8,128)} custom-call(s32[5]{0:T(128)S(1)} %stack.23.at_ref.place_ref, bf16[2,32,1024]{2,1,0:T(8,128)(2,1)S(1)} %get-tuple-element.83.refs_0_, bf16[2,32,512]{2,1,0:T(8,128)(2,1)S(1)} %get-tuple-element.90.refs_1_, bf16[2,32,1024]{2,1,0:T(8,128)(2,1)S(1)} %collective-permute-done.22.refs_2_, ...), custom_call_target="tpu_custom_call" | custom-call | flops 1000 | bytes 10485760 | tf_op jit(solution)/shard_map/finish/pallas_call | solution.py:174
  (27 shorter events, 1.4 us)
Async XLA Ops:
  0.0 22.6 %copy-start.1 = (s32[512]{0:T(512)S(1)}, s32[512]{0:T(512)}, u32[]{:S(2)}) copy-start(s32[512]{0:T(512)} %param.3) | copy-start | bytes 6148
  0.1 1.2 %copy-start = (bf16[2,2,512,256]{3,2,1,0:T(8,128)(2,1)S(1)}, bf16[2,2,512,256]{3,2,1,0:T(8,128)(2,1)}, u32[]{:S(2)}) copy-start(bf16[2,2,512,256]{3,2,1,0:T(8,128)(2,1)} %x_ref.1) | copy-start | bytes 3145732
  1.9 12.6 %collective-permute-start = (bf16[128,2048]{1,0:T(8,128)(2,1)S(1)}, bf16[128,2048]{1,0:T(8,128)(2,1)S(1)}, u32[]{:S(2)}, u32[]{:S(2)}) collective-permute-start(bf16[128,2048]{1,0:T(8,128)(2,1)S(1)} %whiten.2.a_ref.refs_2_), channel_id=1, source_target_pairs={{0,32},{1,225},{2,34},{3,227},{4,36},{5,229},{6,38},{7,231},{8,40}... | collective-permute-start | bytes 1572872 | tf_op jit(solution)/shard_map/ppermute | solution.py:43
  8.4 14.0 %collective-permute-start.1 = (bf16[128,2048]{1,0:T(8,128)(2,1)S(1)}, bf16[128,2048]{1,0:T(8,128)(2,1)S(1)}, u32[]{:S(2)}, u32[]{:S(2)}) collective-permute-start(bf16[128,2048]{1,0:T(8,128)(2,1)S(1)} %whiten.2.a_ref.refs_2_), channel_id=1, source_target_pairs={{0,16},{1,17},{2,18},{3,19},{4,20},{5,21},{6,22},{7,23},{8,24},{9,... | collective-permute-start | bytes 1572872 | tf_op jit(solution)/shard_map/ppermute | solution.py:43
  10.3 13.5 %collective-permute-start.2 = (bf16[128,2048]{1,0:T(8,128)(2,1)S(1)}, bf16[128,2048]{1,0:T(8,128)(2,1)S(1)}, u32[]{:S(2)}, u32[]{:S(2)}) collective-permute-start(bf16[128,2048]{1,0:T(8,128)(2,1)S(1)} %whiten.3.b_ref.refs_3_), channel_id=1, source_target_pairs={{0,32},{1,225},{2,34},{3,227},{4,36},{5,229},{6,38},{7,231},{8,40}... | collective-permute-start | bytes 1572872 | tf_op jit(solution)/shard_map/ppermute | solution.py:43
  11.1 19.9 %collective-permute-start.4 = (bf16[128,2048]{1,0:T(8,128)(2,1)S(1)}, bf16[128,2048]{1,0:T(8,128)(2,1)S(1)}, u32[]{:S(2)}, u32[]{:S(2)}) collective-permute-start(bf16[128,2048]{1,0:T(8,128)(2,1)S(1)} %whiten.3.b_ref.refs_3_), channel_id=1, source_target_pairs={{0,16},{1,17},{2,18},{3,19},{4,20},{5,21},{6,22},{7,23},{8,24},{9,... | collective-permute-start | bytes 1572872 | tf_op jit(solution)/shard_map/ppermute | solution.py:43
  22.4 8.6 %collective-permute-start.5 = (bf16[128,2048]{1,0:T(8,128)(2,1)S(1)}, bf16[128,2048]{1,0:T(8,128)(2,1)S(1)}, u32[]{:S(2)}, u32[]{:S(2)}) collective-permute-start(bf16[128,2048]{1,0:T(8,128)(2,1)S(1)} %collective-permute-done.refs_0_), channel_id=1, source_target_pairs={{0,32},{1,225},{2,34},{3,227},{4,36},{5,229},{6,38},{7,231},{8,40}... | collective-permute-start | bytes 1572872 | tf_op jit(solution)/shard_map/ppermute | solution.py:43
  26.2 8.6 %collective-permute-start.3 = (bf16[2,2,2,32,768]{4,3,2,1,0:T(8,128)(2,1)S(1)}, bf16[2,2,2,32,768]{4,3,2,1,0:T(8,128)(2,1)S(1)}, u32[]{:S(2)}, u32[]{:S(2)}) collective-permute-start(bf16[2,2,2,32,768]{4,3,2,1,0:T(8,128)(2,1)S(1)} %get-tuple-element.54), channel_id=1, source_target_pairs={{0,2},{1,7},{2,0},{3,5},{4,6},{5,3},{6,4},{7,1},{8,10},{9,15},{10,... | collective-permute-start | bytes 1179656 | tf_op jit(solution)/shard_map/ppermute | solution.py:43
  28.8 8.5 %collective-permute-start.6 = (bf16[128,2048]{1,0:T(8,128)(2,1)S(1)}, bf16[128,2048]{1,0:T(8,128)(2,1)S(1)}, u32[]{:S(2)}, u32[]{:S(2)}) collective-permute-start(bf16[128,2048]{1,0:T(8,128)(2,1)S(1)} %collective-permute-done.2.refs_1_), channel_id=1, source_target_pairs={{0,32},{1,225},{2,34},{3,227},{4,36},{5,229},{6,38},{7,231},{8,40}... | collective-permute-start | bytes 1572872 | tf_op jit(solution)/shard_map/ppermute | solution.py:43
  31.1 12.1 %collective-permute-start.8 = (bf16[128,2048]{1,0:T(8,128)(2,1)S(1)}, bf16[128,2048]{1,0:T(8,128)(2,1)S(1)}, u32[]{:S(2)}, u32[]{:S(2)}) collective-permute-start(bf16[128,2048]{1,0:T(8,128)(2,1)S(1)} %collective-permute-done.5.refs_0_), channel_id=1, source_target_pairs={{0,32},{1,225},{2,34},{3,227},{4,36},{5,229},{6,38},{7,231},{8,40}... | collective-permute-start | bytes 1572872 | tf_op jit(solution)/shard_map/ppermute | solution.py:43
  37.3 11.0 %collective-permute-start.9 = (bf16[128,2048]{1,0:T(8,128)(2,1)S(1)}, bf16[128,2048]{1,0:T(8,128)(2,1)S(1)}, u32[]{:S(2)}, u32[]{:S(2)}) collective-permute-start(bf16[128,2048]{1,0:T(8,128)(2,1)S(1)} %collective-permute-done.6.refs_1_), channel_id=1, source_target_pairs={{0,32},{1,225},{2,34},{3,227},{4,36},{5,229},{6,38},{7,231},{8,40}... | collective-permute-start | bytes 1572872 | tf_op jit(solution)/shard_map/ppermute | solution.py:43
  38.1 11.2 %collective-permute-start.7 = (bf16[2,2,2,32,768]{4,3,2,1,0:T(8,128)(2,1)S(1)}, bf16[2,2,2,32,768]{4,3,2,1,0:T(8,128)(2,1)S(1)}, u32[]{:S(2)}, u32[]{:S(2)}) collective-permute-start(bf16[2,2,2,32,768]{4,3,2,1,0:T(8,128)(2,1)S(1)} %get-tuple-element.61), channel_id=1, source_target_pairs={{0,2},{1,7},{2,0},{3,5},{4,6},{5,3},{6,4},{7,1},{8,10},{9,15},{10,... | collective-permute-start | bytes 1179656 | tf_op jit(solution)/shard_map/ppermute | solution.py:43
  43.2 10.8 %collective-permute-start.10 = (bf16[128,2048]{1,0:T(8,128)(2,1)S(1)}, bf16[128,2048]{1,0:T(8,128)(2,1)S(1)}, u32[]{:S(2)}, u32[]{:S(2)}) collective-permute-start(bf16[128,2048]{1,0:T(8,128)(2,1)S(1)} %collective-permute-done.8.refs_0_), channel_id=1, source_target_pairs={{0,32},{1,225},{2,34},{3,227},{4,36},{5,229},{6,38},{7,231},{8,40}... | collective-permute-start | bytes 1572872 | tf_op jit(solution)/shard_map/ppermute | solution.py:43
  43.7 10.3 %collective-permute-start.11 = (bf16[2,2,2,32,1024]{4,3,2,1,0:T(8,128)(2,1)S(1)}, bf16[2,2,2,32,1024]{4,3,2,1,0:T(8,128)(2,1)S(1)}, u32[]{:S(2)}, u32[]{:S(2)}) collective-permute-start(bf16[2,2,2,32,1024]{4,3,2,1,0:T(8,128)(2,1)S(1)} %get-tuple-element.68), channel_id=1, source_target_pairs={{0,2},{1,7},{2,0},{3,5},{4,6},{5,3},{6,4},{7,1},{8,10},{9,15},{10,... | collective-permute-start | bytes 1572872 | tf_op jit(solution)/shard_map/ppermute | solution.py:43
  48.4 11.2 %collective-permute-start.12 = (bf16[128,2048]{1,0:T(8,128)(2,1)S(1)}, bf16[128,2048]{1,0:T(8,128)(2,1)S(1)}, u32[]{:S(2)}, u32[]{:S(2)}) collective-permute-start(bf16[128,2048]{1,0:T(8,128)(2,1)S(1)} %collective-permute-done.9.refs_1_), channel_id=1, source_target_pairs={{0,32},{1,225},{2,34},{3,227},{4,36},{5,229},{6,38},{7,231},{8,40}... | collective-permute-start | bytes 1572872 | tf_op jit(solution)/shard_map/ppermute | solution.py:43
  54.3 9.8 %collective-permute-start.13 = (bf16[2,2,32,2560]{3,2,1,0:T(8,128)(2,1)S(1)}, bf16[2,2,32,2560]{3,2,1,0:T(8,128)(2,1)S(1)}, u32[]{:S(2)}, u32[]{:S(2)}) collective-permute-start(bf16[2,2,32,2560]{3,2,1,0:T(8,128)(2,1)S(1)} %get-tuple-element.73), channel_id=1, source_target_pairs={{0,6},{1,3},{2,4},{3,1},{4,2},{5,7},{6,0},{7,5},{8,14},{9,11},{10,... | collective-permute-start | bytes 1966088 | tf_op jit(solution)/shard_map/ppermute | solution.py:43
  54.8 12.2 %collective-permute-start.14 = (bf16[4,2,32,1024]{3,2,1,0:T(8,128)(2,1)S(1)}, bf16[4,2,32,1024]{3,2,1,0:T(8,128)(2,1)S(1)}, u32[]{:S(2)}, u32[]{:S(2)}) collective-permute-start(bf16[4,2,32,1024]{3,2,1,0:T(8,128)(2,1)S(1)} %get-tuple-element.76), channel_id=1, source_target_pairs={{0,8},{1,9},{2,10},{3,11},{4,12},{5,13},{6,14},{7,15},{8,0},{9,1},... | collective-permute-start | bytes 1572872 | tf_op jit(solution)/shard_map/ppermute | solution.py:43
  61.5 5.6 %collective-permute-start.15 = (bf16[2,2,2,32,512]{4,3,2,1,0:T(8,128)(2,1)S(1)}, bf16[2,2,2,32,512]{4,3,2,1,0:T(8,128)(2,1)S(1)}, u32[]{:S(2)}, u32[]{:S(2)}) collective-permute-start(bf16[2,2,2,32,512]{4,3,2,1,0:T(8,128)(2,1)S(1)} %get-tuple-element.77), channel_id=1, source_target_pairs={{0,6},{1,3},{2,4},{3,1},{4,2},{5,7},{6,0},{7,5},{8,14},{9,11},{10,... | collective-permute-start | bytes 786440 | tf_op jit(solution)/shard_map/ppermute | solution.py:43
  67.3 8.0 %collective-permute-start.16 = (bf16[2,2,32,1536]{3,2,1,0:T(8,128)(2,1)S(1)}, bf16[2,2,32,1536]{3,2,1,0:T(8,128)(2,1)S(1)}, u32[]{:S(2)}, u32[]{:S(2)}) collective-permute-start(bf16[2,2,32,1536]{3,2,1,0:T(8,128)(2,1)S(1)} %get-tuple-element.79), channel_id=1, source_target_pairs={{0,2},{1,7},{2,0},{3,5},{4,6},{5,3},{6,4},{7,1},{8,10},{9,15},{10,... | collective-permute-start | bytes 1179656 | tf_op jit(solution)/shard_map/ppermute | solution.py:43
  70.1 8.6 %collective-permute-start.17 = (bf16[2,32,2560]{2,1,0:T(8,128)(2,1)S(1)}, bf16[2,32,2560]{2,1,0:T(8,128)(2,1)S(1)}, u32[]{:S(2)}, u32[]{:S(2)}) collective-permute-start(bf16[2,32,2560]{2,1,0:T(8,128)(2,1)S(1)} %get-tuple-element.82), channel_id=1, source_target_pairs={{0,8},{1,9},{2,10},{3,11},{4,12},{5,13},{6,14},{7,15},{8,0},{9,1},... | collective-permute-start | bytes 983048 | tf_op jit(solution)/shard_map/ppermute | solution.py:43
  75.9 9.6 %collective-permute-start.20 = (bf16[2,32,1024]{2,1,0:T(8,128)(2,1)S(1)}, bf16[2,32,1024]{2,1,0:T(8,128)(2,1)S(1)}, u32[]{:S(2)}, u32[]{:S(2)}) collective-permute-start(bf16[2,32,1024]{2,1,0:T(8,128)(2,1)S(1)} %get-tuple-element.87), channel_id=1, source_target_pairs={{0,6},{1,3},{2,4},{3,1},{4,2},{5,7},{6,0},{7,5},{8,14},{9,11},{10,... | collective-permute-start | bytes 393224 | tf_op jit(solution)/shard_map/ppermute | solution.py:43
  78.7 4.4 %collective-permute-start.18 = (bf16[2,32,512]{2,1,0:T(8,128)(2,1)S(1)}, bf16[2,32,512]{2,1,0:T(8,128)(2,1)S(1)}, u32[]{:S(2)}, u32[]{:S(2)}) collective-permute-start(bf16[2,32,512]{2,1,0:T(8,128)(2,1)S(1)} %get-tuple-element.84), channel_id=1, source_target_pairs={{0,224},{1,33},{2,226},{3,35},{4,228},{5,37},{6,230},{7,39},{8,232... | collective-permute-start | bytes 196616 | tf_op jit(solution)/shard_map/ppermute | solution.py:43
  78.8 6.7 %collective-permute-start.19 = (bf16[2,32,512]{2,1,0:T(8,128)(2,1)S(1)}, bf16[2,32,512]{2,1,0:T(8,128)(2,1)S(1)}, u32[]{:S(2)}, u32[]{:S(2)}) collective-permute-start(bf16[2,32,512]{2,1,0:T(8,128)(2,1)S(1)} %get-tuple-element.85), channel_id=1, source_target_pairs={{0,192},{1,65},{2,194},{3,67},{4,196},{5,69},{6,198},{7,71},{8,200... | collective-permute-start | bytes 196616 | tf_op jit(solution)/shard_map/ppermute | solution.py:43
  79.1 6.4 %collective-permute-start.21 = (bf16[2,32,512]{2,1,0:T(8,128)(2,1)S(1)}, bf16[2,32,512]{2,1,0:T(8,128)(2,1)S(1)}, u32[]{:S(2)}, u32[]{:S(2)}) collective-permute-start(bf16[2,32,512]{2,1,0:T(8,128)(2,1)S(1)} %get-tuple-element.88), channel_id=1, source_target_pairs={{0,8},{1,9},{2,10},{3,11},{4,12},{5,13},{6,14},{7,15},{8,0},{9,1},... | collective-permute-start | bytes 196616 | tf_op jit(solution)/shard_map/ppermute | solution.py:43
  85.6 7.5 %collective-permute-start.22 = (bf16[2,32,1024]{2,1,0:T(8,128)(2,1)S(1)}, bf16[2,32,1024]{2,1,0:T(8,128)(2,1)S(1)}, u32[]{:S(2)}, u32[]{:S(2)}) collective-permute-start(bf16[2,32,1024]{2,1,0:T(8,128)(2,1)S(1)} %get-tuple-element.91), channel_id=1, source_target_pairs={{0,16},{1,17},{2,18},{3,19},{4,20},{5,21},{6,22},{7,23},{8,24},{9,... | collective-permute-start | bytes 393224 | tf_op jit(solution)/shard_map/ppermute | solution.py:43
  87.0 6.1 %collective-permute-start.23 = (bf16[2,32,512]{2,1,0:T(8,128)(2,1)S(1)}, bf16[2,32,512]{2,1,0:T(8,128)(2,1)S(1)}, u32[]{:S(2)}, u32[]{:S(2)}) collective-permute-start(bf16[2,32,512]{2,1,0:T(8,128)(2,1)S(1)} %get-tuple-element.92), channel_id=1, source_target_pairs={{0,160},{1,97},{2,162},{3,99},{4,164},{5,101},{6,166},{7,103},{8,1... | collective-permute-start | bytes 196616 | tf_op jit(solution)/shard_map/ppermute | solution.py:43
  93.7 9.9 %collective-permute-start.24 = (bf16[2,16,4096]{2,1,0:T(8,128)(2,1)S(1)}, bf16[2,16,4096]{2,1,0:T(8,128)(2,1)S(1)}, u32[]{:S(2)}, u32[]{:S(2)}) collective-permute-start(bf16[2,16,4096]{2,1,0:T(8,128)(2,1)S(1)} %split.1), channel_id=1, source_target_pairs={{0,1},{1,0},{2,3},{3,2},{4,5},{5,4},{6,7},{7,6},{8,9},{9,8},{10,11... | collective-permute-start | bytes 786440 | tf_op jit(solution)/shard_map/ppermute | solution.py:43

commit v10 on v9

--- a/solution.py
+++ b/solution.py
@@ -351,8 +351,7 @@
     own = [whiten(spectra, 0), whiten(spectra, 1)]
     near = [move(b, y_step) for b in own]
     first = [move(b, chain_step) for b in own]
-    first[0] = after(first[0], near[0])
-    second = [move(b, chain_step) for b in first]
+    second = [move(b, chain_step) for b in (first[0], first[1])]
 
     cosine, sine = phases(bin_index)
     own_plus, own_minus = rotations(own, cosine, sine)
@@ -390,7 +389,7 @@
 
     keep_o, send_o = products(place, own_pairs, first + own + rotated[:2], 3 * BLOCK, scale, "pairs_own")
     recv_o = move(send_o, x_near)
-    third = [move(after(second[0], near[1], keep_o), chain_step)]
+    third = [move(after(second[0], near[0], near[1], keep_o), chain_step)]
     at = after(place, recv_o)
     near_rotated = [own_plus, near_plus, near_minus]
     keep_n, send_n = products(at, near_pairs, first + near + near_rotated, 3 * BLOCK, scale, "pairs_near")

time: 105 us -> 105 us (level); the launches traced: 105 us -> 104 us
  waiting for transfers between devices: 38.2 us -> 35 us
  starting transfers between devices: 45.5 us -> 47.4 us
    ppermute x25, waiting for transfers between devices: 38.2 us -> 35 us  [move(): return lax.ppermute(x, AXES, pairs)]
    ppermute x25, starting transfers between devices: 45.5 us -> 47.4 us  [move(): return lax.ppermute(x, AXES, pairs)]
where the time goes in v10:
time: 105 us; the launch traced here: 104 us
  starting transfers between devices  47.4 us (45%)
  waiting for transfers between devices  35 us (33%)
  Pallas kernels  19.8 us (19%)
  local copies, waits for them, and re-layouts  1.31 us (1%)
    ppermute x25, starting transfers between devices, move(): return lax.ppermute(x, AXES, pairs)  47.4 us
    ppermute x25, waiting for transfers between devices, move(): return lax.ppermute(x, AXES, pairs)  35 us
    pallas_call x5, Pallas kernels, products(): pl.pallas_call(kernel, in_specs=[pl.BlockSpec(memory_space=pltpu.SMEM)] +...  12.7 us
    pallas_call x8, Pallas kernels, call(): pl.pallas_call(kernel, in_specs=[pl.BlockSpec(memory_space=pltpu.SMEM)] *...  3.96 us
  transfers between devices with their start and end apart: 25, of which 15 were waited for; matrix products, arithmetic and copies ran while one was open for 0% of the time, Pallas kernels for 16%

profile of v10, /device:TPU:1, one launch (start us, length us, event | category | flops | bytes accessed | tf_op | source)
XLA Modules:
  0.0 103.8 jit_solution(11894226387463778204)
XLA Ops:
  0.1 1.2 %copy-done = bf16[2,2,512,256]{3,2,1,0:T(8,128)(2,1)S(1)} copy-done((bf16[2,2,512,256]{3,2,1,0:T(8,128)(2,1)S(1)}, bf16[2,2,512,256]{3,2,1,0:T(8,128)(2,1)}, u32[]{:S(2)}) %copy-start) | copy-done | bytes 1048600
  1.3 0.6 whiten.2.a_ref.refs_2_
  1.9 6.5 %collective-permute-start = (bf16[128,2048]{1,0:T(8,128)(2,1)S(1)}, bf16[128,2048]{1,0:T(8,128)(2,1)S(1)}, u32[]{:S(2)}, u32[]{:S(2)}) collective-permute-start(bf16[128,2048]{1,0:T(8,128)(2,1)S(1)} %whiten.2.a_ref.refs_2_), channel_id=1, source_target_pairs={{0,32},{1,225},{2,34},{3,227},{4,36},{5,229},{6,38},{7,231},{8,40}... | collective-permute-start | bytes 1572872 | tf_op jit(solution)/shard_map/ppermute | solution.py:43
  8.4 0.6 whiten.3.b_ref.refs_3_
  9.0 0.8 collective-permute-start.1
  9.8 1.3 %collective-permute-start.3 = (bf16[128,2048]{1,0:T(8,128)(2,1)S(1)}, bf16[128,2048]{1,0:T(8,128)(2,1)S(1)}, u32[]{:S(2)}, u32[]{:S(2)}) collective-permute-start(bf16[128,2048]{1,0:T(8,128)(2,1)S(1)} %whiten.2.a_ref.refs_2_), channel_id=1, source_target_pairs={{0,16},{1,17},{2,18},{3,19},{4,20},{5,21},{6,22},{7,23},{8,24},{9,... | collective-permute-start | bytes 1572872 | tf_op jit(solution)/shard_map/ppermute | solution.py:43
  11.3 3.2 %collective-permute-done.refs_0_ = bf16[128,2048]{1,0:T(8,128)(2,1)S(1)} collective-permute-done((bf16[128,2048]{1,0:T(8,128)(2,1)S(1)}, bf16[128,2048]{1,0:T(8,128)(2,1)S(1)}, u32[]{:S(2)}, u32[]{:S(2)}) %collective-permute-start) | collective-permute-done | bytes 524320 | tf_op jit(solution)/shard_map/ppermute | solution.py:43
  14.5 3.1 %collective-permute-start.5 = (bf16[128,2048]{1,0:T(8,128)(2,1)S(1)}, bf16[128,2048]{1,0:T(8,128)(2,1)S(1)}, u32[]{:S(2)}, u32[]{:S(2)}) collective-permute-start(bf16[128,2048]{1,0:T(8,128)(2,1)S(1)} %collective-permute-done.refs_0_), channel_id=1, source_target_pairs={{0,32},{1,225},{2,34},{3,227},{4,36},{5,229},{6,38},{7,231},{8,40}... | collective-permute-start | bytes 1572872 | tf_op jit(solution)/shard_map/ppermute | solution.py:43
  17.8 1.0 rotate.2
  18.8 1.4 %collective-permute-done.1.refs_1_ = bf16[128,2048]{1,0:T(8,128)(2,1)S(1)} collective-permute-done((bf16[128,2048]{1,0:T(8,128)(2,1)S(1)}, bf16[128,2048]{1,0:T(8,128)(2,1)S(1)}, u32[]{:S(2)}, u32[]{:S(2)}) %collective-permute-start.1) | collective-permute-done | bytes 524320 | tf_op jit(solution)/shard_map/ppermute | solution.py:43
  20.2 2.4 %pairs_own.1 = (bf16[2,2,2,32,768]{4,3,2,1,0:T(8,128)(2,1)S(1)}, bf16[2,2,2,32,768]{4,3,2,1,0:T(8,128)(2,1)S(1)}) custom-call(s32[5]{0:T(128)S(1)} %stack.23.at_ref.place_ref, bf16[128,2048]{1,0:T(8,128)(2,1)S(1)} %collective-permute-done.refs_0_, bf16[128,2048]{1,0:T(8,128)(2,1)S(1)} %collective-permute-done.1.refs_1_, ...), custom_call_target="tpu_custom_call" | custom-call | flops 1610612736 | bytes 8388608 | tf_op jit(solution)/shard_map/pairs_own/pallas_call | solution.py:155
  22.6 2.6 %collective-permute-start.2 = (bf16[2,2,2,32,768]{4,3,2,1,0:T(8,128)(2,1)S(1)}, bf16[2,2,2,32,768]{4,3,2,1,0:T(8,128)(2,1)S(1)}, u32[]{:S(2)}, u32[]{:S(2)}) collective-permute-start(bf16[2,2,2,32,768]{4,3,2,1,0:T(8,128)(2,1)S(1)} %get-tuple-element.52), channel_id=1, source_target_pairs={{0,2},{1,7},{2,0},{3,5},{4,6},{5,3},{6,4},{7,1},{8,10},{9,15},{10,... | collective-permute-start | bytes 1179656 | tf_op jit(solution)/shard_map/ppermute | solution.py:43
  25.1 3.1 %collective-permute-start.6 = (bf16[128,2048]{1,0:T(8,128)(2,1)S(1)}, bf16[128,2048]{1,0:T(8,128)(2,1)S(1)}, u32[]{:S(2)}, u32[]{:S(2)}) collective-permute-start(bf16[128,2048]{1,0:T(8,128)(2,1)S(1)} %collective-permute-done.1.refs_1_), channel_id=1, source_target_pairs={{0,32},{1,225},{2,34},{3,227},{4,36},{5,229},{6,38},{7,231},{8,40}... | collective-permute-start | bytes 1572872 | tf_op jit(solution)/shard_map/ppermute | solution.py:43
  28.3 5.4 %collective-permute-done.4.b_ref.refs_3_ = bf16[128,2048]{1,0:T(8,128)(2,1)S(1)} collective-permute-done((bf16[128,2048]{1,0:T(8,128)(2,1)S(1)}, bf16[128,2048]{1,0:T(8,128)(2,1)S(1)}, u32[]{:S(2)}, u32[]{:S(2)}) %collective-permute-start.4) | collective-permute-done | bytes 524320 | tf_op jit(solution)/shard_map/ppermute | solution.py:43
  33.7 1.9 %collective-permute-start.8 = (bf16[128,2048]{1,0:T(8,128)(2,1)S(1)}, bf16[128,2048]{1,0:T(8,128)(2,1)S(1)}, u32[]{:S(2)}, u32[]{:S(2)}) collective-permute-start(bf16[128,2048]{1,0:T(8,128)(2,1)S(1)} %collective-permute-done.5.refs_0_), channel_id=1, source_target_pairs={{0,32},{1,225},{2,34},{3,227},{4,36},{5,229},{6,38},{7,231},{8,40}... | collective-permute-start | bytes 1572872 | tf_op jit(solution)/shard_map/ppermute | solution.py:43
  35.5 1.0 rotate.3
  36.5 2.4 %pairs_near.1 = (bf16[2,2,2,32,768]{4,3,2,1,0:T(8,128)(2,1)S(1)}, bf16[2,2,2,32,768]{4,3,2,1,0:T(8,128)(2,1)S(1)}) custom-call(s32[5]{0:T(128)S(1)} %stack.23.at_ref.place_ref, bf16[128,2048]{1,0:T(8,128)(2,1)S(1)} %collective-permute-done.refs_0_, bf16[128,2048]{1,0:T(8,128)(2,1)S(1)} %collective-permute-done.1.refs_1_, ...), custom_call_target="tpu_custom_call" | custom-call | flops 1610612736 | bytes 8388608 | tf_op jit(solution)/shard_map/pairs_near/pallas_call | solution.py:155
  39.2 2.6 %collective-permute-start.7 = (bf16[2,2,2,32,768]{4,3,2,1,0:T(8,128)(2,1)S(1)}, bf16[2,2,2,32,768]{4,3,2,1,0:T(8,128)(2,1)S(1)}, u32[]{:S(2)}, u32[]{:S(2)}) collective-permute-start(bf16[2,2,2,32,768]{4,3,2,1,0:T(8,128)(2,1)S(1)} %get-tuple-element.59), channel_id=1, source_target_pairs={{0,2},{1,7},{2,0},{3,5},{4,6},{5,3},{6,4},{7,1},{8,10},{9,15},{10,... | collective-permute-start | bytes 1179656 | tf_op jit(solution)/shard_map/ppermute | solution.py:43
  41.8 3.0 %pairs_2.1 = (bf16[2,2,2,32,1024]{4,3,2,1,0:T(8,128)(2,1)S(1)}, bf16[2,2,2,32,1024]{4,3,2,1,0:T(8,128)(2,1)S(1)}) custom-call(s32[5]{0:T(128)S(1)} %stack.23.at_ref.place_ref, bf16[128,2048]{1,0:T(8,128)(2,1)S(1)} %collective-permute-done.5.refs_0_, bf16[128,2048]{1,0:T(8,128)(2,1)S(1)} %collective-permute-done.6.refs_1_, ...), custom_call_target="tpu_custom_call" | custom-call | flops 2147483648 | bytes 8388608 | tf_op jit(solution)/shard_map/pairs_2/pallas_call | solution.py:155
  45.1 2.2 %collective-permute-start.11 = (bf16[2,2,2,32,1024]{4,3,2,1,0:T(8,128)(2,1)S(1)}, bf16[2,2,2,32,1024]{4,3,2,1,0:T(8,128)(2,1)S(1)}, u32[]{:S(2)}, u32[]{:S(2)}) collective-permute-start(bf16[2,2,2,32,1024]{4,3,2,1,0:T(8,128)(2,1)S(1)} %get-tuple-element.66), channel_id=1, source_target_pairs={{0,2},{1,7},{2,0},{3,5},{4,6},{5,3},{6,4},{7,1},{8,10},{9,15},{10,... | collective-permute-start | bytes 1572872 | tf_op jit(solution)/shard_map/ppermute | solution.py:43
  47.2 0.4 collective-permute-done.9.refs_1_
  47.6 2.8 %collective-permute-start.12 = (bf16[128,2048]{1,0:T(8,128)(2,1)S(1)}, bf16[128,2048]{1,0:T(8,128)(2,1)S(1)}, u32[]{:S(2)}, u32[]{:S(2)}) collective-permute-start(bf16[128,2048]{1,0:T(8,128)(2,1)S(1)} %collective-permute-done.9.refs_1_), channel_id=1, source_target_pairs={{0,32},{1,225},{2,34},{3,227},{4,36},{5,229},{6,38},{7,231},{8,40}... | collective-permute-start | bytes 1572872 | tf_op jit(solution)/shard_map/ppermute | solution.py:43
  50.4 3.0 %pairs_3.1 = (bf16[4,2,32,1024]{3,2,1,0:T(8,128)(2,1)S(1)}, bf16[4,2,32,1024]{3,2,1,0:T(8,128)(2,1)S(1)}) custom-call(s32[5]{0:T(128)S(1)} %stack.23.at_ref.place_ref, bf16[128,2048]{1,0:T(8,128)(2,1)S(1)} %collective-permute-done.8.refs_0_, bf16[128,2048]{1,0:T(8,128)(2,1)S(1)} %collective-permute-done.9.refs_1_, ...), custom_call_target="tpu_custom_call" | custom-call | flops 2147483648 | bytes 8388608 | tf_op jit(solution)/shard_map/pairs_3/pallas_call | solution.py:155
  53.4 1.2 %collective-permute-done.11.refs_5_ = bf16[2,2,2,32,1024]{4,3,2,1,0:T(8,128)(2,1)S(1)} collective-permute-done((bf16[2,2,2,32,1024]{4,3,2,1,0:T(8,128)(2,1)S(1)}, bf16[2,2,2,32,1024]{4,3,2,1,0:T(8,128)(2,1)S(1)}, u32[]{:S(2)}, u32[]{:S(2)}) %collective-permute-start.11) | collective-permute-done | bytes 524320 | tf_op jit(solution)/shard_map/ppermute | solution.py:43
  55.0 3.0 %collective-permute-start.14 = (bf16[4,2,32,1024]{3,2,1,0:T(8,128)(2,1)S(1)}, bf16[4,2,32,1024]{3,2,1,0:T(8,128)(2,1)S(1)}, u32[]{:S(2)}, u32[]{:S(2)}) collective-permute-start(bf16[4,2,32,1024]{3,2,1,0:T(8,128)(2,1)S(1)} %get-tuple-element.74), channel_id=1, source_target_pairs={{0,8},{1,9},{2,10},{3,11},{4,12},{5,13},{6,14},{7,15},{8,0},{9,1},... | collective-permute-start | bytes 1572872 | tf_op jit(solution)/shard_map/ppermute | solution.py:43
  58.0 0.9 collective-permute-done.12.refs_1_
  58.9 1.9 %pairs_4.1 = (bf16[2,2,2,32,512]{4,3,2,1,0:T(8,128)(2,1)S(1)}, bf16[2,2,2,32,512]{4,3,2,1,0:T(8,128)(2,1)S(1)}) custom-call(s32[5]{0:T(128)S(1)} %stack.23.at_ref.place_ref, bf16[128,2048]{1,0:T(8,128)(2,1)S(1)} %collective-permute-done.10.refs_0_, bf16[128,2048]{1,0:T(8,128)(2,1)S(1)} %collective-permute-done.12.refs_1_, ...), custom_call_target="tpu_custom_call" | custom-call | flops 1073741824 | bytes 8388608 | tf_op jit(solution)/shard_map/pairs_4/pallas_call | solution.py:155
  60.7 1.3 %collective-permute-start.15 = (bf16[2,2,2,32,512]{4,3,2,1,0:T(8,128)(2,1)S(1)}, bf16[2,2,2,32,512]{4,3,2,1,0:T(8,128)(2,1)S(1)}, u32[]{:S(2)}, u32[]{:S(2)}) collective-permute-start(bf16[2,2,2,32,512]{4,3,2,1,0:T(8,128)(2,1)S(1)} %get-tuple-element.75), channel_id=1, source_target_pairs={{0,6},{1,3},{2,4},{3,1},{4,2},{5,7},{6,0},{7,5},{8,14},{9,11},{10,... | collective-permute-start | bytes 786440 | tf_op jit(solution)/shard_map/ppermute | solution.py:43
  62.0 2.7 %collective-permute-done.13.refs_1_ = bf16[2,2,32,2560]{3,2,1,0:T(8,128)(2,1)S(1)} collective-permute-done((bf16[2,2,32,2560]{3,2,1,0:T(8,128)(2,1)S(1)}, bf16[2,2,32,2560]{3,2,1,0:T(8,128)(2,1)S(1)}, u32[]{:S(2)}, u32[]{:S(2)}) %collective-permute-start.13) | collective-permute-done | bytes 655392 | tf_op jit(solution)/shard_map/ppermute | solution.py:43
  64.7 0.7 sum_2.1
  65.4 1.3 %collective-permute-done.14.rc_ref = bf16[4,2,32,1024]{3,2,1,0:T(8,128)(2,1)S(1)} collective-permute-done((bf16[4,2,32,1024]{3,2,1,0:T(8,128)(2,1)S(1)}, bf16[4,2,32,1024]{3,2,1,0:T(8,128)(2,1)S(1)}, u32[]{:S(2)}, u32[]{:S(2)}) %collective-permute-start.14) | collective-permute-done | bytes 524320 | tf_op jit(solution)/shard_map/ppermute | solution.py:43
  66.7 0.8 collective-permute-done.15.rd_ref
  67.7 3.5 %collective-permute-start.16 = (bf16[2,2,32,1536]{3,2,1,0:T(8,128)(2,1)S(1)}, bf16[2,2,32,1536]{3,2,1,0:T(8,128)(2,1)S(1)}, u32[]{:S(2)}, u32[]{:S(2)}) collective-permute-start(bf16[2,2,32,1536]{3,2,1,0:T(8,128)(2,1)S(1)} %get-tuple-element.77), channel_id=1, source_target_pairs={{0,2},{1,7},{2,0},{3,5},{4,6},{5,3},{6,4},{7,1},{8,10},{9,15},{10,... | collective-permute-start | bytes 1179656 | tf_op jit(solution)/shard_map/ppermute | solution.py:43
  71.2 2.9 %collective-permute-start.17 = (bf16[2,32,2560]{2,1,0:T(8,128)(2,1)S(1)}, bf16[2,32,2560]{2,1,0:T(8,128)(2,1)S(1)}, u32[]{:S(2)}, u32[]{:S(2)}) collective-permute-start(bf16[2,32,2560]{2,1,0:T(8,128)(2,1)S(1)} %get-tuple-element.80), channel_id=1, source_target_pairs={{0,8},{1,9},{2,10},{3,11},{4,12},{5,13},{6,14},{7,15},{8,0},{9,1},... | collective-permute-start | bytes 983048 | tf_op jit(solution)/shard_map/ppermute | solution.py:43
  74.1 2.2 %collective-permute-done.16.recv_ref = bf16[2,2,32,1536]{3,2,1,0:T(8,128)(2,1)S(1)} collective-permute-done((bf16[2,2,32,1536]{3,2,1,0:T(8,128)(2,1)S(1)}, bf16[2,2,32,1536]{3,2,1,0:T(8,128)(2,1)S(1)}, u32[]{:S(2)}, u32[]{:S(2)}) %collective-permute-start.16) | collective-permute-done | bytes 393248 | tf_op jit(solution)/shard_map/ppermute | solution.py:43
  76.4 0.6 sum_n.1
  77.0 2.0 %collective-permute-start.20 = (bf16[2,32,1024]{2,1,0:T(8,128)(2,1)S(1)}, bf16[2,32,1024]{2,1,0:T(8,128)(2,1)S(1)}, u32[]{:S(2)}, u32[]{:S(2)}) collective-permute-start(bf16[2,32,1024]{2,1,0:T(8,128)(2,1)S(1)} %get-tuple-element.85), channel_id=1, source_target_pairs={{0,6},{1,3},{2,4},{3,1},{4,2},{5,7},{6,0},{7,5},{8,14},{9,11},{10,... | collective-permute-start | bytes 393224 | tf_op jit(solution)/shard_map/ppermute | solution.py:43
  79.0 1.3 %collective-permute-done.17.refs_1_ = bf16[2,32,2560]{2,1,0:T(8,128)(2,1)S(1)} collective-permute-done((bf16[2,32,2560]{2,1,0:T(8,128)(2,1)S(1)}, bf16[2,32,2560]{2,1,0:T(8,128)(2,1)S(1)}, u32[]{:S(2)}, u32[]{:S(2)}) %collective-permute-start.17) | collective-permute-done | bytes 327712 | tf_op jit(solution)/shard_map/ppermute | solution.py:43
  80.3 0.8 collective-permute-start.18
  81.1 2.9 %collective-permute-start.21 = (bf16[2,32,512]{2,1,0:T(8,128)(2,1)S(1)}, bf16[2,32,512]{2,1,0:T(8,128)(2,1)S(1)}, u32[]{:S(2)}, u32[]{:S(2)}) collective-permute-start(bf16[2,32,512]{2,1,0:T(8,128)(2,1)S(1)} %get-tuple-element.86), channel_id=1, source_target_pairs={{0,8},{1,9},{2,10},{3,11},{4,12},{5,13},{6,14},{7,15},{8,0},{9,1},... | collective-permute-start | bytes 196616 | tf_op jit(solution)/shard_map/ppermute | solution.py:43
  84.0 3.6 %collective-permute-done.18.refs_3_ = bf16[2,32,512]{2,1,0:T(8,128)(2,1)S(1)} collective-permute-done((bf16[2,32,512]{2,1,0:T(8,128)(2,1)S(1)}, bf16[2,32,512]{2,1,0:T(8,128)(2,1)S(1)}, u32[]{:S(2)}, u32[]{:S(2)}) %collective-permute-start.18) | collective-permute-done | bytes 65568 | tf_op jit(solution)/shard_map/ppermute | solution.py:43
  87.7 2.6 %collective-permute-done.19.refs_4_ = bf16[2,32,512]{2,1,0:T(8,128)(2,1)S(1)} collective-permute-done((bf16[2,32,512]{2,1,0:T(8,128)(2,1)S(1)}, bf16[2,32,512]{2,1,0:T(8,128)(2,1)S(1)}, u32[]{:S(2)}, u32[]{:S(2)}) %collective-permute-start.19) | collective-permute-done | bytes 65568 | tf_op jit(solution)/shard_map/ppermute | solution.py:43
  90.3 1.4 %collective-permute-start.22 = (bf16[2,32,1024]{2,1,0:T(8,128)(2,1)S(1)}, bf16[2,32,1024]{2,1,0:T(8,128)(2,1)S(1)}, u32[]{:S(2)}, u32[]{:S(2)}) collective-permute-start(bf16[2,32,1024]{2,1,0:T(8,128)(2,1)S(1)} %get-tuple-element.89), channel_id=1, source_target_pairs={{0,16},{1,17},{2,18},{3,19},{4,20},{5,21},{6,22},{7,23},{8,24},{9,... | collective-permute-start | bytes 393224 | tf_op jit(solution)/shard_map/ppermute | solution.py:43
  91.7 6.8 %collective-permute-done.23.refs_5_ = bf16[2,32,512]{2,1,0:T(8,128)(2,1)S(1)} collective-permute-done((bf16[2,32,512]{2,1,0:T(8,128)(2,1)S(1)}, bf16[2,32,512]{2,1,0:T(8,128)(2,1)S(1)}, u32[]{:S(2)}, u32[]{:S(2)}) %collective-permute-start.23) | collective-permute-done | bytes 65568 | tf_op jit(solution)/shard_map/ppermute | solution.py:43
  98.5 0.6 split.1
  99.1 2.0 %collective-permute-start.24 = (bf16[2,16,4096]{2,1,0:T(8,128)(2,1)S(1)}, bf16[2,16,4096]{2,1,0:T(8,128)(2,1)S(1)}, u32[]{:S(2)}, u32[]{:S(2)}) collective-permute-start(bf16[2,16,4096]{2,1,0:T(8,128)(2,1)S(1)} %split.1), channel_id=1, source_target_pairs={{0,1},{1,0},{2,3},{3,2},{4,5},{5,4},{6,7},{7,6},{8,9},{9,8},{10,11... | collective-permute-start | bytes 786440 | tf_op jit(solution)/shard_map/ppermute | solution.py:43
  101.1 1.2 %collective-permute-done.24.refs_6_ = bf16[2,16,4096]{2,1,0:T(8,128)(2,1)S(1)} collective-permute-done((bf16[2,16,4096]{2,1,0:T(8,128)(2,1)S(1)}, bf16[2,16,4096]{2,1,0:T(8,128)(2,1)S(1)}, u32[]{:S(2)}, u32[]{:S(2)}) %collective-permute-start.24) | collective-permute-done | bytes 262176 | tf_op jit(solution)/shard_map/ppermute | solution.py:43
  102.3 1.5 %finish.1 = f32[2,16,4096]{2,1,0:T(8,128)} custom-call(s32[5]{0:T(128)S(1)} %stack.23.at_ref.place_ref, bf16[2,32,1024]{2,1,0:T(8,128)(2,1)S(1)} %get-tuple-element.81.refs_0_, bf16[2,32,512]{2,1,0:T(8,128)(2,1)S(1)} %get-tuple-element.88.refs_1_, bf16[2,32,1024]{2,1,0:T(8,128)(2,1)S(1)} %collective-permute-done.22.refs_2_, ...), custom_call_target="tpu_custom_call" | custom-call | flops 1000 | bytes 10485760 | tf_op jit(solution)/shard_map/finish/pallas_call | solution.py:174
  (27 shorter events, 1.6 us)
Async XLA Ops:
  0.0 17.7 %copy-start.1 = (s32[512]{0:T(512)S(1)}, s32[512]{0:T(512)}, u32[]{:S(2)}) copy-start(s32[512]{0:T(512)} %param.3) | copy-start | bytes 6148
  0.1 1.2 %copy-start = (bf16[2,2,512,256]{3,2,1,0:T(8,128)(2,1)S(1)}, bf16[2,2,512,256]{3,2,1,0:T(8,128)(2,1)}, u32[]{:S(2)}) copy-start(bf16[2,2,512,256]{3,2,1,0:T(8,128)(2,1)} %x_ref.1) | copy-start | bytes 3145732
  1.9 12.6 %collective-permute-start = (bf16[128,2048]{1,0:T(8,128)(2,1)S(1)}, bf16[128,2048]{1,0:T(8,128)(2,1)S(1)}, u32[]{:S(2)}, u32[]{:S(2)}) collective-permute-start(bf16[128,2048]{1,0:T(8,128)(2,1)S(1)} %whiten.2.a_ref.refs_2_), channel_id=1, source_target_pairs={{0,32},{1,225},{2,34},{3,227},{4,36},{5,229},{6,38},{7,231},{8,40}... | collective-permute-start | bytes 1572872 | tf_op jit(solution)/shard_map/ppermute | solution.py:43
  9.0 11.1 %collective-permute-start.1 = (bf16[128,2048]{1,0:T(8,128)(2,1)S(1)}, bf16[128,2048]{1,0:T(8,128)(2,1)S(1)}, u32[]{:S(2)}, u32[]{:S(2)}) collective-permute-start(bf16[128,2048]{1,0:T(8,128)(2,1)S(1)} %whiten.3.b_ref.refs_3_), channel_id=1, source_target_pairs={{0,32},{1,225},{2,34},{3,227},{4,36},{5,229},{6,38},{7,231},{8,40}... | collective-permute-start | bytes 1572872 | tf_op jit(solution)/shard_map/ppermute | solution.py:43
  9.8 18.5 %collective-permute-start.3 = (bf16[128,2048]{1,0:T(8,128)(2,1)S(1)}, bf16[128,2048]{1,0:T(8,128)(2,1)S(1)}, u32[]{:S(2)}, u32[]{:S(2)}) collective-permute-start(bf16[128,2048]{1,0:T(8,128)(2,1)S(1)} %whiten.2.a_ref.refs_2_), channel_id=1, source_target_pairs={{0,16},{1,17},{2,18},{3,19},{4,20},{5,21},{6,22},{7,23},{8,24},{9,... | collective-permute-start | bytes 1572872 | tf_op jit(solution)/shard_map/ppermute | solution.py:43
  11.1 22.5 %collective-permute-start.4 = (bf16[128,2048]{1,0:T(8,128)(2,1)S(1)}, bf16[128,2048]{1,0:T(8,128)(2,1)S(1)}, u32[]{:S(2)}, u32[]{:S(2)}) collective-permute-start(bf16[128,2048]{1,0:T(8,128)(2,1)S(1)} %whiten.3.b_ref.refs_3_), channel_id=1, source_target_pairs={{0,16},{1,17},{2,18},{3,19},{4,20},{5,21},{6,22},{7,23},{8,24},{9,... | collective-permute-start | bytes 1572872 | tf_op jit(solution)/shard_map/ppermute | solution.py:43
  14.5 19.1 %collective-permute-start.5 = (bf16[128,2048]{1,0:T(8,128)(2,1)S(1)}, bf16[128,2048]{1,0:T(8,128)(2,1)S(1)}, u32[]{:S(2)}, u32[]{:S(2)}) collective-permute-start(bf16[128,2048]{1,0:T(8,128)(2,1)S(1)} %collective-permute-done.refs_0_), channel_id=1, source_target_pairs={{0,32},{1,225},{2,34},{3,227},{4,36},{5,229},{6,38},{7,231},{8,40}... | collective-permute-start | bytes 1572872 | tf_op jit(solution)/shard_map/ppermute | solution.py:43
  22.6 13.9 %collective-permute-start.2 = (bf16[2,2,2,32,768]{4,3,2,1,0:T(8,128)(2,1)S(1)}, bf16[2,2,2,32,768]{4,3,2,1,0:T(8,128)(2,1)S(1)}, u32[]{:S(2)}, u32[]{:S(2)}) collective-permute-start(bf16[2,2,2,32,768]{4,3,2,1,0:T(8,128)(2,1)S(1)} %get-tuple-element.52), channel_id=1, source_target_pairs={{0,2},{1,7},{2,0},{3,5},{4,6},{5,3},{6,4},{7,1},{8,10},{9,15},{10,... | collective-permute-start | bytes 1179656 | tf_op jit(solution)/shard_map/ppermute | solution.py:43
  25.1 13.8 %collective-permute-start.6 = (bf16[128,2048]{1,0:T(8,128)(2,1)S(1)}, bf16[128,2048]{1,0:T(8,128)(2,1)S(1)}, u32[]{:S(2)}, u32[]{:S(2)}) collective-permute-start(bf16[128,2048]{1,0:T(8,128)(2,1)S(1)} %collective-permute-done.1.refs_1_), channel_id=1, source_target_pairs={{0,32},{1,225},{2,34},{3,227},{4,36},{5,229},{6,38},{7,231},{8,40}... | collective-permute-start | bytes 1572872 | tf_op jit(solution)/shard_map/ppermute | solution.py:43
  33.7 11.1 %collective-permute-start.8 = (bf16[128,2048]{1,0:T(8,128)(2,1)S(1)}, bf16[128,2048]{1,0:T(8,128)(2,1)S(1)}, u32[]{:S(2)}, u32[]{:S(2)}) collective-permute-start(bf16[128,2048]{1,0:T(8,128)(2,1)S(1)} %collective-permute-done.5.refs_0_), channel_id=1, source_target_pairs={{0,32},{1,225},{2,34},{3,227},{4,36},{5,229},{6,38},{7,231},{8,40}... | collective-permute-start | bytes 1572872 | tf_op jit(solution)/shard_map/ppermute | solution.py:43
  39.0 8.6 %collective-permute-start.9 = (bf16[128,2048]{1,0:T(8,128)(2,1)S(1)}, bf16[128,2048]{1,0:T(8,128)(2,1)S(1)}, u32[]{:S(2)}, u32[]{:S(2)}) collective-permute-start(bf16[128,2048]{1,0:T(8,128)(2,1)S(1)} %collective-permute-done.6.refs_1_), channel_id=1, source_target_pairs={{0,32},{1,225},{2,34},{3,227},{4,36},{5,229},{6,38},{7,231},{8,40}... | collective-permute-start | bytes 1572872 | tf_op jit(solution)/shard_map/ppermute | solution.py:43
  39.2 11.2 %collective-permute-start.7 = (bf16[2,2,2,32,768]{4,3,2,1,0:T(8,128)(2,1)S(1)}, bf16[2,2,2,32,768]{4,3,2,1,0:T(8,128)(2,1)S(1)}, u32[]{:S(2)}, u32[]{:S(2)}) collective-permute-start(bf16[2,2,2,32,768]{4,3,2,1,0:T(8,128)(2,1)S(1)} %get-tuple-element.59), channel_id=1, source_target_pairs={{0,2},{1,7},{2,0},{3,5},{4,6},{5,3},{6,4},{7,1},{8,10},{9,15},{10,... | collective-permute-start | bytes 1179656 | tf_op jit(solution)/shard_map/ppermute | solution.py:43
  44.8 8.6 %collective-permute-start.10 = (bf16[128,2048]{1,0:T(8,128)(2,1)S(1)}, bf16[128,2048]{1,0:T(8,128)(2,1)S(1)}, u32[]{:S(2)}, u32[]{:S(2)}) collective-permute-start(bf16[128,2048]{1,0:T(8,128)(2,1)S(1)} %collective-permute-done.8.refs_0_), channel_id=1, source_target_pairs={{0,32},{1,225},{2,34},{3,227},{4,36},{5,229},{6,38},{7,231},{8,40}... | collective-permute-start | bytes 1572872 | tf_op jit(solution)/shard_map/ppermute | solution.py:43
  45.1 9.5 %collective-permute-start.11 = (bf16[2,2,2,32,1024]{4,3,2,1,0:T(8,128)(2,1)S(1)}, bf16[2,2,2,32,1024]{4,3,2,1,0:T(8,128)(2,1)S(1)}, u32[]{:S(2)}, u32[]{:S(2)}) collective-permute-start(bf16[2,2,2,32,1024]{4,3,2,1,0:T(8,128)(2,1)S(1)} %get-tuple-element.66), channel_id=1, source_target_pairs={{0,2},{1,7},{2,0},{3,5},{4,6},{5,3},{6,4},{7,1},{8,10},{9,15},{10,... | collective-permute-start | bytes 1572872 | tf_op jit(solution)/shard_map/ppermute | solution.py:43
  47.6 11.2 %collective-permute-start.12 = (bf16[128,2048]{1,0:T(8,128)(2,1)S(1)}, bf16[128,2048]{1,0:T(8,128)(2,1)S(1)}, u32[]{:S(2)}, u32[]{:S(2)}) collective-permute-start(bf16[128,2048]{1,0:T(8,128)(2,1)S(1)} %collective-permute-done.9.refs_1_), channel_id=1, source_target_pairs={{0,32},{1,225},{2,34},{3,227},{4,36},{5,229},{6,38},{7,231},{8,40}... | collective-permute-start | bytes 1572872 | tf_op jit(solution)/shard_map/ppermute | solution.py:43
  54.9 9.8 %collective-permute-start.13 = (bf16[2,2,32,2560]{3,2,1,0:T(8,128)(2,1)S(1)}, bf16[2,2,32,2560]{3,2,1,0:T(8,128)(2,1)S(1)}, u32[]{:S(2)}, u32[]{:S(2)}) collective-permute-start(bf16[2,2,32,2560]{3,2,1,0:T(8,128)(2,1)S(1)} %get-tuple-element.71), channel_id=1, source_target_pairs={{0,6},{1,3},{2,4},{3,1},{4,2},{5,7},{6,0},{7,5},{8,14},{9,11},{10,... | collective-permute-start | bytes 1966088 | tf_op jit(solution)/shard_map/ppermute | solution.py:43
  55.0 11.8 %collective-permute-start.14 = (bf16[4,2,32,1024]{3,2,1,0:T(8,128)(2,1)S(1)}, bf16[4,2,32,1024]{3,2,1,0:T(8,128)(2,1)S(1)}, u32[]{:S(2)}, u32[]{:S(2)}) collective-permute-start(bf16[4,2,32,1024]{3,2,1,0:T(8,128)(2,1)S(1)} %get-tuple-element.74), channel_id=1, source_target_pairs={{0,8},{1,9},{2,10},{3,11},{4,12},{5,13},{6,14},{7,15},{8,0},{9,1},... | collective-permute-start | bytes 1572872 | tf_op jit(solution)/shard_map/ppermute | solution.py:43
  60.7 6.8 %collective-permute-start.15 = (bf16[2,2,2,32,512]{4,3,2,1,0:T(8,128)(2,1)S(1)}, bf16[2,2,2,32,512]{4,3,2,1,0:T(8,128)(2,1)S(1)}, u32[]{:S(2)}, u32[]{:S(2)}) collective-permute-start(bf16[2,2,2,32,512]{4,3,2,1,0:T(8,128)(2,1)S(1)} %get-tuple-element.75), channel_id=1, source_target_pairs={{0,6},{1,3},{2,4},{3,1},{4,2},{5,7},{6,0},{7,5},{8,14},{9,11},{10,... | collective-permute-start | bytes 786440 | tf_op jit(solution)/shard_map/ppermute | solution.py:43
  67.7 8.7 %collective-permute-start.16 = (bf16[2,2,32,1536]{3,2,1,0:T(8,128)(2,1)S(1)}, bf16[2,2,32,1536]{3,2,1,0:T(8,128)(2,1)S(1)}, u32[]{:S(2)}, u32[]{:S(2)}) collective-permute-start(bf16[2,2,32,1536]{3,2,1,0:T(8,128)(2,1)S(1)} %get-tuple-element.77), channel_id=1, source_target_pairs={{0,2},{1,7},{2,0},{3,5},{4,6},{5,3},{6,4},{7,1},{8,10},{9,15},{10,... | collective-permute-start | bytes 1179656 | tf_op jit(solution)/shard_map/ppermute | solution.py:43
  71.2 9.1 %collective-permute-start.17 = (bf16[2,32,2560]{2,1,0:T(8,128)(2,1)S(1)}, bf16[2,32,2560]{2,1,0:T(8,128)(2,1)S(1)}, u32[]{:S(2)}, u32[]{:S(2)}) collective-permute-start(bf16[2,32,2560]{2,1,0:T(8,128)(2,1)S(1)} %get-tuple-element.80), channel_id=1, source_target_pairs={{0,8},{1,9},{2,10},{3,11},{4,12},{5,13},{6,14},{7,15},{8,0},{9,1},... | collective-permute-start | bytes 983048 | tf_op jit(solution)/shard_map/ppermute | solution.py:43
  77.0 13.3 %collective-permute-start.20 = (bf16[2,32,1024]{2,1,0:T(8,128)(2,1)S(1)}, bf16[2,32,1024]{2,1,0:T(8,128)(2,1)S(1)}, u32[]{:S(2)}, u32[]{:S(2)}) collective-permute-start(bf16[2,32,1024]{2,1,0:T(8,128)(2,1)S(1)} %get-tuple-element.85), channel_id=1, source_target_pairs={{0,6},{1,3},{2,4},{3,1},{4,2},{5,7},{6,0},{7,5},{8,14},{9,11},{10,... | collective-permute-start | bytes 393224 | tf_op jit(solution)/shard_map/ppermute | solution.py:43
  80.3 7.3 %collective-permute-start.18 = (bf16[2,32,512]{2,1,0:T(8,128)(2,1)S(1)}, bf16[2,32,512]{2,1,0:T(8,128)(2,1)S(1)}, u32[]{:S(2)}, u32[]{:S(2)}) collective-permute-start(bf16[2,32,512]{2,1,0:T(8,128)(2,1)S(1)} %get-tuple-element.82), channel_id=1, source_target_pairs={{0,224},{1,33},{2,226},{3,35},{4,228},{5,37},{6,230},{7,39},{8,232... | collective-permute-start | bytes 196616 | tf_op jit(solution)/shard_map/ppermute | solution.py:43
  81.1 9.2 %collective-permute-start.19 = (bf16[2,32,512]{2,1,0:T(8,128)(2,1)S(1)}, bf16[2,32,512]{2,1,0:T(8,128)(2,1)S(1)}, u32[]{:S(2)}, u32[]{:S(2)}) collective-permute-start(bf16[2,32,512]{2,1,0:T(8,128)(2,1)S(1)} %get-tuple-element.83), channel_id=1, source_target_pairs={{0,192},{1,65},{2,194},{3,67},{4,196},{5,69},{6,198},{7,71},{8,200... | collective-permute-start | bytes 196616 | tf_op jit(solution)/shard_map/ppermute | solution.py:43
  81.1 9.2 %collective-permute-start.21 = (bf16[2,32,512]{2,1,0:T(8,128)(2,1)S(1)}, bf16[2,32,512]{2,1,0:T(8,128)(2,1)S(1)}, u32[]{:S(2)}, u32[]{:S(2)}) collective-permute-start(bf16[2,32,512]{2,1,0:T(8,128)(2,1)S(1)} %get-tuple-element.86), channel_id=1, source_target_pairs={{0,8},{1,9},{2,10},{3,11},{4,12},{5,13},{6,14},{7,15},{8,0},{9,1},... | collective-permute-start | bytes 196616 | tf_op jit(solution)/shard_map/ppermute | solution.py:43
  90.3 8.2 %collective-permute-start.22 = (bf16[2,32,1024]{2,1,0:T(8,128)(2,1)S(1)}, bf16[2,32,1024]{2,1,0:T(8,128)(2,1)S(1)}, u32[]{:S(2)}, u32[]{:S(2)}) collective-permute-start(bf16[2,32,1024]{2,1,0:T(8,128)(2,1)S(1)} %get-tuple-element.89), channel_id=1, source_target_pairs={{0,16},{1,17},{2,18},{3,19},{4,20},{5,21},{6,22},{7,23},{8,24},{9,... | collective-permute-start | bytes 393224 | tf_op jit(solution)/shard_map/ppermute | solution.py:43
  91.7 6.8 %collective-permute-start.23 = (bf16[2,32,512]{2,1,0:T(8,128)(2,1)S(1)}, bf16[2,32,512]{2,1,0:T(8,128)(2,1)S(1)}, u32[]{:S(2)}, u32[]{:S(2)}) collective-permute-start(bf16[2,32,512]{2,1,0:T(8,128)(2,1)S(1)} %get-tuple-element.90), channel_id=1, source_target_pairs={{0,160},{1,97},{2,162},{3,99},{4,164},{5,101},{6,166},{7,103},{8,1... | collective-permute-start | bytes 196616 | tf_op jit(solution)/shard_map/ppermute | solution.py:43
  99.1 3.2 %collective-permute-start.24 = (bf16[2,16,4096]{2,1,0:T(8,128)(2,1)S(1)}, bf16[2,16,4096]{2,1,0:T(8,128)(2,1)S(1)}, u32[]{:S(2)}, u32[]{:S(2)}) collective-permute-start(bf16[2,16,4096]{2,1,0:T(8,128)(2,1)S(1)} %split.1), channel_id=1, source_target_pairs={{0,1},{1,0},{2,3},{3,2},{4,5},{5,4},{6,7},{7,6},{8,9},{9,8},{10,11... | collective-permute-start | bytes 786440 | tf_op jit(solution)/shard_map/ppermute | solution.py:43

commit v11 on v10

--- a/solution.py
+++ b/solution.py
@@ -389,7 +389,7 @@
 
     keep_o, send_o = products(place, own_pairs, first + own + rotated[:2], 3 * BLOCK, scale, "pairs_own")
     recv_o = move(send_o, x_near)
-    third = [move(after(second[0], near[0], near[1], keep_o), chain_step)]
+    third = [move(after(second[0], near[0], keep_o), chain_step)]
     at = after(place, recv_o)
     near_rotated = [own_plus, near_plus, near_minus]
     keep_n, send_n = products(at, near_pairs, first + near + near_rotated, 3 * BLOCK, scale, "pairs_near")
@@ -419,7 +419,7 @@
     own_ab, near_ab, ret_1, ret_2 = sum_y(after(keep_ab, keep_cd), [recv_ab], outputs)
     ret_1, ret_2 = move(ret_1, back(1)), move(ret_2, back(2))
     outputs = [[(0, 256), (1024, 256)], [(256, 256), (1280, 256)], [(512, 512)]]
-    own_cd, near_all, ret_3 = sum_y(after(keep_cd, ret_1, ret_2), recv_cd, outputs, near_ab)
+    own_cd, near_all, ret_3 = sum_y(after(keep_cd, own_ab), recv_cd, outputs, near_ab)
     ret_3 = move(ret_3, back(3))
     near_all = move(near_all, y_step)
     arrays = [own_ab, own_cd, near_all, ret_1, ret_2, ret_3]

time: 105 us -> 102 us (0.971)
  waiting for transfers between devices: 35 us -> 32.9 us
    ppermute x25, waiting for transfers between devices: 35 us -> 32.9 us  [move(): return lax.ppermute(x, AXES, pairs)]
  transfers between devices with their start and end apart: 25 -> 25, of which waited for: 15 -> 15; matrix products, arithmetic and copies ran while one was open for 0% -> 0% of each run, Pallas kernels for 16% -> 17%
where the time goes in v11:
time: 102 us; the launch traced here: 101 us
  starting transfers between devices  46.4 us (45%)
  waiting for transfers between devices  32.9 us (32%)
  Pallas kernels  19.8 us (19%)
  local copies, waits for them, and re-layouts  1.31 us (1%)
    ppermute x25, starting transfers between devices, move(): return lax.ppermute(x, AXES, pairs)  46.4 us
    ppermute x25, waiting for transfers between devices, move(): return lax.ppermute(x, AXES, pairs)  32.9 us
    pallas_call x5, Pallas kernels, products(): pl.pallas_call(kernel, in_specs=[pl.BlockSpec(memory_space=pltpu.SMEM)] +...  12.7 us
    pallas_call x8, Pallas kernels, call(): pl.pallas_call(kernel, in_specs=[pl.BlockSpec(memory_space=pltpu.SMEM)] *...  3.96 us
  transfers between devices with their start and end apart: 25, of which 15 were waited for; matrix products, arithmetic and copies ran while one was open for 0% of the time, Pallas kernels for 17%

profile of v11, /device:TPU:1, one launch (start us, length us, event | category | flops | bytes accessed | tf_op | source)
XLA Modules:
  0.0 100.8 jit_solution(15435429161603534298)
XLA Ops:
  0.1 1.2 %copy-done = bf16[2,2,512,256]{3,2,1,0:T(8,128)(2,1)S(1)} copy-done((bf16[2,2,512,256]{3,2,1,0:T(8,128)(2,1)S(1)}, bf16[2,2,512,256]{3,2,1,0:T(8,128)(2,1)}, u32[]{:S(2)}) %copy-start) | copy-done | bytes 1048600
  1.3 0.6 whiten.2.a_ref.refs_2_
  1.9 6.5 %collective-permute-start = (bf16[128,2048]{1,0:T(8,128)(2,1)S(1)}, bf16[128,2048]{1,0:T(8,128)(2,1)S(1)}, u32[]{:S(2)}, u32[]{:S(2)}) collective-permute-start(bf16[128,2048]{1,0:T(8,128)(2,1)S(1)} %whiten.2.a_ref.refs_2_), channel_id=1, source_target_pairs={{0,32},{1,225},{2,34},{3,227},{4,36},{5,229},{6,38},{7,231},{8,40}... | collective-permute-start | bytes 1572872 | tf_op jit(solution)/shard_map/ppermute | solution.py:43
  8.4 0.6 whiten.3.b_ref.refs_3_
  9.0 0.8 collective-permute-start.1
  9.8 1.3 %collective-permute-start.3 = (bf16[128,2048]{1,0:T(8,128)(2,1)S(1)}, bf16[128,2048]{1,0:T(8,128)(2,1)S(1)}, u32[]{:S(2)}, u32[]{:S(2)}) collective-permute-start(bf16[128,2048]{1,0:T(8,128)(2,1)S(1)} %whiten.2.a_ref.refs_2_), channel_id=1, source_target_pairs={{0,16},{1,17},{2,18},{3,19},{4,20},{5,21},{6,22},{7,23},{8,24},{9,... | collective-permute-start | bytes 1572872 | tf_op jit(solution)/shard_map/ppermute | solution.py:43
  11.3 3.2 %collective-permute-done.refs_0_ = bf16[128,2048]{1,0:T(8,128)(2,1)S(1)} collective-permute-done((bf16[128,2048]{1,0:T(8,128)(2,1)S(1)}, bf16[128,2048]{1,0:T(8,128)(2,1)S(1)}, u32[]{:S(2)}, u32[]{:S(2)}) %collective-permute-start) | collective-permute-done | bytes 524320 | tf_op jit(solution)/shard_map/ppermute | solution.py:43
  14.5 3.1 %collective-permute-start.5 = (bf16[128,2048]{1,0:T(8,128)(2,1)S(1)}, bf16[128,2048]{1,0:T(8,128)(2,1)S(1)}, u32[]{:S(2)}, u32[]{:S(2)}) collective-permute-start(bf16[128,2048]{1,0:T(8,128)(2,1)S(1)} %collective-permute-done.refs_0_), channel_id=1, source_target_pairs={{0,32},{1,225},{2,34},{3,227},{4,36},{5,229},{6,38},{7,231},{8,40}... | collective-permute-start | bytes 1572872 | tf_op jit(solution)/shard_map/ppermute | solution.py:43
  17.8 1.0 rotate.2
  18.8 1.4 %collective-permute-done.1.refs_1_ = bf16[128,2048]{1,0:T(8,128)(2,1)S(1)} collective-permute-done((bf16[128,2048]{1,0:T(8,128)(2,1)S(1)}, bf16[128,2048]{1,0:T(8,128)(2,1)S(1)}, u32[]{:S(2)}, u32[]{:S(2)}) %collective-permute-start.1) | collective-permute-done | bytes 524320 | tf_op jit(solution)/shard_map/ppermute | solution.py:43
  20.2 2.4 %pairs_own.1 = (bf16[2,2,2,32,768]{4,3,2,1,0:T(8,128)(2,1)S(1)}, bf16[2,2,2,32,768]{4,3,2,1,0:T(8,128)(2,1)S(1)}) custom-call(s32[5]{0:T(128)S(1)} %stack.23.at_ref.place_ref, bf16[128,2048]{1,0:T(8,128)(2,1)S(1)} %collective-permute-done.refs_0_, bf16[128,2048]{1,0:T(8,128)(2,1)S(1)} %collective-permute-done.1.refs_1_, ...), custom_call_target="tpu_custom_call" | custom-call | flops 1610612736 | bytes 8388608 | tf_op jit(solution)/shard_map/pairs_own/pallas_call | solution.py:155
  22.6 2.6 %collective-permute-start.2 = (bf16[2,2,2,32,768]{4,3,2,1,0:T(8,128)(2,1)S(1)}, bf16[2,2,2,32,768]{4,3,2,1,0:T(8,128)(2,1)S(1)}, u32[]{:S(2)}, u32[]{:S(2)}) collective-permute-start(bf16[2,2,2,32,768]{4,3,2,1,0:T(8,128)(2,1)S(1)} %get-tuple-element.52), channel_id=1, source_target_pairs={{0,2},{1,7},{2,0},{3,5},{4,6},{5,3},{6,4},{7,1},{8,10},{9,15},{10,... | collective-permute-start | bytes 1179656 | tf_op jit(solution)/shard_map/ppermute | solution.py:43
  25.1 3.1 %collective-permute-start.6 = (bf16[128,2048]{1,0:T(8,128)(2,1)S(1)}, bf16[128,2048]{1,0:T(8,128)(2,1)S(1)}, u32[]{:S(2)}, u32[]{:S(2)}) collective-permute-start(bf16[128,2048]{1,0:T(8,128)(2,1)S(1)} %collective-permute-done.1.refs_1_), channel_id=1, source_target_pairs={{0,32},{1,225},{2,34},{3,227},{4,36},{5,229},{6,38},{7,231},{8,40}... | collective-permute-start | bytes 1572872 | tf_op jit(solution)/shard_map/ppermute | solution.py:43
  28.3 0.6 collective-permute-start.8
  28.9 4.8 %collective-permute-done.4.b_ref.refs_3_ = bf16[128,2048]{1,0:T(8,128)(2,1)S(1)} collective-permute-done((bf16[128,2048]{1,0:T(8,128)(2,1)S(1)}, bf16[128,2048]{1,0:T(8,128)(2,1)S(1)}, u32[]{:S(2)}, u32[]{:S(2)}) %collective-permute-start.4) | collective-permute-done | bytes 524320 | tf_op jit(solution)/shard_map/ppermute | solution.py:43
  33.7 1.0 rotate.3
  34.7 2.4 %pairs_near.1 = (bf16[2,2,2,32,768]{4,3,2,1,0:T(8,128)(2,1)S(1)}, bf16[2,2,2,32,768]{4,3,2,1,0:T(8,128)(2,1)S(1)}) custom-call(s32[5]{0:T(128)S(1)} %stack.23.at_ref.place_ref, bf16[128,2048]{1,0:T(8,128)(2,1)S(1)} %collective-permute-done.refs_0_, bf16[128,2048]{1,0:T(8,128)(2,1)S(1)} %collective-permute-done.1.refs_1_, ...), custom_call_target="tpu_custom_call" | custom-call | flops 1610612736 | bytes 8388608 | tf_op jit(solution)/shard_map/pairs_near/pallas_call | solution.py:155
  37.1 1.9 %collective-permute-start.9 = (bf16[128,2048]{1,0:T(8,128)(2,1)S(1)}, bf16[128,2048]{1,0:T(8,128)(2,1)S(1)}, u32[]{:S(2)}, u32[]{:S(2)}) collective-permute-start(bf16[128,2048]{1,0:T(8,128)(2,1)S(1)} %collective-permute-done.6.refs_1_), channel_id=1, source_target_pairs={{0,32},{1,225},{2,34},{3,227},{4,36},{5,229},{6,38},{7,231},{8,40}... | collective-permute-start | bytes 1572872 | tf_op jit(solution)/shard_map/ppermute | solution.py:43
  39.0 2.5 %collective-permute-start.7 = (bf16[2,2,2,32,768]{4,3,2,1,0:T(8,128)(2,1)S(1)}, bf16[2,2,2,32,768]{4,3,2,1,0:T(8,128)(2,1)S(1)}, u32[]{:S(2)}, u32[]{:S(2)}) collective-permute-start(bf16[2,2,2,32,768]{4,3,2,1,0:T(8,128)(2,1)S(1)} %get-tuple-element.59), channel_id=1, source_target_pairs={{0,2},{1,7},{2,0},{3,5},{4,6},{5,3},{6,4},{7,1},{8,10},{9,15},{10,... | collective-permute-start | bytes 1179656 | tf_op jit(solution)/shard_map/ppermute | solution.py:43
  41.5 3.0 %pairs_2.1 = (bf16[2,2,2,32,1024]{4,3,2,1,0:T(8,128)(2,1)S(1)}, bf16[2,2,2,32,1024]{4,3,2,1,0:T(8,128)(2,1)S(1)}) custom-call(s32[5]{0:T(128)S(1)} %stack.23.at_ref.place_ref, bf16[128,2048]{1,0:T(8,128)(2,1)S(1)} %collective-permute-done.5.refs_0_, bf16[128,2048]{1,0:T(8,128)(2,1)S(1)} %collective-permute-done.6.refs_1_, ...), custom_call_target="tpu_custom_call" | custom-call | flops 2147483648 | bytes 8388608 | tf_op jit(solution)/shard_map/pairs_2/pallas_call | solution.py:155
  45.1 0.6 collective-permute-done.9.refs_1_
  45.7 3.0 %collective-permute-start.12 = (bf16[128,2048]{1,0:T(8,128)(2,1)S(1)}, bf16[128,2048]{1,0:T(8,128)(2,1)S(1)}, u32[]{:S(2)}, u32[]{:S(2)}) collective-permute-start(bf16[128,2048]{1,0:T(8,128)(2,1)S(1)} %collective-permute-done.9.refs_1_), channel_id=1, source_target_pairs={{0,32},{1,225},{2,34},{3,227},{4,36},{5,229},{6,38},{7,231},{8,40}... | collective-permute-start | bytes 1572872 | tf_op jit(solution)/shard_map/ppermute | solution.py:43
  48.7 3.0 %pairs_3.1 = (bf16[4,2,32,1024]{3,2,1,0:T(8,128)(2,1)S(1)}, bf16[4,2,32,1024]{3,2,1,0:T(8,128)(2,1)S(1)}) custom-call(s32[5]{0:T(128)S(1)} %stack.23.at_ref.place_ref, bf16[128,2048]{1,0:T(8,128)(2,1)S(1)} %collective-permute-done.8.refs_0_, bf16[128,2048]{1,0:T(8,128)(2,1)S(1)} %collective-permute-done.9.refs_1_, ...), custom_call_target="tpu_custom_call" | custom-call | flops 2147483648 | bytes 8388608 | tf_op jit(solution)/shard_map/pairs_3/pallas_call | solution.py:155
  51.7 1.2 %collective-permute-done.10.refs_0_ = bf16[128,2048]{1,0:T(8,128)(2,1)S(1)} collective-permute-done((bf16[128,2048]{1,0:T(8,128)(2,1)S(1)}, bf16[128,2048]{1,0:T(8,128)(2,1)S(1)}, u32[]{:S(2)}, u32[]{:S(2)}) %collective-permute-start.10) | collective-permute-done | bytes 524320 | tf_op jit(solution)/shard_map/ppermute | solution.py:43
  52.9 1.5 %collective-permute-done.11.refs_5_ = bf16[2,2,2,32,1024]{4,3,2,1,0:T(8,128)(2,1)S(1)} collective-permute-done((bf16[2,2,2,32,1024]{4,3,2,1,0:T(8,128)(2,1)S(1)}, bf16[2,2,2,32,1024]{4,3,2,1,0:T(8,128)(2,1)S(1)}, u32[]{:S(2)}, u32[]{:S(2)}) %collective-permute-start.11) | collective-permute-done | bytes 524320 | tf_op jit(solution)/shard_map/ppermute | solution.py:43
  54.8 3.0 %collective-permute-start.14 = (bf16[4,2,32,1024]{3,2,1,0:T(8,128)(2,1)S(1)}, bf16[4,2,32,1024]{3,2,1,0:T(8,128)(2,1)S(1)}, u32[]{:S(2)}, u32[]{:S(2)}) collective-permute-start(bf16[4,2,32,1024]{3,2,1,0:T(8,128)(2,1)S(1)} %get-tuple-element.74), channel_id=1, source_target_pairs={{0,8},{1,9},{2,10},{3,11},{4,12},{5,13},{6,14},{7,15},{8,0},{9,1},... | collective-permute-start | bytes 1572872 | tf_op jit(solution)/shard_map/ppermute | solution.py:43
  57.8 0.7 collective-permute-done.12.refs_1_
  58.5 1.9 %pairs_4.1 = (bf16[2,2,2,32,512]{4,3,2,1,0:T(8,128)(2,1)S(1)}, bf16[2,2,2,32,512]{4,3,2,1,0:T(8,128)(2,1)S(1)}) custom-call(s32[5]{0:T(128)S(1)} %stack.23.at_ref.place_ref, bf16[128,2048]{1,0:T(8,128)(2,1)S(1)} %collective-permute-done.10.refs_0_, bf16[128,2048]{1,0:T(8,128)(2,1)S(1)} %collective-permute-done.12.refs_1_, ...), custom_call_target="tpu_custom_call" | custom-call | flops 1073741824 | bytes 8388608 | tf_op jit(solution)/shard_map/pairs_4/pallas_call | solution.py:155
  60.4 0.7 collective-permute-start.15
  61.1 3.4 %collective-permute-done.13.refs_1_ = bf16[2,2,32,2560]{3,2,1,0:T(8,128)(2,1)S(1)} collective-permute-done((bf16[2,2,32,2560]{3,2,1,0:T(8,128)(2,1)S(1)}, bf16[2,2,32,2560]{3,2,1,0:T(8,128)(2,1)S(1)}, u32[]{:S(2)}, u32[]{:S(2)}) %collective-permute-start.13) | collective-permute-done | bytes 655392 | tf_op jit(solution)/shard_map/ppermute | solution.py:43
  64.5 0.7 sum_2.1
  65.2 2.9 %collective-permute-done.14.rc_ref = bf16[4,2,32,1024]{3,2,1,0:T(8,128)(2,1)S(1)} collective-permute-done((bf16[4,2,32,1024]{3,2,1,0:T(8,128)(2,1)S(1)}, bf16[4,2,32,1024]{3,2,1,0:T(8,128)(2,1)S(1)}, u32[]{:S(2)}, u32[]{:S(2)}) %collective-permute-start.14) | collective-permute-done | bytes 524320 | tf_op jit(solution)/shard_map/ppermute | solution.py:43
  68.3 0.9 collective-permute-start.16
  69.3 2.9 %collective-permute-start.17 = (bf16[2,32,2560]{2,1,0:T(8,128)(2,1)S(1)}, bf16[2,32,2560]{2,1,0:T(8,128)(2,1)S(1)}, u32[]{:S(2)}, u32[]{:S(2)}) collective-permute-start(bf16[2,32,2560]{2,1,0:T(8,128)(2,1)S(1)} %get-tuple-element.80), channel_id=1, source_target_pairs={{0,8},{1,9},{2,10},{3,11},{4,12},{5,13},{6,14},{7,15},{8,0},{9,1},... | collective-permute-start | bytes 983048 | tf_op jit(solution)/shard_map/ppermute | solution.py:43
  72.2 4.1 %collective-permute-done.16.recv_ref = bf16[2,2,32,1536]{3,2,1,0:T(8,128)(2,1)S(1)} collective-permute-done((bf16[2,2,32,1536]{3,2,1,0:T(8,128)(2,1)S(1)}, bf16[2,2,32,1536]{3,2,1,0:T(8,128)(2,1)S(1)}, u32[]{:S(2)}, u32[]{:S(2)}) %collective-permute-start.16) | collective-permute-done | bytes 393248 | tf_op jit(solution)/shard_map/ppermute | solution.py:43
  76.2 0.6 sum_n.1
  76.9 1.6 %collective-permute-start.18 = (bf16[2,32,1024]{2,1,0:T(8,128)(2,1)S(1)}, bf16[2,32,1024]{2,1,0:T(8,128)(2,1)S(1)}, u32[]{:S(2)}, u32[]{:S(2)}) collective-permute-start(bf16[2,32,1024]{2,1,0:T(8,128)(2,1)S(1)} %get-tuple-element.83), channel_id=1, source_target_pairs={{0,6},{1,3},{2,4},{3,1},{4,2},{5,7},{6,0},{7,5},{8,14},{9,11},{10,... | collective-permute-start | bytes 393224 | tf_op jit(solution)/shard_map/ppermute | solution.py:43
  78.5 2.9 %collective-permute-start.19 = (bf16[2,32,512]{2,1,0:T(8,128)(2,1)S(1)}, bf16[2,32,512]{2,1,0:T(8,128)(2,1)S(1)}, u32[]{:S(2)}, u32[]{:S(2)}) collective-permute-start(bf16[2,32,512]{2,1,0:T(8,128)(2,1)S(1)} %get-tuple-element.84), channel_id=1, source_target_pairs={{0,8},{1,9},{2,10},{3,11},{4,12},{5,13},{6,14},{7,15},{8,0},{9,1},... | collective-permute-start | bytes 196616 | tf_op jit(solution)/shard_map/ppermute | solution.py:43
  81.5 1.6 %collective-permute-done.19.refs_2_ = bf16[2,32,512]{2,1,0:T(8,128)(2,1)S(1)} collective-permute-done((bf16[2,32,512]{2,1,0:T(8,128)(2,1)S(1)}, bf16[2,32,512]{2,1,0:T(8,128)(2,1)S(1)}, u32[]{:S(2)}, u32[]{:S(2)}) %collective-permute-start.19) | collective-permute-done | bytes 65568 | tf_op jit(solution)/shard_map/ppermute | solution.py:43
  83.2 1.4 %collective-permute-start.20 = (bf16[2,32,1024]{2,1,0:T(8,128)(2,1)S(1)}, bf16[2,32,1024]{2,1,0:T(8,128)(2,1)S(1)}, u32[]{:S(2)}, u32[]{:S(2)}) collective-permute-start(bf16[2,32,1024]{2,1,0:T(8,128)(2,1)S(1)} %get-tuple-element.87), channel_id=1, source_target_pairs={{0,16},{1,17},{2,18},{3,19},{4,20},{5,21},{6,22},{7,23},{8,24},{9,... | collective-permute-start | bytes 393224 | tf_op jit(solution)/shard_map/ppermute | solution.py:43
  84.6 2.2 %collective-permute-start.21 = (bf16[2,32,512]{2,1,0:T(8,128)(2,1)S(1)}, bf16[2,32,512]{2,1,0:T(8,128)(2,1)S(1)}, u32[]{:S(2)}, u32[]{:S(2)}) collective-permute-start(bf16[2,32,512]{2,1,0:T(8,128)(2,1)S(1)} %get-tuple-element.88), channel_id=1, source_target_pairs={{0,224},{1,33},{2,226},{3,35},{4,228},{5,37},{6,230},{7,39},{8,232... | collective-permute-start | bytes 196616 | tf_op jit(solution)/shard_map/ppermute | solution.py:43
  86.8 2.1 %collective-permute-done.21.refs_3_ = bf16[2,32,512]{2,1,0:T(8,128)(2,1)S(1)} collective-permute-done((bf16[2,32,512]{2,1,0:T(8,128)(2,1)S(1)}, bf16[2,32,512]{2,1,0:T(8,128)(2,1)S(1)}, u32[]{:S(2)}, u32[]{:S(2)}) %collective-permute-start.21) | collective-permute-done | bytes 65568 | tf_op jit(solution)/shard_map/ppermute | solution.py:43
  88.9 3.2 %collective-permute-done.22.refs_4_ = bf16[2,32,512]{2,1,0:T(8,128)(2,1)S(1)} collective-permute-done((bf16[2,32,512]{2,1,0:T(8,128)(2,1)S(1)}, bf16[2,32,512]{2,1,0:T(8,128)(2,1)S(1)}, u32[]{:S(2)}, u32[]{:S(2)}) %collective-permute-start.22) | collective-permute-done | bytes 65568 | tf_op jit(solution)/shard_map/ppermute | solution.py:43
  92.1 1.0 collective-permute-done.23.refs_5_
  93.1 0.6 split.1
  93.7 4.4 %collective-permute-start.24 = (bf16[2,16,4096]{2,1,0:T(8,128)(2,1)S(1)}, bf16[2,16,4096]{2,1,0:T(8,128)(2,1)S(1)}, u32[]{:S(2)}, u32[]{:S(2)}) collective-permute-start(bf16[2,16,4096]{2,1,0:T(8,128)(2,1)S(1)} %split.1), channel_id=1, source_target_pairs={{0,1},{1,0},{2,3},{3,2},{4,5},{5,4},{6,7},{7,6},{8,9},{9,8},{10,11... | collective-permute-start | bytes 786440 | tf_op jit(solution)/shard_map/ppermute | solution.py:43
  98.1 1.2 %collective-permute-done.24.refs_6_ = bf16[2,16,4096]{2,1,0:T(8,128)(2,1)S(1)} collective-permute-done((bf16[2,16,4096]{2,1,0:T(8,128)(2,1)S(1)}, bf16[2,16,4096]{2,1,0:T(8,128)(2,1)S(1)}, u32[]{:S(2)}, u32[]{:S(2)}) %collective-permute-start.24) | collective-permute-done | bytes 262176 | tf_op jit(solution)/shard_map/ppermute | solution.py:43
  99.3 1.5 %finish.1 = f32[2,16,4096]{2,1,0:T(8,128)} custom-call(s32[5]{0:T(128)S(1)} %stack.23.at_ref.place_ref, bf16[2,32,1024]{2,1,0:T(8,128)(2,1)S(1)} %get-tuple-element.81.refs_0_, bf16[2,32,512]{2,1,0:T(8,128)(2,1)S(1)} %get-tuple-element.86.refs_1_, bf16[2,32,1024]{2,1,0:T(8,128)(2,1)S(1)} %collective-permute-done.20.refs_2_, ...), custom_call_target="tpu_custom_call" | custom-call | flops 1000 | bytes 10485760 | tf_op jit(solution)/shard_map/finish/pallas_call | solution.py:174
  (27 shorter events, 1.6 us)
Async XLA Ops:
  0.0 17.7 %copy-start.1 = (s32[512]{0:T(512)S(1)}, s32[512]{0:T(512)}, u32[]{:S(2)}) copy-start(s32[512]{0:T(512)} %param.3) | copy-start | bytes 6148
  0.1 1.2 %copy-start = (bf16[2,2,512,256]{3,2,1,0:T(8,128)(2,1)S(1)}, bf16[2,2,512,256]{3,2,1,0:T(8,128)(2,1)}, u32[]{:S(2)}) copy-start(bf16[2,2,512,256]{3,2,1,0:T(8,128)(2,1)} %x_ref.1) | copy-start | bytes 3145732
  1.9 12.6 %collective-permute-start = (bf16[128,2048]{1,0:T(8,128)(2,1)S(1)}, bf16[128,2048]{1,0:T(8,128)(2,1)S(1)}, u32[]{:S(2)}, u32[]{:S(2)}) collective-permute-start(bf16[128,2048]{1,0:T(8,128)(2,1)S(1)} %whiten.2.a_ref.refs_2_), channel_id=1, source_target_pairs={{0,32},{1,225},{2,34},{3,227},{4,36},{5,229},{6,38},{7,231},{8,40}... | collective-permute-start | bytes 1572872 | tf_op jit(solution)/shard_map/ppermute | solution.py:43
  9.0 11.1 %collective-permute-start.1 = (bf16[128,2048]{1,0:T(8,128)(2,1)S(1)}, bf16[128,2048]{1,0:T(8,128)(2,1)S(1)}, u32[]{:S(2)}, u32[]{:S(2)}) collective-permute-start(bf16[128,2048]{1,0:T(8,128)(2,1)S(1)} %whiten.3.b_ref.refs_3_), channel_id=1, source_target_pairs={{0,32},{1,225},{2,34},{3,227},{4,36},{5,229},{6,38},{7,231},{8,40}... | collective-permute-start | bytes 1572872 | tf_op jit(solution)/shard_map/ppermute | solution.py:43
  9.8 18.4 %collective-permute-start.3 = (bf16[128,2048]{1,0:T(8,128)(2,1)S(1)}, bf16[128,2048]{1,0:T(8,128)(2,1)S(1)}, u32[]{:S(2)}, u32[]{:S(2)}) collective-permute-start(bf16[128,2048]{1,0:T(8,128)(2,1)S(1)} %whiten.2.a_ref.refs_2_), channel_id=1, source_target_pairs={{0,16},{1,17},{2,18},{3,19},{4,20},{5,21},{6,22},{7,23},{8,24},{9,... | collective-permute-start | bytes 1572872 | tf_op jit(solution)/shard_map/ppermute | solution.py:43
  11.1 22.5 %collective-permute-start.4 = (bf16[128,2048]{1,0:T(8,128)(2,1)S(1)}, bf16[128,2048]{1,0:T(8,128)(2,1)S(1)}, u32[]{:S(2)}, u32[]{:S(2)}) collective-permute-start(bf16[128,2048]{1,0:T(8,128)(2,1)S(1)} %whiten.3.b_ref.refs_3_), channel_id=1, source_target_pairs={{0,16},{1,17},{2,18},{3,19},{4,20},{5,21},{6,22},{7,23},{8,24},{9,... | collective-permute-start | bytes 1572872 | tf_op jit(solution)/shard_map/ppermute | solution.py:43
  14.5 13.7 %collective-permute-start.5 = (bf16[128,2048]{1,0:T(8,128)(2,1)S(1)}, bf16[128,2048]{1,0:T(8,128)(2,1)S(1)}, u32[]{:S(2)}, u32[]{:S(2)}) collective-permute-start(bf16[128,2048]{1,0:T(8,128)(2,1)S(1)} %collective-permute-done.refs_0_), channel_id=1, source_target_pairs={{0,32},{1,225},{2,34},{3,227},{4,36},{5,229},{6,38},{7,231},{8,40}... | collective-permute-start | bytes 1572872 | tf_op jit(solution)/shard_map/ppermute | solution.py:43
  22.6 12.1 %collective-permute-start.2 = (bf16[2,2,2,32,768]{4,3,2,1,0:T(8,128)(2,1)S(1)}, bf16[2,2,2,32,768]{4,3,2,1,0:T(8,128)(2,1)S(1)}, u32[]{:S(2)}, u32[]{:S(2)}) collective-permute-start(bf16[2,2,2,32,768]{4,3,2,1,0:T(8,128)(2,1)S(1)} %get-tuple-element.52), channel_id=1, source_target_pairs={{0,2},{1,7},{2,0},{3,5},{4,6},{5,3},{6,4},{7,1},{8,10},{9,15},{10,... | collective-permute-start | bytes 1179656 | tf_op jit(solution)/shard_map/ppermute | solution.py:43
  25.1 12.0 %collective-permute-start.6 = (bf16[128,2048]{1,0:T(8,128)(2,1)S(1)}, bf16[128,2048]{1,0:T(8,128)(2,1)S(1)}, u32[]{:S(2)}, u32[]{:S(2)}) collective-permute-start(bf16[128,2048]{1,0:T(8,128)(2,1)S(1)} %collective-permute-done.1.refs_1_), channel_id=1, source_target_pairs={{0,32},{1,225},{2,34},{3,227},{4,36},{5,229},{6,38},{7,231},{8,40}... | collective-permute-start | bytes 1572872 | tf_op jit(solution)/shard_map/ppermute | solution.py:43
  28.3 16.2 %collective-permute-start.8 = (bf16[128,2048]{1,0:T(8,128)(2,1)S(1)}, bf16[128,2048]{1,0:T(8,128)(2,1)S(1)}, u32[]{:S(2)}, u32[]{:S(2)}) collective-permute-start(bf16[128,2048]{1,0:T(8,128)(2,1)S(1)} %collective-permute-done.5.refs_0_), channel_id=1, source_target_pairs={{0,32},{1,225},{2,34},{3,227},{4,36},{5,229},{6,38},{7,231},{8,40}... | collective-permute-start | bytes 1572872 | tf_op jit(solution)/shard_map/ppermute | solution.py:43
  37.1 8.6 %collective-permute-start.9 = (bf16[128,2048]{1,0:T(8,128)(2,1)S(1)}, bf16[128,2048]{1,0:T(8,128)(2,1)S(1)}, u32[]{:S(2)}, u32[]{:S(2)}) collective-permute-start(bf16[128,2048]{1,0:T(8,128)(2,1)S(1)} %collective-permute-done.6.refs_1_), channel_id=1, source_target_pairs={{0,32},{1,225},{2,34},{3,227},{4,36},{5,229},{6,38},{7,231},{8,40}... | collective-permute-start | bytes 1572872 | tf_op jit(solution)/shard_map/ppermute | solution.py:43
  39.0 9.7 %collective-permute-start.7 = (bf16[2,2,2,32,768]{4,3,2,1,0:T(8,128)(2,1)S(1)}, bf16[2,2,2,32,768]{4,3,2,1,0:T(8,128)(2,1)S(1)}, u32[]{:S(2)}, u32[]{:S(2)}) collective-permute-start(bf16[2,2,2,32,768]{4,3,2,1,0:T(8,128)(2,1)S(1)} %get-tuple-element.59), channel_id=1, source_target_pairs={{0,2},{1,7},{2,0},{3,5},{4,6},{5,3},{6,4},{7,1},{8,10},{9,15},{10,... | collective-permute-start | bytes 1179656 | tf_op jit(solution)/shard_map/ppermute | solution.py:43
  44.5 8.4 %collective-permute-start.10 = (bf16[128,2048]{1,0:T(8,128)(2,1)S(1)}, bf16[128,2048]{1,0:T(8,128)(2,1)S(1)}, u32[]{:S(2)}, u32[]{:S(2)}) collective-permute-start(bf16[128,2048]{1,0:T(8,128)(2,1)S(1)} %collective-permute-done.8.refs_0_), channel_id=1, source_target_pairs={{0,32},{1,225},{2,34},{3,227},{4,36},{5,229},{6,38},{7,231},{8,40}... | collective-permute-start | bytes 1572872 | tf_op jit(solution)/shard_map/ppermute | solution.py:43
  44.9 9.5 %collective-permute-start.11 = (bf16[2,2,2,32,1024]{4,3,2,1,0:T(8,128)(2,1)S(1)}, bf16[2,2,2,32,1024]{4,3,2,1,0:T(8,128)(2,1)S(1)}, u32[]{:S(2)}, u32[]{:S(2)}) collective-permute-start(bf16[2,2,2,32,1024]{4,3,2,1,0:T(8,128)(2,1)S(1)} %get-tuple-element.66), channel_id=1, source_target_pairs={{0,2},{1,7},{2,0},{3,5},{4,6},{5,3},{6,4},{7,1},{8,10},{9,15},{10,... | collective-permute-start | bytes 1572872 | tf_op jit(solution)/shard_map/ppermute | solution.py:43
  45.7 12.8 %collective-permute-start.12 = (bf16[128,2048]{1,0:T(8,128)(2,1)S(1)}, bf16[128,2048]{1,0:T(8,128)(2,1)S(1)}, u32[]{:S(2)}, u32[]{:S(2)}) collective-permute-start(bf16[128,2048]{1,0:T(8,128)(2,1)S(1)} %collective-permute-done.9.refs_1_), channel_id=1, source_target_pairs={{0,32},{1,225},{2,34},{3,227},{4,36},{5,229},{6,38},{7,231},{8,40}... | collective-permute-start | bytes 1572872 | tf_op jit(solution)/shard_map/ppermute | solution.py:43
  54.7 9.8 %collective-permute-start.13 = (bf16[2,2,32,2560]{3,2,1,0:T(8,128)(2,1)S(1)}, bf16[2,2,32,2560]{3,2,1,0:T(8,128)(2,1)S(1)}, u32[]{:S(2)}, u32[]{:S(2)}) collective-permute-start(bf16[2,2,32,2560]{3,2,1,0:T(8,128)(2,1)S(1)} %get-tuple-element.71), channel_id=1, source_target_pairs={{0,6},{1,3},{2,4},{3,1},{4,2},{5,7},{6,0},{7,5},{8,14},{9,11},{10,... | collective-permute-start | bytes 1966088 | tf_op jit(solution)/shard_map/ppermute | solution.py:43
  54.8 13.3 %collective-permute-start.14 = (bf16[4,2,32,1024]{3,2,1,0:T(8,128)(2,1)S(1)}, bf16[4,2,32,1024]{3,2,1,0:T(8,128)(2,1)S(1)}, u32[]{:S(2)}, u32[]{:S(2)}) collective-permute-start(bf16[4,2,32,1024]{3,2,1,0:T(8,128)(2,1)S(1)} %get-tuple-element.74), channel_id=1, source_target_pairs={{0,8},{1,9},{2,10},{3,11},{4,12},{5,13},{6,14},{7,15},{8,0},{9,1},... | collective-permute-start | bytes 1572872 | tf_op jit(solution)/shard_map/ppermute | solution.py:43
  60.4 7.7 %collective-permute-start.15 = (bf16[2,2,2,32,512]{4,3,2,1,0:T(8,128)(2,1)S(1)}, bf16[2,2,2,32,512]{4,3,2,1,0:T(8,128)(2,1)S(1)}, u32[]{:S(2)}, u32[]{:S(2)}) collective-permute-start(bf16[2,2,2,32,512]{4,3,2,1,0:T(8,128)(2,1)S(1)} %get-tuple-element.75), channel_id=1, source_target_pairs={{0,6},{1,3},{2,4},{3,1},{4,2},{5,7},{6,0},{7,5},{8,14},{9,11},{10,... | collective-permute-start | bytes 786440 | tf_op jit(solution)/shard_map/ppermute | solution.py:43
  68.3 7.9 %collective-permute-start.16 = (bf16[2,2,32,1536]{3,2,1,0:T(8,128)(2,1)S(1)}, bf16[2,2,32,1536]{3,2,1,0:T(8,128)(2,1)S(1)}, u32[]{:S(2)}, u32[]{:S(2)}) collective-permute-start(bf16[2,2,32,1536]{3,2,1,0:T(8,128)(2,1)S(1)} %get-tuple-element.77), channel_id=1, source_target_pairs={{0,2},{1,7},{2,0},{3,5},{4,6},{5,3},{6,4},{7,1},{8,10},{9,15},{10,... | collective-permute-start | bytes 1179656 | tf_op jit(solution)/shard_map/ppermute | solution.py:43
  69.3 12.2 %collective-permute-start.17 = (bf16[2,32,2560]{2,1,0:T(8,128)(2,1)S(1)}, bf16[2,32,2560]{2,1,0:T(8,128)(2,1)S(1)}, u32[]{:S(2)}, u32[]{:S(2)}) collective-permute-start(bf16[2,32,2560]{2,1,0:T(8,128)(2,1)S(1)} %get-tuple-element.80), channel_id=1, source_target_pairs={{0,8},{1,9},{2,10},{3,11},{4,12},{5,13},{6,14},{7,15},{8,0},{9,1},... | collective-permute-start | bytes 983048 | tf_op jit(solution)/shard_map/ppermute | solution.py:43
  76.9 6.3 %collective-permute-start.18 = (bf16[2,32,1024]{2,1,0:T(8,128)(2,1)S(1)}, bf16[2,32,1024]{2,1,0:T(8,128)(2,1)S(1)}, u32[]{:S(2)}, u32[]{:S(2)}) collective-permute-start(bf16[2,32,1024]{2,1,0:T(8,128)(2,1)S(1)} %get-tuple-element.83), channel_id=1, source_target_pairs={{0,6},{1,3},{2,4},{3,1},{4,2},{5,7},{6,0},{7,5},{8,14},{9,11},{10,... | collective-permute-start | bytes 393224 | tf_op jit(solution)/shard_map/ppermute | solution.py:43
  78.5 4.6 %collective-permute-start.19 = (bf16[2,32,512]{2,1,0:T(8,128)(2,1)S(1)}, bf16[2,32,512]{2,1,0:T(8,128)(2,1)S(1)}, u32[]{:S(2)}, u32[]{:S(2)}) collective-permute-start(bf16[2,32,512]{2,1,0:T(8,128)(2,1)S(1)} %get-tuple-element.84), channel_id=1, source_target_pairs={{0,8},{1,9},{2,10},{3,11},{4,12},{5,13},{6,14},{7,15},{8,0},{9,1},... | collective-permute-start | bytes 196616 | tf_op jit(solution)/shard_map/ppermute | solution.py:43
  83.2 10.0 %collective-permute-start.20 = (bf16[2,32,1024]{2,1,0:T(8,128)(2,1)S(1)}, bf16[2,32,1024]{2,1,0:T(8,128)(2,1)S(1)}, u32[]{:S(2)}, u32[]{:S(2)}) collective-permute-start(bf16[2,32,1024]{2,1,0:T(8,128)(2,1)S(1)} %get-tuple-element.87), channel_id=1, source_target_pairs={{0,16},{1,17},{2,18},{3,19},{4,20},{5,21},{6,22},{7,23},{8,24},{9,... | collective-permute-start | bytes 393224 | tf_op jit(solution)/shard_map/ppermute | solution.py:43
  84.6 4.3 %collective-permute-start.21 = (bf16[2,32,512]{2,1,0:T(8,128)(2,1)S(1)}, bf16[2,32,512]{2,1,0:T(8,128)(2,1)S(1)}, u32[]{:S(2)}, u32[]{:S(2)}) collective-permute-start(bf16[2,32,512]{2,1,0:T(8,128)(2,1)S(1)} %get-tuple-element.88), channel_id=1, source_target_pairs={{0,224},{1,33},{2,226},{3,35},{4,228},{5,37},{6,230},{7,39},{8,232... | collective-permute-start | bytes 196616 | tf_op jit(solution)/shard_map/ppermute | solution.py:43
  86.8 5.3 %collective-permute-start.22 = (bf16[2,32,512]{2,1,0:T(8,128)(2,1)S(1)}, bf16[2,32,512]{2,1,0:T(8,128)(2,1)S(1)}, u32[]{:S(2)}, u32[]{:S(2)}) collective-permute-start(bf16[2,32,512]{2,1,0:T(8,128)(2,1)S(1)} %get-tuple-element.89), channel_id=1, source_target_pairs={{0,192},{1,65},{2,194},{3,67},{4,196},{5,69},{6,198},{7,71},{8,200... | collective-permute-start | bytes 196616 | tf_op jit(solution)/shard_map/ppermute | solution.py:43
  86.8 6.3 %collective-permute-start.23 = (bf16[2,32,512]{2,1,0:T(8,128)(2,1)S(1)}, bf16[2,32,512]{2,1,0:T(8,128)(2,1)S(1)}, u32[]{:S(2)}, u32[]{:S(2)}) collective-permute-start(bf16[2,32,512]{2,1,0:T(8,128)(2,1)S(1)} %get-tuple-element.90), channel_id=1, source_target_pairs={{0,160},{1,97},{2,162},{3,99},{4,164},{5,101},{6,166},{7,103},{8,1... | collective-permute-start | bytes 196616 | tf_op jit(solution)/shard_map/ppermute | solution.py:43
  93.7 5.6 %collective-permute-start.24 = (bf16[2,16,4096]{2,1,0:T(8,128)(2,1)S(1)}, bf16[2,16,4096]{2,1,0:T(8,128)(2,1)S(1)}, u32[]{:S(2)}, u32[]{:S(2)}) collective-permute-start(bf16[2,16,4096]{2,1,0:T(8,128)(2,1)S(1)} %split.1), channel_id=1, source_target_pairs={{0,1},{1,0},{2,3},{3,2},{4,5},{5,4},{6,7},{7,6},{8,9},{9,8},{10,11... | collective-permute-start | bytes 786440 | tf_op jit(solution)/shard_map/ppermute | solution.py:43

commit v12 on v11

--- a/solution.py
+++ b/solution.py
@@ -394,7 +394,7 @@
     near_rotated = [own_plus, near_plus, near_minus]
     keep_n, send_n = products(at, near_pairs, first + near + near_rotated, 3 * BLOCK, scale, "pairs_near")
     recv_n = move(send_n, x_near)
-    third.append(move(after(second[1], keep_n), chain_step))
+    third.append(move(second[1], chain_step))
     at = after(place, keep_n)
     keep_b, send_b = products(at, all_pairs, second + rotated, 4 * BLOCK, scale, "pairs_2")
     recv_b = move(send_b, x_near)
@@ -409,10 +409,10 @@
     at = after(place, kept_ab)
     keep_d, send_d = products(at, last_pairs, fourth + [own_plus, near_plus], 2 * BLOCK, scale, "pairs_4", "far")
     recv_d = move(send_d, x_far)
-    keep_ab, send_ab = sum_2(place, [(after(kept_ab, keep_d), recv_ab)])
+    kept_cd, send_cd = sum_h(keep_c, recv_c, keep_d, recv_d)
+    recv_cd = move(send_cd, x_near)
+    keep_ab, send_ab = sum_2(place, [(after(kept_ab, kept_cd), recv_ab)])
     recv_ab = move(send_ab, yhi_step)
-    kept_cd, send_cd = sum_h(after(keep_c, keep_ab), recv_c, keep_d, recv_d)
-    recv_cd = move(send_cd, x_near)
     keep_cd, send_c, send_d = sum_n(place, kept_cd, recv_cd, 4 * BLOCK)
     recv_cd = [move(send_c, x_far), move(send_d, yhi_step)]
     outputs = [[(0, 768), (1536, 256)], [(768, 256), (1792, 256)], [(1024, 512)], [(2048, 512)]]

time: 102 us -> 103 us (level); the launches traced: 101 us -> 101 us
  starting transfers between devices: 46.4 us -> 45.1 us
  waiting for transfers between devices: 32.9 us -> 34.1 us
    ppermute x25, starting transfers between devices: 46.4 us -> 45.1 us  [move(): return lax.ppermute(x, AXES, pairs)]
    ppermute x25, waiting for transfers between devices: 32.9 us -> 34.1 us  [move(): return lax.ppermute(x, AXES, pairs)]
where the time goes in v12:
time: 103 us; the launch traced here: 101 us
  starting transfers between devices  45.1 us (44%)
  waiting for transfers between devices  34.1 us (33%)
  Pallas kernels  19.8 us (19%)
  local copies, waits for them, and re-layouts  1.31 us (1%)
    ppermute x25, starting transfers between devices, move(): return lax.ppermute(x, AXES, pairs)  45.1 us
    ppermute x25, waiting for transfers between devices, move(): return lax.ppermute(x, AXES, pairs)  34.1 us
    pallas_call x5, Pallas kernels, products(): pl.pallas_call(kernel, in_specs=[pl.BlockSpec(memory_space=pltpu.SMEM)] +...  12.7 us
    pallas_call x8, Pallas kernels, call(): pl.pallas_call(kernel, in_specs=[pl.BlockSpec(memory_space=pltpu.SMEM)] *...  3.94 us
  transfers between devices with their start and end apart: 25, of which 15 were waited for; matrix products, arithmetic and copies ran while one was open for 0% of the time, Pallas kernels for 17%

profile of v12, /device:TPU:1, one launch (start us, length us, event | category | flops | bytes accessed | tf_op | source)
XLA Modules:
  0.0 100.6 jit_solution(11623930960203111551)
XLA Ops:
  0.1 1.2 %copy-done = bf16[2,2,512,256]{3,2,1,0:T(8,128)(2,1)S(1)} copy-done((bf16[2,2,512,256]{3,2,1,0:T(8,128)(2,1)S(1)}, bf16[2,2,512,256]{3,2,1,0:T(8,128)(2,1)}, u32[]{:S(2)}) %copy-start) | copy-done | bytes 1048600
  1.3 0.6 whiten.2.a_ref.refs_2_
  1.9 6.5 %collective-permute-start = (bf16[128,2048]{1,0:T(8,128)(2,1)S(1)}, bf16[128,2048]{1,0:T(8,128)(2,1)S(1)}, u32[]{:S(2)}, u32[]{:S(2)}) collective-permute-start(bf16[128,2048]{1,0:T(8,128)(2,1)S(1)} %whiten.2.a_ref.refs_2_), channel_id=1, source_target_pairs={{0,32},{1,225},{2,34},{3,227},{4,36},{5,229},{6,38},{7,231},{8,40}... | collective-permute-start | bytes 1572872 | tf_op jit(solution)/shard_map/ppermute | solution.py:43
  8.4 0.6 whiten.3.b_ref.refs_3_
  9.0 0.8 collective-permute-start.1
  9.8 1.3 %collective-permute-start.3 = (bf16[128,2048]{1,0:T(8,128)(2,1)S(1)}, bf16[128,2048]{1,0:T(8,128)(2,1)S(1)}, u32[]{:S(2)}, u32[]{:S(2)}) collective-permute-start(bf16[128,2048]{1,0:T(8,128)(2,1)S(1)} %whiten.2.a_ref.refs_2_), channel_id=1, source_target_pairs={{0,16},{1,17},{2,18},{3,19},{4,20},{5,21},{6,22},{7,23},{8,24},{9,... | collective-permute-start | bytes 1572872 | tf_op jit(solution)/shard_map/ppermute | solution.py:43
  11.3 3.2 %collective-permute-done.refs_0_ = bf16[128,2048]{1,0:T(8,128)(2,1)S(1)} collective-permute-done((bf16[128,2048]{1,0:T(8,128)(2,1)S(1)}, bf16[128,2048]{1,0:T(8,128)(2,1)S(1)}, u32[]{:S(2)}, u32[]{:S(2)}) %collective-permute-start) | collective-permute-done | bytes 524320 | tf_op jit(solution)/shard_map/ppermute | solution.py:43
  14.5 3.1 %collective-permute-start.5 = (bf16[128,2048]{1,0:T(8,128)(2,1)S(1)}, bf16[128,2048]{1,0:T(8,128)(2,1)S(1)}, u32[]{:S(2)}, u32[]{:S(2)}) collective-permute-start(bf16[128,2048]{1,0:T(8,128)(2,1)S(1)} %collective-permute-done.refs_0_), channel_id=1, source_target_pairs={{0,32},{1,225},{2,34},{3,227},{4,36},{5,229},{6,38},{7,231},{8,40}... | collective-permute-start | bytes 1572872 | tf_op jit(solution)/shard_map/ppermute | solution.py:43
  17.8 2.3 %collective-permute-done.1.refs_1_ = bf16[128,2048]{1,0:T(8,128)(2,1)S(1)} collective-permute-done((bf16[128,2048]{1,0:T(8,128)(2,1)S(1)}, bf16[128,2048]{1,0:T(8,128)(2,1)S(1)}, u32[]{:S(2)}, u32[]{:S(2)}) %collective-permute-start.1) | collective-permute-done | bytes 524320 | tf_op jit(solution)/shard_map/ppermute | solution.py:43
  20.2 3.1 %collective-permute-start.6 = (bf16[128,2048]{1,0:T(8,128)(2,1)S(1)}, bf16[128,2048]{1,0:T(8,128)(2,1)S(1)}, u32[]{:S(2)}, u32[]{:S(2)}) collective-permute-start(bf16[128,2048]{1,0:T(8,128)(2,1)S(1)} %collective-permute-done.1.refs_1_), channel_id=1, source_target_pairs={{0,32},{1,225},{2,34},{3,227},{4,36},{5,229},{6,38},{7,231},{8,40}... | collective-permute-start | bytes 1572872 | tf_op jit(solution)/shard_map/ppermute | solution.py:43
  23.3 1.0 rotate.2
  24.3 2.4 %pairs_own.1 = (bf16[2,2,2,32,768]{4,3,2,1,0:T(8,128)(2,1)S(1)}, bf16[2,2,2,32,768]{4,3,2,1,0:T(8,128)(2,1)S(1)}) custom-call(s32[5]{0:T(128)S(1)} %stack.23.at_ref.place_ref, bf16[128,2048]{1,0:T(8,128)(2,1)S(1)} %collective-permute-done.refs_0_, bf16[128,2048]{1,0:T(8,128)(2,1)S(1)} %collective-permute-done.1.refs_1_, ...), custom_call_target="tpu_custom_call" | custom-call | flops 1610612736 | bytes 8388608 | tf_op jit(solution)/shard_map/pairs_own/pallas_call | solution.py:155
  26.7 2.6 %collective-permute-start.2 = (bf16[2,2,2,32,768]{4,3,2,1,0:T(8,128)(2,1)S(1)}, bf16[2,2,2,32,768]{4,3,2,1,0:T(8,128)(2,1)S(1)}, u32[]{:S(2)}, u32[]{:S(2)}) collective-permute-start(bf16[2,2,2,32,768]{4,3,2,1,0:T(8,128)(2,1)S(1)} %get-tuple-element.50), channel_id=1, source_target_pairs={{0,2},{1,7},{2,0},{3,5},{4,6},{5,3},{6,4},{7,1},{8,10},{9,15},{10,... | collective-permute-start | bytes 1179656 | tf_op jit(solution)/shard_map/ppermute | solution.py:43
  29.3 2.1 %collective-permute-done.6.refs_1_ = bf16[128,2048]{1,0:T(8,128)(2,1)S(1)} collective-permute-done((bf16[128,2048]{1,0:T(8,128)(2,1)S(1)}, bf16[128,2048]{1,0:T(8,128)(2,1)S(1)}, u32[]{:S(2)}, u32[]{:S(2)}) %collective-permute-start.6) | collective-permute-done | bytes 524320 | tf_op jit(solution)/shard_map/ppermute | solution.py:43
  31.4 3.1 %collective-permute-start.9 = (bf16[128,2048]{1,0:T(8,128)(2,1)S(1)}, bf16[128,2048]{1,0:T(8,128)(2,1)S(1)}, u32[]{:S(2)}, u32[]{:S(2)}) collective-permute-start(bf16[128,2048]{1,0:T(8,128)(2,1)S(1)} %collective-permute-done.6.refs_1_), channel_id=1, source_target_pairs={{0,32},{1,225},{2,34},{3,227},{4,36},{5,229},{6,38},{7,231},{8,40}... | collective-permute-start | bytes 1572872 | tf_op jit(solution)/shard_map/ppermute | solution.py:43
  34.5 1.0 rotate.3
  35.5 2.4 %pairs_near.1 = (bf16[2,2,2,32,768]{4,3,2,1,0:T(8,128)(2,1)S(1)}, bf16[2,2,2,32,768]{4,3,2,1,0:T(8,128)(2,1)S(1)}) custom-call(s32[5]{0:T(128)S(1)} %stack.23.at_ref.place_ref, bf16[128,2048]{1,0:T(8,128)(2,1)S(1)} %collective-permute-done.refs_0_, bf16[128,2048]{1,0:T(8,128)(2,1)S(1)} %collective-permute-done.1.refs_1_, ...), custom_call_target="tpu_custom_call" | custom-call | flops 1610612736 | bytes 8388608 | tf_op jit(solution)/shard_map/pairs_near/pallas_call | solution.py:155
  37.9 2.7 %collective-permute-start.7 = (bf16[2,2,2,32,768]{4,3,2,1,0:T(8,128)(2,1)S(1)}, bf16[2,2,2,32,768]{4,3,2,1,0:T(8,128)(2,1)S(1)}, u32[]{:S(2)}, u32[]{:S(2)}) collective-permute-start(bf16[2,2,2,32,768]{4,3,2,1,0:T(8,128)(2,1)S(1)} %get-tuple-element.57), channel_id=1, source_target_pairs={{0,2},{1,7},{2,0},{3,5},{4,6},{5,3},{6,4},{7,1},{8,10},{9,15},{10,... | collective-permute-start | bytes 1179656 | tf_op jit(solution)/shard_map/ppermute | solution.py:43
  40.7 3.0 %pairs_2.1 = (bf16[2,2,2,32,1024]{4,3,2,1,0:T(8,128)(2,1)S(1)}, bf16[2,2,2,32,1024]{4,3,2,1,0:T(8,128)(2,1)S(1)}) custom-call(s32[5]{0:T(128)S(1)} %stack.23.at_ref.place_ref, bf16[128,2048]{1,0:T(8,128)(2,1)S(1)} %collective-permute-done.5.refs_0_, bf16[128,2048]{1,0:T(8,128)(2,1)S(1)} %collective-permute-done.6.refs_1_, ...), custom_call_target="tpu_custom_call" | custom-call | flops 2147483648 | bytes 8388608 | tf_op jit(solution)/shard_map/pairs_2/pallas_call | solution.py:155
  43.7 1.1 %collective-permute-start.10 = (bf16[128,2048]{1,0:T(8,128)(2,1)S(1)}, bf16[128,2048]{1,0:T(8,128)(2,1)S(1)}, u32[]{:S(2)}, u32[]{:S(2)}) collective-permute-start(bf16[128,2048]{1,0:T(8,128)(2,1)S(1)} %collective-permute-done.8.refs_0_), channel_id=1, source_target_pairs={{0,32},{1,225},{2,34},{3,227},{4,36},{5,229},{6,38},{7,231},{8,40}... | collective-permute-start | bytes 1572872 | tf_op jit(solution)/shard_map/ppermute | solution.py:43
  44.8 0.2 collective-permute-start.11
  45.0 0.8 collective-permute-start.13
  45.7 0.6 collective-permute-done.7.refs_3_
  46.3 3.0 %pairs_3.1 = (bf16[4,2,32,1024]{3,2,1,0:T(8,128)(2,1)S(1)}, bf16[4,2,32,1024]{3,2,1,0:T(8,128)(2,1)S(1)}) custom-call(s32[5]{0:T(128)S(1)} %stack.23.at_ref.place_ref, bf16[128,2048]{1,0:T(8,128)(2,1)S(1)} %collective-permute-done.8.refs_0_, bf16[128,2048]{1,0:T(8,128)(2,1)S(1)} %collective-permute-done.9.refs_1_, ...), custom_call_target="tpu_custom_call" | custom-call | flops 2147483648 | bytes 8388608 | tf_op jit(solution)/shard_map/pairs_3/pallas_call | solution.py:155
  49.3 3.0 %collective-permute-start.12 = (bf16[4,2,32,1024]{3,2,1,0:T(8,128)(2,1)S(1)}, bf16[4,2,32,1024]{3,2,1,0:T(8,128)(2,1)S(1)}, u32[]{:S(2)}, u32[]{:S(2)}) collective-permute-start(bf16[4,2,32,1024]{3,2,1,0:T(8,128)(2,1)S(1)} %get-tuple-element.65), channel_id=1, source_target_pairs={{0,8},{1,9},{2,10},{3,11},{4,12},{5,13},{6,14},{7,15},{8,0},{9,1},... | collective-permute-start | bytes 1572872 | tf_op jit(solution)/shard_map/ppermute | solution.py:43
  52.3 2.0 %collective-permute-done.11.refs_5_ = bf16[2,2,2,32,1024]{4,3,2,1,0:T(8,128)(2,1)S(1)} collective-permute-done((bf16[2,2,2,32,1024]{4,3,2,1,0:T(8,128)(2,1)S(1)}, bf16[2,2,2,32,1024]{4,3,2,1,0:T(8,128)(2,1)S(1)}, u32[]{:S(2)}, u32[]{:S(2)}) %collective-permute-start.11) | collective-permute-done | bytes 524320 | tf_op jit(solution)/shard_map/ppermute | solution.py:43
  54.3 0.3 sum_1.1
  54.7 3.0 %collective-permute-done.13.refs_1_ = bf16[128,2048]{1,0:T(8,128)(2,1)S(1)} collective-permute-done((bf16[128,2048]{1,0:T(8,128)(2,1)S(1)}, bf16[128,2048]{1,0:T(8,128)(2,1)S(1)}, u32[]{:S(2)}, u32[]{:S(2)}) %collective-permute-start.13) | collective-permute-done | bytes 524320 | tf_op jit(solution)/shard_map/ppermute | solution.py:43
  57.7 1.9 %pairs_4.1 = (bf16[2,2,2,32,512]{4,3,2,1,0:T(8,128)(2,1)S(1)}, bf16[2,2,2,32,512]{4,3,2,1,0:T(8,128)(2,1)S(1)}) custom-call(s32[5]{0:T(128)S(1)} %stack.23.at_ref.place_ref, bf16[128,2048]{1,0:T(8,128)(2,1)S(1)} %collective-permute-done.10.refs_0_, bf16[128,2048]{1,0:T(8,128)(2,1)S(1)} %collective-permute-done.13.refs_1_, ...), custom_call_target="tpu_custom_call" | custom-call | flops 1073741824 | bytes 8388608 | tf_op jit(solution)/shard_map/pairs_4/pallas_call | solution.py:155
  59.7 3.9 %collective-permute-done.12.rc_ref = bf16[4,2,32,1024]{3,2,1,0:T(8,128)(2,1)S(1)} collective-permute-done((bf16[4,2,32,1024]{3,2,1,0:T(8,128)(2,1)S(1)}, bf16[4,2,32,1024]{3,2,1,0:T(8,128)(2,1)S(1)}, u32[]{:S(2)}, u32[]{:S(2)}) %collective-permute-start.12) | collective-permute-done | bytes 524320 | tf_op jit(solution)/shard_map/ppermute | solution.py:43
  63.5 3.7 %collective-permute-done.14.rd_ref = bf16[2,2,2,32,512]{4,3,2,1,0:T(8,128)(2,1)S(1)} collective-permute-done((bf16[2,2,2,32,512]{4,3,2,1,0:T(8,128)(2,1)S(1)}, bf16[2,2,2,32,512]{4,3,2,1,0:T(8,128)(2,1)S(1)}, u32[]{:S(2)}, u32[]{:S(2)}) %collective-permute-start.14) | collective-permute-done | bytes 262176 | tf_op jit(solution)/shard_map/ppermute | solution.py:43
  67.4 0.6 collective-permute-start.16
  68.0 0.7 sum_2.1
  68.7 2.7 %collective-permute-start.17 = (bf16[2,32,2560]{2,1,0:T(8,128)(2,1)S(1)}, bf16[2,32,2560]{2,1,0:T(8,128)(2,1)S(1)}, u32[]{:S(2)}, u32[]{:S(2)}) collective-permute-start(bf16[2,32,2560]{2,1,0:T(8,128)(2,1)S(1)} %get-tuple-element.76), channel_id=1, source_target_pairs={{0,8},{1,9},{2,10},{3,11},{4,12},{5,13},{6,14},{7,15},{8,0},{9,1},... | collective-permute-start | bytes 983048 | tf_op jit(solution)/shard_map/ppermute | solution.py:43
  71.4 4.2 %collective-permute-done.16.recv_ref = bf16[2,2,32,1536]{3,2,1,0:T(8,128)(2,1)S(1)} collective-permute-done((bf16[2,2,32,1536]{3,2,1,0:T(8,128)(2,1)S(1)}, bf16[2,2,32,1536]{3,2,1,0:T(8,128)(2,1)S(1)}, u32[]{:S(2)}, u32[]{:S(2)}) %collective-permute-start.16) | collective-permute-done | bytes 393248 | tf_op jit(solution)/shard_map/ppermute | solution.py:43
  75.6 0.6 sum_n.1
  76.3 2.8 %collective-permute-start.19 = (bf16[2,32,512]{2,1,0:T(8,128)(2,1)S(1)}, bf16[2,32,512]{2,1,0:T(8,128)(2,1)S(1)}, u32[]{:S(2)}, u32[]{:S(2)}) collective-permute-start(bf16[2,32,512]{2,1,0:T(8,128)(2,1)S(1)} %get-tuple-element.80), channel_id=1, source_target_pairs={{0,8},{1,9},{2,10},{3,11},{4,12},{5,13},{6,14},{7,15},{8,0},{9,1},... | collective-permute-start | bytes 196616 | tf_op jit(solution)/shard_map/ppermute | solution.py:43
  79.3 1.7 %collective-permute-done.19.refs_2_ = bf16[2,32,512]{2,1,0:T(8,128)(2,1)S(1)} collective-permute-done((bf16[2,32,512]{2,1,0:T(8,128)(2,1)S(1)}, bf16[2,32,512]{2,1,0:T(8,128)(2,1)S(1)}, u32[]{:S(2)}, u32[]{:S(2)}) %collective-permute-start.19) | collective-permute-done | bytes 65568 | tf_op jit(solution)/shard_map/ppermute | solution.py:43
  81.1 1.5 %collective-permute-start.20 = (bf16[2,32,1024]{2,1,0:T(8,128)(2,1)S(1)}, bf16[2,32,1024]{2,1,0:T(8,128)(2,1)S(1)}, u32[]{:S(2)}, u32[]{:S(2)}) collective-permute-start(bf16[2,32,1024]{2,1,0:T(8,128)(2,1)S(1)} %get-tuple-element.83), channel_id=1, source_target_pairs={{0,16},{1,17},{2,18},{3,19},{4,20},{5,21},{6,22},{7,23},{8,24},{9,... | collective-permute-start | bytes 393224 | tf_op jit(solution)/shard_map/ppermute | solution.py:43
  82.6 0.2 collective-permute-start.22
  82.9 1.6 %collective-permute-start.23 = (bf16[2,32,512]{2,1,0:T(8,128)(2,1)S(1)}, bf16[2,32,512]{2,1,0:T(8,128)(2,1)S(1)}, u32[]{:S(2)}, u32[]{:S(2)}) collective-permute-start(bf16[2,32,512]{2,1,0:T(8,128)(2,1)S(1)} %get-tuple-element.86), channel_id=1, source_target_pairs={{0,160},{1,97},{2,162},{3,99},{4,164},{5,101},{6,166},{7,103},{8,1... | collective-permute-start | bytes 196616 | tf_op jit(solution)/shard_map/ppermute | solution.py:43
  84.5 2.5 %collective-permute-done.21.refs_3_ = bf16[2,32,512]{2,1,0:T(8,128)(2,1)S(1)} collective-permute-done((bf16[2,32,512]{2,1,0:T(8,128)(2,1)S(1)}, bf16[2,32,512]{2,1,0:T(8,128)(2,1)S(1)}, u32[]{:S(2)}, u32[]{:S(2)}) %collective-permute-start.21) | collective-permute-done | bytes 65568 | tf_op jit(solution)/shard_map/ppermute | solution.py:43
  86.9 1.0 collective-permute-done.22.refs_4_
  87.9 2.6 %collective-permute-done.23.refs_5_ = bf16[2,32,512]{2,1,0:T(8,128)(2,1)S(1)} collective-permute-done((bf16[2,32,512]{2,1,0:T(8,128)(2,1)S(1)}, bf16[2,32,512]{2,1,0:T(8,128)(2,1)S(1)}, u32[]{:S(2)}, u32[]{:S(2)}) %collective-permute-start.23) | collective-permute-done | bytes 65568 | tf_op jit(solution)/shard_map/ppermute | solution.py:43
  90.5 0.6 split.1
  91.1 6.8 %collective-permute-start.24 = (bf16[2,16,4096]{2,1,0:T(8,128)(2,1)S(1)}, bf16[2,16,4096]{2,1,0:T(8,128)(2,1)S(1)}, u32[]{:S(2)}, u32[]{:S(2)}) collective-permute-start(bf16[2,16,4096]{2,1,0:T(8,128)(2,1)S(1)} %split.1), channel_id=1, source_target_pairs={{0,1},{1,0},{2,3},{3,2},{4,5},{5,4},{6,7},{7,6},{8,9},{9,8},{10,11... | collective-permute-start | bytes 786440 | tf_op jit(solution)/shard_map/ppermute | solution.py:43
  97.9 1.2 %collective-permute-done.24.refs_6_ = bf16[2,16,4096]{2,1,0:T(8,128)(2,1)S(1)} collective-permute-done((bf16[2,16,4096]{2,1,0:T(8,128)(2,1)S(1)}, bf16[2,16,4096]{2,1,0:T(8,128)(2,1)S(1)}, u32[]{:S(2)}, u32[]{:S(2)}) %collective-permute-start.24) | collective-permute-done | bytes 262176 | tf_op jit(solution)/shard_map/ppermute | solution.py:43
  99.1 1.5 %finish.1 = f32[2,16,4096]{2,1,0:T(8,128)} custom-call(s32[5]{0:T(128)S(1)} %stack.23.at_ref.place_ref, bf16[2,32,1024]{2,1,0:T(8,128)(2,1)S(1)} %get-tuple-element.77.refs_0_, bf16[2,32,512]{2,1,0:T(8,128)(2,1)S(1)} %get-tuple-element.82.refs_1_, bf16[2,32,1024]{2,1,0:T(8,128)(2,1)S(1)} %collective-permute-done.20.refs_2_, ...), custom_call_target="tpu_custom_call" | custom-call | flops 1000 | bytes 10485760 | tf_op jit(solution)/shard_map/finish/pallas_call | solution.py:174
  (27 shorter events, 1.1 us)
Async XLA Ops:
  0.0 17.7 %copy-start.1 = (s32[512]{0:T(512)S(1)}, s32[512]{0:T(512)}, u32[]{:S(2)}) copy-start(s32[512]{0:T(512)} %param.3) | copy-start | bytes 6148
  0.1 1.2 %copy-start = (bf16[2,2,512,256]{3,2,1,0:T(8,128)(2,1)S(1)}, bf16[2,2,512,256]{3,2,1,0:T(8,128)(2,1)}, u32[]{:S(2)}) copy-start(bf16[2,2,512,256]{3,2,1,0:T(8,128)(2,1)} %x_ref.1) | copy-start | bytes 3145732
  1.9 12.6 %collective-permute-start = (bf16[128,2048]{1,0:T(8,128)(2,1)S(1)}, bf16[128,2048]{1,0:T(8,128)(2,1)S(1)}, u32[]{:S(2)}, u32[]{:S(2)}) collective-permute-start(bf16[128,2048]{1,0:T(8,128)(2,1)S(1)} %whiten.2.a_ref.refs_2_), channel_id=1, source_target_pairs={{0,32},{1,225},{2,34},{3,227},{4,36},{5,229},{6,38},{7,231},{8,40}... | collective-permute-start | bytes 1572872 | tf_op jit(solution)/shard_map/ppermute | solution.py:43
  9.0 11.1 %collective-permute-start.1 = (bf16[128,2048]{1,0:T(8,128)(2,1)S(1)}, bf16[128,2048]{1,0:T(8,128)(2,1)S(1)}, u32[]{:S(2)}, u32[]{:S(2)}) collective-permute-start(bf16[128,2048]{1,0:T(8,128)(2,1)S(1)} %whiten.3.b_ref.refs_3_), channel_id=1, source_target_pairs={{0,32},{1,225},{2,34},{3,227},{4,36},{5,229},{6,38},{7,231},{8,40}... | collective-permute-start | bytes 1572872 | tf_op jit(solution)/shard_map/ppermute | solution.py:43
  9.8 19.4 %collective-permute-start.3 = (bf16[128,2048]{1,0:T(8,128)(2,1)S(1)}, bf16[128,2048]{1,0:T(8,128)(2,1)S(1)}, u32[]{:S(2)}, u32[]{:S(2)}) collective-permute-start(bf16[128,2048]{1,0:T(8,128)(2,1)S(1)} %whiten.2.a_ref.refs_2_), channel_id=1, source_target_pairs={{0,16},{1,17},{2,18},{3,19},{4,20},{5,21},{6,22},{7,23},{8,24},{9,... | collective-permute-start | bytes 1572872 | tf_op jit(solution)/shard_map/ppermute | solution.py:43
  11.1 23.4 %collective-permute-start.4 = (bf16[128,2048]{1,0:T(8,128)(2,1)S(1)}, bf16[128,2048]{1,0:T(8,128)(2,1)S(1)}, u32[]{:S(2)}, u32[]{:S(2)}) collective-permute-start(bf16[128,2048]{1,0:T(8,128)(2,1)S(1)} %whiten.3.b_ref.refs_3_), channel_id=1, source_target_pairs={{0,16},{1,17},{2,18},{3,19},{4,20},{5,21},{6,22},{7,23},{8,24},{9,... | collective-permute-start | bytes 1572872 | tf_op jit(solution)/shard_map/ppermute | solution.py:43
  14.5 14.7 %collective-permute-start.5 = (bf16[128,2048]{1,0:T(8,128)(2,1)S(1)}, bf16[128,2048]{1,0:T(8,128)(2,1)S(1)}, u32[]{:S(2)}, u32[]{:S(2)}) collective-permute-start(bf16[128,2048]{1,0:T(8,128)(2,1)S(1)} %collective-permute-done.refs_0_), channel_id=1, source_target_pairs={{0,32},{1,225},{2,34},{3,227},{4,36},{5,229},{6,38},{7,231},{8,40}... | collective-permute-start | bytes 1572872 | tf_op jit(solution)/shard_map/ppermute | solution.py:43
  20.2 11.2 %collective-permute-start.6 = (bf16[128,2048]{1,0:T(8,128)(2,1)S(1)}, bf16[128,2048]{1,0:T(8,128)(2,1)S(1)}, u32[]{:S(2)}, u32[]{:S(2)}) collective-permute-start(bf16[128,2048]{1,0:T(8,128)(2,1)S(1)} %collective-permute-done.1.refs_1_), channel_id=1, source_target_pairs={{0,32},{1,225},{2,34},{3,227},{4,36},{5,229},{6,38},{7,231},{8,40}... | collective-permute-start | bytes 1572872 | tf_op jit(solution)/shard_map/ppermute | solution.py:43
  26.7 8.8 %collective-permute-start.2 = (bf16[2,2,2,32,768]{4,3,2,1,0:T(8,128)(2,1)S(1)}, bf16[2,2,2,32,768]{4,3,2,1,0:T(8,128)(2,1)S(1)}, u32[]{:S(2)}, u32[]{:S(2)}) collective-permute-start(bf16[2,2,2,32,768]{4,3,2,1,0:T(8,128)(2,1)S(1)} %get-tuple-element.50), channel_id=1, source_target_pairs={{0,2},{1,7},{2,0},{3,5},{4,6},{5,3},{6,4},{7,1},{8,10},{9,15},{10,... | collective-permute-start | bytes 1179656 | tf_op jit(solution)/shard_map/ppermute | solution.py:43
  29.3 14.4 %collective-permute-start.8 = (bf16[128,2048]{1,0:T(8,128)(2,1)S(1)}, bf16[128,2048]{1,0:T(8,128)(2,1)S(1)}, u32[]{:S(2)}, u32[]{:S(2)}) collective-permute-start(bf16[128,2048]{1,0:T(8,128)(2,1)S(1)} %collective-permute-done.5.refs_0_), channel_id=1, source_target_pairs={{0,32},{1,225},{2,34},{3,227},{4,36},{5,229},{6,38},{7,231},{8,40}... | collective-permute-start | bytes 1572872 | tf_op jit(solution)/shard_map/ppermute | solution.py:43
  31.4 13.6 %collective-permute-start.9 = (bf16[128,2048]{1,0:T(8,128)(2,1)S(1)}, bf16[128,2048]{1,0:T(8,128)(2,1)S(1)}, u32[]{:S(2)}, u32[]{:S(2)}) collective-permute-start(bf16[128,2048]{1,0:T(8,128)(2,1)S(1)} %collective-permute-done.6.refs_1_), channel_id=1, source_target_pairs={{0,32},{1,225},{2,34},{3,227},{4,36},{5,229},{6,38},{7,231},{8,40}... | collective-permute-start | bytes 1572872 | tf_op jit(solution)/shard_map/ppermute | solution.py:43
  37.9 8.4 %collective-permute-start.7 = (bf16[2,2,2,32,768]{4,3,2,1,0:T(8,128)(2,1)S(1)}, bf16[2,2,2,32,768]{4,3,2,1,0:T(8,128)(2,1)S(1)}, u32[]{:S(2)}, u32[]{:S(2)}) collective-permute-start(bf16[2,2,2,32,768]{4,3,2,1,0:T(8,128)(2,1)S(1)} %get-tuple-element.57), channel_id=1, source_target_pairs={{0,2},{1,7},{2,0},{3,5},{4,6},{5,3},{6,4},{7,1},{8,10},{9,15},{10,... | collective-permute-start | bytes 1179656 | tf_op jit(solution)/shard_map/ppermute | solution.py:43
  43.7 8.7 %collective-permute-start.10 = (bf16[128,2048]{1,0:T(8,128)(2,1)S(1)}, bf16[128,2048]{1,0:T(8,128)(2,1)S(1)}, u32[]{:S(2)}, u32[]{:S(2)}) collective-permute-start(bf16[128,2048]{1,0:T(8,128)(2,1)S(1)} %collective-permute-done.8.refs_0_), channel_id=1, source_target_pairs={{0,32},{1,225},{2,34},{3,227},{4,36},{5,229},{6,38},{7,231},{8,40}... | collective-permute-start | bytes 1572872 | tf_op jit(solution)/shard_map/ppermute | solution.py:43
  44.8 9.5 %collective-permute-start.11 = (bf16[2,2,2,32,1024]{4,3,2,1,0:T(8,128)(2,1)S(1)}, bf16[2,2,2,32,1024]{4,3,2,1,0:T(8,128)(2,1)S(1)}, u32[]{:S(2)}, u32[]{:S(2)}) collective-permute-start(bf16[2,2,2,32,1024]{4,3,2,1,0:T(8,128)(2,1)S(1)} %get-tuple-element.63), channel_id=1, source_target_pairs={{0,2},{1,7},{2,0},{3,5},{4,6},{5,3},{6,4},{7,1},{8,10},{9,15},{10,... | collective-permute-start | bytes 1572872 | tf_op jit(solution)/shard_map/ppermute | solution.py:43
  45.0 12.7 %collective-permute-start.13 = (bf16[128,2048]{1,0:T(8,128)(2,1)S(1)}, bf16[128,2048]{1,0:T(8,128)(2,1)S(1)}, u32[]{:S(2)}, u32[]{:S(2)}) collective-permute-start(bf16[128,2048]{1,0:T(8,128)(2,1)S(1)} %collective-permute-done.9.refs_1_), channel_id=1, source_target_pairs={{0,32},{1,225},{2,34},{3,227},{4,36},{5,229},{6,38},{7,231},{8,40}... | collective-permute-start | bytes 1572872 | tf_op jit(solution)/shard_map/ppermute | solution.py:43
  49.3 14.2 %collective-permute-start.12 = (bf16[4,2,32,1024]{3,2,1,0:T(8,128)(2,1)S(1)}, bf16[4,2,32,1024]{3,2,1,0:T(8,128)(2,1)S(1)}, u32[]{:S(2)}, u32[]{:S(2)}) collective-permute-start(bf16[4,2,32,1024]{3,2,1,0:T(8,128)(2,1)S(1)} %get-tuple-element.65), channel_id=1, source_target_pairs={{0,8},{1,9},{2,10},{3,11},{4,12},{5,13},{6,14},{7,15},{8,0},{9,1},... | collective-permute-start | bytes 1572872 | tf_op jit(solution)/shard_map/ppermute | solution.py:43
  54.6 13.4 %collective-permute-start.15 = (bf16[2,2,32,2560]{3,2,1,0:T(8,128)(2,1)S(1)}, bf16[2,2,32,2560]{3,2,1,0:T(8,128)(2,1)S(1)}, u32[]{:S(2)}, u32[]{:S(2)}) collective-permute-start(bf16[2,2,32,2560]{3,2,1,0:T(8,128)(2,1)S(1)} %get-tuple-element.71), channel_id=1, source_target_pairs={{0,6},{1,3},{2,4},{3,1},{4,2},{5,7},{6,0},{7,5},{8,14},{9,11},{10,... | collective-permute-start | bytes 1966088 | tf_op jit(solution)/shard_map/ppermute | solution.py:43
  59.6 7.6 %collective-permute-start.14 = (bf16[2,2,2,32,512]{4,3,2,1,0:T(8,128)(2,1)S(1)}, bf16[2,2,2,32,512]{4,3,2,1,0:T(8,128)(2,1)S(1)}, u32[]{:S(2)}, u32[]{:S(2)}) collective-permute-start(bf16[2,2,2,32,512]{4,3,2,1,0:T(8,128)(2,1)S(1)} %get-tuple-element.68), channel_id=1, source_target_pairs={{0,6},{1,3},{2,4},{3,1},{4,2},{5,7},{6,0},{7,5},{8,14},{9,11},{10,... | collective-permute-start | bytes 786440 | tf_op jit(solution)/shard_map/ppermute | solution.py:43
  67.4 8.2 %collective-permute-start.16 = (bf16[2,2,32,1536]{3,2,1,0:T(8,128)(2,1)S(1)}, bf16[2,2,32,1536]{3,2,1,0:T(8,128)(2,1)S(1)}, u32[]{:S(2)}, u32[]{:S(2)}) collective-permute-start(bf16[2,2,32,1536]{3,2,1,0:T(8,128)(2,1)S(1)} %get-tuple-element.73), channel_id=1, source_target_pairs={{0,2},{1,7},{2,0},{3,5},{4,6},{5,3},{6,4},{7,1},{8,10},{9,15},{10,... | collective-permute-start | bytes 1179656 | tf_op jit(solution)/shard_map/ppermute | solution.py:43
  68.7 10.5 %collective-permute-start.17 = (bf16[2,32,2560]{2,1,0:T(8,128)(2,1)S(1)}, bf16[2,32,2560]{2,1,0:T(8,128)(2,1)S(1)}, u32[]{:S(2)}, u32[]{:S(2)}) collective-permute-start(bf16[2,32,2560]{2,1,0:T(8,128)(2,1)S(1)} %get-tuple-element.76), channel_id=1, source_target_pairs={{0,8},{1,9},{2,10},{3,11},{4,12},{5,13},{6,14},{7,15},{8,0},{9,1},... | collective-permute-start | bytes 983048 | tf_op jit(solution)/shard_map/ppermute | solution.py:43
  76.2 4.8 %collective-permute-start.18 = (bf16[2,32,1024]{2,1,0:T(8,128)(2,1)S(1)}, bf16[2,32,1024]{2,1,0:T(8,128)(2,1)S(1)}, u32[]{:S(2)}, u32[]{:S(2)}) collective-permute-start(bf16[2,32,1024]{2,1,0:T(8,128)(2,1)S(1)} %get-tuple-element.79), channel_id=1, source_target_pairs={{0,6},{1,3},{2,4},{3,1},{4,2},{5,7},{6,0},{7,5},{8,14},{9,11},{10,... | collective-permute-start | bytes 393224 | tf_op jit(solution)/shard_map/ppermute | solution.py:43
  76.3 4.7 %collective-permute-start.19 = (bf16[2,32,512]{2,1,0:T(8,128)(2,1)S(1)}, bf16[2,32,512]{2,1,0:T(8,128)(2,1)S(1)}, u32[]{:S(2)}, u32[]{:S(2)}) collective-permute-start(bf16[2,32,512]{2,1,0:T(8,128)(2,1)S(1)} %get-tuple-element.80), channel_id=1, source_target_pairs={{0,8},{1,9},{2,10},{3,11},{4,12},{5,13},{6,14},{7,15},{8,0},{9,1},... | collective-permute-start | bytes 196616 | tf_op jit(solution)/shard_map/ppermute | solution.py:43
  81.1 9.4 %collective-permute-start.20 = (bf16[2,32,1024]{2,1,0:T(8,128)(2,1)S(1)}, bf16[2,32,1024]{2,1,0:T(8,128)(2,1)S(1)}, u32[]{:S(2)}, u32[]{:S(2)}) collective-permute-start(bf16[2,32,1024]{2,1,0:T(8,128)(2,1)S(1)} %get-tuple-element.83), channel_id=1, source_target_pairs={{0,16},{1,17},{2,18},{3,19},{4,20},{5,21},{6,22},{7,23},{8,24},{9,... | collective-permute-start | bytes 393224 | tf_op jit(solution)/shard_map/ppermute | solution.py:43
  82.6 4.3 %collective-permute-start.21 = (bf16[2,32,512]{2,1,0:T(8,128)(2,1)S(1)}, bf16[2,32,512]{2,1,0:T(8,128)(2,1)S(1)}, u32[]{:S(2)}, u32[]{:S(2)}) collective-permute-start(bf16[2,32,512]{2,1,0:T(8,128)(2,1)S(1)} %get-tuple-element.84), channel_id=1, source_target_pairs={{0,224},{1,33},{2,226},{3,35},{4,228},{5,37},{6,230},{7,39},{8,232... | collective-permute-start | bytes 196616 | tf_op jit(solution)/shard_map/ppermute | solution.py:43
  82.6 5.3 %collective-permute-start.22 = (bf16[2,32,512]{2,1,0:T(8,128)(2,1)S(1)}, bf16[2,32,512]{2,1,0:T(8,128)(2,1)S(1)}, u32[]{:S(2)}, u32[]{:S(2)}) collective-permute-start(bf16[2,32,512]{2,1,0:T(8,128)(2,1)S(1)} %get-tuple-element.85), channel_id=1, source_target_pairs={{0,192},{1,65},{2,194},{3,67},{4,196},{5,69},{6,198},{7,71},{8,200... | collective-permute-start | bytes 196616 | tf_op jit(solution)/shard_map/ppermute | solution.py:43
  82.9 7.7 %collective-permute-start.23 = (bf16[2,32,512]{2,1,0:T(8,128)(2,1)S(1)}, bf16[2,32,512]{2,1,0:T(8,128)(2,1)S(1)}, u32[]{:S(2)}, u32[]{:S(2)}) collective-permute-start(bf16[2,32,512]{2,1,0:T(8,128)(2,1)S(1)} %get-tuple-element.86), channel_id=1, source_target_pairs={{0,160},{1,97},{2,162},{3,99},{4,164},{5,101},{6,166},{7,103},{8,1... | collective-permute-start | bytes 196616 | tf_op jit(solution)/shard_map/ppermute | solution.py:43
  91.1 8.0 %collective-permute-start.24 = (bf16[2,16,4096]{2,1,0:T(8,128)(2,1)S(1)}, bf16[2,16,4096]{2,1,0:T(8,128)(2,1)S(1)}, u32[]{:S(2)}, u32[]{:S(2)}) collective-permute-start(bf16[2,16,4096]{2,1,0:T(8,128)(2,1)S(1)} %split.1), channel_id=1, source_target_pairs={{0,1},{1,0},{2,3},{3,2},{4,5},{5,4},{6,7},{7,6},{8,9},{9,8},{10,11... | collective-permute-start | bytes 786440 | tf_op jit(solution)/shard_map/ppermute | solution.py:43

commit v13 on v12

--- a/solution.py
+++ b/solution.py
@@ -1,3 +1,4 @@
+import functools
 import math
 
 import jax
@@ -47,13 +48,16 @@
     return 1 - 2 * c
 
 
-def whiten_kernel(x_ref, o_ref):
+def whiten_kernel(half, spectra_ref, o_ref, x_ref, sem):
+    copy = pltpu.make_async_copy(spectra_ref.at[:, :, :, pl.ds(half * 128, 128)], x_ref, sem)
+    copy.start()
     row = lax.broadcasted_iota(jnp.int32, (BINS, BINS), 0)
     col = lax.broadcasted_iota(jnp.int32, (BINS, BINS), 1)
     window = (jnp.abs(row - col) <= HALF).astype(F32).astype(BF16)
     pos = lax.broadcasted_iota(jnp.int32, (1, BINS), 1)
     count = jnp.minimum(pos + HALF, BINS - 1) - jnp.maximum(pos - HALF, 0) + 1
     inverse = 1.0 / count.astype(F32)
+    copy.wait()
     for s in range(2):
         re = x_ref[0, s].astype(F32).T
         im = x_ref[1, s].astype(F32).T
@@ -69,12 +73,12 @@
 
 def whiten(spectra, half):
     return pl.pallas_call(
-        whiten_kernel,
-        grid=(1,),
-        in_specs=[pl.BlockSpec((2, 2, BINS, 128), lambda i: (0, 0, 0, half))],
-        out_specs=pl.BlockSpec((128, DEPTH), lambda i: (0, 0)),
+        functools.partial(whiten_kernel, half),
+        in_specs=[pl.BlockSpec(memory_space=pl.ANY)],
+        out_specs=pl.BlockSpec(memory_space=pltpu.VMEM),
         out_shape=jax.ShapeDtypeStruct((128, DEPTH), BF16),
-        compiler_params=params(12),
+        scratch_shapes=[pltpu.VMEM((2, 2, BINS, 128), BF16), pltpu.SemaphoreType.DMA],
+        compiler_params=params(60),
         cost_estimate=cost(2 * 4 * 128 * 512 * 512, MIB),
         name="whiten",
     )(spectra)

time: 103 us -> 106 us (1.029)
  Pallas kernels: 19.8 us -> 23.3 us
  local copies, waits for them, and re-layouts: 1.31 us -> 3.2 us
  waiting for transfers between devices: 34.1 us -> 32.3 us
    pallas_call x2, Pallas kernels: 1.21 us -> 4.83 us  [whiten(): pl.pallas_call(functools.partial(whiten_kernel, half), in_specs=[pl.Block...]
    unnamed x4 -> x10, local copies, waits for them, and re-layouts: 1.23 us -> 3.12 us
    ppermute x25, waiting for transfers between devices: 34.1 us -> 32.3 us  [move(): return lax.ppermute(x, AXES, pairs)]
  transfers between devices with their start and end apart: 25 -> 25, of which waited for: 15 -> 15; matrix products, arithmetic and copies ran while one was open for 0% -> 0% of each run, Pallas kernels for 17% -> 18%
where the time goes in v13:
time: 106 us; the launch traced here: 104 us
  starting transfers between devices  44.9 us (42%)
  waiting for transfers between devices  32.3 us (30%)
  Pallas kernels  23.3 us (22%)
  local copies, waits for them, and re-layouts  3.2 us (3%)
    ppermute x25, starting transfers between devices, move(): return lax.ppermute(x, AXES, pairs)  44.9 us
    ppermute x25, waiting for transfers between devices, move(): return lax.ppermute(x, AXES, pairs)  32.3 us
    pallas_call x5, Pallas kernels, products(): pl.pallas_call(kernel, in_specs=[pl.BlockSpec(memory_space=pltpu.SMEM)] +...  12.6 us
    pallas_call x2, Pallas kernels, whiten(): pl.pallas_call(functools.partial(whiten_kernel, half), in_specs=[pl.Block...  4.83 us
    pallas_call x8, Pallas kernels, call(): pl.pallas_call(kernel, in_specs=[pl.BlockSpec(memory_space=pltpu.SMEM)] *...  3.92 us
    unnamed x10, local copies, waits for them, and re-layouts  3.12 us
  transfers between devices with their start and end apart: 25, of which 15 were waited for; matrix products, arithmetic and copies ran while one was open for 0% of the time, Pallas kernels for 18%

profile of v13, /device:TPU:1, one launch (start us, length us, event | category | flops | bytes accessed | tf_op | source)
XLA Modules:
  0.0 104.1 jit_solution(10363416908426294367)
XLA Ops:
  0.1 2.4 %whiten.2.a_ref.refs_2_ = bf16[128,2048]{1,0:T(8,128)(2,1)} custom-call(bf16[2,2,512,256]{3,2,1,0:T(8,128)(2,1)} %spectra_ref.1), custom_call_target="tpu_custom_call" | custom-call | flops 268435456 | bytes 1048576 | tf_op jit(solution)/shard_map/whiten/pallas_call | solution.py:75
  2.5 6.5 %collective-permute-start = (bf16[128,2048]{1,0:T(8,128)(2,1)}, bf16[128,2048]{1,0:T(8,128)(2,1)S(1)}, u32[]{:S(2)}, u32[]{:S(2)}) collective-permute-start(bf16[128,2048]{1,0:T(8,128)(2,1)} %whiten.2.a_ref.refs_2_), channel_id=1, source_target_pairs={{0,32},{1,225},{2,34},{3,227},{4,36},{5,229},{6,38},{7,231},{8,40}... | collective-permute-start | bytes 1572872 | tf_op jit(solution)/shard_map/ppermute | solution.py:44
  9.0 2.4 %whiten.3.b_ref.refs_3_ = bf16[128,2048]{1,0:T(8,128)(2,1)} custom-call(bf16[2,2,512,256]{3,2,1,0:T(8,128)(2,1)} %spectra_ref.1), custom_call_target="tpu_custom_call" | custom-call | flops 268435456 | bytes 1048576 | tf_op jit(solution)/shard_map/whiten/pallas_call | solution.py:75
  11.4 0.8 collective-permute-start.1
  12.2 1.3 %collective-permute-start.3 = (bf16[128,2048]{1,0:T(8,128)(2,1)}, bf16[128,2048]{1,0:T(8,128)(2,1)S(1)}, u32[]{:S(2)}, u32[]{:S(2)}) collective-permute-start(bf16[128,2048]{1,0:T(8,128)(2,1)} %whiten.2.a_ref.refs_2_), channel_id=1, source_target_pairs={{0,16},{1,17},{2,18},{3,19},{4,20},{5,21},{6,22},{7,23},{8,24},{9,... | collective-permute-start | bytes 1572872 | tf_op jit(solution)/shard_map/ppermute | solution.py:44
  13.7 1.7 %collective-permute-done.refs_0_ = bf16[128,2048]{1,0:T(8,128)(2,1)S(1)} collective-permute-done((bf16[128,2048]{1,0:T(8,128)(2,1)}, bf16[128,2048]{1,0:T(8,128)(2,1)S(1)}, u32[]{:S(2)}, u32[]{:S(2)}) %collective-permute-start) | collective-permute-done | bytes 524320 | tf_op jit(solution)/shard_map/ppermute | solution.py:44
  15.4 3.0 %collective-permute-start.5 = (bf16[128,2048]{1,0:T(8,128)(2,1)S(1)}, bf16[128,2048]{1,0:T(8,128)(2,1)S(1)}, u32[]{:S(2)}, u32[]{:S(2)}) collective-permute-start(bf16[128,2048]{1,0:T(8,128)(2,1)S(1)} %collective-permute-done.refs_0_), channel_id=1, source_target_pairs={{0,32},{1,225},{2,34},{3,227},{4,36},{5,229},{6,38},{7,231},{8,40}... | collective-permute-start | bytes 1572872 | tf_op jit(solution)/shard_map/ppermute | solution.py:44
  18.6 2.5 %collective-permute-done.1.refs_1_ = bf16[128,2048]{1,0:T(8,128)(2,1)S(1)} collective-permute-done((bf16[128,2048]{1,0:T(8,128)(2,1)}, bf16[128,2048]{1,0:T(8,128)(2,1)S(1)}, u32[]{:S(2)}, u32[]{:S(2)}) %collective-permute-start.1) | collective-permute-done | bytes 524320 | tf_op jit(solution)/shard_map/ppermute | solution.py:44
  21.1 3.0 %collective-permute-start.6 = (bf16[128,2048]{1,0:T(8,128)(2,1)S(1)}, bf16[128,2048]{1,0:T(8,128)(2,1)S(1)}, u32[]{:S(2)}, u32[]{:S(2)}) collective-permute-start(bf16[128,2048]{1,0:T(8,128)(2,1)S(1)} %collective-permute-done.1.refs_1_), channel_id=1, source_target_pairs={{0,32},{1,225},{2,34},{3,227},{4,36},{5,229},{6,38},{7,231},{8,40}... | collective-permute-start | bytes 1572872 | tf_op jit(solution)/shard_map/ppermute | solution.py:44
  24.1 1.0 copy-done
  25.1 1.0 copy-done.2
  26.2 1.0 rotate.2
  27.2 1.0 copy-done.1
  28.2 2.4 %pairs_own.1 = (bf16[2,2,2,32,768]{4,3,2,1,0:T(8,128)(2,1)S(1)}, bf16[2,2,2,32,768]{4,3,2,1,0:T(8,128)(2,1)S(1)}) custom-call(s32[5]{0:T(128)S(1)} %stack.23.at_ref.place_ref, bf16[128,2048]{1,0:T(8,128)(2,1)S(1)} %collective-permute-done.refs_0_, bf16[128,2048]{1,0:T(8,128)(2,1)S(1)} %collective-permute-done.1.refs_1_, bf16[128,2048]{1,0:T(8,128)(2,1)S(1)} %copy-done.3, ...), custom_call_target="tpu_custom_call" | custom-call | flops 1610612736 | bytes 8388608 | tf_op jit(solution)/shard_map/pairs_own/pallas_call | solution.py:159
  30.6 2.6 %collective-permute-start.2 = (bf16[2,2,2,32,768]{4,3,2,1,0:T(8,128)(2,1)S(1)}, bf16[2,2,2,32,768]{4,3,2,1,0:T(8,128)(2,1)S(1)}, u32[]{:S(2)}, u32[]{:S(2)}) collective-permute-start(bf16[2,2,2,32,768]{4,3,2,1,0:T(8,128)(2,1)S(1)} %get-tuple-element.50), channel_id=1, source_target_pairs={{0,2},{1,7},{2,0},{3,5},{4,6},{5,3},{6,4},{7,1},{8,10},{9,15},{10,... | collective-permute-start | bytes 1179656 | tf_op jit(solution)/shard_map/ppermute | solution.py:44
  33.2 2.1 %collective-permute-start.9 = (bf16[128,2048]{1,0:T(8,128)(2,1)S(1)}, bf16[128,2048]{1,0:T(8,128)(2,1)S(1)}, u32[]{:S(2)}, u32[]{:S(2)}) collective-permute-start(bf16[128,2048]{1,0:T(8,128)(2,1)S(1)} %collective-permute-done.6.refs_1_), channel_id=1, source_target_pairs={{0,32},{1,225},{2,34},{3,227},{4,36},{5,229},{6,38},{7,231},{8,40}... | collective-permute-start | bytes 1572872 | tf_op jit(solution)/shard_map/ppermute | solution.py:44
  35.3 1.0 collective-permute-done.4.b_ref.refs_3_
  36.3 1.0 rotate.3
  37.3 1.6 %collective-permute-done.2.refs_1_ = bf16[2,2,2,32,768]{4,3,2,1,0:T(8,128)(2,1)S(1)} collective-permute-done((bf16[2,2,2,32,768]{4,3,2,1,0:T(8,128)(2,1)S(1)}, bf16[2,2,2,32,768]{4,3,2,1,0:T(8,128)(2,1)S(1)}, u32[]{:S(2)}, u32[]{:S(2)}) %collective-permute-start.2) | collective-permute-done | bytes 393248 | tf_op jit(solution)/shard_map/ppermute | solution.py:44
  38.8 2.4 %pairs_near.1 = (bf16[2,2,2,32,768]{4,3,2,1,0:T(8,128)(2,1)S(1)}, bf16[2,2,2,32,768]{4,3,2,1,0:T(8,128)(2,1)S(1)}) custom-call(s32[5]{0:T(128)S(1)} %stack.23.at_ref.place_ref, bf16[128,2048]{1,0:T(8,128)(2,1)S(1)} %collective-permute-done.refs_0_, bf16[128,2048]{1,0:T(8,128)(2,1)S(1)} %collective-permute-done.1.refs_1_, ...), custom_call_target="tpu_custom_call" | custom-call | flops 1610612736 | bytes 8388608 | tf_op jit(solution)/shard_map/pairs_near/pallas_call | solution.py:159
  41.3 2.7 %collective-permute-start.7 = (bf16[2,2,2,32,768]{4,3,2,1,0:T(8,128)(2,1)S(1)}, bf16[2,2,2,32,768]{4,3,2,1,0:T(8,128)(2,1)S(1)}, u32[]{:S(2)}, u32[]{:S(2)}) collective-permute-start(bf16[2,2,2,32,768]{4,3,2,1,0:T(8,128)(2,1)S(1)} %get-tuple-element.57), channel_id=1, source_target_pairs={{0,2},{1,7},{2,0},{3,5},{4,6},{5,3},{6,4},{7,1},{8,10},{9,15},{10,... | collective-permute-start | bytes 1179656 | tf_op jit(solution)/shard_map/ppermute | solution.py:44
  44.0 3.0 %pairs_2.1 = (bf16[2,2,2,32,1024]{4,3,2,1,0:T(8,128)(2,1)S(1)}, bf16[2,2,2,32,1024]{4,3,2,1,0:T(8,128)(2,1)S(1)}) custom-call(s32[5]{0:T(128)S(1)} %stack.23.at_ref.place_ref, bf16[128,2048]{1,0:T(8,128)(2,1)S(1)} %collective-permute-done.5.refs_0_, bf16[128,2048]{1,0:T(8,128)(2,1)S(1)} %collective-permute-done.6.refs_1_, ...), custom_call_target="tpu_custom_call" | custom-call | flops 2147483648 | bytes 8388608 | tf_op jit(solution)/shard_map/pairs_2/pallas_call | solution.py:159
  47.0 0.4 collective-permute-start.10
  47.6 0.4 collective-permute-start.13
  48.1 1.6 %collective-permute-done.7.refs_3_ = bf16[2,2,2,32,768]{4,3,2,1,0:T(8,128)(2,1)S(1)} collective-permute-done((bf16[2,2,2,32,768]{4,3,2,1,0:T(8,128)(2,1)S(1)}, bf16[2,2,2,32,768]{4,3,2,1,0:T(8,128)(2,1)S(1)}, u32[]{:S(2)}, u32[]{:S(2)}) %collective-permute-start.7) | collective-permute-done | bytes 393248 | tf_op jit(solution)/shard_map/ppermute | solution.py:44
  49.7 3.0 %pairs_3.1 = (bf16[4,2,32,1024]{3,2,1,0:T(8,128)(2,1)S(1)}, bf16[4,2,32,1024]{3,2,1,0:T(8,128)(2,1)S(1)}) custom-call(s32[5]{0:T(128)S(1)} %stack.23.at_ref.place_ref, bf16[128,2048]{1,0:T(8,128)(2,1)S(1)} %collective-permute-done.8.refs_0_, bf16[128,2048]{1,0:T(8,128)(2,1)S(1)} %collective-permute-done.9.refs_1_, ...), custom_call_target="tpu_custom_call" | custom-call | flops 2147483648 | bytes 8388608 | tf_op jit(solution)/shard_map/pairs_3/pallas_call | solution.py:159
  52.6 3.0 %collective-permute-start.12 = (bf16[4,2,32,1024]{3,2,1,0:T(8,128)(2,1)S(1)}, bf16[4,2,32,1024]{3,2,1,0:T(8,128)(2,1)S(1)}, u32[]{:S(2)}, u32[]{:S(2)}) collective-permute-start(bf16[4,2,32,1024]{3,2,1,0:T(8,128)(2,1)S(1)} %get-tuple-element.65), channel_id=1, source_target_pairs={{0,8},{1,9},{2,10},{3,11},{4,12},{5,13},{6,14},{7,15},{8,0},{9,1},... | collective-permute-start | bytes 1572872 | tf_op jit(solution)/shard_map/ppermute | solution.py:44
  55.7 1.3 %collective-permute-done.11.refs_5_ = bf16[2,2,2,32,1024]{4,3,2,1,0:T(8,128)(2,1)S(1)} collective-permute-done((bf16[2,2,2,32,1024]{4,3,2,1,0:T(8,128)(2,1)S(1)}, bf16[2,2,2,32,1024]{4,3,2,1,0:T(8,128)(2,1)S(1)}, u32[]{:S(2)}, u32[]{:S(2)}) %collective-permute-start.11) | collective-permute-done | bytes 524320 | tf_op jit(solution)/shard_map/ppermute | solution.py:44
  57.4 3.6 %collective-permute-done.13.refs_1_ = bf16[128,2048]{1,0:T(8,128)(2,1)S(1)} collective-permute-done((bf16[128,2048]{1,0:T(8,128)(2,1)S(1)}, bf16[128,2048]{1,0:T(8,128)(2,1)S(1)}, u32[]{:S(2)}, u32[]{:S(2)}) %collective-permute-start.13) | collective-permute-done | bytes 524320 | tf_op jit(solution)/shard_map/ppermute | solution.py:44
  61.0 1.9 %pairs_4.1 = (bf16[2,2,2,32,512]{4,3,2,1,0:T(8,128)(2,1)S(1)}, bf16[2,2,2,32,512]{4,3,2,1,0:T(8,128)(2,1)S(1)}) custom-call(s32[5]{0:T(128)S(1)} %stack.23.at_ref.place_ref, bf16[128,2048]{1,0:T(8,128)(2,1)S(1)} %collective-permute-done.10.refs_0_, bf16[128,2048]{1,0:T(8,128)(2,1)S(1)} %collective-permute-done.13.refs_1_, ...), custom_call_target="tpu_custom_call" | custom-call | flops 1073741824 | bytes 8388608 | tf_op jit(solution)/shard_map/pairs_4/pallas_call | solution.py:159
  63.0 3.5 %collective-permute-done.12.rc_ref = bf16[4,2,32,1024]{3,2,1,0:T(8,128)(2,1)S(1)} collective-permute-done((bf16[4,2,32,1024]{3,2,1,0:T(8,128)(2,1)S(1)}, bf16[4,2,32,1024]{3,2,1,0:T(8,128)(2,1)S(1)}, u32[]{:S(2)}, u32[]{:S(2)}) %collective-permute-start.12) | collective-permute-done | bytes 524320 | tf_op jit(solution)/shard_map/ppermute | solution.py:44
  66.5 3.4 %collective-permute-done.14.rd_ref = bf16[2,2,2,32,512]{4,3,2,1,0:T(8,128)(2,1)S(1)} collective-permute-done((bf16[2,2,2,32,512]{4,3,2,1,0:T(8,128)(2,1)S(1)}, bf16[2,2,2,32,512]{4,3,2,1,0:T(8,128)(2,1)S(1)}, u32[]{:S(2)}, u32[]{:S(2)}) %collective-permute-start.14) | collective-permute-done | bytes 262176 | tf_op jit(solution)/shard_map/ppermute | solution.py:44
  70.1 1.3 %collective-permute-start.16 = (bf16[2,2,32,1536]{3,2,1,0:T(8,128)(2,1)S(1)}, bf16[2,2,32,1536]{3,2,1,0:T(8,128)(2,1)S(1)}, u32[]{:S(2)}, u32[]{:S(2)}) collective-permute-start(bf16[2,2,32,1536]{3,2,1,0:T(8,128)(2,1)S(1)} %get-tuple-element.73), channel_id=1, source_target_pairs={{0,2},{1,7},{2,0},{3,5},{4,6},{5,3},{6,4},{7,1},{8,10},{9,15},{10,... | collective-permute-start | bytes 1179656 | tf_op jit(solution)/shard_map/ppermute | solution.py:44
  71.3 0.7 sum_2.1
  72.0 2.6 %collective-permute-start.17 = (bf16[2,32,2560]{2,1,0:T(8,128)(2,1)S(1)}, bf16[2,32,2560]{2,1,0:T(8,128)(2,1)S(1)}, u32[]{:S(2)}, u32[]{:S(2)}) collective-permute-start(bf16[2,32,2560]{2,1,0:T(8,128)(2,1)S(1)} %get-tuple-element.76), channel_id=1, source_target_pairs={{0,8},{1,9},{2,10},{3,11},{4,12},{5,13},{6,14},{7,15},{8,0},{9,1},... | collective-permute-start | bytes 983048 | tf_op jit(solution)/shard_map/ppermute | solution.py:44
  74.6 3.7 %collective-permute-done.16.recv_ref = bf16[2,2,32,1536]{3,2,1,0:T(8,128)(2,1)S(1)} collective-permute-done((bf16[2,2,32,1536]{3,2,1,0:T(8,128)(2,1)S(1)}, bf16[2,2,32,1536]{3,2,1,0:T(8,128)(2,1)S(1)}, u32[]{:S(2)}, u32[]{:S(2)}) %collective-permute-start.16) | collective-permute-done | bytes 393248 | tf_op jit(solution)/shard_map/ppermute | solution.py:44
  78.3 0.6 sum_n.1
  79.0 2.8 %collective-permute-start.19 = (bf16[2,32,512]{2,1,0:T(8,128)(2,1)S(1)}, bf16[2,32,512]{2,1,0:T(8,128)(2,1)S(1)}, u32[]{:S(2)}, u32[]{:S(2)}) collective-permute-start(bf16[2,32,512]{2,1,0:T(8,128)(2,1)S(1)} %get-tuple-element.80), channel_id=1, source_target_pairs={{0,8},{1,9},{2,10},{3,11},{4,12},{5,13},{6,14},{7,15},{8,0},{9,1},... | collective-permute-start | bytes 196616 | tf_op jit(solution)/shard_map/ppermute | solution.py:44
  81.8 1.4 %collective-permute-done.17.refs_1_ = bf16[2,32,2560]{2,1,0:T(8,128)(2,1)S(1)} collective-permute-done((bf16[2,32,2560]{2,1,0:T(8,128)(2,1)S(1)}, bf16[2,32,2560]{2,1,0:T(8,128)(2,1)S(1)}, u32[]{:S(2)}, u32[]{:S(2)}) %collective-permute-start.17) | collective-permute-done | bytes 327712 | tf_op jit(solution)/shard_map/ppermute | solution.py:44
  83.8 1.5 %collective-permute-start.20 = (bf16[2,32,1024]{2,1,0:T(8,128)(2,1)S(1)}, bf16[2,32,1024]{2,1,0:T(8,128)(2,1)S(1)}, u32[]{:S(2)}, u32[]{:S(2)}) collective-permute-start(bf16[2,32,1024]{2,1,0:T(8,128)(2,1)S(1)} %get-tuple-element.83), channel_id=1, source_target_pairs={{0,16},{1,17},{2,18},{3,19},{4,20},{5,21},{6,22},{7,23},{8,24},{9,... | collective-permute-start | bytes 393224 | tf_op jit(solution)/shard_map/ppermute | solution.py:44
  85.3 0.8 collective-permute-start.21
  86.5 0.7 collective-permute-start.23
  87.3 2.3 %collective-permute-done.21.refs_3_ = bf16[2,32,512]{2,1,0:T(8,128)(2,1)S(1)} collective-permute-done((bf16[2,32,512]{2,1,0:T(8,128)(2,1)S(1)}, bf16[2,32,512]{2,1,0:T(8,128)(2,1)S(1)}, u32[]{:S(2)}, u32[]{:S(2)}) %collective-permute-start.21) | collective-permute-done | bytes 65568 | tf_op jit(solution)/shard_map/ppermute | solution.py:44
  89.6 3.1 %collective-permute-done.22.refs_4_ = bf16[2,32,512]{2,1,0:T(8,128)(2,1)S(1)} collective-permute-done((bf16[2,32,512]{2,1,0:T(8,128)(2,1)S(1)}, bf16[2,32,512]{2,1,0:T(8,128)(2,1)S(1)}, u32[]{:S(2)}, u32[]{:S(2)}) %collective-permute-start.22) | collective-permute-done | bytes 65568 | tf_op jit(solution)/shard_map/ppermute | solution.py:44
  92.7 0.6 split.1
  93.3 8.1 %collective-permute-start.24 = (bf16[2,16,4096]{2,1,0:T(8,128)(2,1)S(1)}, bf16[2,16,4096]{2,1,0:T(8,128)(2,1)S(1)}, u32[]{:S(2)}, u32[]{:S(2)}) collective-permute-start(bf16[2,16,4096]{2,1,0:T(8,128)(2,1)S(1)} %split.1), channel_id=1, source_target_pairs={{0,1},{1,0},{2,3},{3,2},{4,5},{5,4},{6,7},{7,6},{8,9},{9,8},{10,11... | collective-permute-start | bytes 786440 | tf_op jit(solution)/shard_map/ppermute | solution.py:44
  101.5 1.2 %collective-permute-done.24.refs_6_ = bf16[2,16,4096]{2,1,0:T(8,128)(2,1)S(1)} collective-permute-done((bf16[2,16,4096]{2,1,0:T(8,128)(2,1)S(1)}, bf16[2,16,4096]{2,1,0:T(8,128)(2,1)S(1)}, u32[]{:S(2)}, u32[]{:S(2)}) %collective-permute-start.24) | collective-permute-done | bytes 262176 | tf_op jit(solution)/shard_map/ppermute | solution.py:44
  102.6 1.5 %finish.1 = f32[2,16,4096]{2,1,0:T(8,128)} custom-call(s32[5]{0:T(128)S(1)} %stack.23.at_ref.place_ref, bf16[2,32,1024]{2,1,0:T(8,128)(2,1)S(1)} %get-tuple-element.77.refs_0_, bf16[2,32,512]{2,1,0:T(8,128)(2,1)S(1)} %get-tuple-element.82.refs_1_, bf16[2,32,1024]{2,1,0:T(8,128)(2,1)S(1)} %collective-permute-done.20.refs_2_, ...), custom_call_target="tpu_custom_call" | custom-call | flops 1000 | bytes 10485760 | tf_op jit(solution)/shard_map/finish/pallas_call | solution.py:178
  (33 shorter events, 2.4 us)
Async XLA Ops:
  0.0 18.5 %copy-start.4 = (s32[512]{0:T(512)S(1)}, s32[512]{0:T(512)}, u32[]{:S(2)}) copy-start(s32[512]{0:T(512)} %param.3) | copy-start | bytes 6148
  2.5 24.6 %copy-start.3 = (bf16[128,2048]{1,0:T(8,128)(2,1)S(1)}, bf16[128,2048]{1,0:T(8,128)(2,1)}, u32[]{:S(2)}) copy-start(bf16[128,2048]{1,0:T(8,128)(2,1)} %whiten.2.a_ref.refs_2_) | copy-start | bytes 1572868
  2.5 12.9 %collective-permute-start = (bf16[128,2048]{1,0:T(8,128)(2,1)}, bf16[128,2048]{1,0:T(8,128)(2,1)S(1)}, u32[]{:S(2)}, u32[]{:S(2)}) collective-permute-start(bf16[128,2048]{1,0:T(8,128)(2,1)} %whiten.2.a_ref.refs_2_), channel_id=1, source_target_pairs={{0,32},{1,225},{2,34},{3,227},{4,36},{5,229},{6,38},{7,231},{8,40}... | collective-permute-start | bytes 1572872 | tf_op jit(solution)/shard_map/ppermute | solution.py:44
  11.4 9.6 %collective-permute-start.1 = (bf16[128,2048]{1,0:T(8,128)(2,1)}, bf16[128,2048]{1,0:T(8,128)(2,1)S(1)}, u32[]{:S(2)}, u32[]{:S(2)}) collective-permute-start(bf16[128,2048]{1,0:T(8,128)(2,1)} %whiten.3.b_ref.refs_3_), channel_id=1, source_target_pairs={{0,32},{1,225},{2,34},{3,227},{4,36},{5,229},{6,38},{7,231},{8,40}... | collective-permute-start | bytes 1572872 | tf_op jit(solution)/shard_map/ppermute | solution.py:44
  12.2 21.0 %collective-permute-start.3 = (bf16[128,2048]{1,0:T(8,128)(2,1)}, bf16[128,2048]{1,0:T(8,128)(2,1)S(1)}, u32[]{:S(2)}, u32[]{:S(2)}) collective-permute-start(bf16[128,2048]{1,0:T(8,128)(2,1)} %whiten.2.a_ref.refs_2_), channel_id=1, source_target_pairs={{0,16},{1,17},{2,18},{3,19},{4,20},{5,21},{6,22},{7,23},{8,24},{9,... | collective-permute-start | bytes 1572872 | tf_op jit(solution)/shard_map/ppermute | solution.py:44
  13.5 22.8 %collective-permute-start.4 = (bf16[128,2048]{1,0:T(8,128)(2,1)}, bf16[128,2048]{1,0:T(8,128)(2,1)S(1)}, u32[]{:S(2)}, u32[]{:S(2)}) collective-permute-start(bf16[128,2048]{1,0:T(8,128)(2,1)} %whiten.3.b_ref.refs_3_), channel_id=1, source_target_pairs={{0,16},{1,17},{2,18},{3,19},{4,20},{5,21},{6,22},{7,23},{8,24},{9,... | collective-permute-start | bytes 1572872 | tf_op jit(solution)/shard_map/ppermute | solution.py:44
  15.4 17.8 %collective-permute-start.5 = (bf16[128,2048]{1,0:T(8,128)(2,1)S(1)}, bf16[128,2048]{1,0:T(8,128)(2,1)S(1)}, u32[]{:S(2)}, u32[]{:S(2)}) collective-permute-start(bf16[128,2048]{1,0:T(8,128)(2,1)S(1)} %collective-permute-done.refs_0_), channel_id=1, source_target_pairs={{0,32},{1,225},{2,34},{3,227},{4,36},{5,229},{6,38},{7,231},{8,40}... | collective-permute-start | bytes 1572872 | tf_op jit(solution)/shard_map/ppermute | solution.py:44
  21.1 12.1 %collective-permute-start.6 = (bf16[128,2048]{1,0:T(8,128)(2,1)S(1)}, bf16[128,2048]{1,0:T(8,128)(2,1)S(1)}, u32[]{:S(2)}, u32[]{:S(2)}) collective-permute-start(bf16[128,2048]{1,0:T(8,128)(2,1)S(1)} %collective-permute-done.1.refs_1_), channel_id=1, source_target_pairs={{0,32},{1,225},{2,34},{3,227},{4,36},{5,229},{6,38},{7,231},{8,40}... | collective-permute-start | bytes 1572872 | tf_op jit(solution)/shard_map/ppermute | solution.py:44
  24.1 1.0 %copy-start = (bf16[128,2048]{1,0:T(8,128)(2,1)S(1)}, bf16[128,2048]{1,0:T(8,128)(2,1)}, u32[]{:S(2)}) copy-start(bf16[128,2048]{1,0:T(8,128)(2,1)} %whiten.3.b_ref.refs_3_) | copy-start | bytes 1572868
  25.1 1.0 %copy-start.2 = (bf16[128,2048]{1,0:T(8,128)(2,1)S(1)}, bf16[128,2048]{1,0:T(8,128)(2,1)}, u32[]{:S(2)}) copy-start(bf16[128,2048]{1,0:T(8,128)(2,1)} %whiten.2.a_ref.refs_2_) | copy-start | bytes 1572868
  27.2 1.0 %copy-start.1 = (bf16[128,2048]{1,0:T(8,128)(2,1)S(1)}, bf16[128,2048]{1,0:T(8,128)(2,1)}, u32[]{:S(2)}) copy-start(bf16[128,2048]{1,0:T(8,128)(2,1)} %whiten.3.b_ref.refs_3_) | copy-start | bytes 1572868
  30.6 8.2 %collective-permute-start.2 = (bf16[2,2,2,32,768]{4,3,2,1,0:T(8,128)(2,1)S(1)}, bf16[2,2,2,32,768]{4,3,2,1,0:T(8,128)(2,1)S(1)}, u32[]{:S(2)}, u32[]{:S(2)}) collective-permute-start(bf16[2,2,2,32,768]{4,3,2,1,0:T(8,128)(2,1)S(1)} %get-tuple-element.50), channel_id=1, source_target_pairs={{0,2},{1,7},{2,0},{3,5},{4,6},{5,3},{6,4},{7,1},{8,10},{9,15},{10,... | collective-permute-start | bytes 1179656 | tf_op jit(solution)/shard_map/ppermute | solution.py:44
  33.2 13.8 %collective-permute-start.8 = (bf16[128,2048]{1,0:T(8,128)(2,1)S(1)}, bf16[128,2048]{1,0:T(8,128)(2,1)S(1)}, u32[]{:S(2)}, u32[]{:S(2)}) collective-permute-start(bf16[128,2048]{1,0:T(8,128)(2,1)S(1)} %collective-permute-done.5.refs_0_), channel_id=1, source_target_pairs={{0,32},{1,225},{2,34},{3,227},{4,36},{5,229},{6,38},{7,231},{8,40}... | collective-permute-start | bytes 1572872 | tf_op jit(solution)/shard_map/ppermute | solution.py:44
  33.2 14.4 %collective-permute-start.9 = (bf16[128,2048]{1,0:T(8,128)(2,1)S(1)}, bf16[128,2048]{1,0:T(8,128)(2,1)S(1)}, u32[]{:S(2)}, u32[]{:S(2)}) collective-permute-start(bf16[128,2048]{1,0:T(8,128)(2,1)S(1)} %collective-permute-done.6.refs_1_), channel_id=1, source_target_pairs={{0,32},{1,225},{2,34},{3,227},{4,36},{5,229},{6,38},{7,231},{8,40}... | collective-permute-start | bytes 1572872 | tf_op jit(solution)/shard_map/ppermute | solution.py:44
  41.3 8.4 %collective-permute-start.7 = (bf16[2,2,2,32,768]{4,3,2,1,0:T(8,128)(2,1)S(1)}, bf16[2,2,2,32,768]{4,3,2,1,0:T(8,128)(2,1)S(1)}, u32[]{:S(2)}, u32[]{:S(2)}) collective-permute-start(bf16[2,2,2,32,768]{4,3,2,1,0:T(8,128)(2,1)S(1)} %get-tuple-element.57), channel_id=1, source_target_pairs={{0,2},{1,7},{2,0},{3,5},{4,6},{5,3},{6,4},{7,1},{8,10},{9,15},{10,... | collective-permute-start | bytes 1179656 | tf_op jit(solution)/shard_map/ppermute | solution.py:44
  47.0 8.7 %collective-permute-start.10 = (bf16[128,2048]{1,0:T(8,128)(2,1)S(1)}, bf16[128,2048]{1,0:T(8,128)(2,1)S(1)}, u32[]{:S(2)}, u32[]{:S(2)}) collective-permute-start(bf16[128,2048]{1,0:T(8,128)(2,1)S(1)} %collective-permute-done.8.refs_0_), channel_id=1, source_target_pairs={{0,32},{1,225},{2,34},{3,227},{4,36},{5,229},{6,38},{7,231},{8,40}... | collective-permute-start | bytes 1572872 | tf_op jit(solution)/shard_map/ppermute | solution.py:44
  47.4 9.5 %collective-permute-start.11 = (bf16[2,2,2,32,1024]{4,3,2,1,0:T(8,128)(2,1)S(1)}, bf16[2,2,2,32,1024]{4,3,2,1,0:T(8,128)(2,1)S(1)}, u32[]{:S(2)}, u32[]{:S(2)}) collective-permute-start(bf16[2,2,2,32,1024]{4,3,2,1,0:T(8,128)(2,1)S(1)} %get-tuple-element.63), channel_id=1, source_target_pairs={{0,2},{1,7},{2,0},{3,5},{4,6},{5,3},{6,4},{7,1},{8,10},{9,15},{10,... | collective-permute-start | bytes 1572872 | tf_op jit(solution)/shard_map/ppermute | solution.py:44
  47.6 13.4 %collective-permute-start.13 = (bf16[128,2048]{1,0:T(8,128)(2,1)S(1)}, bf16[128,2048]{1,0:T(8,128)(2,1)S(1)}, u32[]{:S(2)}, u32[]{:S(2)}) collective-permute-start(bf16[128,2048]{1,0:T(8,128)(2,1)S(1)} %collective-permute-done.9.refs_1_), channel_id=1, source_target_pairs={{0,32},{1,225},{2,34},{3,227},{4,36},{5,229},{6,38},{7,231},{8,40}... | collective-permute-start | bytes 1572872 | tf_op jit(solution)/shard_map/ppermute | solution.py:44
  52.6 13.9 %collective-permute-start.12 = (bf16[4,2,32,1024]{3,2,1,0:T(8,128)(2,1)S(1)}, bf16[4,2,32,1024]{3,2,1,0:T(8,128)(2,1)S(1)}, u32[]{:S(2)}, u32[]{:S(2)}) collective-permute-start(bf16[4,2,32,1024]{3,2,1,0:T(8,128)(2,1)S(1)} %get-tuple-element.65), channel_id=1, source_target_pairs={{0,8},{1,9},{2,10},{3,11},{4,12},{5,13},{6,14},{7,15},{8,0},{9,1},... | collective-permute-start | bytes 1572872 | tf_op jit(solution)/shard_map/ppermute | solution.py:44
  57.3 14.1 %collective-permute-start.15 = (bf16[2,2,32,2560]{3,2,1,0:T(8,128)(2,1)S(1)}, bf16[2,2,32,2560]{3,2,1,0:T(8,128)(2,1)S(1)}, u32[]{:S(2)}, u32[]{:S(2)}) collective-permute-start(bf16[2,2,32,2560]{3,2,1,0:T(8,128)(2,1)S(1)} %get-tuple-element.71), channel_id=1, source_target_pairs={{0,6},{1,3},{2,4},{3,1},{4,2},{5,7},{6,0},{7,5},{8,14},{9,11},{10,... | collective-permute-start | bytes 1966088 | tf_op jit(solution)/shard_map/ppermute | solution.py:44
  62.9 7.0 %collective-permute-start.14 = (bf16[2,2,2,32,512]{4,3,2,1,0:T(8,128)(2,1)S(1)}, bf16[2,2,2,32,512]{4,3,2,1,0:T(8,128)(2,1)S(1)}, u32[]{:S(2)}, u32[]{:S(2)}) collective-permute-start(bf16[2,2,2,32,512]{4,3,2,1,0:T(8,128)(2,1)S(1)} %get-tuple-element.68), channel_id=1, source_target_pairs={{0,6},{1,3},{2,4},{3,1},{4,2},{5,7},{6,0},{7,5},{8,14},{9,11},{10,... | collective-permute-start | bytes 786440 | tf_op jit(solution)/shard_map/ppermute | solution.py:44
  70.1 8.2 %collective-permute-start.16 = (bf16[2,2,32,1536]{3,2,1,0:T(8,128)(2,1)S(1)}, bf16[2,2,32,1536]{3,2,1,0:T(8,128)(2,1)S(1)}, u32[]{:S(2)}, u32[]{:S(2)}) collective-permute-start(bf16[2,2,32,1536]{3,2,1,0:T(8,128)(2,1)S(1)} %get-tuple-element.73), channel_id=1, source_target_pairs={{0,2},{1,7},{2,0},{3,5},{4,6},{5,3},{6,4},{7,1},{8,10},{9,15},{10,... | collective-permute-start | bytes 1179656 | tf_op jit(solution)/shard_map/ppermute | solution.py:44
  72.0 11.3 %collective-permute-start.17 = (bf16[2,32,2560]{2,1,0:T(8,128)(2,1)S(1)}, bf16[2,32,2560]{2,1,0:T(8,128)(2,1)S(1)}, u32[]{:S(2)}, u32[]{:S(2)}) collective-permute-start(bf16[2,32,2560]{2,1,0:T(8,128)(2,1)S(1)} %get-tuple-element.76), channel_id=1, source_target_pairs={{0,8},{1,9},{2,10},{3,11},{4,12},{5,13},{6,14},{7,15},{8,0},{9,1},... | collective-permute-start | bytes 983048 | tf_op jit(solution)/shard_map/ppermute | solution.py:44
  78.9 4.8 %collective-permute-start.18 = (bf16[2,32,1024]{2,1,0:T(8,128)(2,1)S(1)}, bf16[2,32,1024]{2,1,0:T(8,128)(2,1)S(1)}, u32[]{:S(2)}, u32[]{:S(2)}) collective-permute-start(bf16[2,32,1024]{2,1,0:T(8,128)(2,1)S(1)} %get-tuple-element.79), channel_id=1, source_target_pairs={{0,6},{1,3},{2,4},{3,1},{4,2},{5,7},{6,0},{7,5},{8,14},{9,11},{10,... | collective-permute-start | bytes 393224 | tf_op jit(solution)/shard_map/ppermute | solution.py:44
  79.0 4.7 %collective-permute-start.19 = (bf16[2,32,512]{2,1,0:T(8,128)(2,1)S(1)}, bf16[2,32,512]{2,1,0:T(8,128)(2,1)S(1)}, u32[]{:S(2)}, u32[]{:S(2)}) collective-permute-start(bf16[2,32,512]{2,1,0:T(8,128)(2,1)S(1)} %get-tuple-element.80), channel_id=1, source_target_pairs={{0,8},{1,9},{2,10},{3,11},{4,12},{5,13},{6,14},{7,15},{8,0},{9,1},... | collective-permute-start | bytes 196616 | tf_op jit(solution)/shard_map/ppermute | solution.py:44
  83.8 9.0 %collective-permute-start.20 = (bf16[2,32,1024]{2,1,0:T(8,128)(2,1)S(1)}, bf16[2,32,1024]{2,1,0:T(8,128)(2,1)S(1)}, u32[]{:S(2)}, u32[]{:S(2)}) collective-permute-start(bf16[2,32,1024]{2,1,0:T(8,128)(2,1)S(1)} %get-tuple-element.83), channel_id=1, source_target_pairs={{0,16},{1,17},{2,18},{3,19},{4,20},{5,21},{6,22},{7,23},{8,24},{9,... | collective-permute-start | bytes 393224 | tf_op jit(solution)/shard_map/ppermute | solution.py:44
  85.3 4.3 %collective-permute-start.21 = (bf16[2,32,512]{2,1,0:T(8,128)(2,1)S(1)}, bf16[2,32,512]{2,1,0:T(8,128)(2,1)S(1)}, u32[]{:S(2)}, u32[]{:S(2)}) collective-permute-start(bf16[2,32,512]{2,1,0:T(8,128)(2,1)S(1)} %get-tuple-element.84), channel_id=1, source_target_pairs={{0,224},{1,33},{2,226},{3,35},{4,228},{5,37},{6,230},{7,39},{8,232... | collective-permute-start | bytes 196616 | tf_op jit(solution)/shard_map/ppermute | solution.py:44
  86.1 6.6 %collective-permute-start.22 = (bf16[2,32,512]{2,1,0:T(8,128)(2,1)S(1)}, bf16[2,32,512]{2,1,0:T(8,128)(2,1)S(1)}, u32[]{:S(2)}, u32[]{:S(2)}) collective-permute-start(bf16[2,32,512]{2,1,0:T(8,128)(2,1)S(1)} %get-tuple-element.85), channel_id=1, source_target_pairs={{0,192},{1,65},{2,194},{3,67},{4,196},{5,69},{6,198},{7,71},{8,200... | collective-permute-start | bytes 196616 | tf_op jit(solution)/shard_map/ppermute | solution.py:44
  86.5 6.2 %collective-permute-start.23 = (bf16[2,32,512]{2,1,0:T(8,128)(2,1)S(1)}, bf16[2,32,512]{2,1,0:T(8,128)(2,1)S(1)}, u32[]{:S(2)}, u32[]{:S(2)}) collective-permute-start(bf16[2,32,512]{2,1,0:T(8,128)(2,1)S(1)} %get-tuple-element.86), channel_id=1, source_target_pairs={{0,160},{1,97},{2,162},{3,99},{4,164},{5,101},{6,166},{7,103},{8,1... | collective-permute-start | bytes 196616 | tf_op jit(solution)/shard_map/ppermute | solution.py:44
  93.3 9.3 %collective-permute-start.24 = (bf16[2,16,4096]{2,1,0:T(8,128)(2,1)S(1)}, bf16[2,16,4096]{2,1,0:T(8,128)(2,1)S(1)}, u32[]{:S(2)}, u32[]{:S(2)}) collective-permute-start(bf16[2,16,4096]{2,1,0:T(8,128)(2,1)S(1)} %split.1), channel_id=1, source_target_pairs={{0,1},{1,0},{2,3},{3,2},{4,5},{5,4},{6,7},{7,6},{8,9},{9,8},{10,11... | collective-permute-start | bytes 786440 | tf_op jit(solution)/shard_map/ppermute | solution.py:44

commit v14 on v11

--- a/solution.py
+++ b/solution.py
@@ -394,7 +394,7 @@
     near_rotated = [own_plus, near_plus, near_minus]
     keep_n, send_n = products(at, near_pairs, first + near + near_rotated, 3 * BLOCK, scale, "pairs_near")
     recv_n = move(send_n, x_near)
-    third.append(move(after(second[1], keep_n), chain_step))
+    third.append(move(second[1], chain_step))
     at = after(place, keep_n)
     keep_b, send_b = products(at, all_pairs, second + rotated, 4 * BLOCK, scale, "pairs_2")
     recv_b = move(send_b, x_near)

time: 102 us -> 103 us (level); the launches traced: 101 us -> 103 us
  waiting for transfers between devices: 32.9 us -> 35.8 us
    ppermute x25, waiting for transfers between devices: 32.9 us -> 35.8 us  [move(): return lax.ppermute(x, AXES, pairs)]
  transfers between devices with their start and end apart: 25 -> 25, of which waited for: 15 -> 15; matrix products, arithmetic and copies ran while one was open for 0% -> 0% of each run, Pallas kernels for 17% -> 16%
where the time goes in v14:
time: 103 us
  starting transfers between devices  46 us (45%)
  waiting for transfers between devices  35.8 us (35%)
  Pallas kernels  19.8 us (19%)
  local copies, waits for them, and re-layouts  1.31 us (1%)
    ppermute x25, starting transfers between devices, move(): return lax.ppermute(x, AXES, pairs)  46 us
    ppermute x25, waiting for transfers between devices, move(): return lax.ppermute(x, AXES, pairs)  35.8 us
    pallas_call x5, Pallas kernels, products(): pl.pallas_call(kernel, in_specs=[pl.BlockSpec(memory_space=pltpu.SMEM)] +...  12.7 us
    pallas_call x8, Pallas kernels, call(): pl.pallas_call(kernel, in_specs=[pl.BlockSpec(memory_space=pltpu.SMEM)] *...  3.96 us
  transfers between devices with their start and end apart: 25, of which 15 were waited for; matrix products, arithmetic and copies ran while one was open for 0% of the time, Pallas kernels for 16%

profile of v14, /device:TPU:1, one launch (start us, length us, event | category | flops | bytes accessed | tf_op | source)
XLA Modules:
  0.0 103.2 jit_solution(948982901639663658)
XLA Ops:
  0.1 1.2 %copy-done = bf16[2,2,512,256]{3,2,1,0:T(8,128)(2,1)S(1)} copy-done((bf16[2,2,512,256]{3,2,1,0:T(8,128)(2,1)S(1)}, bf16[2,2,512,256]{3,2,1,0:T(8,128)(2,1)}, u32[]{:S(2)}) %copy-start) | copy-done | bytes 1048600
  1.3 0.6 whiten.2.a_ref.refs_2_
  1.9 6.5 %collective-permute-start = (bf16[128,2048]{1,0:T(8,128)(2,1)S(1)}, bf16[128,2048]{1,0:T(8,128)(2,1)S(1)}, u32[]{:S(2)}, u32[]{:S(2)}) collective-permute-start(bf16[128,2048]{1,0:T(8,128)(2,1)S(1)} %whiten.2.a_ref.refs_2_), channel_id=1, source_target_pairs={{0,32},{1,225},{2,34},{3,227},{4,36},{5,229},{6,38},{7,231},{8,40}... | collective-permute-start | bytes 1572872 | tf_op jit(solution)/shard_map/ppermute | solution.py:43
  8.4 0.6 whiten.3.b_ref.refs_3_
  9.0 0.8 collective-permute-start.1
  9.8 1.3 %collective-permute-start.3 = (bf16[128,2048]{1,0:T(8,128)(2,1)S(1)}, bf16[128,2048]{1,0:T(8,128)(2,1)S(1)}, u32[]{:S(2)}, u32[]{:S(2)}) collective-permute-start(bf16[128,2048]{1,0:T(8,128)(2,1)S(1)} %whiten.2.a_ref.refs_2_), channel_id=1, source_target_pairs={{0,16},{1,17},{2,18},{3,19},{4,20},{5,21},{6,22},{7,23},{8,24},{9,... | collective-permute-start | bytes 1572872 | tf_op jit(solution)/shard_map/ppermute | solution.py:43
  11.3 3.2 %collective-permute-done.refs_0_ = bf16[128,2048]{1,0:T(8,128)(2,1)S(1)} collective-permute-done((bf16[128,2048]{1,0:T(8,128)(2,1)S(1)}, bf16[128,2048]{1,0:T(8,128)(2,1)S(1)}, u32[]{:S(2)}, u32[]{:S(2)}) %collective-permute-start) | collective-permute-done | bytes 524320 | tf_op jit(solution)/shard_map/ppermute | solution.py:43
  14.5 3.1 %collective-permute-start.5 = (bf16[128,2048]{1,0:T(8,128)(2,1)S(1)}, bf16[128,2048]{1,0:T(8,128)(2,1)S(1)}, u32[]{:S(2)}, u32[]{:S(2)}) collective-permute-start(bf16[128,2048]{1,0:T(8,128)(2,1)S(1)} %collective-permute-done.refs_0_), channel_id=1, source_target_pairs={{0,32},{1,225},{2,34},{3,227},{4,36},{5,229},{6,38},{7,231},{8,40}... | collective-permute-start | bytes 1572872 | tf_op jit(solution)/shard_map/ppermute | solution.py:43
  17.8 1.0 rotate.2
  18.8 1.4 %collective-permute-done.1.refs_1_ = bf16[128,2048]{1,0:T(8,128)(2,1)S(1)} collective-permute-done((bf16[128,2048]{1,0:T(8,128)(2,1)S(1)}, bf16[128,2048]{1,0:T(8,128)(2,1)S(1)}, u32[]{:S(2)}, u32[]{:S(2)}) %collective-permute-start.1) | collective-permute-done | bytes 524320 | tf_op jit(solution)/shard_map/ppermute | solution.py:43
  20.2 3.1 %collective-permute-start.6 = (bf16[128,2048]{1,0:T(8,128)(2,1)S(1)}, bf16[128,2048]{1,0:T(8,128)(2,1)S(1)}, u32[]{:S(2)}, u32[]{:S(2)}) collective-permute-start(bf16[128,2048]{1,0:T(8,128)(2,1)S(1)} %collective-permute-done.1.refs_1_), channel_id=1, source_target_pairs={{0,32},{1,225},{2,34},{3,227},{4,36},{5,229},{6,38},{7,231},{8,40}... | collective-permute-start | bytes 1572872 | tf_op jit(solution)/shard_map/ppermute | solution.py:43
  23.3 2.4 %pairs_own.1 = (bf16[2,2,2,32,768]{4,3,2,1,0:T(8,128)(2,1)S(1)}, bf16[2,2,2,32,768]{4,3,2,1,0:T(8,128)(2,1)S(1)}) custom-call(s32[5]{0:T(128)S(1)} %stack.23.at_ref.place_ref, bf16[128,2048]{1,0:T(8,128)(2,1)S(1)} %collective-permute-done.refs_0_, bf16[128,2048]{1,0:T(8,128)(2,1)S(1)} %collective-permute-done.1.refs_1_, ...), custom_call_target="tpu_custom_call" | custom-call | flops 1610612736 | bytes 8388608 | tf_op jit(solution)/shard_map/pairs_own/pallas_call | solution.py:155
  25.7 2.6 %collective-permute-start.2 = (bf16[2,2,2,32,768]{4,3,2,1,0:T(8,128)(2,1)S(1)}, bf16[2,2,2,32,768]{4,3,2,1,0:T(8,128)(2,1)S(1)}, u32[]{:S(2)}, u32[]{:S(2)}) collective-permute-start(bf16[2,2,2,32,768]{4,3,2,1,0:T(8,128)(2,1)S(1)} %get-tuple-element.51), channel_id=1, source_target_pairs={{0,2},{1,7},{2,0},{3,5},{4,6},{5,3},{6,4},{7,1},{8,10},{9,15},{10,... | collective-permute-start | bytes 1179656 | tf_op jit(solution)/shard_map/ppermute | solution.py:43
  28.3 0.6 collective-permute-start.8
  28.9 4.8 %collective-permute-done.4.b_ref.refs_3_ = bf16[128,2048]{1,0:T(8,128)(2,1)S(1)} collective-permute-done((bf16[128,2048]{1,0:T(8,128)(2,1)S(1)}, bf16[128,2048]{1,0:T(8,128)(2,1)S(1)}, u32[]{:S(2)}, u32[]{:S(2)}) %collective-permute-start.4) | collective-permute-done | bytes 524320 | tf_op jit(solution)/shard_map/ppermute | solution.py:43
  33.7 1.0 rotate.3
  34.7 1.9 %collective-permute-start.9 = (bf16[128,2048]{1,0:T(8,128)(2,1)S(1)}, bf16[128,2048]{1,0:T(8,128)(2,1)S(1)}, u32[]{:S(2)}, u32[]{:S(2)}) collective-permute-start(bf16[128,2048]{1,0:T(8,128)(2,1)S(1)} %collective-permute-done.6.refs_1_), channel_id=1, source_target_pairs={{0,32},{1,225},{2,34},{3,227},{4,36},{5,229},{6,38},{7,231},{8,40}... | collective-permute-start | bytes 1572872 | tf_op jit(solution)/shard_map/ppermute | solution.py:43
  36.6 2.4 %pairs_near.1 = (bf16[2,2,2,32,768]{4,3,2,1,0:T(8,128)(2,1)S(1)}, bf16[2,2,2,32,768]{4,3,2,1,0:T(8,128)(2,1)S(1)}) custom-call(s32[5]{0:T(128)S(1)} %stack.23.at_ref.place_ref, bf16[128,2048]{1,0:T(8,128)(2,1)S(1)} %collective-permute-done.refs_0_, bf16[128,2048]{1,0:T(8,128)(2,1)S(1)} %collective-permute-done.1.refs_1_, ...), custom_call_target="tpu_custom_call" | custom-call | flops 1610612736 | bytes 8388608 | tf_op jit(solution)/shard_map/pairs_near/pallas_call | solution.py:155
  39.0 2.7 %collective-permute-start.7 = (bf16[2,2,2,32,768]{4,3,2,1,0:T(8,128)(2,1)S(1)}, bf16[2,2,2,32,768]{4,3,2,1,0:T(8,128)(2,1)S(1)}, u32[]{:S(2)}, u32[]{:S(2)}) collective-permute-start(bf16[2,2,2,32,768]{4,3,2,1,0:T(8,128)(2,1)S(1)} %get-tuple-element.58), channel_id=1, source_target_pairs={{0,2},{1,7},{2,0},{3,5},{4,6},{5,3},{6,4},{7,1},{8,10},{9,15},{10,... | collective-permute-start | bytes 1179656 | tf_op jit(solution)/shard_map/ppermute | solution.py:43
  41.8 3.0 %pairs_2.1 = (bf16[2,2,2,32,1024]{4,3,2,1,0:T(8,128)(2,1)S(1)}, bf16[2,2,2,32,1024]{4,3,2,1,0:T(8,128)(2,1)S(1)}) custom-call(s32[5]{0:T(128)S(1)} %stack.23.at_ref.place_ref, bf16[128,2048]{1,0:T(8,128)(2,1)S(1)} %collective-permute-done.5.refs_0_, bf16[128,2048]{1,0:T(8,128)(2,1)S(1)} %collective-permute-done.6.refs_1_, ...), custom_call_target="tpu_custom_call" | custom-call | flops 2147483648 | bytes 8388608 | tf_op jit(solution)/shard_map/pairs_2/pallas_call | solution.py:155
  45.2 0.6 collective-permute-start.12
  45.8 1.3 %collective-permute-done.7.refs_3_ = bf16[2,2,2,32,768]{4,3,2,1,0:T(8,128)(2,1)S(1)} collective-permute-done((bf16[2,2,2,32,768]{4,3,2,1,0:T(8,128)(2,1)S(1)}, bf16[2,2,2,32,768]{4,3,2,1,0:T(8,128)(2,1)S(1)}, u32[]{:S(2)}, u32[]{:S(2)}) %collective-permute-start.7) | collective-permute-done | bytes 393248 | tf_op jit(solution)/shard_map/ppermute | solution.py:43
  47.2 3.0 %pairs_3.1 = (bf16[4,2,32,1024]{3,2,1,0:T(8,128)(2,1)S(1)}, bf16[4,2,32,1024]{3,2,1,0:T(8,128)(2,1)S(1)}) custom-call(s32[5]{0:T(128)S(1)} %stack.23.at_ref.place_ref, bf16[128,2048]{1,0:T(8,128)(2,1)S(1)} %collective-permute-done.8.refs_0_, bf16[128,2048]{1,0:T(8,128)(2,1)S(1)} %collective-permute-done.9.refs_1_, ...), custom_call_target="tpu_custom_call" | custom-call | flops 2147483648 | bytes 8388608 | tf_op jit(solution)/shard_map/pairs_3/pallas_call | solution.py:155
  50.1 3.1 %collective-permute-done.10.refs_0_ = bf16[128,2048]{1,0:T(8,128)(2,1)S(1)} collective-permute-done((bf16[128,2048]{1,0:T(8,128)(2,1)S(1)}, bf16[128,2048]{1,0:T(8,128)(2,1)S(1)}, u32[]{:S(2)}, u32[]{:S(2)}) %collective-permute-start.10) | collective-permute-done | bytes 524320 | tf_op jit(solution)/shard_map/ppermute | solution.py:43
  53.2 1.4 %collective-permute-done.11.refs_5_ = bf16[2,2,2,32,1024]{4,3,2,1,0:T(8,128)(2,1)S(1)} collective-permute-done((bf16[2,2,2,32,1024]{4,3,2,1,0:T(8,128)(2,1)S(1)}, bf16[2,2,2,32,1024]{4,3,2,1,0:T(8,128)(2,1)S(1)}, u32[]{:S(2)}, u32[]{:S(2)}) %collective-permute-start.11) | collective-permute-done | bytes 524320 | tf_op jit(solution)/shard_map/ppermute | solution.py:43
  55.0 3.0 %collective-permute-start.14 = (bf16[4,2,32,1024]{3,2,1,0:T(8,128)(2,1)S(1)}, bf16[4,2,32,1024]{3,2,1,0:T(8,128)(2,1)S(1)}, u32[]{:S(2)}, u32[]{:S(2)}) collective-permute-start(bf16[4,2,32,1024]{3,2,1,0:T(8,128)(2,1)S(1)} %get-tuple-element.72), channel_id=1, source_target_pairs={{0,8},{1,9},{2,10},{3,11},{4,12},{5,13},{6,14},{7,15},{8,0},{9,1},... | collective-permute-start | bytes 1572872 | tf_op jit(solution)/shard_map/ppermute | solution.py:43
  57.9 0.9 collective-permute-done.12.refs_1_
  58.8 1.9 %pairs_4.1 = (bf16[2,2,2,32,512]{4,3,2,1,0:T(8,128)(2,1)S(1)}, bf16[2,2,2,32,512]{4,3,2,1,0:T(8,128)(2,1)S(1)}) custom-call(s32[5]{0:T(128)S(1)} %stack.23.at_ref.place_ref, bf16[128,2048]{1,0:T(8,128)(2,1)S(1)} %collective-permute-done.10.refs_0_, bf16[128,2048]{1,0:T(8,128)(2,1)S(1)} %collective-permute-done.12.refs_1_, ...), custom_call_target="tpu_custom_call" | custom-call | flops 1073741824 | bytes 8388608 | tf_op jit(solution)/shard_map/pairs_4/pallas_call | solution.py:155
  60.7 0.6 collective-permute-start.15
  61.3 3.4 %collective-permute-done.13.refs_1_ = bf16[2,2,32,2560]{3,2,1,0:T(8,128)(2,1)S(1)} collective-permute-done((bf16[2,2,32,2560]{3,2,1,0:T(8,128)(2,1)S(1)}, bf16[2,2,32,2560]{3,2,1,0:T(8,128)(2,1)S(1)}, u32[]{:S(2)}, u32[]{:S(2)}) %collective-permute-start.13) | collective-permute-done | bytes 655392 | tf_op jit(solution)/shard_map/ppermute | solution.py:43
  64.7 0.7 sum_2.1
  65.4 2.8 %collective-permute-done.14.rc_ref = bf16[4,2,32,1024]{3,2,1,0:T(8,128)(2,1)S(1)} collective-permute-done((bf16[4,2,32,1024]{3,2,1,0:T(8,128)(2,1)S(1)}, bf16[4,2,32,1024]{3,2,1,0:T(8,128)(2,1)S(1)}, u32[]{:S(2)}, u32[]{:S(2)}) %collective-permute-start.14) | collective-permute-done | bytes 524320 | tf_op jit(solution)/shard_map/ppermute | solution.py:43
  68.3 1.2 %collective-permute-start.16 = (bf16[2,2,32,1536]{3,2,1,0:T(8,128)(2,1)S(1)}, bf16[2,2,32,1536]{3,2,1,0:T(8,128)(2,1)S(1)}, u32[]{:S(2)}, u32[]{:S(2)}) collective-permute-start(bf16[2,2,32,1536]{3,2,1,0:T(8,128)(2,1)S(1)} %get-tuple-element.75), channel_id=1, source_target_pairs={{0,2},{1,7},{2,0},{3,5},{4,6},{5,3},{6,4},{7,1},{8,10},{9,15},{10,... | collective-permute-start | bytes 1179656 | tf_op jit(solution)/shard_map/ppermute | solution.py:43
  69.5 2.9 %collective-permute-start.17 = (bf16[2,32,2560]{2,1,0:T(8,128)(2,1)S(1)}, bf16[2,32,2560]{2,1,0:T(8,128)(2,1)S(1)}, u32[]{:S(2)}, u32[]{:S(2)}) collective-permute-start(bf16[2,32,2560]{2,1,0:T(8,128)(2,1)S(1)} %get-tuple-element.78), channel_id=1, source_target_pairs={{0,8},{1,9},{2,10},{3,11},{4,12},{5,13},{6,14},{7,15},{8,0},{9,1},... | collective-permute-start | bytes 983048 | tf_op jit(solution)/shard_map/ppermute | solution.py:43
  72.4 3.8 %collective-permute-done.16.recv_ref = bf16[2,2,32,1536]{3,2,1,0:T(8,128)(2,1)S(1)} collective-permute-done((bf16[2,2,32,1536]{3,2,1,0:T(8,128)(2,1)S(1)}, bf16[2,2,32,1536]{3,2,1,0:T(8,128)(2,1)S(1)}, u32[]{:S(2)}, u32[]{:S(2)}) %collective-permute-start.16) | collective-permute-done | bytes 393248 | tf_op jit(solution)/shard_map/ppermute | solution.py:43
  76.3 0.6 sum_n.1
  76.9 1.6 %collective-permute-start.18 = (bf16[2,32,1024]{2,1,0:T(8,128)(2,1)S(1)}, bf16[2,32,1024]{2,1,0:T(8,128)(2,1)S(1)}, u32[]{:S(2)}, u32[]{:S(2)}) collective-permute-start(bf16[2,32,1024]{2,1,0:T(8,128)(2,1)S(1)} %get-tuple-element.81), channel_id=1, source_target_pairs={{0,6},{1,3},{2,4},{3,1},{4,2},{5,7},{6,0},{7,5},{8,14},{9,11},{10,... | collective-permute-start | bytes 393224 | tf_op jit(solution)/shard_map/ppermute | solution.py:43
  78.5 2.9 %collective-permute-start.19 = (bf16[2,32,512]{2,1,0:T(8,128)(2,1)S(1)}, bf16[2,32,512]{2,1,0:T(8,128)(2,1)S(1)}, u32[]{:S(2)}, u32[]{:S(2)}) collective-permute-start(bf16[2,32,512]{2,1,0:T(8,128)(2,1)S(1)} %get-tuple-element.82), channel_id=1, source_target_pairs={{0,8},{1,9},{2,10},{3,11},{4,12},{5,13},{6,14},{7,15},{8,0},{9,1},... | collective-permute-start | bytes 196616 | tf_op jit(solution)/shard_map/ppermute | solution.py:43
  81.5 1.6 %collective-permute-done.19.refs_2_ = bf16[2,32,512]{2,1,0:T(8,128)(2,1)S(1)} collective-permute-done((bf16[2,32,512]{2,1,0:T(8,128)(2,1)S(1)}, bf16[2,32,512]{2,1,0:T(8,128)(2,1)S(1)}, u32[]{:S(2)}, u32[]{:S(2)}) %collective-permute-start.19) | collective-permute-done | bytes 65568 | tf_op jit(solution)/shard_map/ppermute | solution.py:43
  83.2 1.4 %collective-permute-start.20 = (bf16[2,32,1024]{2,1,0:T(8,128)(2,1)S(1)}, bf16[2,32,1024]{2,1,0:T(8,128)(2,1)S(1)}, u32[]{:S(2)}, u32[]{:S(2)}) collective-permute-start(bf16[2,32,1024]{2,1,0:T(8,128)(2,1)S(1)} %get-tuple-element.85), channel_id=1, source_target_pairs={{0,16},{1,17},{2,18},{3,19},{4,20},{5,21},{6,22},{7,23},{8,24},{9,... | collective-permute-start | bytes 393224 | tf_op jit(solution)/shard_map/ppermute | solution.py:43
  84.6 1.6 %collective-permute-start.21 = (bf16[2,32,512]{2,1,0:T(8,128)(2,1)S(1)}, bf16[2,32,512]{2,1,0:T(8,128)(2,1)S(1)}, u32[]{:S(2)}, u32[]{:S(2)}) collective-permute-start(bf16[2,32,512]{2,1,0:T(8,128)(2,1)S(1)} %get-tuple-element.86), channel_id=1, source_target_pairs={{0,224},{1,33},{2,226},{3,35},{4,228},{5,37},{6,230},{7,39},{8,232... | collective-permute-start | bytes 196616 | tf_op jit(solution)/shard_map/ppermute | solution.py:43
  86.7 2.2 %collective-permute-done.21.refs_3_ = bf16[2,32,512]{2,1,0:T(8,128)(2,1)S(1)} collective-permute-done((bf16[2,32,512]{2,1,0:T(8,128)(2,1)S(1)}, bf16[2,32,512]{2,1,0:T(8,128)(2,1)S(1)}, u32[]{:S(2)}, u32[]{:S(2)}) %collective-permute-start.21) | collective-permute-done | bytes 65568 | tf_op jit(solution)/shard_map/ppermute | solution.py:43
  88.9 2.8 %collective-permute-done.22.refs_4_ = bf16[2,32,512]{2,1,0:T(8,128)(2,1)S(1)} collective-permute-done((bf16[2,32,512]{2,1,0:T(8,128)(2,1)S(1)}, bf16[2,32,512]{2,1,0:T(8,128)(2,1)S(1)}, u32[]{:S(2)}, u32[]{:S(2)}) %collective-permute-start.22) | collective-permute-done | bytes 65568 | tf_op jit(solution)/shard_map/ppermute | solution.py:43
  91.7 1.9 %collective-permute-done.23.refs_5_ = bf16[2,32,512]{2,1,0:T(8,128)(2,1)S(1)} collective-permute-done((bf16[2,32,512]{2,1,0:T(8,128)(2,1)S(1)}, bf16[2,32,512]{2,1,0:T(8,128)(2,1)S(1)}, u32[]{:S(2)}, u32[]{:S(2)}) %collective-permute-start.23) | collective-permute-done | bytes 65568 | tf_op jit(solution)/shard_map/ppermute | solution.py:43
  93.6 0.6 split.1
  94.2 6.3 %collective-permute-start.24 = (bf16[2,16,4096]{2,1,0:T(8,128)(2,1)S(1)}, bf16[2,16,4096]{2,1,0:T(8,128)(2,1)S(1)}, u32[]{:S(2)}, u32[]{:S(2)}) collective-permute-start(bf16[2,16,4096]{2,1,0:T(8,128)(2,1)S(1)} %split.1), channel_id=1, source_target_pairs={{0,1},{1,0},{2,3},{3,2},{4,5},{5,4},{6,7},{7,6},{8,9},{9,8},{10,11... | collective-permute-start | bytes 786440 | tf_op jit(solution)/shard_map/ppermute | solution.py:43
  100.5 1.2 %collective-permute-done.24.refs_6_ = bf16[2,16,4096]{2,1,0:T(8,128)(2,1)S(1)} collective-permute-done((bf16[2,16,4096]{2,1,0:T(8,128)(2,1)S(1)}, bf16[2,16,4096]{2,1,0:T(8,128)(2,1)S(1)}, u32[]{:S(2)}, u32[]{:S(2)}) %collective-permute-start.24) | collective-permute-done | bytes 262176 | tf_op jit(solution)/shard_map/ppermute | solution.py:43
  101.6 1.5 %finish.1 = f32[2,16,4096]{2,1,0:T(8,128)} custom-call(s32[5]{0:T(128)S(1)} %stack.23.at_ref.place_ref, bf16[2,32,1024]{2,1,0:T(8,128)(2,1)S(1)} %get-tuple-element.79.refs_0_, bf16[2,32,512]{2,1,0:T(8,128)(2,1)S(1)} %get-tuple-element.84.refs_1_, bf16[2,32,1024]{2,1,0:T(8,128)(2,1)S(1)} %collective-permute-done.20.refs_2_, ...), custom_call_target="tpu_custom_call" | custom-call | flops 1000 | bytes 10485760 | tf_op jit(solution)/shard_map/finish/pallas_call | solution.py:174
  (27 shorter events, 2.1 us)
Async XLA Ops:
  0.0 17.7 %copy-start.1 = (s32[512]{0:T(512)S(1)}, s32[512]{0:T(512)}, u32[]{:S(2)}) copy-start(s32[512]{0:T(512)} %param.3) | copy-start | bytes 6148
  0.1 1.2 %copy-start = (bf16[2,2,512,256]{3,2,1,0:T(8,128)(2,1)S(1)}, bf16[2,2,512,256]{3,2,1,0:T(8,128)(2,1)}, u32[]{:S(2)}) copy-start(bf16[2,2,512,256]{3,2,1,0:T(8,128)(2,1)} %x_ref.1) | copy-start | bytes 3145732
  1.9 12.6 %collective-permute-start = (bf16[128,2048]{1,0:T(8,128)(2,1)S(1)}, bf16[128,2048]{1,0:T(8,128)(2,1)S(1)}, u32[]{:S(2)}, u32[]{:S(2)}) collective-permute-start(bf16[128,2048]{1,0:T(8,128)(2,1)S(1)} %whiten.2.a_ref.refs_2_), channel_id=1, source_target_pairs={{0,32},{1,225},{2,34},{3,227},{4,36},{5,229},{6,38},{7,231},{8,40}... | collective-permute-start | bytes 1572872 | tf_op jit(solution)/shard_map/ppermute | solution.py:43
  9.0 11.1 %collective-permute-start.1 = (bf16[128,2048]{1,0:T(8,128)(2,1)S(1)}, bf16[128,2048]{1,0:T(8,128)(2,1)S(1)}, u32[]{:S(2)}, u32[]{:S(2)}) collective-permute-start(bf16[128,2048]{1,0:T(8,128)(2,1)S(1)} %whiten.3.b_ref.refs_3_), channel_id=1, source_target_pairs={{0,32},{1,225},{2,34},{3,227},{4,36},{5,229},{6,38},{7,231},{8,40}... | collective-permute-start | bytes 1572872 | tf_op jit(solution)/shard_map/ppermute | solution.py:43
  9.8 18.4 %collective-permute-start.3 = (bf16[128,2048]{1,0:T(8,128)(2,1)S(1)}, bf16[128,2048]{1,0:T(8,128)(2,1)S(1)}, u32[]{:S(2)}, u32[]{:S(2)}) collective-permute-start(bf16[128,2048]{1,0:T(8,128)(2,1)S(1)} %whiten.2.a_ref.refs_2_), channel_id=1, source_target_pairs={{0,16},{1,17},{2,18},{3,19},{4,20},{5,21},{6,22},{7,23},{8,24},{9,... | collective-permute-start | bytes 1572872 | tf_op jit(solution)/shard_map/ppermute | solution.py:43
  11.1 22.5 %collective-permute-start.4 = (bf16[128,2048]{1,0:T(8,128)(2,1)S(1)}, bf16[128,2048]{1,0:T(8,128)(2,1)S(1)}, u32[]{:S(2)}, u32[]{:S(2)}) collective-permute-start(bf16[128,2048]{1,0:T(8,128)(2,1)S(1)} %whiten.3.b_ref.refs_3_), channel_id=1, source_target_pairs={{0,16},{1,17},{2,18},{3,19},{4,20},{5,21},{6,22},{7,23},{8,24},{9,... | collective-permute-start | bytes 1572872 | tf_op jit(solution)/shard_map/ppermute | solution.py:43
  14.5 13.7 %collective-permute-start.5 = (bf16[128,2048]{1,0:T(8,128)(2,1)S(1)}, bf16[128,2048]{1,0:T(8,128)(2,1)S(1)}, u32[]{:S(2)}, u32[]{:S(2)}) collective-permute-start(bf16[128,2048]{1,0:T(8,128)(2,1)S(1)} %collective-permute-done.refs_0_), channel_id=1, source_target_pairs={{0,32},{1,225},{2,34},{3,227},{4,36},{5,229},{6,38},{7,231},{8,40}... | collective-permute-start | bytes 1572872 | tf_op jit(solution)/shard_map/ppermute | solution.py:43
  20.2 14.5 %collective-permute-start.6 = (bf16[128,2048]{1,0:T(8,128)(2,1)S(1)}, bf16[128,2048]{1,0:T(8,128)(2,1)S(1)}, u32[]{:S(2)}, u32[]{:S(2)}) collective-permute-start(bf16[128,2048]{1,0:T(8,128)(2,1)S(1)} %collective-permute-done.1.refs_1_), channel_id=1, source_target_pairs={{0,32},{1,225},{2,34},{3,227},{4,36},{5,229},{6,38},{7,231},{8,40}... | collective-permute-start | bytes 1572872 | tf_op jit(solution)/shard_map/ppermute | solution.py:43
  25.7 8.9 %collective-permute-start.2 = (bf16[2,2,2,32,768]{4,3,2,1,0:T(8,128)(2,1)S(1)}, bf16[2,2,2,32,768]{4,3,2,1,0:T(8,128)(2,1)S(1)}, u32[]{:S(2)}, u32[]{:S(2)}) collective-permute-start(bf16[2,2,2,32,768]{4,3,2,1,0:T(8,128)(2,1)S(1)} %get-tuple-element.51), channel_id=1, source_target_pairs={{0,2},{1,7},{2,0},{3,5},{4,6},{5,3},{6,4},{7,1},{8,10},{9,15},{10,... | collective-permute-start | bytes 1179656 | tf_op jit(solution)/shard_map/ppermute | solution.py:43
  28.3 16.5 %collective-permute-start.8 = (bf16[128,2048]{1,0:T(8,128)(2,1)S(1)}, bf16[128,2048]{1,0:T(8,128)(2,1)S(1)}, u32[]{:S(2)}, u32[]{:S(2)}) collective-permute-start(bf16[128,2048]{1,0:T(8,128)(2,1)S(1)} %collective-permute-done.5.refs_0_), channel_id=1, source_target_pairs={{0,32},{1,225},{2,34},{3,227},{4,36},{5,229},{6,38},{7,231},{8,40}... | collective-permute-start | bytes 1572872 | tf_op jit(solution)/shard_map/ppermute | solution.py:43
  34.7 10.6 %collective-permute-start.9 = (bf16[128,2048]{1,0:T(8,128)(2,1)S(1)}, bf16[128,2048]{1,0:T(8,128)(2,1)S(1)}, u32[]{:S(2)}, u32[]{:S(2)}) collective-permute-start(bf16[128,2048]{1,0:T(8,128)(2,1)S(1)} %collective-permute-done.6.refs_1_), channel_id=1, source_target_pairs={{0,32},{1,225},{2,34},{3,227},{4,36},{5,229},{6,38},{7,231},{8,40}... | collective-permute-start | bytes 1572872 | tf_op jit(solution)/shard_map/ppermute | solution.py:43
  39.0 8.1 %collective-permute-start.7 = (bf16[2,2,2,32,768]{4,3,2,1,0:T(8,128)(2,1)S(1)}, bf16[2,2,2,32,768]{4,3,2,1,0:T(8,128)(2,1)S(1)}, u32[]{:S(2)}, u32[]{:S(2)}) collective-permute-start(bf16[2,2,2,32,768]{4,3,2,1,0:T(8,128)(2,1)S(1)} %get-tuple-element.58), channel_id=1, source_target_pairs={{0,2},{1,7},{2,0},{3,5},{4,6},{5,3},{6,4},{7,1},{8,10},{9,15},{10,... | collective-permute-start | bytes 1179656 | tf_op jit(solution)/shard_map/ppermute | solution.py:43
  44.8 8.4 %collective-permute-start.10 = (bf16[128,2048]{1,0:T(8,128)(2,1)S(1)}, bf16[128,2048]{1,0:T(8,128)(2,1)S(1)}, u32[]{:S(2)}, u32[]{:S(2)}) collective-permute-start(bf16[128,2048]{1,0:T(8,128)(2,1)S(1)} %collective-permute-done.8.refs_0_), channel_id=1, source_target_pairs={{0,32},{1,225},{2,34},{3,227},{4,36},{5,229},{6,38},{7,231},{8,40}... | collective-permute-start | bytes 1572872 | tf_op jit(solution)/shard_map/ppermute | solution.py:43
  45.0 9.5 %collective-permute-start.11 = (bf16[2,2,2,32,1024]{4,3,2,1,0:T(8,128)(2,1)S(1)}, bf16[2,2,2,32,1024]{4,3,2,1,0:T(8,128)(2,1)S(1)}, u32[]{:S(2)}, u32[]{:S(2)}) collective-permute-start(bf16[2,2,2,32,1024]{4,3,2,1,0:T(8,128)(2,1)S(1)} %get-tuple-element.64), channel_id=1, source_target_pairs={{0,2},{1,7},{2,0},{3,5},{4,6},{5,3},{6,4},{7,1},{8,10},{9,15},{10,... | collective-permute-start | bytes 1572872 | tf_op jit(solution)/shard_map/ppermute | solution.py:43
  45.2 13.6 %collective-permute-start.12 = (bf16[128,2048]{1,0:T(8,128)(2,1)S(1)}, bf16[128,2048]{1,0:T(8,128)(2,1)S(1)}, u32[]{:S(2)}, u32[]{:S(2)}) collective-permute-start(bf16[128,2048]{1,0:T(8,128)(2,1)S(1)} %collective-permute-done.9.refs_1_), channel_id=1, source_target_pairs={{0,32},{1,225},{2,34},{3,227},{4,36},{5,229},{6,38},{7,231},{8,40}... | collective-permute-start | bytes 1572872 | tf_op jit(solution)/shard_map/ppermute | solution.py:43
  54.9 9.8 %collective-permute-start.13 = (bf16[2,2,32,2560]{3,2,1,0:T(8,128)(2,1)S(1)}, bf16[2,2,32,2560]{3,2,1,0:T(8,128)(2,1)S(1)}, u32[]{:S(2)}, u32[]{:S(2)}) collective-permute-start(bf16[2,2,32,2560]{3,2,1,0:T(8,128)(2,1)S(1)} %get-tuple-element.69), channel_id=1, source_target_pairs={{0,6},{1,3},{2,4},{3,1},{4,2},{5,7},{6,0},{7,5},{8,14},{9,11},{10,... | collective-permute-start | bytes 1966088 | tf_op jit(solution)/shard_map/ppermute | solution.py:43
  55.0 13.2 %collective-permute-start.14 = (bf16[4,2,32,1024]{3,2,1,0:T(8,128)(2,1)S(1)}, bf16[4,2,32,1024]{3,2,1,0:T(8,128)(2,1)S(1)}, u32[]{:S(2)}, u32[]{:S(2)}) collective-permute-start(bf16[4,2,32,1024]{3,2,1,0:T(8,128)(2,1)S(1)} %get-tuple-element.72), channel_id=1, source_target_pairs={{0,8},{1,9},{2,10},{3,11},{4,12},{5,13},{6,14},{7,15},{8,0},{9,1},... | collective-permute-start | bytes 1572872 | tf_op jit(solution)/shard_map/ppermute | solution.py:43
  60.7 7.5 %collective-permute-start.15 = (bf16[2,2,2,32,512]{4,3,2,1,0:T(8,128)(2,1)S(1)}, bf16[2,2,2,32,512]{4,3,2,1,0:T(8,128)(2,1)S(1)}, u32[]{:S(2)}, u32[]{:S(2)}) collective-permute-start(bf16[2,2,2,32,512]{4,3,2,1,0:T(8,128)(2,1)S(1)} %get-tuple-element.73), channel_id=1, source_target_pairs={{0,6},{1,3},{2,4},{3,1},{4,2},{5,7},{6,0},{7,5},{8,14},{9,11},{10,... | collective-permute-start | bytes 786440 | tf_op jit(solution)/shard_map/ppermute | solution.py:43
  68.3 7.9 %collective-permute-start.16 = (bf16[2,2,32,1536]{3,2,1,0:T(8,128)(2,1)S(1)}, bf16[2,2,32,1536]{3,2,1,0:T(8,128)(2,1)S(1)}, u32[]{:S(2)}, u32[]{:S(2)}) collective-permute-start(bf16[2,2,32,1536]{3,2,1,0:T(8,128)(2,1)S(1)} %get-tuple-element.75), channel_id=1, source_target_pairs={{0,2},{1,7},{2,0},{3,5},{4,6},{5,3},{6,4},{7,1},{8,10},{9,15},{10,... | collective-permute-start | bytes 1179656 | tf_op jit(solution)/shard_map/ppermute | solution.py:43
  69.5 11.9 %collective-permute-start.17 = (bf16[2,32,2560]{2,1,0:T(8,128)(2,1)S(1)}, bf16[2,32,2560]{2,1,0:T(8,128)(2,1)S(1)}, u32[]{:S(2)}, u32[]{:S(2)}) collective-permute-start(bf16[2,32,2560]{2,1,0:T(8,128)(2,1)S(1)} %get-tuple-element.78), channel_id=1, source_target_pairs={{0,8},{1,9},{2,10},{3,11},{4,12},{5,13},{6,14},{7,15},{8,0},{9,1},... | collective-permute-start | bytes 983048 | tf_op jit(solution)/shard_map/ppermute | solution.py:43
  76.9 6.2 %collective-permute-start.18 = (bf16[2,32,1024]{2,1,0:T(8,128)(2,1)S(1)}, bf16[2,32,1024]{2,1,0:T(8,128)(2,1)S(1)}, u32[]{:S(2)}, u32[]{:S(2)}) collective-permute-start(bf16[2,32,1024]{2,1,0:T(8,128)(2,1)S(1)} %get-tuple-element.81), channel_id=1, source_target_pairs={{0,6},{1,3},{2,4},{3,1},{4,2},{5,7},{6,0},{7,5},{8,14},{9,11},{10,... | collective-permute-start | bytes 393224 | tf_op jit(solution)/shard_map/ppermute | solution.py:43
  78.5 4.6 %collective-permute-start.19 = (bf16[2,32,512]{2,1,0:T(8,128)(2,1)S(1)}, bf16[2,32,512]{2,1,0:T(8,128)(2,1)S(1)}, u32[]{:S(2)}, u32[]{:S(2)}) collective-permute-start(bf16[2,32,512]{2,1,0:T(8,128)(2,1)S(1)} %get-tuple-element.82), channel_id=1, source_target_pairs={{0,8},{1,9},{2,10},{3,11},{4,12},{5,13},{6,14},{7,15},{8,0},{9,1},... | collective-permute-start | bytes 196616 | tf_op jit(solution)/shard_map/ppermute | solution.py:43
  83.2 10.4 %collective-permute-start.20 = (bf16[2,32,1024]{2,1,0:T(8,128)(2,1)S(1)}, bf16[2,32,1024]{2,1,0:T(8,128)(2,1)S(1)}, u32[]{:S(2)}, u32[]{:S(2)}) collective-permute-start(bf16[2,32,1024]{2,1,0:T(8,128)(2,1)S(1)} %get-tuple-element.85), channel_id=1, source_target_pairs={{0,16},{1,17},{2,18},{3,19},{4,20},{5,21},{6,22},{7,23},{8,24},{9,... | collective-permute-start | bytes 393224 | tf_op jit(solution)/shard_map/ppermute | solution.py:43
  84.6 4.3 %collective-permute-start.21 = (bf16[2,32,512]{2,1,0:T(8,128)(2,1)S(1)}, bf16[2,32,512]{2,1,0:T(8,128)(2,1)S(1)}, u32[]{:S(2)}, u32[]{:S(2)}) collective-permute-start(bf16[2,32,512]{2,1,0:T(8,128)(2,1)S(1)} %get-tuple-element.86), channel_id=1, source_target_pairs={{0,224},{1,33},{2,226},{3,35},{4,228},{5,37},{6,230},{7,39},{8,232... | collective-permute-start | bytes 196616 | tf_op jit(solution)/shard_map/ppermute | solution.py:43
  86.1 5.5 %collective-permute-start.22 = (bf16[2,32,512]{2,1,0:T(8,128)(2,1)S(1)}, bf16[2,32,512]{2,1,0:T(8,128)(2,1)S(1)}, u32[]{:S(2)}, u32[]{:S(2)}) collective-permute-start(bf16[2,32,512]{2,1,0:T(8,128)(2,1)S(1)} %get-tuple-element.87), channel_id=1, source_target_pairs={{0,192},{1,65},{2,194},{3,67},{4,196},{5,69},{6,198},{7,71},{8,200... | collective-permute-start | bytes 196616 | tf_op jit(solution)/shard_map/ppermute | solution.py:43
  86.7 6.9 %collective-permute-start.23 = (bf16[2,32,512]{2,1,0:T(8,128)(2,1)S(1)}, bf16[2,32,512]{2,1,0:T(8,128)(2,1)S(1)}, u32[]{:S(2)}, u32[]{:S(2)}) collective-permute-start(bf16[2,32,512]{2,1,0:T(8,128)(2,1)S(1)} %get-tuple-element.88), channel_id=1, source_target_pairs={{0,160},{1,97},{2,162},{3,99},{4,164},{5,101},{6,166},{7,103},{8,1... | collective-permute-start | bytes 196616 | tf_op jit(solution)/shard_map/ppermute | solution.py:43
  94.2 7.5 %collective-permute-start.24 = (bf16[2,16,4096]{2,1,0:T(8,128)(2,1)S(1)}, bf16[2,16,4096]{2,1,0:T(8,128)(2,1)S(1)}, u32[]{:S(2)}, u32[]{:S(2)}) collective-permute-start(bf16[2,16,4096]{2,1,0:T(8,128)(2,1)S(1)} %split.1), channel_id=1, source_target_pairs={{0,1},{1,0},{2,3},{3,2},{4,5},{5,4},{6,7},{7,6},{8,9},{9,8},{10,11... | collective-permute-start | bytes 786440 | tf_op jit(solution)/shard_map/ppermute | solution.py:43
